TPU v7x, 32 devices: a whole 2x2x4 slice. The times are simulated.
32 devices in a mesh: replica: 2 (over x), shard: 16 (over z, y, core).
Axes of the slice: x: 2, y: 2, z: 4, core: 2. Of those that a mesh axis runs over, the one named last changes fastest.
Arguments:
- tokens: bfloat16 [5120, 1024], P(('replica', 'shard')), may hold values from -6 to 6
- segments: int32 [5120], P(('replica', 'shard')), may hold values from 0 to 9, as said below
- counts: int32 [32], P(('replica', 'shard')), may hold values from 80 to 160, as said below
- ln1_gain: bfloat16 [1024], P('shard'), may hold values from 0.5 to 1.5
- ln1_bias: bfloat16 [1024], P('shard'), may hold values from -3 to 3
- w_qkv: bfloat16 [1024, 3072], P('shard'), may hold values from -0.1875 to 0.1875
- bias_query: bfloat16 [1024], P('shard'), may hold values from -3 to 3
- bias_value: bfloat16 [1024], P('shard'), may hold values from -3 to 3
- w_proj: bfloat16 [1024, 1024], P('shard'), may hold values from -0.75 to 0.75
- bias_proj: bfloat16 [1024], P('shard'), may hold values from -3 to 3
- ln2_gain: bfloat16 [1024], P('shard'), may hold values from 0.5 to 1.5
- ln2_bias: bfloat16 [1024], P('shard'), may hold values from -3 to 3
- w_fc: bfloat16 [1024, 4096], P('shard'), may hold values from -0.1875 to 0.1875
- bias_fc: bfloat16 [4096], P('shard'), may hold values from -3 to 3
- w_out: bfloat16 [4096, 1024], P('shard'), may hold values from -0.09375 to 0.09375
- bias_out: bfloat16 [1024], P('shard'), may hold values from -3 to 3
- cotangent: bfloat16 [5120, 1024], P(('replica', 'shard')), may hold values from -6 to 6
Outputs:
- mixed: bfloat16 [5120, 1024], P(('replica', 'shard'))
- grad_tokens: float32 [5120, 1024], P(('replica', 'shard'))
- grad_ln1_gain: float32 [1024], P('shard')
- grad_ln1_bias: float32 [1024], P('shard')
- grad_w_qkv: float32 [1024, 3072], P('shard')
- grad_bias_query: float32 [1024], P('shard')
- grad_bias_value: float32 [1024], P('shard')
- grad_w_proj: float32 [1024, 1024], P('shard')
- grad_bias_proj: float32 [1024], P('shard')
- grad_ln2_gain: float32 [1024], P('shard')
- grad_ln2_bias: float32 [1024], P('shard')
- grad_w_fc: float32 [1024, 4096], P('shard')
- grad_bias_fc: float32 [4096], P('shard')
- grad_w_out: float32 [4096, 1024], P('shard')
- grad_bias_out: float32 [1024], P('shard')
Inputs may be any that keep to these rules, and one draw needn't show every extreme that they name: `counts`: in every draw one device has all 160 slots in use. `segments`: on each device the ids start at 0 on its first row, never fall and rise by at most one a row; slots at or beyond the device's count repeat the id of its last slot in use.
All inputs are finite; a program needn't handle non-finite values.
Results may differ from a plain program's by a relative error of at most 0.019.
Values may be sent and summed in bfloat16 or wider, within the bound.
No kernel may reach another device: no remote copies, remote signals or barrier semaphores. Data moves between devices by JAX's collectives and lax.ppermute only.
A program may use at most 128 MiB of HBM per device.

v0:
```python
import functools

import jax
import jax.numpy as jnp
from jax import lax
from jax.experimental import pallas as pl
from jax.experimental.pallas import tpu as pltpu
from jax.sharding import PartitionSpec as P

HEADS = 16
RANKS = 4
MESH_AXES = ("replica", "shard")
BF16 = jnp.bfloat16
F32 = jnp.float32
SMALL_ROWS = 16


def layer_norm(values, gain, shift):
    center = values - jnp.mean(values, axis=-1, keepdims=True)
    spread = jnp.mean(center * center, axis=-1, keepdims=True)
    return center * lax.rsqrt(spread + 1e-05) * gain + shift


def unit_norm(values):
    center = values - jnp.mean(values, axis=-1, keepdims=True)
    spread = jnp.mean(center * center, axis=-1, keepdims=True)
    return center * lax.rsqrt(spread + 1e-05)


def smooth_gate(values):
    return jax.nn.gelu(values, approximate=True)


def dot_rows(left, right):
    return lax.dot_general(left, right, (((0,), (0,)), ((), ())), preferred_element_type=F32)


def dot_cols(left, right):
    return lax.dot_general(left, right, (((1,), (1,)), ((), ())), preferred_element_type=F32)


def dot(left, right):
    return jnp.dot(left, right, preferred_element_type=F32)


def make_local(n_replica, n_shard):
    n_pos = n_shard // 2
    half = n_pos // 2
    head_a_shard = n_shard == HEADS
    n_pairs = n_replica // 2
    pair_groups = [[2 * i + j for i in range(n_pairs)] for j in range(2)]

    def every(move):
        pairs = []
        for r in range(n_replica):
            for p in range(n_pos):
                for c in range(2):
                    to = move(r, p, c)
                    if to is not None:
                        pairs.append((r * n_shard + p * 2 + c, to[0] * n_shard + to[1] * 2 + to[2]))
        return pairs

    ring = list(range(0, n_pos, 2)) + list(range(n_pos - 1, 0, -2))
    after = {p: ring[(i + 1) % n_pos] for i, p in enumerate(ring)}
    before = {p: ring[i - 1] for i, p in enumerate(ring)}
    core_pairs = every(lambda r, p, c: (r, p, 1 - c))
    copy_pairs = every(lambda r, p, c: (r ^ 1, p, c))
    next_pairs = every(lambda r, p, c: (r, after[p], c))
    back_pairs = every(lambda r, p, c: (r, before[p], c))
    lend_pairs = every(lambda r, p, c: (r, p ^ 1, c) if p % 2 == r % 2 else None)
    give_pairs = every(lambda r, p, c: (r, p ^ 1, c) if p % 2 != r % 2 else None)
    share_pairs = every(lambda r, p, c: (r ^ 1, p, c) if p % 2 == r % 2 else None)

    def to_core(v):
        return lax.ppermute(v, MESH_AXES, core_pairs)

    def to_copy(v):
        return lax.ppermute(v, MESH_AXES, copy_pairs)

    def to_next(v):
        return lax.ppermute(v, MESH_AXES, next_pairs)

    def to_back(v):
        return lax.ppermute(v, MESH_AXES, back_pairs)

    def cut(rows):
        return max(16, rows // 32 * 16)

    def ring_gather(chunk, place, origin):
        low = cut(chunk.shape[0])
        full = jnp.zeros((n_pos,) + chunk.shape, chunk.dtype)

        def put(full, value, offset, row=0):
            return lax.dynamic_update_slice(full, value[None], (origin(place + offset), row, 0))

        full = put(full, chunk, 0)
        forth = back = chunk
        for step in range(1, half):
            forth = to_next(forth)
            back = to_back(back)
            full = put(full, forth, -step)
            full = put(full, back, step)
        forth = to_next(forth[:low])
        back = to_back(back[low:])
        full = put(full, forth, half)
        full = put(full, back, half, low)
        return full

    def ring_scatter(full, place, origin):
        low = cut(full.shape[1])

        def term(offset):
            return lax.dynamic_index_in_dim(full, origin(place + offset), 0, keepdims=False)

        def add(left, right):
            return (left.astype(F32) + right.astype(F32)).astype(BF16)

        far = term(half)
        forth = to_next(far[:low])
        back = to_back(far[low:])
        ahead = term(half - 1)
        behind = term(1 - half)
        forth = to_next(jnp.concatenate([add(forth, ahead[:low]), ahead[low:]]))
        back = to_back(jnp.concatenate([behind[:low], add(back, behind[low:])]))
        for step in range(half - 2, 0, -1):
            forth = to_next(add(forth, term(step)))
            back = to_back(add(back, term(-step)))
        return term(0).astype(F32) + forth.astype(F32) + back.astype(F32)

    def group_gather(block):
        other = to_copy(block)
        return jnp.stack([block, to_core(block), other, to_core(other)])

    def group_scatter(parts):
        near = to_core(jnp.stack([parts[1], parts[3]]).astype(BF16)).astype(F32)
        away = to_copy((parts[2] + near[1]).astype(BF16)).astype(F32)
        return parts[0] + near[0] + away

    def local(
        tokens,
        segments,
        counts,
        ln1_gain,
        ln1_bias,
        w_qkv,
        bias_query,
        bias_value,
        w_proj,
        bias_proj,
        ln2_gain,
        ln2_bias,
        w_fc,
        bias_fc,
        w_out,
        bias_out,
        cotangent,
    ):
        row_count, width = tokens.shape
        head_width = width // HEADS
        own_rows = width // n_shard
        chip_rows = 2 * own_rows
        own_hidden = w_out.shape[0]
        piece = own_hidden // 2
        groups = HEADS // RANKS
        scale = head_width ** (-0.5)
        replica_at = lax.axis_index("replica")
        shard_at = lax.axis_index("shard")
        x = replica_at % 2
        c = shard_at % 2
        p = shard_at // 2
        rank = 2 * x + c
        place = jnp.where(p % 2 == 0, p // 2, n_pos - 1 - p // 2)

        def origin(index):
            index = index % n_pos
            return jnp.where(index < half, 2 * index, 2 * (n_pos - 1 - index) + 1)

        def by_core(mine, other):
            return jnp.where(c == 0, jnp.stack([mine, other]), jnp.stack([other, mine]))

        position = jnp.arange(row_count, dtype=jnp.int32)
        in_use = (position < counts[0]).astype(F32)
        notes = jnp.stack([segments.astype(BF16), in_use.astype(BF16)])
        notes = jnp.pad(notes, ((0, SMALL_ROWS - 2), (0, width - row_count)))
        seen = group_gather(jnp.concatenate([tokens, notes]))
        tokens_all = seen[:, :row_count].reshape(RANKS * row_count, width)
        seg_all = seen[:, row_count, :row_count]
        use_all = seen[:, row_count + 1, :row_count]

        def qkv_part(which):
            view = w_qkv.reshape(own_rows, 3, groups, RANKS, head_width)
            return lax.dynamic_index_in_dim(view, which, 3, keepdims=False).reshape(own_rows, -1)

        def fc_part(core):
            view = w_fc.reshape(own_rows, n_pos, 4, piece)
            part = lax.dynamic_index_in_dim(view, 2 * core + x, 2, keepdims=False)
            return part.reshape(own_rows, -1)

        vectors = [ln1_gain, ln1_bias, bias_query, bias_value, bias_proj, ln2_gain, ln2_bias, bias_out, bias_fc]
        starts = [0]
        for vector in vectors:
            starts.append(starts[-1] + vector.shape[0])
        n_small = starts[-1]
        qkv_width = 3 * groups * head_width
        small = jnp.concatenate(vectors)[None]
        small = jnp.pad(small, ((0, SMALL_ROWS - 1), (0, 0)))
        both_small = by_core(small[0], to_core(small)[0])
        qkv_chunk = by_core(qkv_part(rank), to_core(qkv_part(rank ^ 1))).reshape(chip_rows, qkv_width)
        if head_a_shard:
            lent = lax.ppermute(w_proj[:, width // 2 :], MESH_AXES, lend_pairs)
            proj_half = jnp.where(p % 2 == x, w_proj[:, : width // 2], lent)
            proj_chunk = jnp.concatenate([proj_half[:, : width // 4], proj_half[:, width // 4 :]])
        else:
            proj_chunk = jnp.zeros((chip_rows, width // 4), BF16)
        small_chunk = jnp.pad(both_small, ((0, SMALL_ROWS - 2), (0, width - n_small)))
        first_chunk = jnp.concatenate(
            [jnp.concatenate([qkv_chunk, proj_chunk], axis=1), small_chunk]
        )
        fc_chunk = by_core(fc_part(c), to_core(fc_part(1 - c))).reshape(chip_rows, n_pos * piece)
        out_chunk = lax.dynamic_slice_in_dim(w_out, x * piece, piece, 0)

        first_full = ring_gather(first_chunk, place, origin)
        fc_weight = ring_gather(fc_chunk, place, origin).reshape(width, n_pos * piece)
        out_weight = ring_gather(out_chunk, place, origin).reshape(n_pos * piece, width)

        qkv_weight = first_full[:, :chip_rows, :qkv_width].reshape(width, qkv_width)
        if head_a_shard:
            proj_full = first_full[:, :chip_rows, qkv_width:].reshape(
                n_pos // 2, 2, 2, own_rows, width // 4
            )
            proj_full = jnp.where(x == 0, proj_full, proj_full[:, ::-1])
            proj_weight = proj_full.transpose(0, 3, 1, 2, 4).reshape(groups * head_width, width)
        else:
            proj_full = lax.all_gather(w_proj, "shard", axis=0, tiled=True)
            proj_full = proj_full.reshape(groups, RANKS, head_width, width)
            proj_weight = lax.dynamic_index_in_dim(proj_full, rank, 1, keepdims=False)
            proj_weight = proj_weight.reshape(groups * head_width, width)
        smalls = first_full[:, chip_rows : chip_rows + 2, :n_small].reshape(n_shard, n_small)
        params = [
            smalls[:, starts[i] : starts[i + 1]].reshape(-1).astype(F32) for i in range(len(vectors))
        ]
        gain_one, shift_one, query_shift, value_shift, proj_shift, gain_two, shift_two, out_shift, fc_shift = params

        def rank_heads(vector):
            view = vector.reshape(groups, RANKS, head_width)
            return lax.dynamic_index_in_dim(view, rank, 1, keepdims=False).reshape(-1)

        fc_shift = lax.dynamic_index_in_dim(
            fc_shift.reshape(n_pos, 4, piece), 2 * c + x, 1, keepdims=False
        ).reshape(-1)
        qkv_shift = jnp.concatenate(
            [
                rank_heads(query_shift),
                jnp.zeros((groups * head_width,), F32),
                rank_heads(value_shift),
            ]
        )

        unit_one = unit_norm(tokens_all.astype(F32))
        input_one = (unit_one * gain_one + shift_one).astype(BF16)
        qkv_rows = (dot(input_one, qkv_weight) + qkv_shift).astype(BF16)
        qkv_view = qkv_rows.reshape(RANKS, row_count, 3, groups, head_width)
        queries, keys_rows, values_rows = qkv_view[:, :, 0], qkv_view[:, :, 1], qkv_view[:, :, 2]
        visible = (
            (seg_all[:, :, None] == seg_all[:, None, :])
            & (position[None, None, :] <= position[None, :, None])
            & (use_all[:, None, :] > 0)
        )[:, None]
        scores = scale * jnp.einsum("bqhd,bkhd->bhqk", queries, keys_rows, preferred_element_type=F32)
        scores = jnp.where(visible, scores, -1e30)
        top_score = jnp.max(scores, axis=-1, keepdims=True)
        expo = jnp.exp(scores - top_score)
        probs = expo / jnp.sum(expo, axis=-1, keepdims=True)
        probs_low = probs.astype(BF16)
        context = (
            jnp.einsum("bhqk,bkhd->bqhd", probs_low, values_rows, preferred_element_type=F32)
            .reshape(RANKS * row_count, groups * head_width)
            .astype(BF16)
        )
        block_shape = (RANKS, row_count, width)
        stream = tokens.astype(F32)
        middle = stream + proj_shift + group_scatter(dot(context, proj_weight).reshape(block_shape))

        normed_two, norm_two_back = jax.vjp(layer_norm, middle, gain_two, shift_two)
        input_two = group_gather(normed_two.astype(BF16)).reshape(RANKS * row_count, width)
        pre_act = dot(input_two, fc_weight) + fc_shift
        gate_value, gate_back = jax.vjp(smooth_gate, pre_act)
        hidden = gate_value.astype(BF16)
        branch_two = group_scatter(dot(hidden, out_weight).reshape(block_shape)) + out_shift
        mixed = (in_use[:, None] * (middle + branch_two)).astype(BF16)

        d_top = in_use[:, None] * cotangent.astype(F32)
        d_out = group_gather(d_top.astype(BF16)).reshape(RANKS * row_count, width)
        grad_w_out = dot_rows(hidden, d_out).astype(BF16).reshape(n_pos, piece, width)
        d_pre = gate_back(dot_cols(d_out, out_weight))[0].astype(BF16)
        grad_w_fc = dot_rows(input_two, d_pre).astype(BF16).reshape(n_pos, chip_rows, n_pos * piece)
        d_input_two = group_scatter(dot_cols(d_pre, fc_weight).reshape(block_shape))
        d_mid_norm, grad_gain_two, grad_shift_two = norm_two_back(d_input_two)
        d_middle = d_top + d_mid_norm
        own_w_out = ring_scatter(grad_w_out, place, origin)
        own_w_fc = ring_scatter(grad_w_fc, place, origin)

        d_branch = group_gather(d_middle.astype(BF16)).reshape(RANKS * row_count, width)
        grad_w_proj = dot_rows(context, d_branch)
        d_context = (
            dot_cols(d_branch, proj_weight)
            .astype(BF16)
            .reshape(RANKS, row_count, groups, head_width)
        )
        d_values = jnp.einsum("bhqk,bqhd->bkhd", probs_low, d_context, preferred_element_type=F32)
        d_probs = jnp.einsum("bqhd,bkhd->bhqk", d_context, values_rows, preferred_element_type=F32)
        d_scores = (
            probs * (d_probs - jnp.sum(probs * d_probs, axis=-1, keepdims=True))
        ).astype(BF16)
        d_queries = scale * jnp.einsum(
            "bhqk,bkhd->bqhd", d_scores, keys_rows, preferred_element_type=F32
        )
        d_keys = scale * jnp.einsum("bhqk,bqhd->bkhd", d_scores, queries, preferred_element_type=F32)
        d_qkv = (
            jnp.stack([d_queries, d_keys, d_values], axis=2)
            .reshape(RANKS * row_count, qkv_width)
            .astype(BF16)
        )
        grad_w_qkv = dot_rows(input_one, d_qkv).astype(BF16).reshape(n_pos, chip_rows, qkv_width)
        d_input_one = dot_cols(d_qkv, qkv_weight)
        grad_gain_one = jnp.sum(d_input_one * unit_one, axis=0)
        grad_shift_one = jnp.sum(d_input_one, axis=0)
        d_qkv_sums = jnp.sum(d_qkv.astype(F32), axis=0)

        def own_term(values):
            return jnp.sum(values.astype(BF16).astype(F32), axis=0)

        def at_rank(sums):
            view = sums.reshape(groups, 1, head_width)
            mine = jnp.arange(RANKS)[None, :, None] == rank
            return jnp.where(mine, view, 0.0).reshape(-1)

        fc_sums = jnp.sum(d_pre.astype(F32), axis=0).reshape(n_pos, 1, piece)
        fc_sums = jnp.where(jnp.arange(4)[None, :, None] == 2 * c + x, fc_sums, 0.0).reshape(-1)
        small_terms = [
            grad_gain_one,
            grad_shift_one,
            at_rank(d_qkv_sums[: groups * head_width]),
            at_rank(d_qkv_sums[2 * groups * head_width :]),
            own_term(d_middle),
            grad_gain_two,
            grad_shift_two,
            own_term(d_top),
            fc_sums,
        ]
        small_terms = jnp.concatenate(
            [term.reshape(n_shard, -1) for term in small_terms], axis=1
        ).astype(BF16)
        small_terms = jnp.pad(
            small_terms.reshape(n_pos, 2, n_small),
            ((0, 0), (0, SMALL_ROWS - 2), (0, width - n_small)),
        )
        if head_a_shard:
            proj_terms = grad_w_proj.astype(BF16).reshape(n_pos // 2, own_rows, 2, 2, width // 4)
            proj_terms = proj_terms.transpose(0, 2, 3, 1, 4)
            proj_terms = jnp.where(x == 0, proj_terms, proj_terms[:, ::-1])
            proj_terms = proj_terms.reshape(n_pos, chip_rows, width // 4)
        else:
            proj_terms = jnp.zeros((n_pos, chip_rows, width // 4), BF16)
        first_terms = jnp.concatenate(
            [jnp.concatenate([grad_w_qkv, proj_terms], axis=2), small_terms], axis=1
        )
        own_first = ring_scatter(first_terms, place, origin)
        d_in_norm = jax.vjp(unit_norm, stream)[1](
            group_scatter(d_input_one.reshape(block_shape)) * gain_one
        )[0]
        grad_tokens = d_middle + d_in_norm

        def rows_of(chunk, core):
            return lax.dynamic_slice_in_dim(chunk, core * own_rows, own_rows, 0)

        def by_copy(mine, other):
            return jnp.where(x == 0, jnp.stack([mine, other]), jnp.stack([other, mine]))

        own_w_out = own_w_out.astype(BF16)
        grad_w_out = by_copy(own_w_out, to_copy(own_w_out)).reshape(own_hidden, width)

        own_w_fc = own_w_fc.astype(BF16)
        fc_rows = by_core(rows_of(own_w_fc, c), to_core(rows_of(own_w_fc, 1 - c)))
        fc_rows = by_copy(fc_rows, to_copy(fc_rows))
        fc_rows = fc_rows.reshape(2, 2, own_rows, n_pos, piece)
        grad_w_fc = fc_rows.transpose(2, 3, 1, 0, 4).reshape(own_rows, -1)

        own_first = own_first.astype(BF16)
        own_qkv = own_first[:chip_rows, :qkv_width]
        qkv_grad = by_core(rows_of(own_qkv, c), to_core(rows_of(own_qkv, 1 - c)))
        qkv_grad = by_copy(qkv_grad, to_copy(qkv_grad))
        qkv_grad = qkv_grad.reshape(2, 2, own_rows, 3, groups, head_width)
        grad_w_qkv = qkv_grad.transpose(2, 3, 4, 0, 1, 5).reshape(own_rows, -1)

        own_small = own_first[chip_rows:, :n_small]
        near_small = to_core(own_small)
        small_sum = jnp.where(
            c == 0,
            own_small[0].astype(F32) + near_small[0].astype(F32),
            own_small[1].astype(F32) + near_small[1].astype(F32),
        )
        small_send = jnp.pad(small_sum[None].astype(BF16), ((0, SMALL_ROWS - 1), (0, 0)))
        small_sum = small_sum + to_copy(small_send)[0].astype(F32)

        if head_a_shard:
            own_proj = own_first[:chip_rows, qkv_width:]
            given = lax.ppermute(own_proj, MESH_AXES, give_pairs)
            proj_rows = jnp.stack([own_proj, given]).reshape(2, 2, own_rows, width // 4)
            proj_rows = proj_rows.transpose(2, 0, 1, 3).reshape(own_rows, width)
            shared = lax.ppermute(proj_rows, MESH_AXES, share_pairs)
            grad_w_proj = jnp.where(p % 2 == x, proj_rows, shared)
        else:
            proj_rows = grad_w_proj.astype(BF16).reshape(groups, 1, head_width, width)
            mine = jnp.arange(RANKS)[None, :, None, None] == rank
            proj_rows = jnp.where(mine, proj_rows, 0).reshape(width, width)
            proj_rows = lax.psum_scatter(proj_rows, "shard", scatter_dimension=0, tiled=True)
            grad_w_proj = proj_rows.astype(F32) + to_copy(proj_rows).astype(F32)

        if n_pairs > 1:
            grad_w_out, grad_w_fc, grad_w_qkv, grad_w_proj, small_sum = lax.psum(
                tuple(
                    value.astype(BF16)
                    for value in (grad_w_out, grad_w_fc, grad_w_qkv, grad_w_proj, small_sum)
                ),
                "replica",
                axis_index_groups=pair_groups,
            )
        small_sum = small_sum.astype(F32)
        small_grads = [small_sum[starts[i] : starts[i + 1]] for i in range(len(vectors))]
        g_gain_one, g_shift_one, g_query, g_value, g_proj, g_gain_two, g_shift_two, g_out, g_fc = small_grads
        return (
            mixed,
            grad_tokens,
            g_gain_one,
            g_shift_one,
            grad_w_qkv.astype(F32),
            g_query,
            g_value,
            grad_w_proj.astype(F32),
            g_proj,
            g_gain_two,
            g_shift_two,
            grad_w_fc.astype(F32),
            g_fc,
            grad_w_out.astype(F32),
            g_out,
        )

    return local

LANES = 128
HALF = 64
VMEM_BYTES = 56 * 1024 * 1024
ORIGINS = 9
AT_X, AT_C, AT_Y, AT_COUNT = 9, 10, 11, 12
VMEM_SPEC = pl.BlockSpec(memory_space=pltpu.VMEM)
SMEM_SPEC = pl.BlockSpec(memory_space=pltpu.SMEM)
ANY_SPEC = pl.BlockSpec(memory_space=pl.ANY)


def kernel_call(body, in_specs, outs, scratch=(), flops=0, moved=4 << 20):
    return pl.pallas_call(
        body,
        out_shape=tuple(jax.ShapeDtypeStruct(shape, dtype) for shape, dtype in outs),
        in_specs=list(in_specs),
        out_specs=tuple(VMEM_SPEC for _ in outs),
        scratch_shapes=list(scratch),
        compiler_params=pltpu.CompilerParams(vmem_limit_bytes=VMEM_BYTES),
        cost_estimate=pl.CostEstimate(flops=flops, bytes_accessed=moved, transcendentals=0),
    )


def low_half(shape):
    return lax.broadcasted_iota(jnp.int32, shape, len(shape) - 1) < HALF


def turn(values):
    return jnp.concatenate([values[:, HALF:], values[:, :HALF]], axis=1)


def join(c, first, second, low):
    even = jnp.where(low, first, turn(second))
    odd = jnp.where(low, turn(first), second)
    return jnp.where(c == 0, even, odd)


def statistics(values):
    center = values - jnp.mean(values, axis=-1, keepdims=True)
    spread = jnp.mean(center * center, axis=-1, keepdims=True)
    return center, lax.rsqrt(spread + 1e-05)


def norm_back(unit, inverse, d_unit):
    along = jnp.mean(d_unit * unit, axis=-1, keepdims=True)
    return inverse * (d_unit - jnp.mean(d_unit, axis=-1, keepdims=True) - unit * along)


def used_rows(info, rows):
    return (lax.broadcasted_iota(jnp.int32, (rows, 1), 0) < info[AT_COUNT]).astype(F32)


def prepare_body(info, tokens, notes, cotangent, w_qkv, w_fc, vectors, fc_shift, seen, d_out, sent, own):
    rows, width = tokens.shape
    own_rows = w_qkv.shape[0]
    x, c = info[AT_X], info[AT_C]
    seen[:rows, :] = tokens[...]
    seen[rows:, :] = notes[...]
    d_out[...] = (used_rows(info, rows) * cotangent[...].astype(F32)).astype(BF16)
    low = low_half((own_rows, LANES))
    for out in (sent, own):
        core = c if out is own else 1 - c
        for pair in range(w_qkv.shape[1] // (8 * HALF)):
            at = pair * 8 * HALF + x * LANES
            first = w_qkv[:, pl.ds(pl.multiple_of(at, LANES), LANES)].astype(F32)
            second = w_qkv[:, pl.ds(pl.multiple_of(at + 4 * HALF, LANES), LANES)].astype(F32)
            out[:own_rows, pair * LANES : (pair + 1) * LANES] = join(core, first, second, low).astype(BF16)
        for p in range(w_fc.shape[1] // (4 * LANES)):
            at = pl.multiple_of(p * 4 * LANES + (2 * core + x) * LANES, LANES)
            out[own_rows : 2 * own_rows, p * LANES : (p + 1) * LANES] = w_fc[:, pl.ds(at, LANES)]
        out[:own_rows, 3 * width // 4 :] = jnp.zeros((own_rows, width // 4), BF16)
        out[2 * own_rows :, :] = jnp.zeros((SMALL_ROWS, width), BF16)
        shifts = fc_shift[...].astype(F32)
        shift = jnp.broadcast_to(jnp.where(x == 0, shifts[0:1], shifts[1:2]), (8, LANES))
        rest = vectors[...].astype(F32)
        rest = jnp.where(lax.broadcasted_iota(jnp.int32, rest.shape, 0) == 6, shift, rest)
        out[2 * own_rows : 2 * own_rows + 8, :LANES] = rest.astype(BF16)


def chunks_body(info, own, got, w_proj, lent, w_out, first, second):
    own_rows, width = w_proj.shape
    x, c, y = info[AT_X], info[AT_C], info[AT_Y]
    qkv = 3 * width // 4
    for core in range(2):
        rows = slice(core * own_rows, (core + 1) * own_rows)
        mine = c == core
        first[rows, :qkv] = jnp.where(mine, own[:own_rows, :qkv], got[:own_rows, :qkv])
        second[rows, :] = jnp.where(
            mine, own[own_rows : 2 * own_rows, :], got[own_rows : 2 * own_rows, :]
        )
    half = jnp.where(x == y, w_proj[:, : width // 2], lent[...])
    first[:own_rows, qkv:] = half[:, : width // 4]
    first[own_rows : 2 * own_rows, qkv:] = half[:, width // 4 :]
    piece = w_out.shape[0] // 2
    second[2 * own_rows :, :] = w_out[pl.ds(pl.multiple_of(x * piece, piece), piece), :]
    mine = own[2 * own_rows :, :LANES].astype(F32)
    other = got[2 * own_rows :, :LANES].astype(F32)
    low = low_half(mine.shape)
    joined = jnp.where(
        c == 0, jnp.where(low, mine, turn(other)), jnp.where(low, other, turn(mine))
    )
    both = lax.broadcasted_iota(jnp.int32, mine.shape, 0) < 6
    first[2 * own_rows :, :] = jnp.zeros((SMALL_ROWS, width), BF16)
    first[2 * own_rows :, :LANES] = jnp.where(both, joined, mine).astype(BF16)


def run_copies(copies, sems):
    started = []
    for i, (source, target) in enumerate(copies):
        copy = pltpu.make_async_copy(source, target, sems.at[i])
        copy.start()
        started.append(copy)
    return started


def attention_body(info, *refs):
    blocks, chunks = refs[:RANKS], refs[RANKS : RANKS + ORIGINS]
    normed, qkv, probs, context, send, keep_own, keep_away, qkv_weight, proj_weight, smalls = refs[
        RANKS + ORIGINS : RANKS + ORIGINS + 10
    ]
    masks, sems = refs[RANKS + ORIGINS + 10 :]
    x = info[AT_X]
    width = normed.shape[1]
    rows = normed.shape[0] // RANKS
    chip_rows = chunks[0].shape[0] - SMALL_ROWS
    own_rows = chip_rows // 2
    cols = 3 * width // 4
    copies = []
    for i, chunk in enumerate(chunks):
        at = info[i]
        start = chunks[i - 1].shape[0] if i == ORIGINS - 1 else 0
        stop = start + chunk.shape[0]
        for part in range(2):
            top = part * own_rows
            if start <= top and top + own_rows <= stop:
                source = pl.ds(top - start, own_rows)
                copies.append(
                    (
                        chunk.at[source, pl.ds(0, cols)],
                        qkv_weight.at[pl.ds(pl.multiple_of(at * chip_rows + top, own_rows), own_rows), :],
                    )
                )
                side = lax.rem(at + x, 2) * (width // 2) + part * (width // 4)
                copies.append(
                    (
                        chunk.at[source, pl.ds(cols, width // 4)],
                        proj_weight.at[
                            pl.ds(pl.multiple_of(lax.div(at, 2) * own_rows, own_rows), own_rows),
                            pl.ds(pl.multiple_of(side, LANES), width // 4),
                        ],
                    )
                )
        if stop > chip_rows:
            copies.append(
                (
                    chunk.at[pl.ds(chip_rows - start, SMALL_ROWS), pl.ds(0, LANES)],
                    smalls.at[:, pl.ds(pl.multiple_of(at * LANES, LANES), LANES)],
                )
            )
    started = run_copies(copies, sems)

    down = lax.broadcasted_iota(jnp.int32, (rows, rows), 0)
    across = lax.broadcasted_iota(jnp.int32, (rows, rows), 1)
    for b, block in enumerate(blocks):
        notes = block[rows : rows + SMALL_ROWS, : 2 * LANES].astype(F32)
        seg_row, use_row = notes[0:1, :rows], notes[1:2, :rows]
        seg_column = jnp.sum(jnp.where(down == across, seg_row, 0.0), axis=1, keepdims=True)
        visible = (seg_column == seg_row) & (across <= down) & (use_row > 0)
        masks[b] = jnp.where(visible, 1.0, 0.0)
    for copy in started:
        copy.wait()
    gain = smalls[0:1, :].astype(F32)
    shift = smalls[1:2, :].astype(F32)
    for b, block in enumerate(blocks):
        center, inverse = statistics(block[:rows, :].astype(F32))
        normed[b * rows : (b + 1) * rows, :] = (center * inverse * gain + shift).astype(BF16)

    low_row = low_half((8, LANES))
    biases = jnp.broadcast_to(smalls[7:8, :].astype(F32), (8, width))
    query_shift, value_shift = [], []
    for pair in range(2):
        first, second = (
            jnp.where(
                x == 0,
                biases[:, z * 2 * LANES : z * 2 * LANES + LANES],
                biases[:, z * 2 * LANES + LANES : (z + 1) * 2 * LANES],
            )
            for z in (2 * pair, 2 * pair + 1)
        )
        query_shift.append(jnp.where(low_row, first, turn(second))[0:1])
        value_shift.append(jnp.where(low_row, turn(first), second)[0:1])
    third = width // 4
    for n in range(3):
        product = dot(normed[...], qkv_weight[:, n * third : (n + 1) * third])
        if n != 1:
            product = product + jnp.concatenate(value_shift if n else query_shift, axis=1)
        qkv[:, n * third : (n + 1) * third] = product.astype(BF16)

    scale = HALF ** (-0.5)
    low = low_half((1, LANES))
    keep_low = jnp.where(low, 1.0, 0.0).astype(BF16)
    keep_high = jnp.where(low, 0.0, 1.0).astype(BF16)

    def attend(b, carry):
        at = pl.ds(pl.multiple_of(b * rows, rows), rows)
        mask = masks[b] > 0.5
        for pair in range(2):
            lanes = pair * LANES
            queries = qkv[at, lanes : lanes + LANES]
            keys = qkv[at, third + lanes : third + lanes + LANES]
            values = qkv[at, 2 * third + lanes : 2 * third + lanes + LANES]
            outs = []
            for side, keep in enumerate((keep_low, keep_high)):
                scores = jnp.where(mask, scale * dot_cols(queries * keep, keys), -1e30)
                expo = jnp.exp(scores - jnp.max(scores, axis=-1, keepdims=True))
                share = (expo / jnp.sum(expo, axis=-1, keepdims=True)).astype(BF16)
                probs[b * 4 + 2 * pair + side] = share
                outs.append(dot(share, values))
            context[at, lanes : lanes + LANES] = jnp.where(low, outs[0], outs[1]).astype(BF16)
        return carry

    lax.fori_loop(0, RANKS, attend, 0)
    for n in range(4):
        columns = slice(n * third, (n + 1) * third)
        store_parts(dot(context[...], proj_weight[:, columns]), columns, rows, send, keep_own, keep_away)


def store_parts(product, columns, rows, send, keep_own, keep_away):
    keep_own[:, columns] = product[:rows]
    send[0, :, columns] = product[rows : 2 * rows].astype(BF16)
    keep_away[:, columns] = product[2 * rows : 3 * rows]
    send[1, :, columns] = product[3 * rows :].astype(BF16)


def total(keep_own, near, away):
    return keep_own[...] + near[0].astype(F32) + away[...].astype(F32)


def second_norm_body(tokens, keep_own, near, away, smalls, middle, normed):
    values = tokens[...].astype(F32) + smalls[2:3, :].astype(F32) + total(keep_own, near, away)
    middle[...] = values
    center, inverse = statistics(values)
    gain, shift = smalls[3:4, :].astype(F32), smalls[4:5, :].astype(F32)
    normed[...] = (center * inverse * gain + shift).astype(BF16)


def feed_body(info, *refs):
    inputs, d_outs = refs[:RANKS], refs[RANKS : 2 * RANKS]
    chunks, smalls = refs[2 * RANKS : 2 * RANKS + ORIGINS], refs[2 * RANKS + ORIGINS]
    given, d_out, hidden, d_pre, send, keep_own, keep_away, sums, out_weight = refs[
        2 * RANKS + ORIGINS + 1 : 2 * RANKS + ORIGINS + 10
    ]
    fc_weight, sems = refs[2 * RANKS + ORIGINS + 10 :]
    rows = inputs[0].shape[0]
    width = given.shape[1]
    chip_rows = chunks[0].shape[0] // 2
    copies = []
    for i, chunk in enumerate(chunks):
        at = pl.ds(pl.multiple_of(info[i] * chip_rows, chip_rows), chip_rows)
        if i != ORIGINS - 1:
            copies.append((chunk.at[pl.ds(0, chip_rows), :], fc_weight.at[at, :]))
        if i != ORIGINS - 2:
            start = 0 if i == ORIGINS - 1 else chip_rows
            copies.append((chunk.at[pl.ds(start, chip_rows), :], out_weight.at[at, :]))
    started = run_copies(copies, sems)
    for b in range(RANKS):
        given[b * rows : (b + 1) * rows, :] = inputs[b][...]
        d_out[b * rows : (b + 1) * rows, :] = d_outs[b][...]
    for copy in started:
        copy.wait()
    tile = 2 * LANES
    root = (2.0 / jnp.pi) ** 0.5
    sums[...] = jnp.zeros(sums.shape, F32)

    def units(n, carry):
        columns = pl.ds(pl.multiple_of(n * tile, tile), tile)
        pre = dot(given[...], fc_weight[:, columns]) + smalls[6:7, columns].astype(F32)
        d_hidden = dot_cols(d_out[...], out_weight[columns, :])
        square = pre * pre
        bend = jnp.tanh(root * pre * (1.0 + 0.044715 * square))
        hidden[:, columns] = (0.5 * pre * (1.0 + bend)).astype(BF16)
        slope = 0.5 * (1.0 + bend) + 0.5 * pre * (1.0 - bend * bend) * root * (
            1.0 + 3.0 * 0.044715 * square
        )
        low = (d_hidden * slope).astype(BF16)
        d_pre[:, columns] = low
        sums[6:7, columns] = jnp.sum(low.astype(F32), axis=0, keepdims=True)
        return carry

    lax.fori_loop(0, width // tile, units, 0)
    for n in range(width // tile):
        columns = slice(n * tile, (n + 1) * tile)
        product = dot_cols(d_pre[...], fc_weight[columns, :])
        store_parts(product, columns, rows, send, keep_own, keep_away)


def feed_out_body(hidden, out_weight, send, keep_own, keep_away):
    rows = keep_own.shape[0]
    tile = 2 * LANES
    for n in range(out_weight.shape[1] // tile):
        columns = slice(n * tile, (n + 1) * tile)
        store_parts(dot(hidden[...], out_weight[:, columns]), columns, rows, send, keep_own, keep_away)


def mixed_body(info, middle, keep_own, near, away, smalls, mixed):
    values = middle[...] + total(keep_own, near, away) + smalls[5:6, :].astype(F32)
    mixed[...] = (used_rows(info, middle.shape[0]) * values).astype(BF16)


def second_back_body(info, middle, cotangent, keep_own, near, away, smalls, d_middle, d_branch, sums):
    d_values = total(keep_own, near, away)
    d_top = used_rows(info, middle.shape[0]) * cotangent[...].astype(F32)
    center, inverse = statistics(middle[...])
    unit = center * inverse
    result = d_top + norm_back(unit, inverse, d_values * smalls[3:4, :].astype(F32))
    d_middle[...] = result
    low = result.astype(BF16)
    d_branch[...] = low
    sums[...] = jnp.zeros(sums.shape, F32)
    sums[2:3, :] = jnp.sum(low.astype(F32), axis=0, keepdims=True)
    sums[3:4, :] = jnp.sum(d_values * unit, axis=0, keepdims=True)
    sums[4:5, :] = jnp.sum(d_values, axis=0, keepdims=True)
    sums[5:6, :] = jnp.sum(d_top, axis=0, keepdims=True)


def attention_back_body(info, *refs):
    d_branches, blocks = refs[:RANKS], refs[RANKS : 2 * RANKS]
    qkv, probs, qkv_weight, proj_weight, sums_two, sums_fc = refs[2 * RANKS : 2 * RANKS + 6]
    d_branch, d_qkv, send, keep_own, keep_away, sums = refs[2 * RANKS + 6 : 2 * RANKS + 12]
    (d_context,) = refs[2 * RANKS + 12 :]
    rows = d_branches[0].shape[0]
    width = d_branch.shape[1]
    third = width // 4
    x = info[AT_X]
    for b in range(RANKS):
        d_branch[b * rows : (b + 1) * rows, :] = d_branches[b][...]
    d_context[...] = dot_cols(d_branch[...], proj_weight[...]).astype(BF16)
    scale = HALF ** (-0.5)
    low = low_half((1, LANES))
    keep_low = jnp.where(low, 1.0, 0.0).astype(BF16)
    keep_high = jnp.where(low, 0.0, 1.0).astype(BF16)

    def attend(b, carry):
        at = pl.ds(pl.multiple_of(b * rows, rows), rows)
        for pair in range(2):
            lanes = pair * LANES
            queries = qkv[at, lanes : lanes + LANES]
            keys = qkv[at, third + lanes : third + lanes + LANES]
            values = qkv[at, 2 * third + lanes : 2 * third + lanes + LANES]
            d_out = d_context[at, lanes : lanes + LANES]
            results = []
            for side, keep in enumerate((keep_low, keep_high)):
                share = probs[b * 4 + 2 * pair + side]
                wide = share.astype(F32)
                d_values = dot_rows(share, d_out)
                d_probs = dot_cols(d_out * keep, values)
                d_scores = wide * (d_probs - jnp.sum(wide * d_probs, axis=-1, keepdims=True))
                d_scores = d_scores.astype(BF16)
                results.append(
                    (scale * dot(d_scores, keys), scale * dot_rows(d_scores, queries), d_values)
                )
            for n in range(3):
                merged = jnp.where(low, results[0][n], results[1][n]).astype(BF16)
                d_qkv[at, n * third + lanes : n * third + lanes + LANES] = merged
        return carry

    lax.fori_loop(0, RANKS, attend, 0)
    sums[0:8, :] = sums_two[...] + sums_fc[...]
    sums[8:, :] = jnp.zeros((SMALL_ROWS - 8, width), F32)
    stats = []
    for block in blocks:
        values = block[:rows, :].astype(F32)
        mean = jnp.mean(values, axis=-1, keepdims=True)
        center = values - mean
        stats.append((mean, lax.rsqrt(jnp.mean(center * center, axis=-1, keepdims=True) + 1e-05)))
    for n in range(4):
        columns = slice(n * third, (n + 1) * third)
        product = dot_cols(d_qkv[...], qkv_weight[columns, :])
        store_parts(product, columns, rows, send, keep_own, keep_away)
        sums[1:2, columns] = jnp.sum(product, axis=0, keepdims=True)
        along = jnp.zeros((1, third), F32)
        for b, block in enumerate(blocks):
            mean, inverse = stats[b]
            unit = (block[:rows, columns].astype(F32) - mean) * inverse
            along = along + jnp.sum(product[b * rows : (b + 1) * rows] * unit, axis=0, keepdims=True)
        sums[0:1, columns] = along
    low_row = low_half((8, LANES))
    for pair in range(2):
        lanes = pair * LANES
        d_queries = jnp.sum(d_qkv[:, lanes : lanes + LANES].astype(F32), axis=0, keepdims=True)
        d_values = jnp.sum(
            d_qkv[:, 2 * third + lanes : 2 * third + lanes + LANES].astype(F32), axis=0, keepdims=True
        )
        d_queries = jnp.broadcast_to(d_queries, (8, LANES))
        d_values = jnp.broadcast_to(d_values, (8, LANES))
        even = jnp.where(low_row, d_queries, turn(d_values))[0:1]
        odd = jnp.where(low_row, turn(d_queries), d_values)[0:1]
        for z, group in ((2 * pair, even), (2 * pair + 1, odd)):
            for y in range(2):
                start = (2 * z + y) * LANES
                sums[7:8, start : start + LANES] = jnp.where(x == y, group, 0.0)


def first_back_body(tokens, d_middle, keep_own, near, away, smalls, result):
    center, inverse = statistics(tokens[...].astype(F32))
    d_unit = total(keep_own, near, away) * smalls[0:1, :].astype(F32)
    result[...] = d_middle[...] + norm_back(center * inverse, inverse, d_unit)


def hidden_grads_body(info, own_fc, near_fc, other, grad_fc, grad_out):
    x, c = info[AT_X], info[AT_C]
    own_rows = near_fc.shape[0]
    piece = own_fc.shape[0] - 2 * own_rows
    mine = own_fc[pl.ds(pl.multiple_of(c * own_rows, own_rows), own_rows), :].astype(F32)
    near = near_fc[...].astype(F32)
    far_mine = other[:own_rows, :].astype(F32)
    far_near = other[own_rows : 2 * own_rows, :].astype(F32)
    width = own_fc.shape[1]
    for copy in range(2):
        here = x == copy
        same = jnp.where(here, mine, far_mine)
        cross = jnp.where(here, near, far_near)
        for core in range(2):
            part = jnp.where(c == core, same, cross)
            for p in range(width // LANES):
                at = p * 4 * LANES + core * 2 * LANES + copy * LANES
                grad_fc[:, at : at + LANES] = part[:, p * LANES : (p + 1) * LANES]
        grad_out[copy * piece : (copy + 1) * piece, :] = jnp.where(
            here, own_fc[2 * own_rows :, :].astype(F32), other[2 * own_rows :, :].astype(F32)
        )


def first_message_body(info, own, near, given, message):
    c = info[AT_C]
    width = own.shape[1]
    qkv = 3 * width // 4
    own_rows = (own.shape[0] - SMALL_ROWS) // 2
    rows = pl.ds(pl.multiple_of(c * own_rows, own_rows), own_rows)
    message[:own_rows, :qkv] = own[rows, :qkv]
    message[:own_rows, qkv : 2 * qkv] = near[:own_rows, :qkv]
    at = 2 * qkv
    quarter = width // 4
    for source in (own, given):
        shift = qkv if source is own else 0
        for part in range(2):
            message[:own_rows, at : at + quarter] = source[
                part * own_rows : (part + 1) * own_rows, shift : shift + quarter
            ]
            at += quarter
    mine = own[2 * own_rows :, :LANES].astype(F32)
    summed = mine + near[own_rows:, :LANES].astype(F32)
    both = lax.broadcasted_iota(jnp.int32, mine.shape, 0) < 6
    message[own_rows:, :] = jnp.zeros((SMALL_ROWS, message.shape[1]), BF16)
    message[own_rows:, :LANES] = jnp.where(both, summed, mine).astype(BF16)


def first_grads_body(info, message, other, grad_qkv, grad_proj, small):
    x, c, y = info[AT_X], info[AT_C], info[AT_Y]
    own_rows, width = grad_proj.shape
    qkv = 3 * width // 4
    low = low_half((own_rows, LANES))
    for copy in range(2):
        here = x == copy
        same = jnp.where(here, message[:own_rows, :qkv], other[:own_rows, :qkv]).astype(F32)
        cross = jnp.where(
            here, message[:own_rows, qkv : 2 * qkv], other[:own_rows, qkv : 2 * qkv]
        ).astype(F32)
        first = jnp.where(c == 0, same, cross)
        second = jnp.where(c == 0, cross, same)
        for pair in range(qkv // LANES):
            one = first[:, pair * LANES : (pair + 1) * LANES]
            two = second[:, pair * LANES : (pair + 1) * LANES]
            at = pair * 8 * HALF + copy * LANES
            grad_qkv[:, at : at + LANES] = jnp.where(low, one, turn(two))
            at += 4 * HALF
            grad_qkv[:, at : at + LANES] = jnp.where(low, turn(one), two)
    grad_proj[...] = jnp.where(
        x == y, message[:own_rows, 2 * qkv :], other[:own_rows, 2 * qkv :]
    ).astype(F32)
    mine = message[own_rows:, :LANES].astype(F32)
    far = other[own_rows:, :LANES].astype(F32)
    summed = mine + far
    small[0:6, :] = jnp.where(c == 0, summed, turn(summed))[0:6]
    small[6:7, :] = jnp.where(x == 0, mine, far)[6:7]
    small[7:8, :] = jnp.where(x == 0, far, mine)[6:7]
    small[8:9, :] = jnp.where(x == y, mine, far)[7:8]
    small[9:, :] = jnp.zeros((SMALL_ROWS - 9, LANES), F32)


def make_kernel_local(n_replica, n_shard):
    n_pos = n_shard // 2
    half = n_pos // 2

    def every(move):
        pairs = []
        for r in range(n_replica):
            for p in range(n_pos):
                for c in range(2):
                    to = move(r, p, c)
                    if to is not None:
                        pairs.append((r * n_shard + p * 2 + c, to[0] * n_shard + to[1] * 2 + to[2]))
        return pairs

    ring = list(range(0, n_pos, 2)) + list(range(n_pos - 1, 0, -2))
    after = {p: ring[(i + 1) % n_pos] for i, p in enumerate(ring)}
    before = {p: ring[i - 1] for i, p in enumerate(ring)}

    def mover(move):
        pairs = every(move)
        return lambda v: lax.ppermute(v, MESH_AXES, pairs)

    to_core = mover(lambda r, p, c: (r, p, 1 - c))
    to_copy = mover(lambda r, p, c: (r ^ 1, p, c))
    to_next = mover(lambda r, p, c: (r, after[p], c))
    to_back = mover(lambda r, p, c: (r, before[p], c))
    lend = mover(lambda r, p, c: (r, p ^ 1, c) if p % 2 == r % 2 else None)
    give = mover(lambda r, p, c: (r, p ^ 1, c) if p % 2 != r % 2 else None)

    def ring_gather(chunk, low):
        chunks = [chunk]
        forth = back = chunk
        for _ in range(1, half):
            forth = to_next(forth)
            back = to_back(back)
            chunks += [forth, back]
        return chunks + [to_next(forth[:low]), to_back(back[low:])]

    def ring_scatter(term, low):
        def add(left, right):
            return (left.astype(F32) + right.astype(F32)).astype(BF16)

        far = term(half)
        forth = to_next(far[:low])
        back = to_back(far[low:])
        ahead = term(half - 1)
        behind = term(1 - half)
        forth = to_next(jnp.concatenate([add(forth, ahead[:low]), ahead[low:]]))
        back = to_back(jnp.concatenate([behind[:low], add(back, behind[low:])]))
        for step in range(half - 2, 0, -1):
            forth = to_next(add(forth, term(step)))
            back = to_back(add(back, term(-step)))
        return (term(0).astype(F32) + forth.astype(F32) + back.astype(F32)).astype(BF16)

    def group_gather(block):
        other = to_copy(block)
        return [block, to_core(block), other, to_core(other)]

    def group_scatter(send, keep_away):
        near = to_core(send)
        return near, to_copy((keep_away + near[1].astype(F32)).astype(BF16))

    def local(
        tokens,
        segments,
        counts,
        ln1_gain,
        ln1_bias,
        w_qkv,
        bias_query,
        bias_value,
        w_proj,
        bias_proj,
        ln2_gain,
        ln2_bias,
        w_fc,
        bias_fc,
        w_out,
        bias_out,
        cotangent,
    ):
        rows, width = tokens.shape
        own_rows = width // n_shard
        chip_rows = 2 * own_rows
        piece = w_out.shape[0] // 2
        units = n_pos * piece
        all_rows = RANKS * rows
        qkv_cols = 3 * width // 4
        replica_at = lax.axis_index("replica")
        shard_at = lax.axis_index("shard")
        x, c, p = replica_at % 2, shard_at % 2, shard_at // 2
        place = jnp.where(p % 2 == 0, p // 2, n_pos - 1 - p // 2)

        def origin(index):
            index = index % n_pos
            return jnp.where(index < half, 2 * index, 2 * (n_pos - 1 - index) + 1)

        offsets = [0]
        for step in range(1, half):
            offsets += [-step, step]
        offsets += [half, half]
        info = jnp.stack(
            [origin(place + offset) for offset in offsets] + [x, c, p % 2, counts[0]]
        ).astype(jnp.int32)

        position = jnp.arange(rows, dtype=jnp.int32)
        notes = jnp.stack([segments.astype(BF16), (position < counts[0]).astype(BF16)])
        notes = jnp.pad(notes, ((0, SMALL_ROWS - 2), (0, width - rows)))
        none = jnp.zeros((own_rows,), BF16)
        vectors = jnp.stack([ln1_gain, ln1_bias, bias_proj, ln2_gain, ln2_bias, bias_out, none, bias_query])
        others = jnp.stack([none] * 7 + [bias_value])
        vectors = jnp.concatenate([vectors, others], axis=1)
        lent = lend(w_proj[:, width // 2 :])
        block, d_top, sent, own = kernel_call(
            prepare_body,
            [SMEM_SPEC] + [VMEM_SPEC] * 7,
            [
                ((rows + SMALL_ROWS, width), BF16),
                ((rows, width), BF16),
                ((chip_rows + SMALL_ROWS, width), BF16),
                ((chip_rows + SMALL_ROWS, width), BF16),
            ],
        )(info, tokens, notes, cotangent, w_qkv, w_fc, vectors, bias_fc.reshape(2, piece))
        got = to_core(sent)
        first_chunk, second_chunk = kernel_call(
            chunks_body,
            [SMEM_SPEC] + [VMEM_SPEC] * 5,
            [((chip_rows + SMALL_ROWS, width), BF16), ((chip_rows + piece, width), BF16)],
        )(info, own, got, w_proj, lent, w_out)
        first_chunks = ring_gather(first_chunk, own_rows)
        blocks = group_gather(block)
        second_chunks = ring_gather(second_chunk, chip_rows)
        d_outs = group_gather(d_top)

        parts = [((2, rows, width), BF16), ((rows, width), F32), ((rows, width), F32)]
        normed, qkv, probs, context, send, keep_own, keep_away, qkv_weight, proj_weight, smalls = kernel_call(
            attention_body,
            [SMEM_SPEC] + [VMEM_SPEC] * RANKS + [ANY_SPEC] * ORIGINS,
            [
                ((all_rows, width), BF16),
                ((all_rows, qkv_cols), BF16),
                ((4 * RANKS, rows, rows), BF16),
                ((all_rows, width // 4), BF16),
                *parts,
                ((width, qkv_cols), BF16),
                ((width // 4, width), BF16),
                ((SMALL_ROWS, width), BF16),
            ],
            [pltpu.VMEM((RANKS, rows, rows), F32), pltpu.SemaphoreType.DMA((5 * n_pos,))],
            flops=3 * all_rows * width * width,
            moved=12 << 20,
        )(info, *blocks, *first_chunks)
        near, away = group_scatter(send, keep_away)
        middle, normed_two = kernel_call(
            second_norm_body, [VMEM_SPEC] * 5, [((rows, width), F32), ((rows, width), BF16)]
        )(tokens, keep_own, near, away, smalls)

        inputs = group_gather(normed_two)
        given, d_out, hidden, d_pre, send, keep_own, keep_away, sums_fc, out_weight = kernel_call(
            feed_body,
            [SMEM_SPEC] + [VMEM_SPEC] * (2 * RANKS) + [ANY_SPEC] * ORIGINS + [VMEM_SPEC],
            [
                ((all_rows, width), BF16),
                ((all_rows, width), BF16),
                ((all_rows, units), BF16),
                ((all_rows, units), BF16),
                *parts,
                ((8, units), F32),
                ((units, width), BF16),
            ],
            [pltpu.VMEM((width, units), BF16), pltpu.SemaphoreType.DMA((2 * n_pos,))],
            flops=6 * all_rows * width * units,
            moved=16 << 20,
        )(info, *inputs, *d_outs, *second_chunks, smalls)
        near, away = group_scatter(send, keep_away)
        d_middle, d_branch, sums_two = kernel_call(
            second_back_body,
            [SMEM_SPEC] + [VMEM_SPEC] * 6,
            [((rows, width), F32), ((rows, width), BF16), ((8, width), F32)],
        )(info, middle, cotangent, keep_own, near, away, smalls)

        grad_w_out = dot_rows(hidden, d_out).astype(BF16)
        grad_w_fc = dot_rows(given, d_pre).astype(BF16)
        send, keep_own, keep_away = kernel_call(
            feed_out_body, [VMEM_SPEC] * 2, parts, flops=2 * all_rows * width * units, moved=8 << 20
        )(hidden, out_weight)

        def second_term(offset):
            at = origin(place + offset)
            return jnp.concatenate(
                [
                    lax.dynamic_slice_in_dim(grad_w_fc, at * chip_rows, chip_rows, 0),
                    lax.dynamic_slice_in_dim(grad_w_out, at * piece, piece, 0),
                ]
            )

        own_second = ring_scatter(second_term, chip_rows)
        near, away = group_scatter(send, keep_away)
        (mixed,) = kernel_call(mixed_body, [SMEM_SPEC] + [VMEM_SPEC] * 5, [((rows, width), BF16)])(
            info, middle, keep_own, near, away, smalls
        )

        d_branches = group_gather(d_branch)
        d_branch, d_qkv, send, keep_own, keep_away, sums = kernel_call(
            attention_back_body,
            [SMEM_SPEC] + [VMEM_SPEC] * (2 * RANKS + 6),
            [
                ((all_rows, width), BF16),
                ((all_rows, qkv_cols), BF16),
                *parts,
                ((SMALL_ROWS, width), F32),
            ],
            [pltpu.VMEM((all_rows, width // 4), BF16)],
            flops=3 * all_rows * width * width,
            moved=12 << 20,
        )(info, *d_branches, *blocks, qkv, probs, qkv_weight, proj_weight, sums_two, sums_fc)
        near, away = group_scatter(send, keep_away)
        (grad_tokens,) = kernel_call(first_back_body, [VMEM_SPEC] * 6, [((rows, width), F32)])(
            tokens, d_middle, keep_own, near, away, smalls
        )

        grad_w_proj = dot_rows(context, d_branch).astype(BF16)
        grad_w_qkv = dot_rows(normed, d_qkv).astype(BF16).reshape(n_pos, chip_rows, qkv_cols)
        small_terms = sums.astype(BF16).reshape(SMALL_ROWS, n_pos, chip_rows).transpose(1, 0, 2)
        small_terms = jnp.pad(small_terms, ((0, 0), (0, 0), (0, width - chip_rows)))
        proj_terms = grad_w_proj.reshape(n_pos // 2, own_rows, 2, 2, width // 4)
        proj_terms = proj_terms.transpose(0, 2, 3, 1, 4)
        proj_terms = jnp.where(x == 0, proj_terms, proj_terms[:, ::-1])
        proj_terms = proj_terms.reshape(n_pos, chip_rows, width // 4)
        first_terms = jnp.concatenate(
            [jnp.concatenate([grad_w_qkv, proj_terms], axis=2), small_terms], axis=1
        )

        def first_term(offset):
            return lax.dynamic_index_in_dim(first_terms, origin(place + offset), 0, keepdims=False)

        own_first = ring_scatter(first_term, own_rows)

        near_fc = to_core(lax.dynamic_slice_in_dim(own_second, (1 - c) * own_rows, own_rows, 0))
        own_fc = lax.dynamic_slice_in_dim(own_second, c * own_rows, own_rows, 0)
        other = to_copy(jnp.concatenate([own_fc, near_fc, own_second[chip_rows:]]))
        grad_w_fc, grad_w_out = kernel_call(
            hidden_grads_body,
            [SMEM_SPEC] + [VMEM_SPEC] * 3,
            [((own_rows, 4 * units), F32), ((2 * piece, width), F32)],
        )(info, own_second, near_fc, other)

        near_first = to_core(
            jnp.concatenate(
                [
                    lax.dynamic_slice_in_dim(own_first, (1 - c) * own_rows, own_rows, 0)[:, :qkv_cols],
                    own_first[chip_rows:, :qkv_cols],
                ]
            )
        )
        given_proj = give(own_first[:chip_rows, qkv_cols:])
        (message,) = kernel_call(
            first_message_body,
            [SMEM_SPEC] + [VMEM_SPEC] * 3,
            [((own_rows + SMALL_ROWS, 2 * qkv_cols + width), BF16)],
        )(info, own_first, near_first, given_proj)
        grad_w_qkv, grad_w_proj, small = kernel_call(
            first_grads_body,
            [SMEM_SPEC] + [VMEM_SPEC] * 2,
            [((own_rows, 3 * width), F32), ((own_rows, width), F32), ((SMALL_ROWS, LANES), F32)],
        )(info, message, to_copy(message))
        return (
            mixed,
            grad_tokens,
            small[0, :own_rows],
            small[1, :own_rows],
            grad_w_qkv,
            small[8, :own_rows],
            small[8, own_rows:],
            grad_w_proj,
            small[2, :own_rows],
            small[3, :own_rows],
            small[4, :own_rows],
            grad_w_fc,
            small[6:8].reshape(-1),
            grad_w_out,
            small[5, :own_rows],
        )

    return local


def solution(mesh):
    tokens_spec = P(MESH_AXES, None)
    slots_spec = P(MESH_AXES)
    rows_spec = P("shard", None)
    vector_spec = P("shard")
    in_specs = (
        tokens_spec,
        slots_spec,
        slots_spec,
        vector_spec,
        vector_spec,
        rows_spec,
        vector_spec,
        vector_spec,
        rows_spec,
        vector_spec,
        vector_spec,
        vector_spec,
        rows_spec,
        vector_spec,
        rows_spec,
        vector_spec,
        tokens_spec,
    )
    out_specs = (
        tokens_spec,
        tokens_spec,
        vector_spec,
        vector_spec,
        rows_spec,
        vector_spec,
        vector_spec,
        rows_spec,
        vector_spec,
        vector_spec,
        vector_spec,
        rows_spec,
        vector_spec,
        rows_spec,
        vector_spec,
    )
    n_replica, n_shard = mesh.shape["replica"], mesh.shape["shard"]
    make = make_kernel_local if (n_replica, n_shard) == (2, HEADS) else make_local
    local = make(n_replica, n_shard)
    return jax.shard_map(local, mesh=mesh, in_specs=in_specs, out_specs=out_specs, check_vma=False)
```

profile of v0, /device:TPU:0, one launch (start us, length us, event | category | flops | bytes accessed | tf_op | source)
XLA Modules:
  0.0 280.2 jit_solution(16372087297357877493)
XLA Ops:
  5.6 2.7 shard_map.280
  8.7 4.4 %collective-permute-start.4 = (bf16[64,512]{1,0:T(8,128)(2,1)S(1)}, bf16[64,512]{1,0:T(8,128)(2,1)S(1)}, u32[]{:S(2)}, u32[]{:S(2)}) collective-permute-start(bf16[64,512]{1,0:T(8,128)(2,1)S(1)} %slice.98), channel_id=1, source_target_pairs={{0,2},{1,3},{4,6},{5,7},{8,10},{9,11},{12,14},{13,15},{18,16},{19,... | collective-permute-start | bytes 196616 | tf_op jit(solution)/shard_map/ppermute | solution.py:960
  13.2 2.0 collective-permute-done.4.lent
  15.9 2.3 shard_map.281
  18.2 2.5 collective-permute-start.6
  20.7 6.5 %collective-permute-done.6.refs_6_ = bf16[144,1024]{1,0:T(8,128)(2,1)S(1)} collective-permute-done((bf16[144,1024]{1,0:T(8,128)(2,1)}, bf16[144,1024]{1,0:T(8,128)(2,1)S(1)}, u32[]{:S(2)}, u32[]{:S(2)}) %collective-permute-start.6) | collective-permute-done | bytes 294944 | tf_op jit(solution)/shard_map/ppermute | solution.py:960
  27.1 2.4 collective-permute-start.8
  29.6 2.0 collective-permute-start.1
  31.5 3.4 %collective-permute-done.8.refs_8_ = bf16[144,1024]{1,0:T(8,128)(2,1)S(1)} collective-permute-done((bf16[144,1024]{1,0:T(8,128)(2,1)S(1)}, bf16[144,1024]{1,0:T(8,128)(2,1)S(1)}, u32[]{:S(2)}, u32[]{:S(2)}) %collective-permute-start.8) | collective-permute-done | bytes 294944 | tf_op jit(solution)/shard_map/ppermute | solution.py:960
  34.9 2.4 collective-permute-start.10
  38.7 3.2 %collective-permute-done.10.refs_10_ = bf16[144,1024]{1,0:T(8,128)(2,1)S(1)} collective-permute-done((bf16[144,1024]{1,0:T(8,128)(2,1)S(1)}, bf16[144,1024]{1,0:T(8,128)(2,1)S(1)}, u32[]{:S(2)}, u32[]{:S(2)}) %collective-permute-start.10) | collective-permute-done | bytes 294944 | tf_op jit(solution)/shard_map/ppermute | solution.py:960
  41.9 2.5 collective-permute-start.12
  44.7 2.0 collective-permute-start.21
  46.7 4.2 %collective-permute-done.11.refs_11_ = bf16[64,1024]{1,0:T(8,128)(2,1)S(1)} collective-permute-done((bf16[64,1024]{1,0:T(8,128)(2,1)S(1)}, bf16[64,1024]{1,0:T(8,128)(2,1)S(1)}, u32[]{:S(2)}, u32[]{:S(2)}) %collective-permute-start.11) | collective-permute-done | bytes 131104 | tf_op jit(solution)/shard_map/ppermute | solution.py:960
  52.3 11.6 %shard_map.282 = (bf16[640,1024]{1,0:T(8,128)(2,1)}, bf16[640,768]{1,0:T(8,128)(2,1)}, bf16[16,160,160]{2,1,0:T(8,128)(2,1)}, bf16[640,256]{1,0:T(8,128)(2,1)}, ...) custom-call(s32[13]{0:T(128)} %stack.91.info, ...), custom_call_target="tpu_custom_call" | custom-call | flops 2013265920 | bytes 12582912 | tf_op jit(solution)/shard_map/pallas_call | solution.py:1075
  64.0 1.6 collective-permute-start.22
  66.1 12.2 %collective-permute-done.22.refs_10_ = bf16[256,1024]{1,0:T(8,128)(2,1)S(1)} collective-permute-done((bf16[256,1024]{1,0:T(8,128)(2,1)S(1)}, bf16[256,1024]{1,0:T(8,128)(2,1)S(1)}, u32[]{:S(2)}, u32[]{:S(2)}) %collective-permute-start.22) | collective-permute-done | bytes 524320 | tf_op jit(solution)/shard_map/ppermute | solution.py:960
  78.3 1.6 collective-permute-start.24
  82.4 9.4 %collective-permute-done.24.refs_12_ = bf16[256,1024]{1,0:T(8,128)(2,1)S(1)} collective-permute-done((bf16[256,1024]{1,0:T(8,128)(2,1)S(1)}, bf16[256,1024]{1,0:T(8,128)(2,1)S(1)}, u32[]{:S(2)}, u32[]{:S(2)}) %collective-permute-start.24) | collective-permute-done | bytes 524320 | tf_op jit(solution)/shard_map/ppermute | solution.py:960
  91.8 1.6 collective-permute-start.26
  94.1 2.6 shard_map.283
  96.7 2.0 collective-permute-start.16
  98.7 5.4 %collective-permute-done.19.refs_6_ = bf16[160,1024]{1,0:T(8,128)(2,1)} collective-permute-done((bf16[160,1024]{1,0:T(8,128)(2,1)S(1)}, bf16[160,1024]{1,0:T(8,128)(2,1)}, u32[]{:S(2)}, u32[]{:S(2)}) %collective-permute-start.19) | collective-permute-done | bytes 327712 | tf_op jit(solution)/shard_map/ppermute | solution.py:960
  104.6 3.9 %collective-permute-done.16.refs_2_ = bf16[160,1024]{1,0:T(8,128)(2,1)} collective-permute-done((bf16[160,1024]{1,0:T(8,128)(2,1)}, bf16[160,1024]{1,0:T(8,128)(2,1)}, u32[]{:S(2)}, u32[]{:S(2)}) %collective-permute-start.16) | collective-permute-done | bytes 327712 | tf_op jit(solution)/shard_map/ppermute | solution.py:960
  109.9 1.6 collective-permute-start.28
  111.5 6.0 %collective-permute-done.27.refs_15_ = bf16[128,1024]{1,0:T(8,128)(2,1)} collective-permute-done((bf16[128,1024]{1,0:T(8,128)(2,1)S(1)}, bf16[128,1024]{1,0:T(8,128)(2,1)}, u32[]{:S(2)}, u32[]{:S(2)}) %collective-permute-start.27) | collective-permute-done | bytes 262176 | tf_op jit(solution)/shard_map/ppermute | solution.py:960
  119.0 11.7 %shard_map.284 = (bf16[640,1024]{1,0:T(8,128)(2,1)}, bf16[640,1024]{1,0:T(8,128)(2,1)}, bf16[640,1024]{1,0:T(8,128)(2,1)}, bf16[640,1024]{1,0:T(8,128)(2,1)}, bf...) custom-call(s32[13]{0:T(128)} %stack.91.info, ...), custom_call_target="tpu_custom_call" | custom-call | flops 4026531840 | bytes 16777216 | tf_op jit(solution)/shard_map/pallas_call | solution.py:1098
  130.8 3.5 %convolution_convert_fusion = bf16[1024,1024]{1,0:T(8,128)(2,1)S(1)} fusion(bf16[640,1024]{1,0:T(8,128)(2,1)} %get-tuple-element.71.hidden, bf16[640,1024]{1,0:T(8,128)(2,1)} %get-tuple-element.100), kind=kOutput, calls=%fused_computation.3 | convolution fusion | flops 1343225856 | bytes 4718592 | tf_op jit(solution)/shard_map/dot_general | solution.py:35
  135.4 1.6 collective-permute-start.53
  137.0 1.8 convolution_convert_fusion.1
  141.5 2.6 collective-permute-done.53
  145.0 1.6 collective-permute-start.54
  146.6 3.6 %collective-permute-done.32.away = bf16[160,1024]{1,0:T(8,128)(2,1)S(1)} collective-permute-done((bf16[160,1024]{1,0:T(8,128)(2,1)S(1)}, bf16[160,1024]{1,0:T(8,128)(2,1)S(1)}, u32[]{:S(2)}, u32[]{:S(2)}) %collective-permute-start.32) | collective-permute-done | bytes 327712 | tf_op jit(solution)/shard_map/ppermute | solution.py:960
  150.9 3.4 %shard_map.287 = (f32[160,1024]{1,0:T(8,128)}, bf16[160,1024]{1,0:T(8,128)(2,1)}, f32[8,1024]{1,0:T(8,128)}) custom-call(s32[13]{0:T(128)} %stack.91.info, f32[160,1024]{1,0:T(8,128)} %get-tuple-element.67.middle, bf16[160,1024]{1,0:T(8,128)(2,1)} %cotangent.3, f32[160,1024]{1,0:T(8,128)} %get-tuple-element.76.keep_own, bf16[2,160,1024]{2,1,0:T(8,128)(2,1)} %copy-done.5, ...), custom_call_target="tpu_custom_call" | custom-call | bytes 4194304 | tf_op jit(solution)/shard_map/pallas_call | solution.py:1115
  156.5 6.9 %collective-permute-done.34.refs_2_ = bf16[160,1024]{1,0:T(8,128)(2,1)} collective-permute-done((bf16[160,1024]{1,0:T(8,128)(2,1)}, bf16[160,1024]{1,0:T(8,128)(2,1)}, u32[]{:S(2)}, u32[]{:S(2)}) %collective-permute-start.34) | collective-permute-done | bytes 327712 | tf_op jit(solution)/shard_map/ppermute | solution.py:960
  163.5 1.8 pad_maximum_fusion
  165.2 1.6 collective-permute-start.50
  166.9 2.1 add_convert_fusion.2
  170.2 12.8 %shard_map.288 = (bf16[640,1024]{1,0:T(8,128)(2,1)}, bf16[640,768]{1,0:T(8,128)(2,1)}, bf16[2,160,1024]{2,1,0:T(8,128)(2,1)}, f32[160,1024]{1,0:T(8,128)}, f32[160,1024]{1,0:T(8,128)}, /*index=5*/f32[16,1024]{1,0:T(8,128)}) custom-call(s32[13]{0:T(128)} %stack.91.info, bf16[160,1024]{1,0:T(8,128)(2,1)} %get-tuple-element.80.refs_0_, ...), custom_call_target="tpu_custom_call" | custom-call | flops 2013265920 | bytes 12582912 | tf_op jit(solution)/shard_map/pallas_call | solution.py:1143
  183.0 1.9 convolution_convert_fusion.3
  188.5 1.7 collective-permute-start.38
  191.5 1.7 collective-permute-start.51
  194.1 1.6 collective-permute-start.39
  195.7 3.0 %collective-permute-done.42 = bf16[80,1024]{1,0:T(8,128)(2,1)S(1)} collective-permute-done((bf16[80,1024]{1,0:T(8,128)(2,1)S(1)}, bf16[80,1024]{1,0:T(8,128)(2,1)S(1)}, u32[]{:S(2)}, u32[]{:S(2)}) %collective-permute-start.42) | collective-permute-done | bytes 163872 | tf_op jit(solution)/shard_map/ppermute | solution.py:960
  199.2 4.7 %shard_map.285 = (bf16[2,160,1024]{2,1,0:T(8,128)(2,1)}, f32[160,1024]{1,0:T(8,128)}, f32[160,1024]{1,0:T(8,128)}) custom-call(bf16[640,1024]{1,0:T(8,128)(2,1)} %get-tuple-element.71.hidden, bf16[1024,1024]{1,0:T(8,128)(2,1)} %get-tuple-element.72.out_weight), custom_call_target="tpu_custom_call" | custom-call | flops 1342177280 | bytes 8388608 | tf_op jit(solution)/shard_map/pallas_call | solution.py:1123
  204.0 2.0 add_convert_fusion.1
  206.4 5.1 %collective-permute-done.39 = bf16[144,1024]{1,0:T(8,128)(2,1)S(1)} collective-permute-done((bf16[144,1024]{1,0:T(8,128)(2,1)S(1)}, bf16[144,1024]{1,0:T(8,128)(2,1)S(1)}, u32[]{:S(2)}, u32[]{:S(2)}) %collective-permute-start.39) | collective-permute-done | bytes 294944 | tf_op jit(solution)/shard_map/ppermute | solution.py:960
  212.5 1.6 collective-permute-start.40
  215.6 1.6 collective-permute-start.52
  220.0 2.8 collective-permute-done.40
  222.8 4.2 %collective-permute-done.44 = bf16[144,1024]{1,0:T(8,128)(2,1)} collective-permute-done((bf16[144,1024]{1,0:T(8,128)(2,1)}, bf16[144,1024]{1,0:T(8,128)(2,1)}, u32[]{:S(2)}, u32[]{:S(2)}) %collective-permute-start.44) | collective-permute-done | bytes 294944 | tf_op jit(solution)/shard_map/ppermute | solution.py:960
  228.7 1.6 collective-permute-start.41
  230.3 2.9 %collective-permute-done.52 = bf16[256,1024]{1,0:T(8,128)(2,1)} collective-permute-done((bf16[256,1024]{1,0:T(8,128)(2,1)}, bf16[256,1024]{1,0:T(8,128)(2,1)}, u32[]{:S(2)}, u32[]{:S(2)}) %collective-permute-start.52) | collective-permute-done | bytes 524320 | tf_op jit(solution)/shard_map/ppermute | solution.py:960
  234.9 2.1 collective-permute-done.45
  240.0 2.6 collective-permute-start.58
  242.6 2.4 collective-permute-done.47.given
  246.2 1.8 shard_map.290.message
  248.2 2.1 collective-permute-start.37
  251.0 2.5 shard_map.286
  253.5 1.8 collective-permute-done.58.other
  256.1 2.9 %shard_map.292 = (f32[64,4096]{1,0:T(8,128)}, f32[256,1024]{1,0:T(8,128)}) custom-call(s32[13]{0:T(128)} %stack.91.info, bf16[256,1024]{1,0:T(8,128)(2,1)} %copy-done, bf16[64,1024]{1,0:T(8,128)(2,1)} %copy-done.13, bf16[256,1024]{1,0:T(8,128)(2,1)} %copy-done.12), custom_call_target="tpu_custom_call" | custom-call | bytes 4194304 | tf_op jit(solution)/shard_map/pallas_call | solution.py:1181
  259.0 11.7 %collective-permute-done.37.away = bf16[160,1024]{1,0:T(8,128)(2,1)S(1)} collective-permute-done((bf16[160,1024]{1,0:T(8,128)(2,1)S(1)}, bf16[160,1024]{1,0:T(8,128)(2,1)S(1)}, u32[]{:S(2)}, u32[]{:S(2)}) %collective-permute-start.37) | collective-permute-done | bytes 327712 | tf_op jit(solution)/shard_map/ppermute | solution.py:960
  271.4 3.0 %shard_map.289 = f32[160,1024]{1,0:T(8,128)} custom-call(bf16[160,1024]{1,0:T(8,128)(2,1)} %tokens.5, f32[160,1024]{1,0:T(8,128)} %get-tuple-element.79.d_middle, f32[160,1024]{1,0:T(8,128)} %get-tuple-element.87.keep_own, bf16[2,160,1024]{2,1,0:T(8,128)(2,1)} %copy-done.2, bf16[160,1024]{1,0:T(8,128)(2,1)} %copy-done.15, ...), custom_call_target="tpu_custom_call" | custom-call | bytes 4194304 | tf_op jit(solution)/shard_map/pallas_call | solution.py:1157
  275.2 2.3 shard_map.291
  (230 shorter events, 49.2 us)
Async XLA Ops:
  8.3 6.9 %collective-permute-start.3 = (bf16[144,1024]{1,0:T(8,128)(2,1)}, bf16[144,1024]{1,0:T(8,128)(2,1)S(1)}, u32[]{:S(2)}, u32[]{:S(2)}) collective-permute-start(bf16[144,1024]{1,0:T(8,128)(2,1)} %get-tuple-element.61), channel_id=1, source_target_pairs={{0,1},{1,0},{2,3},{3,2},{4,5},{5,4},{6,7},{7,6},{8,9},{9,8},{10,11... | collective-permute-start | bytes 884744 | tf_op jit(solution)/shard_map/ppermute | solution.py:960
  8.7 6.4 %collective-permute-start.4 = (bf16[64,512]{1,0:T(8,128)(2,1)S(1)}, bf16[64,512]{1,0:T(8,128)(2,1)S(1)}, u32[]{:S(2)}, u32[]{:S(2)}) collective-permute-start(bf16[64,512]{1,0:T(8,128)(2,1)S(1)} %slice.98), channel_id=1, source_target_pairs={{0,2},{1,3},{4,6},{5,7},{8,10},{9,11},{12,14},{13,15},{18,16},{19,... | collective-permute-start | bytes 196616 | tf_op jit(solution)/shard_map/ppermute | solution.py:960
  18.2 8.9 %collective-permute-start.6 = (bf16[144,1024]{1,0:T(8,128)(2,1)}, bf16[144,1024]{1,0:T(8,128)(2,1)S(1)}, u32[]{:S(2)}, u32[]{:S(2)}) collective-permute-start(bf16[144,1024]{1,0:T(8,128)(2,1)} %get-tuple-element.62.refs_4_), channel_id=1, source_target_pairs={{0,2},{1,3},{2,6},{3,7},{4,0},{5,1},{6,10},{7,11},{8,4},{9,5},{10,... | collective-permute-start | bytes 884744 | tf_op jit(solution)/shard_map/ppermute | solution.py:960
  20.7 8.8 %collective-permute-start.5 = (bf16[144,1024]{1,0:T(8,128)(2,1)}, bf16[144,1024]{1,0:T(8,128)(2,1)S(1)}, u32[]{:S(2)}, u32[]{:S(2)}) collective-permute-start(bf16[144,1024]{1,0:T(8,128)(2,1)} %get-tuple-element.62.refs_4_), channel_id=1, source_target_pairs={{0,4},{1,5},{2,0},{3,1},{4,8},{5,9},{6,2},{7,3},{8,12},{9,13},{10,... | collective-permute-start | bytes 884744 | tf_op jit(solution)/shard_map/ppermute | solution.py:960
  27.1 7.7 %collective-permute-start.8 = (bf16[144,1024]{1,0:T(8,128)(2,1)S(1)}, bf16[144,1024]{1,0:T(8,128)(2,1)S(1)}, u32[]{:S(2)}, u32[]{:S(2)}) collective-permute-start(bf16[144,1024]{1,0:T(8,128)(2,1)S(1)} %collective-permute-done.6.refs_6_), channel_id=1, source_target_pairs={{0,2},{1,3},{2,6},{3,7},{4,0},{5,1},{6,10},{7,11},{8,4},{9,5},{10,... | collective-permute-start | bytes 884744 | tf_op jit(solution)/shard_map/ppermute | solution.py:960
  29.5 7.7 %collective-permute-start.7 = (bf16[144,1024]{1,0:T(8,128)(2,1)S(1)}, bf16[144,1024]{1,0:T(8,128)(2,1)S(1)}, u32[]{:S(2)}, u32[]{:S(2)}) collective-permute-start(bf16[144,1024]{1,0:T(8,128)(2,1)S(1)} %collective-permute-done.5.refs_5_), channel_id=1, source_target_pairs={{0,4},{1,5},{2,0},{3,1},{4,8},{5,9},{6,2},{7,3},{8,12},{9,13},{10,... | collective-permute-start | bytes 884744 | tf_op jit(solution)/shard_map/ppermute | solution.py:960
  29.6 9.1 %collective-permute-start.1 = (bf16[176,1024]{1,0:T(8,128)(2,1)}, bf16[176,1024]{1,0:T(8,128)(2,1)S(1)}, u32[]{:S(2)}, u32[]{:S(2)}) collective-permute-start(bf16[176,1024]{1,0:T(8,128)(2,1)} %get-tuple-element.59.refs_0_.refs_4_), channel_id=1, source_target_pairs={{0,16},{1,17},{2,18},{3,19},{4,20},{5,21},{6,22},{7,23},{8,24},{9,... | collective-permute-start | bytes 1081352 | tf_op jit(solution)/shard_map/ppermute | solution.py:960
  34.9 7.0 %collective-permute-start.10 = (bf16[144,1024]{1,0:T(8,128)(2,1)S(1)}, bf16[144,1024]{1,0:T(8,128)(2,1)S(1)}, u32[]{:S(2)}, u32[]{:S(2)}) collective-permute-start(bf16[144,1024]{1,0:T(8,128)(2,1)S(1)} %collective-permute-done.8.refs_8_), channel_id=1, source_target_pairs={{0,2},{1,3},{2,6},{3,7},{4,0},{5,1},{6,10},{7,11},{8,4},{9,5},{10,... | collective-permute-start | bytes 884744 | tf_op jit(solution)/shard_map/ppermute | solution.py:960
  37.3 7.2 %collective-permute-start.9 = (bf16[144,1024]{1,0:T(8,128)(2,1)S(1)}, bf16[144,1024]{1,0:T(8,128)(2,1)S(1)}, u32[]{:S(2)}, u32[]{:S(2)}) collective-permute-start(bf16[144,1024]{1,0:T(8,128)(2,1)S(1)} %collective-permute-done.7.refs_7_), channel_id=1, source_target_pairs={{0,4},{1,5},{2,0},{3,1},{4,8},{5,9},{6,2},{7,3},{8,12},{9,13},{10,... | collective-permute-start | bytes 884744 | tf_op jit(solution)/shard_map/ppermute | solution.py:960
  37.3 9.4 %collective-permute-start = (bf16[176,1024]{1,0:T(8,128)(2,1)}, bf16[176,1024]{1,0:T(8,128)(2,1)S(1)}, u32[]{:S(2)}, u32[]{:S(2)}) collective-permute-start(bf16[176,1024]{1,0:T(8,128)(2,1)} %get-tuple-element.59.refs_0_.refs_4_), channel_id=1, source_target_pairs={{0,1},{1,0},{2,3},{3,2},{4,5},{5,4},{6,7},{7,6},{8,9},{9,8},{10,11... | collective-permute-start | bytes 1081352 | tf_op jit(solution)/shard_map/ppermute | solution.py:960
  38.7 8.0 %collective-permute-start.2 = (bf16[176,1024]{1,0:T(8,128)(2,1)S(1)}, bf16[176,1024]{1,0:T(8,128)(2,1)S(1)}, u32[]{:S(2)}, u32[]{:S(2)}) collective-permute-start(bf16[176,1024]{1,0:T(8,128)(2,1)S(1)} %collective-permute-done.1.refs_2_.refs_6_), channel_id=1, source_target_pairs={{0,1},{1,0},{2,3},{3,2},{4,5},{5,4},{6,7},{7,6},{8,9},{9,8},{10,11... | collective-permute-start | bytes 1081352 | tf_op jit(solution)/shard_map/ppermute | solution.py:960
  41.9 9.0 %collective-permute-start.12 = (bf16[80,1024]{1,0:T(8,128)(2,1)S(1)}, bf16[80,1024]{1,0:T(8,128)(2,1)S(1)}, u32[]{:S(2)}, u32[]{:S(2)}) collective-permute-start(bf16[80,1024]{1,0:T(8,128)(2,1)S(1)} %slice.131), channel_id=1, source_target_pairs={{0,2},{1,3},{2,6},{3,7},{4,0},{5,1},{6,10},{7,11},{8,4},{9,5},{10,... | collective-permute-start | bytes 491528 | tf_op jit(solution)/shard_map/ppermute | solution.py:960
  44.5 6.5 %collective-permute-start.11 = (bf16[64,1024]{1,0:T(8,128)(2,1)S(1)}, bf16[64,1024]{1,0:T(8,128)(2,1)S(1)}, u32[]{:S(2)}, u32[]{:S(2)}) collective-permute-start(bf16[64,1024]{1,0:T(8,128)(2,1)S(1)} %slice.130), channel_id=1, source_target_pairs={{0,4},{1,5},{2,0},{3,1},{4,8},{5,9},{6,2},{7,3},{8,12},{9,13},{10,... | collective-permute-start | bytes 393224 | tf_op jit(solution)/shard_map/ppermute | solution.py:960
  44.7 48.7 %copy-start.38 = (bf16[160,1024]{1,0:T(8,128)(2,1)S(1)}, bf16[160,1024]{1,0:T(8,128)(2,1)}, u32[]{:S(2)}) copy-start(bf16[160,1024]{1,0:T(8,128)(2,1)} %get-tuple-element.69.refs_4_) | copy-start | bytes 983044
  44.7 20.9 %collective-permute-start.21 = (bf16[256,1024]{1,0:T(8,128)(2,1)}, bf16[256,1024]{1,0:T(8,128)(2,1)S(1)}, u32[]{:S(2)}, u32[]{:S(2)}) collective-permute-start(bf16[256,1024]{1,0:T(8,128)(2,1)} %get-tuple-element.70.refs_8_), channel_id=1, source_target_pairs={{0,4},{1,5},{2,0},{3,1},{4,8},{5,9},{6,2},{7,3},{8,12},{9,13},{10,... | collective-permute-start | bytes 1572872 | tf_op jit(solution)/shard_map/ppermute | solution.py:960
  63.9 16.0 %collective-permute-start.13 = (bf16[2,160,1024]{2,1,0:T(8,128)(2,1)}, bf16[2,160,1024]{2,1,0:T(8,128)(2,1)S(1)}, u32[]{:S(2)}, u32[]{:S(2)}) collective-permute-start(bf16[2,160,1024]{2,1,0:T(8,128)(2,1)} %get-tuple-element.64), channel_id=1, source_target_pairs={{0,1},{1,0},{2,3},{3,2},{4,5},{5,4},{6,7},{7,6},{8,9},{9,8},{10,11... | collective-permute-start | bytes 1966088 | tf_op jit(solution)/shard_map/ppermute | solution.py:960
  64.0 14.3 %collective-permute-start.22 = (bf16[256,1024]{1,0:T(8,128)(2,1)S(1)}, bf16[256,1024]{1,0:T(8,128)(2,1)S(1)}, u32[]{:S(2)}, u32[]{:S(2)}) collective-permute-start(bf16[256,1024]{1,0:T(8,128)(2,1)S(1)} %copy-done.30), channel_id=1, source_target_pairs={{0,2},{1,3},{2,6},{3,7},{4,0},{5,1},{6,10},{7,11},{8,4},{9,5},{10,... | collective-permute-start | bytes 1572872 | tf_op jit(solution)/shard_map/ppermute | solution.py:960
  65.6 43.5 %copy-start.31 = (bf16[256,1024]{1,0:T(8,128)(2,1)}, bf16[256,1024]{1,0:T(8,128)(2,1)S(1)}, u32[]{:S(2)}) copy-start(bf16[256,1024]{1,0:T(8,128)(2,1)S(1)} %collective-permute-done.21.refs_9_) | copy-start | bytes 1572868
  65.6 15.8 %collective-permute-start.23 = (bf16[256,1024]{1,0:T(8,128)(2,1)S(1)}, bf16[256,1024]{1,0:T(8,128)(2,1)S(1)}, u32[]{:S(2)}, u32[]{:S(2)}) collective-permute-start(bf16[256,1024]{1,0:T(8,128)(2,1)S(1)} %collective-permute-done.21.refs_9_), channel_id=1, source_target_pairs={{0,4},{1,5},{2,0},{3,1},{4,8},{5,9},{6,2},{7,3},{8,12},{9,13},{10,... | collective-permute-start | bytes 1572872 | tf_op jit(solution)/shard_map/ppermute | solution.py:960
  78.3 40.0 %copy-start.32 = (bf16[256,1024]{1,0:T(8,128)(2,1)}, bf16[256,1024]{1,0:T(8,128)(2,1)S(1)}, u32[]{:S(2)}) copy-start(bf16[256,1024]{1,0:T(8,128)(2,1)S(1)} %collective-permute-done.22.refs_10_) | copy-start | bytes 1572868
  78.3 13.5 %collective-permute-start.24 = (bf16[256,1024]{1,0:T(8,128)(2,1)S(1)}, bf16[256,1024]{1,0:T(8,128)(2,1)S(1)}, u32[]{:S(2)}, u32[]{:S(2)}) collective-permute-start(bf16[256,1024]{1,0:T(8,128)(2,1)S(1)} %collective-permute-done.22.refs_10_), channel_id=1, source_target_pairs={{0,2},{1,3},{2,6},{3,7},{4,0},{5,1},{6,10},{7,11},{8,4},{9,5},{10,... | collective-permute-start | bytes 1572872 | tf_op jit(solution)/shard_map/ppermute | solution.py:960
  81.3 12.1 %collective-permute-start.14 = (bf16[160,1024]{1,0:T(8,128)(2,1)S(1)}, bf16[160,1024]{1,0:T(8,128)(2,1)S(1)}, u32[]{:S(2)}, u32[]{:S(2)}) collective-permute-start(bf16[160,1024]{1,0:T(8,128)(2,1)S(1)} %fusion.5), channel_id=1, source_target_pairs={{0,16},{1,17},{2,18},{3,19},{4,20},{5,21},{6,22},{7,23},{8,24},{9,... | collective-permute-start | bytes 983048 | tf_op jit(solution)/shard_map/ppermute | solution.py:960
  81.4 27.8 %copy-start.33 = (bf16[256,1024]{1,0:T(8,128)(2,1)}, bf16[256,1024]{1,0:T(8,128)(2,1)S(1)}, u32[]{:S(2)}) copy-start(bf16[256,1024]{1,0:T(8,128)(2,1)S(1)} %collective-permute-done.23.refs_11_) | copy-start | bytes 1572868
  81.4 22.7 %collective-permute-start.25 = (bf16[256,1024]{1,0:T(8,128)(2,1)S(1)}, bf16[256,1024]{1,0:T(8,128)(2,1)S(1)}, u32[]{:S(2)}, u32[]{:S(2)}) collective-permute-start(bf16[256,1024]{1,0:T(8,128)(2,1)S(1)} %collective-permute-done.23.refs_11_), channel_id=1, source_target_pairs={{0,4},{1,5},{2,0},{3,1},{4,8},{5,9},{6,2},{7,3},{8,12},{9,13},{10,... | collective-permute-start | bytes 1572872 | tf_op jit(solution)/shard_map/ppermute | solution.py:960
  91.8 26.6 %copy-start.34 = (bf16[256,1024]{1,0:T(8,128)(2,1)}, bf16[256,1024]{1,0:T(8,128)(2,1)S(1)}, u32[]{:S(2)}) copy-start(bf16[256,1024]{1,0:T(8,128)(2,1)S(1)} %collective-permute-done.24.refs_12_) | copy-start | bytes 1572868
  91.8 16.8 %collective-permute-start.26 = (bf16[256,1024]{1,0:T(8,128)(2,1)S(1)}, bf16[256,1024]{1,0:T(8,128)(2,1)S(1)}, u32[]{:S(2)}, u32[]{:S(2)}) collective-permute-start(bf16[256,1024]{1,0:T(8,128)(2,1)S(1)} %collective-permute-done.24.refs_12_), channel_id=1, source_target_pairs={{0,2},{1,3},{2,6},{3,7},{4,0},{5,1},{6,10},{7,11},{8,4},{9,5},{10,... | collective-permute-start | bytes 1572872 | tf_op jit(solution)/shard_map/ppermute | solution.py:960
  93.4 10.8 %collective-permute-start.19 = (bf16[160,1024]{1,0:T(8,128)(2,1)S(1)}, bf16[160,1024]{1,0:T(8,128)(2,1)}, u32[]{:S(2)}, u32[]{:S(2)}) collective-permute-start(bf16[160,1024]{1,0:T(8,128)(2,1)S(1)} %copy-done.38), channel_id=1, source_target_pairs={{0,16},{1,17},{2,18},{3,19},{4,20},{5,21},{6,22},{7,23},{8,24},{9,... | collective-permute-start | bytes 983048 | tf_op jit(solution)/shard_map/ppermute | solution.py:960
  96.7 11.9 %collective-permute-start.16 = (bf16[160,1024]{1,0:T(8,128)(2,1)}, bf16[160,1024]{1,0:T(8,128)(2,1)}, u32[]{:S(2)}, u32[]{:S(2)}) collective-permute-start(bf16[160,1024]{1,0:T(8,128)(2,1)} %get-tuple-element.68.refs_0_), channel_id=1, source_target_pairs={{0,16},{1,17},{2,18},{3,19},{4,20},{5,21},{6,22},{7,23},{8,24},{9,... | collective-permute-start | bytes 983048 | tf_op jit(solution)/shard_map/ppermute | solution.py:960
  98.7 10.4 %collective-permute-start.18 = (bf16[160,1024]{1,0:T(8,128)(2,1)S(1)}, bf16[160,1024]{1,0:T(8,128)(2,1)S(1)}, u32[]{:S(2)}, u32[]{:S(2)}) collective-permute-start(bf16[160,1024]{1,0:T(8,128)(2,1)S(1)} %copy-done.38), channel_id=1, source_target_pairs={{0,1},{1,0},{2,3},{3,2},{4,5},{5,4},{6,7},{7,6},{8,9},{9,8},{10,11... | collective-permute-start | bytes 983048 | tf_op jit(solution)/shard_map/ppermute | solution.py:960
  104.1 7.4 %collective-permute-start.20 = (bf16[160,1024]{1,0:T(8,128)(2,1)}, bf16[160,1024]{1,0:T(8,128)(2,1)}, u32[]{:S(2)}, u32[]{:S(2)}) collective-permute-start(bf16[160,1024]{1,0:T(8,128)(2,1)} %collective-permute-done.19.refs_6_), channel_id=1, source_target_pairs={{0,1},{1,0},{2,3},{3,2},{4,5},{5,4},{6,7},{7,6},{8,9},{9,8},{10,11... | collective-permute-start | bytes 983048 | tf_op jit(solution)/shard_map/ppermute | solution.py:960
  104.1 14.2 %collective-permute-start.15 = (bf16[160,1024]{1,0:T(8,128)(2,1)}, bf16[160,1024]{1,0:T(8,128)(2,1)}, u32[]{:S(2)}, u32[]{:S(2)}) collective-permute-start(bf16[160,1024]{1,0:T(8,128)(2,1)} %get-tuple-element.68.refs_0_), channel_id=1, source_target_pairs={{0,1},{1,0},{2,3},{3,2},{4,5},{5,4},{6,7},{7,6},{8,9},{9,8},{10,11... | collective-permute-start | bytes 983048 | tf_op jit(solution)/shard_map/ppermute | solution.py:960
  108.6 9.8 %collective-permute-start.17 = (bf16[160,1024]{1,0:T(8,128)(2,1)}, bf16[160,1024]{1,0:T(8,128)(2,1)}, u32[]{:S(2)}, u32[]{:S(2)}) collective-permute-start(bf16[160,1024]{1,0:T(8,128)(2,1)} %collective-permute-done.16.refs_2_), channel_id=1, source_target_pairs={{0,1},{1,0},{2,3},{3,2},{4,5},{5,4},{6,7},{7,6},{8,9},{9,8},{10,11... | collective-permute-start | bytes 983048 | tf_op jit(solution)/shard_map/ppermute | solution.py:960
  108.6 8.9 %collective-permute-start.27 = (bf16[128,1024]{1,0:T(8,128)(2,1)S(1)}, bf16[128,1024]{1,0:T(8,128)(2,1)}, u32[]{:S(2)}, u32[]{:S(2)}) collective-permute-start(bf16[128,1024]{1,0:T(8,128)(2,1)S(1)} %slice.133), channel_id=1, source_target_pairs={{0,4},{1,5},{2,0},{3,1},{4,8},{5,9},{6,2},{7,3},{8,12},{9,13},{10,... | collective-permute-start | bytes 786440 | tf_op jit(solution)/shard_map/ppermute | solution.py:960
  109.9 8.4 %collective-permute-start.28 = (bf16[128,1024]{1,0:T(8,128)(2,1)S(1)}, bf16[128,1024]{1,0:T(8,128)(2,1)S(1)}, u32[]{:S(2)}, u32[]{:S(2)}) collective-permute-start(bf16[128,1024]{1,0:T(8,128)(2,1)S(1)} %slice.134), channel_id=1, source_target_pairs={{0,2},{1,3},{2,6},{3,7},{4,0},{5,1},{6,10},{7,11},{8,4},{9,5},{10,... | collective-permute-start | bytes 786440 | tf_op jit(solution)/shard_map/ppermute | solution.py:960
  130.8 9.6 %collective-permute-start.31 = (bf16[2,160,1024]{2,1,0:T(8,128)(2,1)}, bf16[2,160,1024]{2,1,0:T(8,128)(2,1)S(1)}, u32[]{:S(2)}, u32[]{:S(2)}) collective-permute-start(bf16[2,160,1024]{2,1,0:T(8,128)(2,1)} %get-tuple-element.77), channel_id=1, source_target_pairs={{0,1},{1,0},{2,3},{3,2},{4,5},{5,4},{6,7},{7,6},{8,9},{9,8},{10,11... | collective-permute-start | bytes 1966088 | tf_op jit(solution)/shard_map/ppermute | solution.py:960
  135.4 8.7 %collective-permute-start.53 = (bf16[128,1024]{1,0:T(8,128)(2,1)S(1)}, bf16[128,1024]{1,0:T(8,128)(2,1)S(1)}, u32[]{:S(2)}, u32[]{:S(2)}) collective-permute-start(bf16[128,1024]{1,0:T(8,128)(2,1)S(1)} %get-tuple-element.121), channel_id=1, source_target_pairs={{0,2},{1,3},{2,6},{3,7},{4,0},{5,1},{6,10},{7,11},{8,4},{9,5},{10,... | collective-permute-start | bytes 786440 | tf_op jit(solution)/shard_map/ppermute | solution.py:960
  139.9 15.5 %collective-permute-start.49 = (bf16[128,1024]{1,0:T(8,128)(2,1)}, bf16[128,1024]{1,0:T(8,128)(2,1)}, u32[]{:S(2)}, u32[]{:S(2)}) collective-permute-start(bf16[128,1024]{1,0:T(8,128)(2,1)} %get-tuple-element.117), channel_id=1, source_target_pairs={{0,4},{1,5},{2,0},{3,1},{4,8},{5,9},{6,2},{7,3},{8,12},{9,13},{10,... | collective-permute-start | bytes 786440 | tf_op jit(solution)/shard_map/ppermute | solution.py:960
  140.5 9.7 %collective-permute-start.32 = (bf16[160,1024]{1,0:T(8,128)(2,1)S(1)}, bf16[160,1024]{1,0:T(8,128)(2,1)S(1)}, u32[]{:S(2)}, u32[]{:S(2)}) collective-permute-start(bf16[160,1024]{1,0:T(8,128)(2,1)S(1)} %fusion.3), channel_id=1, source_target_pairs={{0,16},{1,17},{2,18},{3,19},{4,20},{5,21},{6,22},{7,23},{8,24},{9,... | collective-permute-start | bytes 983048 | tf_op jit(solution)/shard_map/ppermute | solution.py:960
  145.0 21.9 %collective-permute-start.54 = (bf16[256,1024]{1,0:T(8,128)(2,1)}, bf16[256,1024]{1,0:T(8,128)(2,1)}, u32[]{:S(2)}, u32[]{:S(2)}) collective-permute-start(bf16[256,1024]{1,0:T(8,128)(2,1)} %pad_maximum_fusion.1), channel_id=1, source_target_pairs={{0,2},{1,3},{2,6},{3,7},{4,0},{5,1},{6,10},{7,11},{8,4},{9,5},{10,... | collective-permute-start | bytes 1572872 | tf_op jit(solution)/shard_map/ppermute | solution.py:960
  154.3 9.2 %collective-permute-start.34 = (bf16[160,1024]{1,0:T(8,128)(2,1)}, bf16[160,1024]{1,0:T(8,128)(2,1)}, u32[]{:S(2)}, u32[]{:S(2)}) collective-permute-start(bf16[160,1024]{1,0:T(8,128)(2,1)} %get-tuple-element.80.refs_0_), channel_id=1, source_target_pairs={{0,16},{1,17},{2,18},{3,19},{4,20},{5,21},{6,22},{7,23},{8,24},{9,... | collective-permute-start | bytes 983048 | tf_op jit(solution)/shard_map/ppermute | solution.py:960
  156.5 12.9 %collective-permute-start.33 = (bf16[160,1024]{1,0:T(8,128)(2,1)}, bf16[160,1024]{1,0:T(8,128)(2,1)S(1)}, u32[]{:S(2)}, u32[]{:S(2)}) collective-permute-start(bf16[160,1024]{1,0:T(8,128)(2,1)} %get-tuple-element.80.refs_0_), channel_id=1, source_target_pairs={{0,1},{1,0},{2,3},{3,2},{4,5},{5,4},{6,7},{7,6},{8,9},{9,8},{10,11... | collective-permute-start | bytes 983048 | tf_op jit(solution)/shard_map/ppermute | solution.py:960
  163.5 5.9 %collective-permute-start.35 = (bf16[160,1024]{1,0:T(8,128)(2,1)}, bf16[160,1024]{1,0:T(8,128)(2,1)S(1)}, u32[]{:S(2)}, u32[]{:S(2)}) collective-permute-start(bf16[160,1024]{1,0:T(8,128)(2,1)} %collective-permute-done.34.refs_2_), channel_id=1, source_target_pairs={{0,1},{1,0},{2,3},{3,2},{4,5},{5,4},{6,7},{7,6},{8,9},{9,8},{10,11... | collective-permute-start | bytes 983048 | tf_op jit(solution)/shard_map/ppermute | solution.py:960
  165.2 25.0 %collective-permute-start.50 = (bf16[256,1024]{1,0:T(8,128)(2,1)}, bf16[256,1024]{1,0:T(8,128)(2,1)}, u32[]{:S(2)}, u32[]{:S(2)}) collective-permute-start(bf16[256,1024]{1,0:T(8,128)(2,1)} %pad_maximum_fusion), channel_id=1, source_target_pairs={{0,4},{1,5},{2,0},{3,1},{4,8},{5,9},{6,2},{7,3},{8,12},{9,13},{10,... | collective-permute-start | bytes 1572872 | tf_op jit(solution)/shard_map/ppermute | solution.py:960
  169.0 35.0 %collective-permute-start.55 = (bf16[256,1024]{1,0:T(8,128)(2,1)}, bf16[256,1024]{1,0:T(8,128)(2,1)}, u32[]{:S(2)}, u32[]{:S(2)}) collective-permute-start(bf16[256,1024]{1,0:T(8,128)(2,1)} %add_convert_fusion.2), channel_id=1, source_target_pairs={{0,2},{1,3},{2,6},{3,7},{4,0},{5,1},{6,10},{7,11},{8,4},{9,5},{10,... | collective-permute-start | bytes 1572872 | tf_op jit(solution)/shard_map/ppermute | solution.py:960
  188.5 5.5 %collective-permute-start.38 = (bf16[64,1024]{1,0:T(8,128)(2,1)S(1)}, bf16[64,1024]{1,0:T(8,128)(2,1)S(1)}, u32[]{:S(2)}, u32[]{:S(2)}) collective-permute-start(bf16[64,1024]{1,0:T(8,128)(2,1)S(1)} %get-tuple-element.107), channel_id=1, source_target_pairs={{0,4},{1,5},{2,0},{3,1},{4,8},{5,9},{6,2},{7,3},{8,12},{9,13},{10,... | collective-permute-start | bytes 393224 | tf_op jit(solution)/shard_map/ppermute | solution.py:960
  191.5 23.1 %collective-permute-start.51 = (bf16[256,1024]{1,0:T(8,128)(2,1)S(1)}, bf16[256,1024]{1,0:T(8,128)(2,1)S(1)}, u32[]{:S(2)}, u32[]{:S(2)}) collective-permute-start(bf16[256,1024]{1,0:T(8,128)(2,1)S(1)} %add_convert_fusion.4), channel_id=1, source_target_pairs={{0,4},{1,5},{2,0},{3,1},{4,8},{5,9},{6,2},{7,3},{8,12},{9,13},{10,... | collective-permute-start | bytes 1572872 | tf_op jit(solution)/shard_map/ppermute | solution.py:960
  193.2 5.5 %collective-permute-start.42 = (bf16[80,1024]{1,0:T(8,128)(2,1)S(1)}, bf16[80,1024]{1,0:T(8,128)(2,1)S(1)}, u32[]{:S(2)}, u32[]{:S(2)}) collective-permute-start(bf16[80,1024]{1,0:T(8,128)(2,1)S(1)} %get-tuple-element.110), channel_id=1, source_target_pairs={{0,2},{1,3},{2,6},{3,7},{4,0},{5,1},{6,10},{7,11},{8,4},{9,5},{10,... | collective-permute-start | bytes 491528 | tf_op jit(solution)/shard_map/ppermute | solution.py:960
  194.1 17.4 %collective-permute-start.39 = (bf16[144,1024]{1,0:T(8,128)(2,1)S(1)}, bf16[144,1024]{1,0:T(8,128)(2,1)S(1)}, u32[]{:S(2)}, u32[]{:S(2)}) collective-permute-start(bf16[144,1024]{1,0:T(8,128)(2,1)S(1)} %pad_maximum_fusion.3), channel_id=1, source_target_pairs={{0,4},{1,5},{2,0},{3,1},{4,8},{5,9},{6,2},{7,3},{8,12},{9,13},{10,... | collective-permute-start | bytes 884744 | tf_op jit(solution)/shard_map/ppermute | solution.py:960
  198.8 12.7 %collective-permute-start.43 = (bf16[144,1024]{1,0:T(8,128)(2,1)S(1)}, bf16[144,1024]{1,0:T(8,128)(2,1)S(1)}, u32[]{:S(2)}, u32[]{:S(2)}) collective-permute-start(bf16[144,1024]{1,0:T(8,128)(2,1)S(1)} %pad_maximum_fusion.4), channel_id=1, source_target_pairs={{0,2},{1,3},{2,6},{3,7},{4,0},{5,1},{6,10},{7,11},{8,4},{9,5},{10,... | collective-permute-start | bytes 884744 | tf_op jit(solution)/shard_map/ppermute | solution.py:960
  203.9 13.2 %collective-permute-start.29 = (bf16[2,160,1024]{2,1,0:T(8,128)(2,1)}, bf16[2,160,1024]{2,1,0:T(8,128)(2,1)S(1)}, u32[]{:S(2)}, u32[]{:S(2)}) collective-permute-start(bf16[2,160,1024]{2,1,0:T(8,128)(2,1)} %get-tuple-element.74), channel_id=1, source_target_pairs={{0,1},{1,0},{2,3},{3,2},{4,5},{5,4},{6,7},{7,6},{8,9},{9,8},{10,11... | collective-permute-start | bytes 1966088 | tf_op jit(solution)/shard_map/ppermute | solution.py:960
  206.0 22.7 %collective-permute-start.56 = (bf16[256,1024]{1,0:T(8,128)(2,1)}, bf16[256,1024]{1,0:T(8,128)(2,1)}, u32[]{:S(2)}, u32[]{:S(2)}) collective-permute-start(bf16[256,1024]{1,0:T(8,128)(2,1)} %add_convert_fusion.1), channel_id=1, source_target_pairs={{0,2},{1,3},{2,6},{3,7},{4,0},{5,1},{6,10},{7,11},{8,4},{9,5},{10,... | collective-permute-start | bytes 1572872 | tf_op jit(solution)/shard_map/ppermute | solution.py:960
  212.5 10.3 %collective-permute-start.40 = (bf16[144,1024]{1,0:T(8,128)(2,1)}, bf16[144,1024]{1,0:T(8,128)(2,1)}, u32[]{:S(2)}, u32[]{:S(2)}) collective-permute-start(bf16[144,1024]{1,0:T(8,128)(2,1)} %get-tuple-element.105), channel_id=1, source_target_pairs={{0,4},{1,5},{2,0},{3,1},{4,8},{5,9},{6,2},{7,3},{8,12},{9,13},{10,... | collective-permute-start | bytes 884744 | tf_op jit(solution)/shard_map/ppermute | solution.py:960
  214.2 12.8 %collective-permute-start.44 = (bf16[144,1024]{1,0:T(8,128)(2,1)}, bf16[144,1024]{1,0:T(8,128)(2,1)}, u32[]{:S(2)}, u32[]{:S(2)}) collective-permute-start(bf16[144,1024]{1,0:T(8,128)(2,1)} %get-tuple-element.106), channel_id=1, source_target_pairs={{0,2},{1,3},{2,6},{3,7},{4,0},{5,1},{6,10},{7,11},{8,4},{9,5},{10,... | collective-permute-start | bytes 884744 | tf_op jit(solution)/shard_map/ppermute | solution.py:960
  215.6 17.7 %collective-permute-start.52 = (bf16[256,1024]{1,0:T(8,128)(2,1)}, bf16[256,1024]{1,0:T(8,128)(2,1)}, u32[]{:S(2)}, u32[]{:S(2)}) collective-permute-start(bf16[256,1024]{1,0:T(8,128)(2,1)} %add_convert_fusion.3), channel_id=1, source_target_pairs={{0,4},{1,5},{2,0},{3,1},{4,8},{5,9},{6,2},{7,3},{8,12},{9,13},{10,... | collective-permute-start | bytes 1572872 | tf_op jit(solution)/shard_map/ppermute | solution.py:960
  218.6 31.7 %collective-permute-start.30 = (bf16[160,1024]{1,0:T(8,128)(2,1)S(1)}, bf16[160,1024]{1,0:T(8,128)(2,1)S(1)}, u32[]{:S(2)}, u32[]{:S(2)}) collective-permute-start(bf16[160,1024]{1,0:T(8,128)(2,1)S(1)} %fusion.4), channel_id=1, source_target_pairs={{0,16},{1,17},{2,18},{3,19},{4,20},{5,21},{6,22},{7,23},{8,24},{9,... | collective-permute-start | bytes 983048 | tf_op jit(solution)/shard_map/ppermute | solution.py:960
  222.8 25.3 %collective-permute-start.36 = (bf16[2,160,1024]{2,1,0:T(8,128)(2,1)}, bf16[2,160,1024]{2,1,0:T(8,128)(2,1)S(1)}, u32[]{:S(2)}, u32[]{:S(2)}) collective-permute-start(bf16[2,160,1024]{2,1,0:T(8,128)(2,1)} %get-tuple-element.88), channel_id=1, source_target_pairs={{0,1},{1,0},{2,3},{3,2},{4,5},{5,4},{6,7},{7,6},{8,9},{9,8},{10,11... | collective-permute-start | bytes 1966088 | tf_op jit(solution)/shard_map/ppermute | solution.py:960
  228.2 8.7 %collective-permute-start.45 = (bf16[144,1024]{1,0:T(8,128)(2,1)S(1)}, bf16[144,1024]{1,0:T(8,128)(2,1)S(1)}, u32[]{:S(2)}, u32[]{:S(2)}) collective-permute-start(bf16[144,1024]{1,0:T(8,128)(2,1)S(1)} %get-tuple-element.104), channel_id=1, source_target_pairs={{0,2},{1,3},{2,6},{3,7},{4,0},{5,1},{6,10},{7,11},{8,4},{9,5},{10,... | collective-permute-start | bytes 884744 | tf_op jit(solution)/shard_map/ppermute | solution.py:960
  228.7 9.6 %collective-permute-start.41 = (bf16[144,1024]{1,0:T(8,128)(2,1)S(1)}, bf16[144,1024]{1,0:T(8,128)(2,1)S(1)}, u32[]{:S(2)}, u32[]{:S(2)}) collective-permute-start(bf16[144,1024]{1,0:T(8,128)(2,1)S(1)} %get-tuple-element.103), channel_id=1, source_target_pairs={{0,4},{1,5},{2,0},{3,1},{4,8},{5,9},{6,2},{7,3},{8,12},{9,13},{10,... | collective-permute-start | bytes 884744 | tf_op jit(solution)/shard_map/ppermute | solution.py:960
  234.8 5.1 %collective-permute-start.57 = (bf16[64,1024]{1,0:T(8,128)(2,1)S(1)}, bf16[64,1024]{1,0:T(8,128)(2,1)S(1)}, u32[]{:S(2)}, u32[]{:S(2)}) collective-permute-start(bf16[64,1024]{1,0:T(8,128)(2,1)S(1)} %get-tuple-element.126), channel_id=1, source_target_pairs={{0,1},{1,0},{2,3},{3,2},{4,5},{5,4},{6,7},{7,6},{8,9},{9,8},{10,11... | collective-permute-start | bytes 393224 | tf_op jit(solution)/shard_map/ppermute | solution.py:960
  238.5 6.5 %collective-permute-start.46 = (bf16[80,768]{1,0:T(8,128)(2,1)S(1)}, bf16[80,768]{1,0:T(8,128)(2,1)S(1)}, u32[]{:S(2)}, u32[]{:S(2)}) collective-permute-start(bf16[80,768]{1,0:T(8,128)(2,1)S(1)} %pad_maximum_fusion.5), channel_id=1, source_target_pairs={{0,1},{1,0},{2,3},{3,2},{4,5},{5,4},{6,7},{7,6},{8,9},{9,8},{10,11... | collective-permute-start | bytes 368648 | tf_op jit(solution)/shard_map/ppermute | solution.py:960
  238.6 6.4 %collective-permute-start.47 = (bf16[128,256]{1,0:T(8,128)(2,1)S(1)}, bf16[128,256]{1,0:T(8,128)(2,1)S(1)}, u32[]{:S(2)}, u32[]{:S(2)}) collective-permute-start(bf16[128,256]{1,0:T(8,128)(2,1)S(1)} %slice.139), channel_id=1, source_target_pairs={{2,0},{3,1},{6,4},{7,5},{10,8},{11,9},{14,12},{15,13},{16,18},{17,... | collective-permute-start | bytes 196616 | tf_op jit(solution)/shard_map/ppermute | solution.py:960
  240.0 15.3 %collective-permute-start.58 = (bf16[256,1024]{1,0:T(8,128)(2,1)S(1)}, bf16[256,1024]{1,0:T(8,128)(2,1)S(1)}, u32[]{:S(2)}, u32[]{:S(2)}) collective-permute-start(bf16[256,1024]{1,0:T(8,128)(2,1)S(1)} %pad_maximum_fusion.2), channel_id=1, source_target_pairs={{0,16},{1,17},{2,18},{3,19},{4,20},{5,21},{6,22},{7,23},{8,24},{9,... | collective-permute-start | bytes 1572872 | tf_op jit(solution)/shard_map/ppermute | solution.py:960
  248.1 26.4 %collective-permute-start.48 = (bf16[80,2560]{1,0:T(8,128)(2,1)}, bf16[80,2560]{1,0:T(8,128)(2,1)S(1)}, u32[]{:S(2)}, u32[]{:S(2)}) collective-permute-start(bf16[80,2560]{1,0:T(8,128)(2,1)} %shard_map.290.message), channel_id=1, source_target_pairs={{0,16},{1,17},{2,18},{3,19},{4,20},{5,21},{6,22},{7,23},{8,24},{9,... | collective-permute-start | bytes 1228808 | tf_op jit(solution)/shard_map/ppermute | solution.py:960
  248.2 22.5 %collective-permute-start.37 = (bf16[160,1024]{1,0:T(8,128)(2,1)S(1)}, bf16[160,1024]{1,0:T(8,128)(2,1)S(1)}, u32[]{:S(2)}, u32[]{:S(2)}) collective-permute-start(bf16[160,1024]{1,0:T(8,128)(2,1)S(1)} %fusion.2), channel_id=1, source_target_pairs={{0,16},{1,17},{2,18},{3,19},{4,20},{5,21},{6,22},{7,23},{8,24},{9,... | collective-permute-start | bytes 983048 | tf_op jit(solution)/shard_map/ppermute | solution.py:960
  (48 other events, 341.3 us)
where the time goes:
time: 281 us; the launch traced here: 280 us
  waiting for transfers between devices  109 us (39%)
  Pallas kernels  64.3 us (23%)
  starting transfers between devices  57.5 us (20%)
  other arithmetic  20.1 us (7%)
  local copies, waits for them, and re-layouts  18 us (6%)
  matrix products  8.75 us (3%)
    ppermute x59, waiting for transfers between devices, mover(): return lambda v: lax.ppermute(v, MESH_AXES, pairs)  109 us
    ppermute x59, starting transfers between devices, mover(): return lambda v: lax.ppermute(v, MESH_AXES, pairs)  57.5 us
    pallas_call x1, Pallas kernels, local(): kernel_call(attention_back_body, [SMEM_SPEC] + [VMEM_SPEC] * (2 * RANKS +...  12.8 us
    pallas_call x1, Pallas kernels, local(): kernel_call(feed_body, [SMEM_SPEC] + [VMEM_SPEC] * (2 * RANKS) + [ANY_SPE...  11.7 us
    pallas_call x1, Pallas kernels, local(): kernel_call(attention_body, [SMEM_SPEC] + [VMEM_SPEC] * RANKS + [ANY_SPEC...  11.6 us
    unnamed x106, local copies, waits for them, and re-layouts  11.2 us
    convert_element_type x10, other arithmetic, add(): return (left.astype(F32) + right.astype(F32)).astype(BF16)  9.83 us
    dot_general x4, matrix products, dot_rows(): lax.dot_general(left, right, (((0,), (0,)), ((), ())), preferred_element_...  8.75 us
  transfers between devices with their start and end apart: 59, of which 26 were waited for; matrix products, arithmetic and copies ran while one was open for 10% of the time, Pallas kernels for 16%

commit v1 on v0

--- a/solution.py
+++ b/solution.py
@@ -451,7 +451,7 @@
 
 LANES = 128
 HALF = 64
-VMEM_BYTES = 56 * 1024 * 1024
+VMEM_BYTES = 26 * 1024 * 1024
 ORIGINS = 9
 AT_X, AT_C, AT_Y, AT_COUNT = 9, 10, 11, 12
 VMEM_SPEC = pl.BlockSpec(memory_space=pltpu.VMEM)
@@ -459,7 +459,7 @@
 ANY_SPEC = pl.BlockSpec(memory_space=pl.ANY)
 
 
-def kernel_call(body, in_specs, outs, scratch=(), flops=0, moved=4 << 20):
+def kernel_call(body, in_specs, outs, scratch=(), micros=1):
     return pl.pallas_call(
         body,
         out_shape=tuple(jax.ShapeDtypeStruct(shape, dtype) for shape, dtype in outs),
@@ -467,7 +467,9 @@
         out_specs=tuple(VMEM_SPEC for _ in outs),
         scratch_shapes=list(scratch),
         compiler_params=pltpu.CompilerParams(vmem_limit_bytes=VMEM_BYTES),
-        cost_estimate=pl.CostEstimate(flops=flops, bytes_accessed=moved, transcendentals=0),
+        cost_estimate=pl.CostEstimate(
+            flops=0, bytes_accessed=micros * 3_000_000, transcendentals=0
+        ),
     )
 
 
@@ -500,58 +502,53 @@
     return (lax.broadcasted_iota(jnp.int32, (rows, 1), 0) < info[AT_COUNT]).astype(F32)
 
 
-def prepare_body(info, tokens, notes, cotangent, w_qkv, w_fc, vectors, fc_shift, seen, d_out, sent, own):
-    rows, width = tokens.shape
-    own_rows = w_qkv.shape[0]
-    x, c = info[AT_X], info[AT_C]
-    seen[:rows, :] = tokens[...]
-    seen[rows:, :] = notes[...]
+def tokens_body(info, tokens, segments, cotangent, block, d_out):
+    rows = tokens.shape[0]
+    block[:rows, :] = tokens[...]
+    down = lax.broadcasted_iota(jnp.int32, (SMALL_ROWS, rows), 0)
+    across = lax.broadcasted_iota(jnp.int32, (SMALL_ROWS, rows), 1)
+    used = jnp.where(across < info[AT_COUNT], 1.0, 0.0)
+    notes = jnp.where(down == 0, segments[...].astype(F32), jnp.where(down == 1, used, 0.0))
+    block[rows:, :rows] = notes.astype(BF16)
     d_out[...] = (used_rows(info, rows) * cotangent[...].astype(F32)).astype(BF16)
-    low = low_half((own_rows, LANES))
-    for out in (sent, own):
-        core = c if out is own else 1 - c
-        for pair in range(w_qkv.shape[1] // (8 * HALF)):
-            at = pair * 8 * HALF + x * LANES
-            first = w_qkv[:, pl.ds(pl.multiple_of(at, LANES), LANES)].astype(F32)
-            second = w_qkv[:, pl.ds(pl.multiple_of(at + 4 * HALF, LANES), LANES)].astype(F32)
-            out[:own_rows, pair * LANES : (pair + 1) * LANES] = join(core, first, second, low).astype(BF16)
-        for p in range(w_fc.shape[1] // (4 * LANES)):
-            at = pl.multiple_of(p * 4 * LANES + (2 * core + x) * LANES, LANES)
-            out[own_rows : 2 * own_rows, p * LANES : (p + 1) * LANES] = w_fc[:, pl.ds(at, LANES)]
-        out[:own_rows, 3 * width // 4 :] = jnp.zeros((own_rows, width // 4), BF16)
-        out[2 * own_rows :, :] = jnp.zeros((SMALL_ROWS, width), BF16)
-        shifts = fc_shift[...].astype(F32)
-        shift = jnp.broadcast_to(jnp.where(x == 0, shifts[0:1], shifts[1:2]), (8, LANES))
-        rest = vectors[...].astype(F32)
-        rest = jnp.where(lax.broadcasted_iota(jnp.int32, rest.shape, 0) == 6, shift, rest)
-        out[2 * own_rows : 2 * own_rows + 8, :LANES] = rest.astype(BF16)
-
-
-def chunks_body(info, own, got, w_proj, lent, w_out, first, second):
+
+
+def chunks_body(info, w_qkv, got_qkv, w_fc, got_fc, w_proj, lent, w_out, vectors, got_vectors, shifts, first, second):
     own_rows, width = w_proj.shape
     x, c, y = info[AT_X], info[AT_C], info[AT_Y]
     qkv = 3 * width // 4
+    low = low_half((own_rows, LANES))
     for core in range(2):
         rows = slice(core * own_rows, (core + 1) * own_rows)
         mine = c == core
-        first[rows, :qkv] = jnp.where(mine, own[:own_rows, :qkv], got[:own_rows, :qkv])
-        second[rows, :] = jnp.where(
-            mine, own[own_rows : 2 * own_rows, :], got[own_rows : 2 * own_rows, :]
-        )
-    half = jnp.where(x == y, w_proj[:, : width // 2], lent[...])
+        for pair in range(w_qkv.shape[1] // (8 * HALF)):
+            groups = []
+            for z in range(2):
+                at = pl.ds(pl.multiple_of((2 * pair + z) * 4 * HALF + x * LANES, LANES), LANES)
+                groups.append(jnp.where(mine, w_qkv[:, at], got_qkv[:, at]).astype(F32))
+            first[rows, pair * LANES : (pair + 1) * LANES] = join(c, *groups, low).astype(BF16)
+        for p in range(w_fc.shape[1] // (4 * LANES)):
+            at = pl.ds(pl.multiple_of(p * 4 * LANES + (2 * c + x) * LANES, LANES), LANES)
+            second[rows, p * LANES : (p + 1) * LANES] = jnp.where(mine, w_fc[:, at], got_fc[:, at])
+    half = jnp.where(x == y, w_proj[:, : width // 2], lent[:, width // 2 :])
     first[:own_rows, qkv:] = half[:, : width // 4]
     first[own_rows : 2 * own_rows, qkv:] = half[:, width // 4 :]
     piece = w_out.shape[0] // 2
     second[2 * own_rows :, :] = w_out[pl.ds(pl.multiple_of(x * piece, piece), piece), :]
-    mine = own[2 * own_rows :, :LANES].astype(F32)
-    other = got[2 * own_rows :, :LANES].astype(F32)
-    low = low_half(mine.shape)
-    joined = jnp.where(
-        c == 0, jnp.where(low, mine, turn(other)), jnp.where(low, other, turn(mine))
-    )
-    both = lax.broadcasted_iota(jnp.int32, mine.shape, 0) < 6
+    mine = vectors[...].astype(F32)
+    other = got_vectors[...].astype(F32)
+    lower = jnp.where(c == 0, mine[0:8], other[0:8])
+    upper = jnp.where(c == 0, other[0:8], mine[0:8])
+    blank = jnp.zeros(lower.shape, F32)
+    small = jnp.concatenate([lower, blank], axis=1) + turn(jnp.concatenate([upper, blank], axis=1))
+    heads = jnp.concatenate([mine[8:16], blank], axis=1)
+    heads = heads + turn(jnp.concatenate([mine[16:24], blank], axis=1))
+    both = shifts[...].astype(F32)
+    shift = jnp.broadcast_to(jnp.where(x == 0, both[0:1], both[1:2]), small.shape)
+    row = lax.broadcasted_iota(jnp.int32, small.shape, 0)
+    small = jnp.where(row == 6, shift, jnp.where(row == 7, heads, small))
     first[2 * own_rows :, :] = jnp.zeros((SMALL_ROWS, width), BF16)
-    first[2 * own_rows :, :LANES] = jnp.where(both, joined, mine).astype(BF16)
+    first[2 * own_rows : 2 * own_rows + 8, :LANES] = small.astype(BF16)
 
 
 def run_copies(copies, sems):
@@ -857,84 +854,181 @@
     result[...] = d_middle[...] + norm_back(center * inverse, inverse, d_unit)
 
 
-def hidden_grads_body(info, own_fc, near_fc, other, grad_fc, grad_out):
+def second_term(info, index, grad_fc, grad_out):
+    at = info[index]
+    results = []
+    for grad in (grad_fc, grad_out):
+        chip_rows = grad.shape[0] * 2 // HEADS
+        results.append(grad[pl.ds(pl.multiple_of(at * chip_rows, chip_rows), chip_rows), :])
+    return results
+
+
+def add(left, right):
+    return (left.astype(F32) + right.astype(F32)).astype(BF16)
+
+
+def second_far_body(info, grad_fc, grad_out, forth, back):
+    forth[...], back[...] = second_term(info, ORIGINS - 1, grad_fc, grad_out)
+
+
+def second_hop_body(step, info, got_forth, got_back, grad_fc, grad_out, forth, back):
+    rows = forth.shape[0] // 2
+    for target, got, index, part in ((forth, got_forth, 2 * step, 0), (back, got_back, 2 * step - 1, 1)):
+        terms = second_term(info, index, grad_fc, grad_out)
+        for i in range(2):
+            where = slice(i * rows, (i + 1) * rows)
+            if got.shape[0] == rows:
+                target[where, :] = add(terms[i], got[...]) if i == part else terms[i]
+            else:
+                target[where, :] = add(terms[i], got[where, :])
+
+
+def second_last_body(info, got_forth, got_back, grad_fc, grad_out, own):
+    terms = second_term(info, 0, grad_fc, grad_out)
+    rows = own.shape[0] // 2
+    for i in range(2):
+        where = slice(i * rows, (i + 1) * rows)
+        values = got_forth[where, :].astype(F32) + got_back[where, :].astype(F32)
+        own[where, :] = add(values, terms[i])
+
+
+def first_term(info, index, grad_qkv, grad_proj, sums):
+    at = info[index]
+    chip_rows = grad_qkv.shape[0] * 2 // HEADS
+    own_rows = chip_rows // 2
+    quarter = grad_proj.shape[1] // 4
+    side = lax.rem(at + info[AT_X], 2) * 2 * quarter
+    head = pl.ds(pl.multiple_of(lax.div(at, 2) * own_rows, own_rows), own_rows)
+    results = []
+    for part in range(2):
+        rows = pl.ds(pl.multiple_of(at * chip_rows + part * own_rows, own_rows), own_rows)
+        lanes = pl.ds(pl.multiple_of(side + part * quarter, LANES), quarter)
+        results.append((grad_qkv[rows, :], grad_proj[head, lanes]))
+    small = sums[:, pl.ds(pl.multiple_of(at * LANES, LANES), LANES)].astype(BF16)
+    return results, small
+
+
+def put_first(target, row, values, got, got_row):
+    at = 0
+    rows = values[0].shape[0]
+    for value in values:
+        lanes = slice(at, at + value.shape[1])
+        if got is not None:
+            value = add(value, got[got_row : got_row + rows, lanes])
+        target[row : row + rows, lanes] = value
+        at += value.shape[1]
+
+
+def first_far_body(info, grad_qkv, grad_proj, sums, forth, back):
+    (upper, lower), small = first_term(info, ORIGINS - 1, grad_qkv, grad_proj, sums)
+    own_rows = forth.shape[0]
+    put_first(forth, 0, upper, None, 0)
+    put_first(back, 0, lower, None, 0)
+    back[own_rows:, :] = jnp.zeros((SMALL_ROWS, back.shape[1]), BF16)
+    put_first(back, own_rows, (small,), None, 0)
+
+
+def first_hop_body(step, info, got_forth, got_back, grad_qkv, grad_proj, sums, forth, back):
+    own_rows = (forth.shape[0] - SMALL_ROWS) // 2
+    for target, got, index in ((forth, got_forth, 2 * step), (back, got_back, 2 * step - 1)):
+        terms, small = first_term(info, index, grad_qkv, grad_proj, sums)
+        shift = 0
+        if got.shape[0] == own_rows:
+            came = (got, None, None)
+        elif got.shape[0] == own_rows + SMALL_ROWS:
+            came, shift = (None, got, got), own_rows
+        else:
+            came = (got, got, got)
+        target[2 * own_rows :, :] = jnp.zeros((SMALL_ROWS, target.shape[1]), BF16)
+        for i, values in enumerate((*terms, (small,))):
+            put_first(target, i * own_rows, values, came[i], i * own_rows - shift)
+
+
+def first_last_body(info, got_forth, got_back, grad_qkv, grad_proj, sums, own):
+    own_rows = (own.shape[0] - SMALL_ROWS) // 2
+    terms, small = first_term(info, 0, grad_qkv, grad_proj, sums)
+    own[2 * own_rows :, :] = jnp.zeros((SMALL_ROWS, own.shape[1]), BF16)
+    for i, values in enumerate((*terms, (small,))):
+        at = 0
+        rows = slice(i * own_rows, i * own_rows + values[0].shape[0])
+        for value in values:
+            lanes = slice(at, at + value.shape[1])
+            came = got_forth[rows, lanes].astype(F32) + got_back[rows, lanes].astype(F32)
+            own[rows, lanes] = add(came, value)
+            at += value.shape[1]
+
+
+def four_parts(info, own, near, other, cross):
     x, c = info[AT_X], info[AT_C]
-    own_rows = near_fc.shape[0]
-    piece = own_fc.shape[0] - 2 * own_rows
-    mine = own_fc[pl.ds(pl.multiple_of(c * own_rows, own_rows), own_rows), :].astype(F32)
-    near = near_fc[...].astype(F32)
-    far_mine = other[:own_rows, :].astype(F32)
-    far_near = other[own_rows : 2 * own_rows, :].astype(F32)
-    width = own_fc.shape[1]
+
+    def reader(copy, core):
+        def read(rows, lanes):
+            same = jnp.where(c == core, own[rows, lanes], near[rows, lanes])
+            far = jnp.where(c == core, other[rows, lanes], cross[rows, lanes])
+            return jnp.where(x == copy, same, far).astype(F32)
+
+        return read
+
+    return reader
+
+
+def hidden_grads_body(info, own, near, other, cross, grad_fc, grad_out):
+    x, c = info[AT_X], info[AT_C]
+    own_rows = grad_fc.shape[0]
+    width = own.shape[1]
+    piece = grad_out.shape[0] // 2
+    reader = four_parts(info, own, near, other, cross)
+    rows = pl.ds(pl.multiple_of(c * own_rows, own_rows), own_rows)
     for copy in range(2):
-        here = x == copy
-        same = jnp.where(here, mine, far_mine)
-        cross = jnp.where(here, near, far_near)
         for core in range(2):
-            part = jnp.where(c == core, same, cross)
+            read = reader(copy, core)
             for p in range(width // LANES):
                 at = p * 4 * LANES + core * 2 * LANES + copy * LANES
-                grad_fc[:, at : at + LANES] = part[:, p * LANES : (p + 1) * LANES]
+                grad_fc[:, at : at + LANES] = read(rows, slice(p * LANES, (p + 1) * LANES))
         grad_out[copy * piece : (copy + 1) * piece, :] = jnp.where(
-            here, own_fc[2 * own_rows :, :].astype(F32), other[2 * own_rows :, :].astype(F32)
-        )
-
-
-def first_message_body(info, own, near, given, message):
-    c = info[AT_C]
-    width = own.shape[1]
-    qkv = 3 * width // 4
-    own_rows = (own.shape[0] - SMALL_ROWS) // 2
-    rows = pl.ds(pl.multiple_of(c * own_rows, own_rows), own_rows)
-    message[:own_rows, :qkv] = own[rows, :qkv]
-    message[:own_rows, qkv : 2 * qkv] = near[:own_rows, :qkv]
-    at = 2 * qkv
-    quarter = width // 4
-    for source in (own, given):
-        shift = qkv if source is own else 0
-        for part in range(2):
-            message[:own_rows, at : at + quarter] = source[
-                part * own_rows : (part + 1) * own_rows, shift : shift + quarter
-            ]
-            at += quarter
-    mine = own[2 * own_rows :, :LANES].astype(F32)
-    summed = mine + near[own_rows:, :LANES].astype(F32)
-    both = lax.broadcasted_iota(jnp.int32, mine.shape, 0) < 6
-    message[own_rows:, :] = jnp.zeros((SMALL_ROWS, message.shape[1]), BF16)
-    message[own_rows:, :LANES] = jnp.where(both, summed, mine).astype(BF16)
-
-
-def first_grads_body(info, message, other, grad_qkv, grad_proj, small):
+            x == copy, own[2 * own_rows :, :], other[2 * own_rows :, :]
+        ).astype(F32)
+
+
+def first_grads_body(info, own, near, other, cross, given, grad_qkv, grad_proj, *small_outs):
     x, c, y = info[AT_X], info[AT_C], info[AT_Y]
     own_rows, width = grad_proj.shape
     qkv = 3 * width // 4
+    quarter = width // 4
     low = low_half((own_rows, LANES))
+    reader = four_parts(info, own, near, other, cross)
+    rows = pl.ds(pl.multiple_of(c * own_rows, own_rows), own_rows)
     for copy in range(2):
-        here = x == copy
-        same = jnp.where(here, message[:own_rows, :qkv], other[:own_rows, :qkv]).astype(F32)
-        cross = jnp.where(
-            here, message[:own_rows, qkv : 2 * qkv], other[:own_rows, qkv : 2 * qkv]
-        ).astype(F32)
-        first = jnp.where(c == 0, same, cross)
-        second = jnp.where(c == 0, cross, same)
+        first, second = reader(copy, 0), reader(copy, 1)
         for pair in range(qkv // LANES):
-            one = first[:, pair * LANES : (pair + 1) * LANES]
-            two = second[:, pair * LANES : (pair + 1) * LANES]
+            lanes = slice(pair * LANES, (pair + 1) * LANES)
+            one, two = first(rows, lanes), second(rows, lanes)
             at = pair * 8 * HALF + copy * LANES
             grad_qkv[:, at : at + LANES] = jnp.where(low, one, turn(two))
             at += 4 * HALF
             grad_qkv[:, at : at + LANES] = jnp.where(low, turn(one), two)
-    grad_proj[...] = jnp.where(
-        x == y, message[:own_rows, 2 * qkv :], other[:own_rows, 2 * qkv :]
-    ).astype(F32)
-    mine = message[own_rows:, :LANES].astype(F32)
-    far = other[own_rows:, :LANES].astype(F32)
-    summed = mine + far
-    small[0:6, :] = jnp.where(c == 0, summed, turn(summed))[0:6]
-    small[6:7, :] = jnp.where(x == 0, mine, far)[6:7]
-    small[7:8, :] = jnp.where(x == 0, far, mine)[6:7]
-    small[8:9, :] = jnp.where(x == y, mine, far)[7:8]
-    small[9:, :] = jnp.zeros((SMALL_ROWS - 9, LANES), F32)
+    for part in range(2):
+        block = slice(part * own_rows, (part + 1) * own_rows)
+        left = jnp.where(x == y, own[block, qkv:], other[block, qkv:]).astype(F32)
+        grad_proj[:, part * quarter : (part + 1) * quarter] = left
+        right = given[block, :].astype(F32)
+        grad_proj[:, 2 * quarter + part * quarter : 2 * quarter + (part + 1) * quarter] = right
+    mine, side, far, corner = (
+        ref[2 * own_rows :, :LANES].astype(F32) for ref in (own, near, other, cross)
+    )
+    summed = (mine + side) + (far + corner)
+    summed = jnp.where(c == 0, summed, turn(summed))
+    heads = jnp.where(x == y, mine, far)
+    for i in range(6):
+        small_outs[i][...] = summed[i : i + 1, :HALF]
+    small_outs[6][0:1, :] = jnp.where(x == 0, mine, far)[6:7]
+    small_outs[6][1:2, :] = jnp.where(x == 0, far, mine)[6:7]
+    small_outs[7][...] = heads[7:8, :HALF]
+    small_outs[8][...] = turn(heads)[7:8, :HALF]
+
+
+def tie(*values):
+    return lax.optimization_barrier(values)
 
 
 def make_kernel_local(n_replica, n_shard):
@@ -947,8 +1041,7 @@
             for p in range(n_pos):
                 for c in range(2):
                     to = move(r, p, c)
-                    if to is not None:
-                        pairs.append((r * n_shard + p * 2 + c, to[0] * n_shard + to[1] * 2 + to[2]))
+                    pairs.append((r * n_shard + p * 2 + c, to[0] * n_shard + to[1] * 2 + to[2]))
         return pairs
 
     ring = list(range(0, n_pos, 2)) + list(range(n_pos - 1, 0, -2))
@@ -963,41 +1056,7 @@
     to_copy = mover(lambda r, p, c: (r ^ 1, p, c))
     to_next = mover(lambda r, p, c: (r, after[p], c))
     to_back = mover(lambda r, p, c: (r, before[p], c))
-    lend = mover(lambda r, p, c: (r, p ^ 1, c) if p % 2 == r % 2 else None)
-    give = mover(lambda r, p, c: (r, p ^ 1, c) if p % 2 != r % 2 else None)
-
-    def ring_gather(chunk, low):
-        chunks = [chunk]
-        forth = back = chunk
-        for _ in range(1, half):
-            forth = to_next(forth)
-            back = to_back(back)
-            chunks += [forth, back]
-        return chunks + [to_next(forth[:low]), to_back(back[low:])]
-
-    def ring_scatter(term, low):
-        def add(left, right):
-            return (left.astype(F32) + right.astype(F32)).astype(BF16)
-
-        far = term(half)
-        forth = to_next(far[:low])
-        back = to_back(far[low:])
-        ahead = term(half - 1)
-        behind = term(1 - half)
-        forth = to_next(jnp.concatenate([add(forth, ahead[:low]), ahead[low:]]))
-        back = to_back(jnp.concatenate([behind[:low], add(back, behind[low:])]))
-        for step in range(half - 2, 0, -1):
-            forth = to_next(add(forth, term(step)))
-            back = to_back(add(back, term(-step)))
-        return (term(0).astype(F32) + forth.astype(F32) + back.astype(F32)).astype(BF16)
-
-    def group_gather(block):
-        other = to_copy(block)
-        return [block, to_core(block), other, to_core(other)]
-
-    def group_scatter(send, keep_away):
-        near = to_core(send)
-        return near, to_copy((keep_away + near[1].astype(F32)).astype(BF16))
+    to_side = mover(lambda r, p, c: (r, p ^ 1, c))
 
     def local(
         tokens,
@@ -1025,6 +1084,8 @@
         units = n_pos * piece
         all_rows = RANKS * rows
         qkv_cols = 3 * width // 4
+        first_shape = ((chip_rows + SMALL_ROWS, width), BF16)
+        second_shape = ((chip_rows + piece, width), BF16)
         replica_at = lax.axis_index("replica")
         shard_at = lax.axis_index("shard")
         x, c, p = replica_at % 2, shard_at % 2, shard_at // 2
@@ -1042,36 +1103,49 @@
             [origin(place + offset) for offset in offsets] + [x, c, p % 2, counts[0]]
         ).astype(jnp.int32)
 
-        position = jnp.arange(rows, dtype=jnp.int32)
-        notes = jnp.stack([segments.astype(BF16), (position < counts[0]).astype(BF16)])
-        notes = jnp.pad(notes, ((0, SMALL_ROWS - 2), (0, width - rows)))
+        got_qkv, got_fc, lent = to_core(w_qkv), to_core(w_fc), to_side(w_proj)
         none = jnp.zeros((own_rows,), BF16)
-        vectors = jnp.stack([ln1_gain, ln1_bias, bias_proj, ln2_gain, ln2_bias, bias_out, none, bias_query])
-        others = jnp.stack([none] * 7 + [bias_value])
-        vectors = jnp.concatenate([vectors, others], axis=1)
-        lent = lend(w_proj[:, width // 2 :])
-        block, d_top, sent, own = kernel_call(
-            prepare_body,
-            [SMEM_SPEC] + [VMEM_SPEC] * 7,
-            [
-                ((rows + SMALL_ROWS, width), BF16),
-                ((rows, width), BF16),
-                ((chip_rows + SMALL_ROWS, width), BF16),
-                ((chip_rows + SMALL_ROWS, width), BF16),
-            ],
-        )(info, tokens, notes, cotangent, w_qkv, w_fc, vectors, bias_fc.reshape(2, piece))
-        got = to_core(sent)
+        vectors = jnp.stack(
+            [ln1_gain, ln1_bias, bias_proj, ln2_gain, ln2_bias, bias_out]
+            + [none] * 9
+            + [bias_query]
+            + [none] * 7
+            + [bias_value]
+        )
+        got_vectors = to_core(vectors)
+        block, d_top = kernel_call(
+            tokens_body,
+            [SMEM_SPEC] + [VMEM_SPEC] * 3,
+            [((rows + SMALL_ROWS, width), BF16), ((rows, width), BF16)],
+        )(info, tokens, segments.reshape(1, rows), cotangent)
         first_chunk, second_chunk = kernel_call(
-            chunks_body,
-            [SMEM_SPEC] + [VMEM_SPEC] * 5,
-            [((chip_rows + SMALL_ROWS, width), BF16), ((chip_rows + piece, width), BF16)],
-        )(info, own, got, w_proj, lent, w_out)
-        first_chunks = ring_gather(first_chunk, own_rows)
-        blocks = group_gather(block)
-        second_chunks = ring_gather(second_chunk, chip_rows)
-        d_outs = group_gather(d_top)
+            chunks_body, [SMEM_SPEC] + [VMEM_SPEC] * 10, [first_shape, second_shape], micros=2
+        )(
+            info, w_qkv, got_qkv, w_fc, got_fc, w_proj, lent, w_out, vectors, got_vectors,
+            bias_fc.reshape(2, piece),
+        )
+
+        firsts = [first_chunk]
+        forth, back = to_next(first_chunk), to_back(first_chunk)
+        block_other = to_copy(block)
+        for step in range(1, half):
+            firsts += [forth, back]
+            if step < half - 1:
+                forth, back = to_next(forth), to_back(back)
+            if step == 1:
+                block_other, d_top, forth, back = tie(block_other, d_top, forth, back)
+                blocks = [block, to_core(block), block_other, to_core(block_other)]
+                d_other = to_copy(d_top)
+            if step == half - 2:
+                second_chunk, forth, back = tie(second_chunk, forth, back)
+                seconds = [second_chunk]
+                second_forth, second_back = to_next(second_chunk), to_back(second_chunk)
+        d_outs = [d_top, to_core(d_top), d_other, to_core(d_other)]
+        firsts += [to_next(forth[:own_rows]), to_back(back[own_rows:])]
 
         parts = [((2, rows, width), BF16), ((rows, width), F32), ((rows, width), F32)]
+        tied = tie(*firsts, *blocks, *d_outs)
+        firsts, blocks, d_outs = tied[:ORIGINS], tied[ORIGINS : ORIGINS + RANKS], tied[ORIGINS + RANKS :]
         normed, qkv, probs, context, send, keep_own, keep_away, qkv_weight, proj_weight, smalls = kernel_call(
             attention_body,
             [SMEM_SPEC] + [VMEM_SPEC] * RANKS + [ANY_SPEC] * ORIGINS,
@@ -1086,15 +1160,26 @@
                 ((SMALL_ROWS, width), BF16),
             ],
             [pltpu.VMEM((RANKS, rows, rows), F32), pltpu.SemaphoreType.DMA((5 * n_pos,))],
-            flops=3 * all_rows * width * width,
-            moved=12 << 20,
-        )(info, *blocks, *first_chunks)
-        near, away = group_scatter(send, keep_away)
+            micros=8,
+        )(info, *blocks, *firsts)
+        send, second_forth, second_back = tie(send, second_forth, second_back)
+        seconds += [second_forth, second_back]
+        near = to_core(send)
+        second_forth, second_back = to_next(second_forth), to_back(second_back)
+        away = to_copy(add(keep_away, near[1]))
+        away, second_forth, second_back = tie(away, second_forth, second_back)
+        seconds += [second_forth, second_back]
         middle, normed_two = kernel_call(
             second_norm_body, [VMEM_SPEC] * 5, [((rows, width), F32), ((rows, width), BF16)]
         )(tokens, keep_own, near, away, smalls)
-
-        inputs = group_gather(normed_two)
+        second_forth, second_back = to_next(second_forth), to_back(second_back)
+        other = to_copy(normed_two)
+        beside = to_core(normed_two)
+        other, beside, second_forth, second_back = tie(other, beside, second_forth, second_back)
+        seconds += [second_forth, second_back]
+        seconds += [to_next(second_forth[:chip_rows]), to_back(second_back[chip_rows:])]
+        inputs = [normed_two, beside, other, to_core(other)]
+
         given, d_out, hidden, d_pre, send, keep_own, keep_away, sums_fc, out_weight = kernel_call(
             feed_body,
             [SMEM_SPEC] + [VMEM_SPEC] * (2 * RANKS) + [ANY_SPEC] * ORIGINS + [VMEM_SPEC],
@@ -1108,38 +1193,48 @@
                 ((units, width), BF16),
             ],
             [pltpu.VMEM((width, units), BF16), pltpu.SemaphoreType.DMA((2 * n_pos,))],
-            flops=6 * all_rows * width * units,
-            moved=16 << 20,
-        )(info, *inputs, *d_outs, *second_chunks, smalls)
-        near, away = group_scatter(send, keep_away)
+            micros=10,
+        )(info, *inputs, *d_outs, *seconds, smalls)
+
+        near = to_core(send)
+        near, given, d_out, hidden, d_pre = tie(near, given, d_out, hidden, d_pre)
+        away = to_copy(add(keep_away, near[1]))
+        grad_w_out = dot_rows(hidden, d_out).astype(BF16)
+        grad_w_fc = dot_rows(given, d_pre).astype(BF16)
+        away, grad_w_out, grad_w_fc = tie(away, grad_w_out, grad_w_fc)
+        far_forth, far_back = kernel_call(
+            second_far_body,
+            [SMEM_SPEC] + [VMEM_SPEC] * 2,
+            [((chip_rows, width), BF16), ((piece, width), BF16)],
+        )(info, grad_w_fc, grad_w_out)
+        far_forth, far_back = to_next(far_forth), to_back(far_back)
+
+        def second_hop(step, got_forth, got_back):
+            forth, back = kernel_call(
+                functools.partial(second_hop_body, step),
+                [SMEM_SPEC] + [VMEM_SPEC] * 4,
+                [second_shape, second_shape],
+            )(info, got_forth, got_back, grad_w_fc, grad_w_out)
+            return to_next(forth), to_back(back)
+
         d_middle, d_branch, sums_two = kernel_call(
             second_back_body,
             [SMEM_SPEC] + [VMEM_SPEC] * 6,
             [((rows, width), F32), ((rows, width), BF16), ((8, width), F32)],
         )(info, middle, cotangent, keep_own, near, away, smalls)
-
-        grad_w_out = dot_rows(hidden, d_out).astype(BF16)
-        grad_w_fc = dot_rows(given, d_pre).astype(BF16)
-        send, keep_own, keep_away = kernel_call(
-            feed_out_body, [VMEM_SPEC] * 2, parts, flops=2 * all_rows * width * units, moved=8 << 20
+        other, beside = to_copy(d_branch), to_core(d_branch)
+        hidden, out_weight, d_branch = tie(hidden, out_weight, d_branch)
+        mix_send, mix_keep, mix_away = kernel_call(
+            feed_out_body, [VMEM_SPEC] * 2, parts, micros=2
         )(hidden, out_weight)
-
-        def second_term(offset):
-            at = origin(place + offset)
-            return jnp.concatenate(
-                [
-                    lax.dynamic_slice_in_dim(grad_w_fc, at * chip_rows, chip_rows, 0),
-                    lax.dynamic_slice_in_dim(grad_w_out, at * piece, piece, 0),
-                ]
-            )
-
-        own_second = ring_scatter(second_term, chip_rows)
-        near, away = group_scatter(send, keep_away)
-        (mixed,) = kernel_call(mixed_body, [SMEM_SPEC] + [VMEM_SPEC] * 5, [((rows, width), BF16)])(
-            info, middle, keep_own, near, away, smalls
-        )
-
-        d_branches = group_gather(d_branch)
+        mix_near = to_core(mix_send)
+        other, beside, far_forth, far_back, mix_near = tie(
+            other, beside, far_forth, far_back, mix_near
+        )
+        d_branches = [d_branch, beside, other, to_core(other)]
+        second_forth, second_back = second_hop(half - 1, far_forth, far_back)
+        mix_away = to_copy(add(mix_away, mix_near[1]))
+
         d_branch, d_qkv, send, keep_own, keep_away, sums = kernel_call(
             attention_back_body,
             [SMEM_SPEC] + [VMEM_SPEC] * (2 * RANKS + 6),
@@ -1150,75 +1245,87 @@
                 ((SMALL_ROWS, width), F32),
             ],
             [pltpu.VMEM((all_rows, width // 4), BF16)],
-            flops=3 * all_rows * width * width,
-            moved=12 << 20,
+            micros=9,
         )(info, *d_branches, *blocks, qkv, probs, qkv_weight, proj_weight, sums_two, sums_fc)
-        near, away = group_scatter(send, keep_away)
+        send, d_branch, d_qkv, second_forth, second_back, mix_away = tie(
+            send, d_branch, d_qkv, second_forth, second_back, mix_away
+        )
+        second_forth, second_back = second_hop(half - 2, second_forth, second_back)
+        grad_w_proj = dot_rows(context, d_branch).astype(BF16)
+        grad_w_qkv = dot_rows(normed, d_qkv).astype(BF16)
+        firsts = (grad_w_qkv, grad_w_proj, sums)
+        forth, back = kernel_call(
+            first_far_body,
+            [SMEM_SPEC] + [VMEM_SPEC] * 3,
+            [((own_rows, width), BF16), ((own_rows + SMALL_ROWS, width), BF16)],
+        )(info, *firsts)
+        near = to_core(send)
+        forth, back = to_next(forth), to_back(back)
+        (mixed,) = kernel_call(mixed_body, [SMEM_SPEC] + [VMEM_SPEC] * 5, [((rows, width), BF16)])(
+            info, middle, mix_keep, mix_near, mix_away, smalls
+        )
+        away = to_copy(add(keep_away, near[1]))
+        for step in range(half - 1, 0, -1):
+            forth, back = kernel_call(
+                functools.partial(first_hop_body, step),
+                [SMEM_SPEC] + [VMEM_SPEC] * 5,
+                [first_shape, first_shape],
+            )(info, forth, back, *firsts)
+            forth, back = to_next(forth), to_back(back)
+            if step == half - 1:
+                second_forth, second_back, mixed = tie(second_forth, second_back, mixed)
+                for last in range(half - 3, 0, -1):
+                    second_forth, second_back = second_hop(last, second_forth, second_back)
+                forth, back, away = tie(forth, back, away)
+            elif step == half - 2:
+                forth, back, second_forth, second_back = tie(forth, back, second_forth, second_back)
+                (own_second,) = kernel_call(
+                    second_last_body, [SMEM_SPEC] + [VMEM_SPEC] * 4, [second_shape]
+                )(info, second_forth, second_back, grad_w_fc, grad_w_out)
+                near_second, other_second = to_core(own_second), to_copy(own_second)
+        (own_first,) = kernel_call(
+            first_last_body, [SMEM_SPEC] + [VMEM_SPEC] * 5, [first_shape]
+        )(info, forth, back, *firsts)
+        near_first, other_first = to_core(own_first), to_copy(own_first)
         (grad_tokens,) = kernel_call(first_back_body, [VMEM_SPEC] * 6, [((rows, width), F32)])(
             tokens, d_middle, keep_own, near, away, smalls
         )
 
-        grad_w_proj = dot_rows(context, d_branch).astype(BF16)
-        grad_w_qkv = dot_rows(normed, d_qkv).astype(BF16).reshape(n_pos, chip_rows, qkv_cols)
-        small_terms = sums.astype(BF16).reshape(SMALL_ROWS, n_pos, chip_rows).transpose(1, 0, 2)
-        small_terms = jnp.pad(small_terms, ((0, 0), (0, 0), (0, width - chip_rows)))
-        proj_terms = grad_w_proj.reshape(n_pos // 2, own_rows, 2, 2, width // 4)
-        proj_terms = proj_terms.transpose(0, 2, 3, 1, 4)
-        proj_terms = jnp.where(x == 0, proj_terms, proj_terms[:, ::-1])
-        proj_terms = proj_terms.reshape(n_pos, chip_rows, width // 4)
-        first_terms = jnp.concatenate(
-            [jnp.concatenate([grad_w_qkv, proj_terms], axis=2), small_terms], axis=1
-        )
-
-        def first_term(offset):
-            return lax.dynamic_index_in_dim(first_terms, origin(place + offset), 0, keepdims=False)
-
-        own_first = ring_scatter(first_term, own_rows)
-
-        near_fc = to_core(lax.dynamic_slice_in_dim(own_second, (1 - c) * own_rows, own_rows, 0))
-        own_fc = lax.dynamic_slice_in_dim(own_second, c * own_rows, own_rows, 0)
-        other = to_copy(jnp.concatenate([own_fc, near_fc, own_second[chip_rows:]]))
         grad_w_fc, grad_w_out = kernel_call(
             hidden_grads_body,
-            [SMEM_SPEC] + [VMEM_SPEC] * 3,
+            [SMEM_SPEC] + [VMEM_SPEC] * 4,
             [((own_rows, 4 * units), F32), ((2 * piece, width), F32)],
-        )(info, own_second, near_fc, other)
-
-        near_first = to_core(
-            jnp.concatenate(
-                [
-                    lax.dynamic_slice_in_dim(own_first, (1 - c) * own_rows, own_rows, 0)[:, :qkv_cols],
-                    own_first[chip_rows:, :qkv_cols],
-                ]
-            )
-        )
-        given_proj = give(own_first[:chip_rows, qkv_cols:])
-        (message,) = kernel_call(
-            first_message_body,
-            [SMEM_SPEC] + [VMEM_SPEC] * 3,
-            [((own_rows + SMALL_ROWS, 2 * qkv_cols + width), BF16)],
-        )(info, own_first, near_first, given_proj)
-        grad_w_qkv, grad_w_proj, small = kernel_call(
+        )(info, own_second, near_second, other_second, to_core(other_second))
+
+        given = jnp.where(
+            x == p % 2, other_first[:chip_rows, qkv_cols:], own_first[:chip_rows, qkv_cols:]
+        )
+        vector_shape = ((1, own_rows), F32)
+        grad_w_qkv, grad_w_proj, *small = kernel_call(
             first_grads_body,
-            [SMEM_SPEC] + [VMEM_SPEC] * 2,
-            [((own_rows, 3 * width), F32), ((own_rows, width), F32), ((SMALL_ROWS, LANES), F32)],
-        )(info, message, to_copy(message))
+            [SMEM_SPEC] + [VMEM_SPEC] * 5,
+            [((own_rows, 3 * width), F32), ((own_rows, width), F32)]
+            + [vector_shape] * 6
+            + [((2, piece), F32)]
+            + [vector_shape] * 2,
+        )(info, own_first, near_first, other_first, to_core(other_first), to_side(given))
+        small = [value.reshape(-1) for value in small]
         return (
             mixed,
             grad_tokens,
-            small[0, :own_rows],
-            small[1, :own_rows],
+            small[0],
+            small[1],
             grad_w_qkv,
-            small[8, :own_rows],
-            small[8, own_rows:],
+            small[7],
+            small[8],
             grad_w_proj,
-            small[2, :own_rows],
-            small[3, :own_rows],
-            small[4, :own_rows],
+            small[2],
+            small[3],
+            small[4],
             grad_w_fc,
-            small[6:8].reshape(-1),
+            small[6],
             grad_w_out,
-            small[5, :own_rows],
+            small[5],
         )
 
     return local

time: 281 us -> 228 us (0.81)
  other arithmetic: 20.1 us -> 0.34 us
  Pallas kernels: 64.3 us -> 44.6 us
  local copies, waits for them, and re-layouts: 18 us -> 8.03 us
  waiting for transfers between devices: 109 us -> 114 us
  starting transfers between devices: 57.5 us -> 53 us
  matrix products: 8.75 us -> 5.72 us
    convert_element_type x10 -> x4, other arithmetic: 9.83 us -> 0.32 us  [add(): return (left.astype(F32) + right.astype(F32)).astype(BF16)]
    unnamed x106 -> x20, local copies, waits for them, and re-layouts: 11.2 us -> 5.67 us
    convert_element_type x8 -> x0, other arithmetic: 5.23 us -> none  [the longest x4 2.94 us: group_scatter(): return (near, to_copy((keep_away + near[1].astype(F32)).astype(BF16)))]
    ppermute x59 -> x63, waiting for transfers between devices: 109 us -> 114 us  [mover(): return lambda v: lax.ppermute(v, MESH_AXES, pairs)]
    ppermute x59 -> x63, starting transfers between devices: 57.5 us -> 53 us  [mover(): return lambda v: lax.ppermute(v, MESH_AXES, pairs)]
    concatenate x8 -> x0, other arithmetic: 4.32 us -> none  [the longest x2 1.8 us: ring_scatter(): forth = to_next(jnp.concatenate([add(forth, ahead[:low]), ahead[low:]]))]
    pallas_call x1, Pallas kernels: 11.7 us -> 7.82 us  [local(): kernel_call(feed_body, [SMEM_SPEC] + [VMEM_SPEC] * (2 * RANKS) + [ANY_SPE...]
    pallas_call x1, Pallas kernels: 11.6 us -> 7.97 us  [local(): kernel_call(attention_body, [SMEM_SPEC] + [VMEM_SPEC] * RANKS + [ANY_SPEC...]
  transfers between devices with their start and end apart: 59 -> 63, of which waited for: 26 -> 38; matrix products, arithmetic and copies ran while one was open for 10% -> 4% of each run, Pallas kernels for 16% -> 13%
where the time goes in v1:
time: 228 us
  waiting for transfers between devices  114 us (50%)
  starting transfers between devices  53 us (23%)
  Pallas kernels  44.6 us (20%)
  local copies, waits for them, and re-layouts  8.03 us (4%)
  matrix products  5.72 us (3%)
    ppermute x63, waiting for transfers between devices, mover(): return lambda v: lax.ppermute(v, MESH_AXES, pairs)  114 us
    ppermute x63, starting transfers between devices, mover(): return lambda v: lax.ppermute(v, MESH_AXES, pairs)  53 us
    pallas_call x1, Pallas kernels, local(): kernel_call(attention_back_body, [SMEM_SPEC] + [VMEM_SPEC] * (2 * RANKS +...  9.19 us
    pallas_call x1, Pallas kernels, local(): kernel_call(attention_body, [SMEM_SPEC] + [VMEM_SPEC] * RANKS + [ANY_SPEC...  7.97 us
    pallas_call x1, Pallas kernels, local(): kernel_call(feed_body, [SMEM_SPEC] + [VMEM_SPEC] * (2 * RANKS) + [ANY_SPE...  7.82 us
    dot_general x4, matrix products, dot_rows(): lax.dot_general(left, right, (((0,), (0,)), ((), ())), preferred_element_...  5.72 us
    unnamed x20, local copies, waits for them, and re-layouts  5.67 us
  transfers between devices with their start and end apart: 63, of which 38 were waited for; matrix products, arithmetic and copies ran while one was open for 4% of the time, Pallas kernels for 13%

profile of v1, /device:TPU:0, one launch (start us, length us, event | category | flops | bytes accessed | tf_op | source)
XLA Modules:
  0.0 227.6 jit_solution(9320993342050888208)
XLA Ops:
  1.2 2.9 %collective-permute-start.2 = (bf16[64,1024]{1,0:T(8,128)(2,1)}, bf16[64,1024]{1,0:T(8,128)(2,1)S(1)}, u32[]{:S(2)}, u32[]{:S(2)}) collective-permute-start(bf16[64,1024]{1,0:T(8,128)(2,1)} %w_proj.1), channel_id=1, source_target_pairs={{0,2},{1,3},{2,0},{3,1},{4,6},{5,7},{6,4},{7,5},{8,10},{9,11},{10,... | collective-permute-start | bytes 393224 | tf_op jit(solution)/shard_map/ppermute | solution.py:1053
  4.2 2.2 stack.96.vectors
  13.8 1.8 collective-permute-start.5
  16.5 1.8 collective-permute-start.6
  18.3 4.1 %collective-permute-done.5.refs_6_ = bf16[144,1024]{1,0:T(8,128)(2,1)S(1)} collective-permute-done((bf16[144,1024]{1,0:T(8,128)(2,1)S(1)}, bf16[144,1024]{1,0:T(8,128)(2,1)S(1)}, u32[]{:S(2)}, u32[]{:S(2)}) %collective-permute-start.5) | collective-permute-done | bytes 294944 | tf_op jit(solution)/shard_map/ppermute | solution.py:1053
  22.4 1.3 collective-permute-start.8
  24.5 1.5 collective-permute-done.6.refs_2_.refs_6_
  26.0 4.1 %collective-permute-done.8.refs_8_ = bf16[144,1024]{1,0:T(8,128)(2,1)S(1)} collective-permute-done((bf16[144,1024]{1,0:T(8,128)(2,1)S(1)}, bf16[144,1024]{1,0:T(8,128)(2,1)S(1)}, u32[]{:S(2)}, u32[]{:S(2)}) %collective-permute-start.8) | collective-permute-done | bytes 294944 | tf_op jit(solution)/shard_map/ppermute | solution.py:1053
  30.7 1.2 collective-permute-start.9
  32.7 1.7 collective-permute-start.16
  34.4 3.0 %collective-permute-done.9.refs_9_ = bf16[144,1024]{1,0:T(8,128)(2,1)S(1)} collective-permute-done((bf16[144,1024]{1,0:T(8,128)(2,1)S(1)}, bf16[144,1024]{1,0:T(8,128)(2,1)S(1)}, u32[]{:S(2)}, u32[]{:S(2)}) %collective-permute-start.9) | collective-permute-done | bytes 294944 | tf_op jit(solution)/shard_map/ppermute | solution.py:1053
  37.4 2.0 collective-permute-done.10.refs_10_
  39.5 1.5 collective-permute-start.19
  42.1 1.5 collective-permute-done.15.refs_5_
  43.7 1.5 collective-permute-start.12
  45.8 7.2 %collective-permute-done.11.refs_11_ = bf16[64,1024]{1,0:T(8,128)(2,1)S(1)} collective-permute-done((bf16[64,1024]{1,0:T(8,128)(2,1)S(1)}, bf16[64,1024]{1,0:T(8,128)(2,1)S(1)}, u32[]{:S(2)}, u32[]{:S(2)}) %collective-permute-start.11) | collective-permute-done | bytes 131104 | tf_op jit(solution)/shard_map/ppermute | solution.py:1053
  53.3 8.0 %shard_map.282 = (bf16[640,1024]{1,0:T(8,128)(2,1)S(1)}, bf16[640,768]{1,0:T(8,128)(2,1)S(1)}, bf16[16,160,160]{2,1,0:T(8,128)(2,1)S(1)}, bf16[640,256]{1,0:T(8,...) custom-call(s32[13]{0:T(128)S(1)} %stack.84.info, ...), custom_call_target="tpu_custom_call" | custom-call | bytes 24000000 | tf_op jit(solution)/shard_map/pallas_call | solution.py:1149
  61.4 1.4 collective-permute-start.22
  63.6 1.6 collective-permute-start.21
  65.2 10.5 %collective-permute-done.22.refs_11_ = bf16[256,1024]{1,0:T(8,128)(2,1)S(1)} collective-permute-done((bf16[256,1024]{1,0:T(8,128)(2,1)S(1)}, bf16[256,1024]{1,0:T(8,128)(2,1)S(1)}, u32[]{:S(2)}, u32[]{:S(2)}) %collective-permute-start.22) | collective-permute-done | bytes 524320 | tf_op jit(solution)/shard_map/ppermute | solution.py:1053
  75.7 1.0 collective-permute-done.23.refs_12_
  76.8 1.6 collective-permute-start.26
  79.3 1.6 collective-permute-start.24
  80.9 8.5 %collective-permute-done.24.refs_2_ = bf16[160,1024]{1,0:T(8,128)(2,1)S(1)} collective-permute-done((bf16[160,1024]{1,0:T(8,128)(2,1)S(1)}, bf16[160,1024]{1,0:T(8,128)(2,1)S(1)}, u32[]{:S(2)}, u32[]{:S(2)}) %collective-permute-start.24) | collective-permute-done | bytes 327712 | tf_op jit(solution)/shard_map/ppermute | solution.py:1053
  90.0 1.3 collective-permute-done.27.refs_14_
  91.8 1.6 collective-permute-start.29
  93.4 6.7 %collective-permute-done.30.refs_16_ = bf16[128,1024]{1,0:T(8,128)(2,1)S(1)} collective-permute-done((bf16[128,1024]{1,0:T(8,128)(2,1)S(1)}, bf16[128,1024]{1,0:T(8,128)(2,1)S(1)}, u32[]{:S(2)}, u32[]{:S(2)}) %collective-permute-start.30) | collective-permute-done | bytes 262176 | tf_op jit(solution)/shard_map/ppermute | solution.py:1053
  100.3 7.8 %shard_map.284 = (bf16[640,1024]{1,0:T(8,128)(2,1)S(1)}, bf16[640,1024]{1,0:T(8,128)(2,1)S(1)}, bf16[640,1024]{1,0:T(8,128)(2,1)S(1)}, bf16[640,1024]{1,0:T(8,12...) custom-call(s32[13]{0:T(128)S(1)} %stack.84.info, ...), custom_call_target="tpu_custom_call" | custom-call | bytes 30000000 | tf_op jit(solution)/shard_map/pallas_call | solution.py:1183
  108.2 2.1 collective-permute-done.31.near
  110.4 1.6 collective-permute-start.32
  112.0 1.8 convolution_convert_fusion.1.grad_out
  113.8 1.8 convolution_convert_fusion.grad_fc
  115.7 4.6 %collective-permute-done.32.away = bf16[160,1024]{1,0:T(8,128)(2,1)S(1)} collective-permute-done((bf16[160,1024]{1,0:T(8,128)(2,1)S(1)}, bf16[160,1024]{1,0:T(8,128)(2,1)S(1)}, u32[]{:S(2)}, u32[]{:S(2)}) %collective-permute-start.32) | collective-permute-done | bytes 327712 | tf_op jit(solution)/shard_map/ppermute | solution.py:1053
  120.2 1.3 shard_map.285
  121.5 1.5 shard_map.287
  123.6 1.5 collective-permute-start.33
  125.7 1.6 collective-permute-start.35
  127.8 6.0 %collective-permute-done.35.got_forth = bf16[128,1024]{1,0:T(8,128)(2,1)S(1)} collective-permute-done((bf16[128,1024]{1,0:T(8,128)(2,1)S(1)}, bf16[128,1024]{1,0:T(8,128)(2,1)S(1)}, u32[]{:S(2)}, u32[]{:S(2)}) %collective-permute-start.35) | collective-permute-done | bytes 262176 | tf_op jit(solution)/shard_map/ppermute | solution.py:1053
  133.8 1.3 collective-permute-done.36.got_back
  135.8 1.6 collective-permute-start.39
  138.6 9.2 %shard_map.288 = (bf16[640,1024]{1,0:T(8,128)(2,1)S(1)}, bf16[640,768]{1,0:T(8,128)(2,1)S(1)}, bf16[2,160,1024]{2,1,0:T(8,128)(2,1)S(1)}, f32[160,1024]{1,0:T(8,...) custom-call(s32[13]{0:T(128)S(1)} %stack.84.info, bf16[160,1024]{1,0:T(8,128)(2,1)S(1)} %get-tuple-element.206.refs_0_, ...), custom_call_target="tpu_custom_call" | custom-call | bytes 27000000 | tf_op jit(solution)/shard_map/pallas_call | solution.py:1238
  147.8 2.4 %collective-permute-done.39.got_forth = bf16[256,1024]{1,0:T(8,128)(2,1)S(1)} collective-permute-done((bf16[256,1024]{1,0:T(8,128)(2,1)S(1)}, bf16[256,1024]{1,0:T(8,128)(2,1)S(1)}, u32[]{:S(2)}, u32[]{:S(2)}) %collective-permute-start.39) | collective-permute-done | bytes 524320 | tf_op jit(solution)/shard_map/ppermute | solution.py:1053
  150.2 1.2 collective-permute-done.40.got_back
  152.2 1.6 collective-permute-start.42
  154.5 1.4 convolution_convert_fusion.2.grad_qkv
  157.1 1.3 collective-permute-start.45
  159.9 9.7 %collective-permute-done.45.got_forth = bf16[64,1024]{1,0:T(8,128)(2,1)S(1)} collective-permute-done((bf16[64,1024]{1,0:T(8,128)(2,1)S(1)}, bf16[64,1024]{1,0:T(8,128)(2,1)S(1)}, u32[]{:S(2)}, u32[]{:S(2)}) %collective-permute-start.45) | collective-permute-done | bytes 131104 | tf_op jit(solution)/shard_map/ppermute | solution.py:1053
  169.7 1.7 collective-permute-done.46.got_back
  172.9 1.2 collective-permute-start.48
  174.1 1.4 shard_map.291
  177.2 1.2 collective-permute-start.53
  178.4 3.6 %collective-permute-done.47.got_forth = bf16[144,1024]{1,0:T(8,128)(2,1)S(1)} collective-permute-done((bf16[144,1024]{1,0:T(8,128)(2,1)S(1)}, bf16[144,1024]{1,0:T(8,128)(2,1)S(1)}, u32[]{:S(2)}, u32[]{:S(2)}) %collective-permute-start.47) | collective-permute-done | bytes 294944 | tf_op jit(solution)/shard_map/ppermute | solution.py:1053
  184.2 1.4 collective-permute-start.51
  185.6 7.6 %collective-permute-done.52.got_forth = bf16[256,1024]{1,0:T(8,128)(2,1)S(1)} collective-permute-done((bf16[256,1024]{1,0:T(8,128)(2,1)S(1)}, bf16[256,1024]{1,0:T(8,128)(2,1)S(1)}, u32[]{:S(2)}, u32[]{:S(2)}) %collective-permute-start.52) | collective-permute-done | bytes 524320 | tf_op jit(solution)/shard_map/ppermute | solution.py:1053
  194.1 3.8 %collective-permute-done.50.got_forth = bf16[144,1024]{1,0:T(8,128)(2,1)S(1)} collective-permute-done((bf16[144,1024]{1,0:T(8,128)(2,1)S(1)}, bf16[144,1024]{1,0:T(8,128)(2,1)S(1)}, u32[]{:S(2)}, u32[]{:S(2)}) %collective-permute-start.50) | collective-permute-done | bytes 294944 | tf_op jit(solution)/shard_map/ppermute | solution.py:1053
  201.3 1.3 collective-permute-start.55
  202.6 4.8 %collective-permute-done.54.got_forth = bf16[144,1024]{1,0:T(8,128)(2,1)S(1)} collective-permute-done((bf16[144,1024]{1,0:T(8,128)(2,1)S(1)}, bf16[144,1024]{1,0:T(8,128)(2,1)S(1)}, u32[]{:S(2)}, u32[]{:S(2)}) %collective-permute-start.54) | collective-permute-done | bytes 294944 | tf_op jit(solution)/shard_map/ppermute | solution.py:1053
  208.6 1.5 collective-permute-start.57
  210.1 4.1 %collective-permute-done.61.other = bf16[256,1024]{1,0:T(8,128)(2,1)} collective-permute-done((bf16[256,1024]{1,0:T(8,128)(2,1)S(1)}, bf16[256,1024]{1,0:T(8,128)(2,1)}, u32[]{:S(2)}, u32[]{:S(2)}) %collective-permute-start.61) | collective-permute-done | bytes 524320 | tf_op jit(solution)/shard_map/ppermute | solution.py:1053
  214.8 2.9 %collective-permute-done.57.other = bf16[144,1024]{1,0:T(8,128)(2,1)S(1)} collective-permute-done((bf16[144,1024]{1,0:T(8,128)(2,1)S(1)}, bf16[144,1024]{1,0:T(8,128)(2,1)S(1)}, u32[]{:S(2)}, u32[]{:S(2)}) %collective-permute-start.57) | collective-permute-done | bytes 294944 | tf_op jit(solution)/shard_map/ppermute | solution.py:1053
  217.7 1.2 collective-permute-start.59
  219.9 1.4 shard_map.294
  222.3 2.3 %shard_map.299 = (f32[64,3072]{1,0:T(8,128)}, f32[64,1024]{1,0:T(8,128)}, f32[1,64]{1,0:T(1,128)}, f32[1,64]{1,0:T(1,128)}, f32[1,64]{1,0:T(1,128)}, /*index=5*/...) custom-call(s32[13]{0:T(128)S(1)} %stack.84.info, ...), custom_call_target="tpu_custom_call" | custom-call | bytes 3000000 | tf_op jit(solution)/shard_map/pallas_call | solution.py:1304
  224.6 3.0 %shard_map.301 = (f32[64,4096]{1,0:T(8,128)}, f32[256,1024]{1,0:T(8,128)}) custom-call(s32[13]{0:T(128)S(1)} %stack.84.info, bf16[256,1024]{1,0:T(8,128)(2,1)S(1)} %shard_map.300.own, bf16[256,1024]{1,0:T(8,128)(2,1)} %collective-permute-done.60.near, bf16[256,1024]{1,0:T(8,128)(2,1)} %collective-permute-done.61.other, ...), custom_call_target="tpu_custom_call" | custom-call | bytes 3000000 | tf_op jit(solution)/shard_map/pallas_call | solution.py:1294
  (123 shorter events, 36.7 us)
Async XLA Ops:
  0.6 7.5 %collective-permute-start.1 = (bf16[64,4096]{1,0:T(8,128)(2,1)}, bf16[64,4096]{1,0:T(8,128)(2,1)S(1)}, u32[]{:S(2)}, u32[]{:S(2)}) collective-permute-start(bf16[64,4096]{1,0:T(8,128)(2,1)} %w_fc.1), channel_id=1, source_target_pairs={{0,1},{1,0},{2,3},{3,2},{4,5},{5,4},{6,7},{7,6},{8,9},{9,8},{10,11... | collective-permute-start | bytes 1572872 | tf_op jit(solution)/shard_map/ppermute | solution.py:1053
  1.2 7.0 %collective-permute-start = (bf16[64,3072]{1,0:T(8,128)(2,1)}, bf16[64,3072]{1,0:T(8,128)(2,1)S(1)}, u32[]{:S(2)}, u32[]{:S(2)}) collective-permute-start(bf16[64,3072]{1,0:T(8,128)(2,1)} %w_qkv.1), channel_id=1, source_target_pairs={{0,1},{1,0},{2,3},{3,2},{4,5},{5,4},{6,7},{7,6},{8,9},{9,8},{10,11... | collective-permute-start | bytes 1179656 | tf_op jit(solution)/shard_map/ppermute | solution.py:1053
  1.2 6.9 %collective-permute-start.2 = (bf16[64,1024]{1,0:T(8,128)(2,1)}, bf16[64,1024]{1,0:T(8,128)(2,1)S(1)}, u32[]{:S(2)}, u32[]{:S(2)}) collective-permute-start(bf16[64,1024]{1,0:T(8,128)(2,1)} %w_proj.1), channel_id=1, source_target_pairs={{0,2},{1,3},{2,0},{3,1},{4,6},{5,7},{6,4},{7,5},{8,10},{9,11},{10,... | collective-permute-start | bytes 393224 | tf_op jit(solution)/shard_map/ppermute | solution.py:1053
  6.4 1.2 collective-permute-start.3
  12.8 3.1 %copy-start.8 = (s32[160]{0:T(256)S(1)}, s32[160]{0:T(256)}, u32[]{:S(2)}) copy-start(s32[160]{0:T(256)} %param.18) | copy-start | bytes 1924
  13.8 8.6 %collective-permute-start.5 = (bf16[144,1024]{1,0:T(8,128)(2,1)S(1)}, bf16[144,1024]{1,0:T(8,128)(2,1)S(1)}, u32[]{:S(2)}, u32[]{:S(2)}) collective-permute-start(bf16[144,1024]{1,0:T(8,128)(2,1)S(1)} %get-tuple-element.161.refs_4_), channel_id=1, source_target_pairs={{0,2},{1,3},{2,6},{3,7},{4,0},{5,1},{6,10},{7,11},{8,4},{9,5},{10,... | collective-permute-start | bytes 884744 | tf_op jit(solution)/shard_map/ppermute | solution.py:1053
  15.6 8.2 %collective-permute-start.4 = (bf16[144,1024]{1,0:T(8,128)(2,1)S(1)}, bf16[144,1024]{1,0:T(8,128)(2,1)S(1)}, u32[]{:S(2)}, u32[]{:S(2)}) collective-permute-start(bf16[144,1024]{1,0:T(8,128)(2,1)S(1)} %get-tuple-element.161.refs_4_), channel_id=1, source_target_pairs={{0,4},{1,5},{2,0},{3,1},{4,8},{5,9},{6,2},{7,3},{8,12},{9,13},{10,... | collective-permute-start | bytes 884744 | tf_op jit(solution)/shard_map/ppermute | solution.py:1053
  16.5 9.5 %collective-permute-start.6 = (bf16[176,1024]{1,0:T(8,128)(2,1)S(1)}, bf16[176,1024]{1,0:T(8,128)(2,1)S(1)}, u32[]{:S(2)}, u32[]{:S(2)}) collective-permute-start(bf16[176,1024]{1,0:T(8,128)(2,1)S(1)} %get-tuple-element.157.refs_0_.refs_4_), channel_id=1, source_target_pairs={{0,16},{1,17},{2,18},{3,19},{4,20},{5,21},{6,22},{7,23},{8,24},{9,... | collective-permute-start | bytes 1081352 | tf_op jit(solution)/shard_map/ppermute | solution.py:1053
  22.4 7.7 %collective-permute-start.8 = (bf16[144,1024]{1,0:T(8,128)(2,1)S(1)}, bf16[144,1024]{1,0:T(8,128)(2,1)S(1)}, u32[]{:S(2)}, u32[]{:S(2)}) collective-permute-start(bf16[144,1024]{1,0:T(8,128)(2,1)S(1)} %collective-permute-done.5.refs_6_), channel_id=1, source_target_pairs={{0,2},{1,3},{2,6},{3,7},{4,0},{5,1},{6,10},{7,11},{8,4},{9,5},{10,... | collective-permute-start | bytes 884744 | tf_op jit(solution)/shard_map/ppermute | solution.py:1053
  23.7 7.0 %collective-permute-start.7 = (bf16[144,1024]{1,0:T(8,128)(2,1)S(1)}, bf16[144,1024]{1,0:T(8,128)(2,1)S(1)}, u32[]{:S(2)}, u32[]{:S(2)}) collective-permute-start(bf16[144,1024]{1,0:T(8,128)(2,1)S(1)} %collective-permute-done.4.refs_5_), channel_id=1, source_target_pairs={{0,4},{1,5},{2,0},{3,1},{4,8},{5,9},{6,2},{7,3},{8,12},{9,13},{10,... | collective-permute-start | bytes 884744 | tf_op jit(solution)/shard_map/ppermute | solution.py:1053
  24.5 17.1 %collective-permute-start.13 = (bf16[176,1024]{1,0:T(8,128)(2,1)S(1)}, bf16[176,1024]{1,0:T(8,128)(2,1)S(1)}, u32[]{:S(2)}, u32[]{:S(2)}) collective-permute-start(bf16[176,1024]{1,0:T(8,128)(2,1)S(1)} %get-tuple-element.157.refs_0_.refs_4_), channel_id=1, source_target_pairs={{0,1},{1,0},{2,3},{3,2},{4,5},{5,4},{6,7},{7,6},{8,9},{9,8},{10,11... | collective-permute-start | bytes 1081352 | tf_op jit(solution)/shard_map/ppermute | solution.py:1053
  30.7 6.7 %collective-permute-start.9 = (bf16[144,1024]{1,0:T(8,128)(2,1)S(1)}, bf16[144,1024]{1,0:T(8,128)(2,1)S(1)}, u32[]{:S(2)}, u32[]{:S(2)}) collective-permute-start(bf16[144,1024]{1,0:T(8,128)(2,1)S(1)} %collective-permute-done.7.refs_7_), channel_id=1, source_target_pairs={{0,4},{1,5},{2,0},{3,1},{4,8},{5,9},{6,2},{7,3},{8,12},{9,13},{10,... | collective-permute-start | bytes 884744 | tf_op jit(solution)/shard_map/ppermute | solution.py:1053
  31.9 7.6 %collective-permute-start.10 = (bf16[144,1024]{1,0:T(8,128)(2,1)S(1)}, bf16[144,1024]{1,0:T(8,128)(2,1)S(1)}, u32[]{:S(2)}, u32[]{:S(2)}) collective-permute-start(bf16[144,1024]{1,0:T(8,128)(2,1)S(1)} %collective-permute-done.8.refs_8_), channel_id=1, source_target_pairs={{0,2},{1,3},{2,6},{3,7},{4,0},{5,1},{6,10},{7,11},{8,4},{9,5},{10,... | collective-permute-start | bytes 884744 | tf_op jit(solution)/shard_map/ppermute | solution.py:1053
  32.7 9.3 %collective-permute-start.16 = (bf16[160,1024]{1,0:T(8,128)(2,1)S(1)}, bf16[160,1024]{1,0:T(8,128)(2,1)S(1)}, u32[]{:S(2)}, u32[]{:S(2)}) collective-permute-start(bf16[160,1024]{1,0:T(8,128)(2,1)S(1)} %get-tuple-element.184.refs_4_), channel_id=1, source_target_pairs={{0,16},{1,17},{2,18},{3,19},{4,20},{5,21},{6,22},{7,23},{8,24},{9,... | collective-permute-start | bytes 983048 | tf_op jit(solution)/shard_map/ppermute | solution.py:1053
  39.5 21.8 %collective-permute-start.19 = (bf16[256,1024]{1,0:T(8,128)(2,1)S(1)}, bf16[256,1024]{1,0:T(8,128)(2,1)S(1)}, u32[]{:S(2)}, u32[]{:S(2)}) collective-permute-start(bf16[256,1024]{1,0:T(8,128)(2,1)S(1)} %get-tuple-element.172.refs_8_), channel_id=1, source_target_pairs={{0,2},{1,3},{2,6},{3,7},{4,0},{5,1},{6,10},{7,11},{8,4},{9,5},{10,... | collective-permute-start | bytes 1572872 | tf_op jit(solution)/shard_map/ppermute | solution.py:1053
  40.9 20.4 %collective-permute-start.18 = (bf16[256,1024]{1,0:T(8,128)(2,1)S(1)}, bf16[256,1024]{1,0:T(8,128)(2,1)S(1)}, u32[]{:S(2)}, u32[]{:S(2)}) collective-permute-start(bf16[256,1024]{1,0:T(8,128)(2,1)S(1)} %get-tuple-element.172.refs_8_), channel_id=1, source_target_pairs={{0,4},{1,5},{2,0},{3,1},{4,8},{5,9},{6,2},{7,3},{8,12},{9,13},{10,... | collective-permute-start | bytes 1572872 | tf_op jit(solution)/shard_map/ppermute | solution.py:1053
  41.5 3.7 %collective-permute-start.14 = (bf16[176,1024]{1,0:T(8,128)(2,1)S(1)}, bf16[176,1024]{1,0:T(8,128)(2,1)S(1)}, u32[]{:S(2)}, u32[]{:S(2)}) collective-permute-start(bf16[176,1024]{1,0:T(8,128)(2,1)S(1)} %collective-permute-done.6.refs_2_.refs_6_), channel_id=1, source_target_pairs={{0,1},{1,0},{2,3},{3,2},{4,5},{5,4},{6,7},{7,6},{8,9},{9,8},{10,11... | collective-permute-start | bytes 1081352 | tf_op jit(solution)/shard_map/ppermute | solution.py:1053
  41.5 2.1 collective-permute-start.15
  42.0 11.3 %collective-permute-start.17 = (bf16[160,1024]{1,0:T(8,128)(2,1)S(1)}, bf16[160,1024]{1,0:T(8,128)(2,1)S(1)}, u32[]{:S(2)}, u32[]{:S(2)}) collective-permute-start(bf16[160,1024]{1,0:T(8,128)(2,1)S(1)} %collective-permute-done.16.refs_6_), channel_id=1, source_target_pairs={{0,1},{1,0},{2,3},{3,2},{4,5},{5,4},{6,7},{7,6},{8,9},{9,8},{10,11... | collective-permute-start | bytes 983048 | tf_op jit(solution)/shard_map/ppermute | solution.py:1053
  43.7 9.7 %collective-permute-start.12 = (bf16[80,1024]{1,0:T(8,128)(2,1)S(1)}, bf16[80,1024]{1,0:T(8,128)(2,1)S(1)}, u32[]{:S(2)}, u32[]{:S(2)}) collective-permute-start(bf16[80,1024]{1,0:T(8,128)(2,1)S(1)} %slice.31), channel_id=1, source_target_pairs={{0,2},{1,3},{2,6},{3,7},{4,0},{5,1},{6,10},{7,11},{8,4},{9,5},{10,... | collective-permute-start | bytes 491528 | tf_op jit(solution)/shard_map/ppermute | solution.py:1053
  45.2 7.8 %collective-permute-start.11 = (bf16[64,1024]{1,0:T(8,128)(2,1)S(1)}, bf16[64,1024]{1,0:T(8,128)(2,1)S(1)}, u32[]{:S(2)}, u32[]{:S(2)}) collective-permute-start(bf16[64,1024]{1,0:T(8,128)(2,1)S(1)} %slice.30), channel_id=1, source_target_pairs={{0,4},{1,5},{2,0},{3,1},{4,8},{5,9},{6,2},{7,3},{8,12},{9,13},{10,... | collective-permute-start | bytes 393224 | tf_op jit(solution)/shard_map/ppermute | solution.py:1053
  61.3 2.2 collective-permute-start.20
  61.4 14.3 %collective-permute-start.22 = (bf16[256,1024]{1,0:T(8,128)(2,1)S(1)}, bf16[256,1024]{1,0:T(8,128)(2,1)S(1)}, u32[]{:S(2)}, u32[]{:S(2)}) collective-permute-start(bf16[256,1024]{1,0:T(8,128)(2,1)S(1)} %collective-permute-done.18.refs_9_), channel_id=1, source_target_pairs={{0,4},{1,5},{2,0},{3,1},{4,8},{5,9},{6,2},{7,3},{8,12},{9,13},{10,... | collective-permute-start | bytes 1572872 | tf_op jit(solution)/shard_map/ppermute | solution.py:1053
  62.8 14.0 %collective-permute-start.23 = (bf16[256,1024]{1,0:T(8,128)(2,1)S(1)}, bf16[256,1024]{1,0:T(8,128)(2,1)S(1)}, u32[]{:S(2)}, u32[]{:S(2)}) collective-permute-start(bf16[256,1024]{1,0:T(8,128)(2,1)S(1)} %collective-permute-done.19.refs_10_), channel_id=1, source_target_pairs={{0,2},{1,3},{2,6},{3,7},{4,0},{5,1},{6,10},{7,11},{8,4},{9,5},{10,... | collective-permute-start | bytes 1572872 | tf_op jit(solution)/shard_map/ppermute | solution.py:1053
  63.6 13.2 %collective-permute-start.21 = (bf16[160,1024]{1,0:T(8,128)(2,1)S(1)}, bf16[160,1024]{1,0:T(8,128)(2,1)S(1)}, u32[]{:S(2)}, u32[]{:S(2)}) collective-permute-start(bf16[160,1024]{1,0:T(8,128)(2,1)S(1)} %fusion.3), channel_id=1, source_target_pairs={{0,16},{1,17},{2,18},{3,19},{4,20},{5,21},{6,22},{7,23},{8,24},{9,... | collective-permute-start | bytes 983048 | tf_op jit(solution)/shard_map/ppermute | solution.py:1053
  76.8 13.2 %collective-permute-start.26 = (bf16[256,1024]{1,0:T(8,128)(2,1)S(1)}, bf16[256,1024]{1,0:T(8,128)(2,1)S(1)}, u32[]{:S(2)}, u32[]{:S(2)}) collective-permute-start(bf16[256,1024]{1,0:T(8,128)(2,1)S(1)} %collective-permute-done.22.refs_11_), channel_id=1, source_target_pairs={{0,4},{1,5},{2,0},{3,1},{4,8},{5,9},{6,2},{7,3},{8,12},{9,13},{10,... | collective-permute-start | bytes 1572872 | tf_op jit(solution)/shard_map/ppermute | solution.py:1053
  78.4 12.9 %collective-permute-start.27 = (bf16[256,1024]{1,0:T(8,128)(2,1)S(1)}, bf16[256,1024]{1,0:T(8,128)(2,1)S(1)}, u32[]{:S(2)}, u32[]{:S(2)}) collective-permute-start(bf16[256,1024]{1,0:T(8,128)(2,1)S(1)} %collective-permute-done.23.refs_12_), channel_id=1, source_target_pairs={{0,2},{1,3},{2,6},{3,7},{4,0},{5,1},{6,10},{7,11},{8,4},{9,5},{10,... | collective-permute-start | bytes 1572872 | tf_op jit(solution)/shard_map/ppermute | solution.py:1053
  79.2 1.7 collective-permute-start.25
  79.3 10.1 %collective-permute-start.24 = (bf16[160,1024]{1,0:T(8,128)(2,1)S(1)}, bf16[160,1024]{1,0:T(8,128)(2,1)S(1)}, u32[]{:S(2)}, u32[]{:S(2)}) collective-permute-start(bf16[160,1024]{1,0:T(8,128)(2,1)S(1)} %get-tuple-element.179.refs_0_), channel_id=1, source_target_pairs={{0,16},{1,17},{2,18},{3,19},{4,20},{5,21},{6,22},{7,23},{8,24},{9,... | collective-permute-start | bytes 983048 | tf_op jit(solution)/shard_map/ppermute | solution.py:1053
  91.3 9.1 %collective-permute-start.28 = (bf16[160,1024]{1,0:T(8,128)(2,1)S(1)}, bf16[160,1024]{1,0:T(8,128)(2,1)S(1)}, u32[]{:S(2)}, u32[]{:S(2)}) collective-permute-start(bf16[160,1024]{1,0:T(8,128)(2,1)S(1)} %collective-permute-done.24.refs_2_), channel_id=1, source_target_pairs={{0,1},{1,0},{2,3},{3,2},{4,5},{5,4},{6,7},{7,6},{8,9},{9,8},{10,11... | collective-permute-start | bytes 983048 | tf_op jit(solution)/shard_map/ppermute | solution.py:1053
  91.3 8.8 %collective-permute-start.30 = (bf16[128,1024]{1,0:T(8,128)(2,1)S(1)}, bf16[128,1024]{1,0:T(8,128)(2,1)S(1)}, u32[]{:S(2)}, u32[]{:S(2)}) collective-permute-start(bf16[128,1024]{1,0:T(8,128)(2,1)S(1)} %slice.34), channel_id=1, source_target_pairs={{0,2},{1,3},{2,6},{3,7},{4,0},{5,1},{6,10},{7,11},{8,4},{9,5},{10,... | collective-permute-start | bytes 786440 | tf_op jit(solution)/shard_map/ppermute | solution.py:1053
  91.8 8.5 %collective-permute-start.29 = (bf16[128,1024]{1,0:T(8,128)(2,1)S(1)}, bf16[128,1024]{1,0:T(8,128)(2,1)S(1)}, u32[]{:S(2)}, u32[]{:S(2)}) collective-permute-start(bf16[128,1024]{1,0:T(8,128)(2,1)S(1)} %slice.33), channel_id=1, source_target_pairs={{0,4},{1,5},{2,0},{3,1},{4,8},{5,9},{6,2},{7,3},{8,12},{9,13},{10,... | collective-permute-start | bytes 786440 | tf_op jit(solution)/shard_map/ppermute | solution.py:1053
  108.2 2.2 collective-permute-start.31
  110.4 9.8 %collective-permute-start.32 = (bf16[160,1024]{1,0:T(8,128)(2,1)S(1)}, bf16[160,1024]{1,0:T(8,128)(2,1)S(1)}, u32[]{:S(2)}, u32[]{:S(2)}) collective-permute-start(bf16[160,1024]{1,0:T(8,128)(2,1)S(1)} %fusion.2), channel_id=1, source_target_pairs={{0,16},{1,17},{2,18},{3,19},{4,20},{5,21},{6,22},{7,23},{8,24},{9,... | collective-permute-start | bytes 983048 | tf_op jit(solution)/shard_map/ppermute | solution.py:1053
  123.1 12.0 %collective-permute-start.37 = (bf16[2,160,1024]{2,1,0:T(8,128)(2,1)S(1)}, bf16[2,160,1024]{2,1,0:T(8,128)(2,1)S(1)}, u32[]{:S(2)}, u32[]{:S(2)}) collective-permute-start(bf16[2,160,1024]{2,1,0:T(8,128)(2,1)S(1)} %get-tuple-element.213), channel_id=1, source_target_pairs={{0,1},{1,0},{2,3},{3,2},{4,5},{5,4},{6,7},{7,6},{8,9},{9,8},{10,11... | collective-permute-start | bytes 1966088 | tf_op jit(solution)/shard_map/ppermute | solution.py:1053
  123.1 11.9 %collective-permute-start.34 = (bf16[160,1024]{1,0:T(8,128)(2,1)S(1)}, bf16[160,1024]{1,0:T(8,128)(2,1)S(1)}, u32[]{:S(2)}, u32[]{:S(2)}) collective-permute-start(bf16[160,1024]{1,0:T(8,128)(2,1)S(1)} %get-tuple-element.206.refs_0_), channel_id=1, source_target_pairs={{0,1},{1,0},{2,3},{3,2},{4,5},{5,4},{6,7},{7,6},{8,9},{9,8},{10,11... | collective-permute-start | bytes 983048 | tf_op jit(solution)/shard_map/ppermute | solution.py:1053
  123.6 11.4 %collective-permute-start.33 = (bf16[160,1024]{1,0:T(8,128)(2,1)S(1)}, bf16[160,1024]{1,0:T(8,128)(2,1)S(1)}, u32[]{:S(2)}, u32[]{:S(2)}) collective-permute-start(bf16[160,1024]{1,0:T(8,128)(2,1)S(1)} %get-tuple-element.206.refs_0_), channel_id=1, source_target_pairs={{0,16},{1,17},{2,18},{3,19},{4,20},{5,21},{6,22},{7,23},{8,24},{9,... | collective-permute-start | bytes 983048 | tf_op jit(solution)/shard_map/ppermute | solution.py:1053
  125.7 8.1 %collective-permute-start.35 = (bf16[128,1024]{1,0:T(8,128)(2,1)S(1)}, bf16[128,1024]{1,0:T(8,128)(2,1)S(1)}, u32[]{:S(2)}, u32[]{:S(2)}) collective-permute-start(bf16[128,1024]{1,0:T(8,128)(2,1)S(1)} %get-tuple-element.209), channel_id=1, source_target_pairs={{0,4},{1,5},{2,0},{3,1},{4,8},{5,9},{6,2},{7,3},{8,12},{9,13},{10,... | collective-permute-start | bytes 786440 | tf_op jit(solution)/shard_map/ppermute | solution.py:1053
  127.3 7.7 %collective-permute-start.36 = (bf16[128,1024]{1,0:T(8,128)(2,1)S(1)}, bf16[128,1024]{1,0:T(8,128)(2,1)S(1)}, u32[]{:S(2)}, u32[]{:S(2)}) collective-permute-start(bf16[128,1024]{1,0:T(8,128)(2,1)S(1)} %get-tuple-element.210), channel_id=1, source_target_pairs={{0,2},{1,3},{2,6},{3,7},{4,0},{5,1},{6,10},{7,11},{8,4},{9,5},{10,... | collective-permute-start | bytes 786440 | tf_op jit(solution)/shard_map/ppermute | solution.py:1053
  135.1 3.5 %collective-permute-start.38 = (bf16[160,1024]{1,0:T(8,128)(2,1)S(1)}, bf16[160,1024]{1,0:T(8,128)(2,1)S(1)}, u32[]{:S(2)}, u32[]{:S(2)}) collective-permute-start(bf16[160,1024]{1,0:T(8,128)(2,1)S(1)} %collective-permute-done.33.refs_2_), channel_id=1, source_target_pairs={{0,1},{1,0},{2,3},{3,2},{4,5},{5,4},{6,7},{7,6},{8,9},{9,8},{10,11... | collective-permute-start | bytes 983048 | tf_op jit(solution)/shard_map/ppermute | solution.py:1053
  135.8 14.4 %collective-permute-start.39 = (bf16[256,1024]{1,0:T(8,128)(2,1)S(1)}, bf16[256,1024]{1,0:T(8,128)(2,1)S(1)}, u32[]{:S(2)}, u32[]{:S(2)}) collective-permute-start(bf16[256,1024]{1,0:T(8,128)(2,1)S(1)} %get-tuple-element.227), channel_id=1, source_target_pairs={{0,4},{1,5},{2,0},{3,1},{4,8},{5,9},{6,2},{7,3},{8,12},{9,13},{10,... | collective-permute-start | bytes 1572872 | tf_op jit(solution)/shard_map/ppermute | solution.py:1053
  137.4 14.0 %collective-permute-start.40 = (bf16[256,1024]{1,0:T(8,128)(2,1)S(1)}, bf16[256,1024]{1,0:T(8,128)(2,1)S(1)}, u32[]{:S(2)}, u32[]{:S(2)}) collective-permute-start(bf16[256,1024]{1,0:T(8,128)(2,1)S(1)} %get-tuple-element.228), channel_id=1, source_target_pairs={{0,2},{1,3},{2,6},{3,7},{4,0},{5,1},{6,10},{7,11},{8,4},{9,5},{10,... | collective-permute-start | bytes 1572872 | tf_op jit(solution)/shard_map/ppermute | solution.py:1053
  138.0 9.8 %collective-permute-start.41 = (bf16[160,1024]{1,0:T(8,128)(2,1)S(1)}, bf16[160,1024]{1,0:T(8,128)(2,1)S(1)}, u32[]{:S(2)}, u32[]{:S(2)}) collective-permute-start(bf16[160,1024]{1,0:T(8,128)(2,1)S(1)} %fusion.1), channel_id=1, source_target_pairs={{0,16},{1,17},{2,18},{3,19},{4,20},{5,21},{6,22},{7,23},{8,24},{9,... | collective-permute-start | bytes 983048 | tf_op jit(solution)/shard_map/ppermute | solution.py:1053
  151.4 7.8 %collective-permute-start.44 = (bf16[2,160,1024]{2,1,0:T(8,128)(2,1)S(1)}, bf16[2,160,1024]{2,1,0:T(8,128)(2,1)S(1)}, u32[]{:S(2)}, u32[]{:S(2)}) collective-permute-start(bf16[2,160,1024]{2,1,0:T(8,128)(2,1)S(1)} %get-tuple-element.240), channel_id=1, source_target_pairs={{0,1},{1,0},{2,3},{3,2},{4,5},{5,4},{6,7},{7,6},{8,9},{9,8},{10,11... | collective-permute-start | bytes 1966088 | tf_op jit(solution)/shard_map/ppermute | solution.py:1053
  152.2 23.3 %collective-permute-start.42 = (bf16[256,1024]{1,0:T(8,128)(2,1)S(1)}, bf16[256,1024]{1,0:T(8,128)(2,1)S(1)}, u32[]{:S(2)}, u32[]{:S(2)}) collective-permute-start(bf16[256,1024]{1,0:T(8,128)(2,1)S(1)} %get-tuple-element.233), channel_id=1, source_target_pairs={{0,4},{1,5},{2,0},{3,1},{4,8},{5,9},{6,2},{7,3},{8,12},{9,13},{10,... | collective-permute-start | bytes 1572872 | tf_op jit(solution)/shard_map/ppermute | solution.py:1053
  153.8 21.7 %collective-permute-start.43 = (bf16[256,1024]{1,0:T(8,128)(2,1)S(1)}, bf16[256,1024]{1,0:T(8,128)(2,1)S(1)}, u32[]{:S(2)}, u32[]{:S(2)}) collective-permute-start(bf16[256,1024]{1,0:T(8,128)(2,1)S(1)} %get-tuple-element.234), channel_id=1, source_target_pairs={{0,2},{1,3},{2,6},{3,7},{4,0},{5,1},{6,10},{7,11},{8,4},{9,5},{10,... | collective-permute-start | bytes 1572872 | tf_op jit(solution)/shard_map/ppermute | solution.py:1053
  157.1 12.5 %collective-permute-start.45 = (bf16[64,1024]{1,0:T(8,128)(2,1)S(1)}, bf16[64,1024]{1,0:T(8,128)(2,1)S(1)}, u32[]{:S(2)}, u32[]{:S(2)}) collective-permute-start(bf16[64,1024]{1,0:T(8,128)(2,1)S(1)} %get-tuple-element.246), channel_id=1, source_target_pairs={{0,4},{1,5},{2,0},{3,1},{4,8},{5,9},{6,2},{7,3},{8,12},{9,13},{10,... | collective-permute-start | bytes 393224 | tf_op jit(solution)/shard_map/ppermute | solution.py:1053
  158.5 12.9 %collective-permute-start.46 = (bf16[80,1024]{1,0:T(8,128)(2,1)S(1)}, bf16[80,1024]{1,0:T(8,128)(2,1)S(1)}, u32[]{:S(2)}, u32[]{:S(2)}) collective-permute-start(bf16[80,1024]{1,0:T(8,128)(2,1)S(1)} %get-tuple-element.247), channel_id=1, source_target_pairs={{0,2},{1,3},{2,6},{3,7},{4,0},{5,1},{6,10},{7,11},{8,4},{9,5},{10,... | collective-permute-start | bytes 491528 | tf_op jit(solution)/shard_map/ppermute | solution.py:1053
  159.3 23.5 %collective-permute-start.49 = (bf16[160,1024]{1,0:T(8,128)(2,1)S(1)}, bf16[160,1024]{1,0:T(8,128)(2,1)S(1)}, u32[]{:S(2)}, u32[]{:S(2)}) collective-permute-start(bf16[160,1024]{1,0:T(8,128)(2,1)S(1)} %fusion), channel_id=1, source_target_pairs={{0,16},{1,17},{2,18},{3,19},{4,20},{5,21},{6,22},{7,23},{8,24},{9,... | collective-permute-start | bytes 983048 | tf_op jit(solution)/shard_map/ppermute | solution.py:1053
  172.0 10.0 %collective-permute-start.47 = (bf16[144,1024]{1,0:T(8,128)(2,1)S(1)}, bf16[144,1024]{1,0:T(8,128)(2,1)S(1)}, u32[]{:S(2)}, u32[]{:S(2)}) collective-permute-start(bf16[144,1024]{1,0:T(8,128)(2,1)S(1)} %get-tuple-element.248), channel_id=1, source_target_pairs={{0,4},{1,5},{2,0},{3,1},{4,8},{5,9},{6,2},{7,3},{8,12},{9,13},{10,... | collective-permute-start | bytes 884744 | tf_op jit(solution)/shard_map/ppermute | solution.py:1053
  172.9 9.9 %collective-permute-start.48 = (bf16[144,1024]{1,0:T(8,128)(2,1)S(1)}, bf16[144,1024]{1,0:T(8,128)(2,1)S(1)}, u32[]{:S(2)}, u32[]{:S(2)}) collective-permute-start(bf16[144,1024]{1,0:T(8,128)(2,1)S(1)} %get-tuple-element.249), channel_id=1, source_target_pairs={{0,2},{1,3},{2,6},{3,7},{4,0},{5,1},{6,10},{7,11},{8,4},{9,5},{10,... | collective-permute-start | bytes 884744 | tf_op jit(solution)/shard_map/ppermute | solution.py:1053
  176.3 16.9 %collective-permute-start.52 = (bf16[256,1024]{1,0:T(8,128)(2,1)S(1)}, bf16[256,1024]{1,0:T(8,128)(2,1)S(1)}, u32[]{:S(2)}, u32[]{:S(2)}) collective-permute-start(bf16[256,1024]{1,0:T(8,128)(2,1)S(1)} %get-tuple-element.258), channel_id=1, source_target_pairs={{0,4},{1,5},{2,0},{3,1},{4,8},{5,9},{6,2},{7,3},{8,12},{9,13},{10,... | collective-permute-start | bytes 1572872 | tf_op jit(solution)/shard_map/ppermute | solution.py:1053
  177.2 16.9 %collective-permute-start.53 = (bf16[256,1024]{1,0:T(8,128)(2,1)S(1)}, bf16[256,1024]{1,0:T(8,128)(2,1)S(1)}, u32[]{:S(2)}, u32[]{:S(2)}) collective-permute-start(bf16[256,1024]{1,0:T(8,128)(2,1)S(1)} %get-tuple-element.259), channel_id=1, source_target_pairs={{0,2},{1,3},{2,6},{3,7},{4,0},{5,1},{6,10},{7,11},{8,4},{9,5},{10,... | collective-permute-start | bytes 1572872 | tf_op jit(solution)/shard_map/ppermute | solution.py:1053
  183.6 14.3 %collective-permute-start.50 = (bf16[144,1024]{1,0:T(8,128)(2,1)S(1)}, bf16[144,1024]{1,0:T(8,128)(2,1)S(1)}, u32[]{:S(2)}, u32[]{:S(2)}) collective-permute-start(bf16[144,1024]{1,0:T(8,128)(2,1)S(1)} %get-tuple-element.254), channel_id=1, source_target_pairs={{0,4},{1,5},{2,0},{3,1},{4,8},{5,9},{6,2},{7,3},{8,12},{9,13},{10,... | collective-permute-start | bytes 884744 | tf_op jit(solution)/shard_map/ppermute | solution.py:1053
  184.2 14.3 %collective-permute-start.51 = (bf16[144,1024]{1,0:T(8,128)(2,1)S(1)}, bf16[144,1024]{1,0:T(8,128)(2,1)S(1)}, u32[]{:S(2)}, u32[]{:S(2)}) collective-permute-start(bf16[144,1024]{1,0:T(8,128)(2,1)S(1)} %get-tuple-element.255), channel_id=1, source_target_pairs={{0,2},{1,3},{2,6},{3,7},{4,0},{5,1},{6,10},{7,11},{8,4},{9,5},{10,... | collective-permute-start | bytes 884744 | tf_op jit(solution)/shard_map/ppermute | solution.py:1053
  199.2 15.0 %collective-permute-start.61 = (bf16[256,1024]{1,0:T(8,128)(2,1)S(1)}, bf16[256,1024]{1,0:T(8,128)(2,1)}, u32[]{:S(2)}, u32[]{:S(2)}) collective-permute-start(bf16[256,1024]{1,0:T(8,128)(2,1)S(1)} %shard_map.300.own), channel_id=1, source_target_pairs={{0,16},{1,17},{2,18},{3,19},{4,20},{5,21},{6,22},{7,23},{8,24},{9,... | collective-permute-start | bytes 1572872 | tf_op jit(solution)/shard_map/ppermute | solution.py:1053
  200.5 6.9 %collective-permute-start.54 = (bf16[144,1024]{1,0:T(8,128)(2,1)S(1)}, bf16[144,1024]{1,0:T(8,128)(2,1)S(1)}, u32[]{:S(2)}, u32[]{:S(2)}) collective-permute-start(bf16[144,1024]{1,0:T(8,128)(2,1)S(1)} %get-tuple-element.262), channel_id=1, source_target_pairs={{0,4},{1,5},{2,0},{3,1},{4,8},{5,9},{6,2},{7,3},{8,12},{9,13},{10,... | collective-permute-start | bytes 884744 | tf_op jit(solution)/shard_map/ppermute | solution.py:1053
  201.3 6.7 %collective-permute-start.55 = (bf16[144,1024]{1,0:T(8,128)(2,1)S(1)}, bf16[144,1024]{1,0:T(8,128)(2,1)S(1)}, u32[]{:S(2)}, u32[]{:S(2)}) collective-permute-start(bf16[144,1024]{1,0:T(8,128)(2,1)S(1)} %get-tuple-element.263), channel_id=1, source_target_pairs={{0,2},{1,3},{2,6},{3,7},{4,0},{5,1},{6,10},{7,11},{8,4},{9,5},{10,... | collective-permute-start | bytes 884744 | tf_op jit(solution)/shard_map/ppermute | solution.py:1053
  208.6 9.0 %collective-permute-start.57 = (bf16[144,1024]{1,0:T(8,128)(2,1)S(1)}, bf16[144,1024]{1,0:T(8,128)(2,1)S(1)}, u32[]{:S(2)}, u32[]{:S(2)}) collective-permute-start(bf16[144,1024]{1,0:T(8,128)(2,1)S(1)} %shard_map.298.own), channel_id=1, source_target_pairs={{0,16},{1,17},{2,18},{3,19},{4,20},{5,21},{6,22},{7,23},{8,24},{9,... | collective-permute-start | bytes 884744 | tf_op jit(solution)/shard_map/ppermute | solution.py:1053
  210.1 14.5 %collective-permute-start.60 = (bf16[256,1024]{1,0:T(8,128)(2,1)S(1)}, bf16[256,1024]{1,0:T(8,128)(2,1)}, u32[]{:S(2)}, u32[]{:S(2)}) collective-permute-start(bf16[256,1024]{1,0:T(8,128)(2,1)S(1)} %shard_map.300.own), channel_id=1, source_target_pairs={{0,1},{1,0},{2,3},{3,2},{4,5},{5,4},{6,7},{7,6},{8,9},{9,8},{10,11... | collective-permute-start | bytes 1572872 | tf_op jit(solution)/shard_map/ppermute | solution.py:1053
  214.3 10.3 %collective-permute-start.62 = (bf16[256,1024]{1,0:T(8,128)(2,1)}, bf16[256,1024]{1,0:T(8,128)(2,1)}, u32[]{:S(2)}, u32[]{:S(2)}) collective-permute-start(bf16[256,1024]{1,0:T(8,128)(2,1)} %collective-permute-done.61.other), channel_id=1, source_target_pairs={{0,1},{1,0},{2,3},{3,2},{4,5},{5,4},{6,7},{7,6},{8,9},{9,8},{10,11... | collective-permute-start | bytes 1572872 | tf_op jit(solution)/shard_map/ppermute | solution.py:1053
  214.3 7.0 %collective-permute-start.56 = (bf16[144,1024]{1,0:T(8,128)(2,1)S(1)}, bf16[144,1024]{1,0:T(8,128)(2,1)}, u32[]{:S(2)}, u32[]{:S(2)}) collective-permute-start(bf16[144,1024]{1,0:T(8,128)(2,1)S(1)} %shard_map.298.own), channel_id=1, source_target_pairs={{0,1},{1,0},{2,3},{3,2},{4,5},{5,4},{6,7},{7,6},{8,9},{9,8},{10,11... | collective-permute-start | bytes 884744 | tf_op jit(solution)/shard_map/ppermute | solution.py:1053
  217.7 4.6 %collective-permute-start.58 = (bf16[144,1024]{1,0:T(8,128)(2,1)S(1)}, bf16[144,1024]{1,0:T(8,128)(2,1)}, u32[]{:S(2)}, u32[]{:S(2)}) collective-permute-start(bf16[144,1024]{1,0:T(8,128)(2,1)S(1)} %collective-permute-done.57.other), channel_id=1, source_target_pairs={{0,1},{1,0},{2,3},{3,2},{4,5},{5,4},{6,7},{7,6},{8,9},{9,8},{10,11... | collective-permute-start | bytes 884744 | tf_op jit(solution)/shard_map/ppermute | solution.py:1053
  217.7 4.6 %collective-permute-start.59 = (bf16[128,256]{1,0:T(8,128)(2,1)S(1)}, bf16[128,256]{1,0:T(8,128)(2,1)S(1)}, u32[]{:S(2)}, u32[]{:S(2)}) collective-permute-start(bf16[128,256]{1,0:T(8,128)(2,1)S(1)} %slice_select_fusion), channel_id=1, source_target_pairs={{0,2},{1,3},{2,0},{3,1},{4,6},{5,7},{6,4},{7,5},{8,10},{9,11},{10,... | collective-permute-start | bytes 196616 | tf_op jit(solution)/shard_map/ppermute | solution.py:1053
  (9 other events, 12.5 us)

commit v2 on v1

--- a/solution.py
+++ b/solution.py
@@ -457,6 +457,7 @@
 VMEM_SPEC = pl.BlockSpec(memory_space=pltpu.VMEM)
 SMEM_SPEC = pl.BlockSpec(memory_space=pltpu.SMEM)
 ANY_SPEC = pl.BlockSpec(memory_space=pl.ANY)
+HBM_SPEC = pl.BlockSpec(memory_space=pltpu.HBM)
 
 
 def kernel_call(body, in_specs, outs, scratch=(), micros=1):
@@ -513,42 +514,67 @@
     d_out[...] = (used_rows(info, rows) * cotangent[...].astype(F32)).astype(BF16)
 
 
-def chunks_body(info, w_qkv, got_qkv, w_fc, got_fc, w_proj, lent, w_out, vectors, got_vectors, shifts, first, second):
-    own_rows, width = w_proj.shape
+def own_part_body(info, w_qkv, w_proj, groups, half):
+    x = info[AT_X]
+    for z in range(w_qkv.shape[1] // (4 * HALF)):
+        at = pl.ds(pl.multiple_of(z * 4 * HALF + x * LANES, LANES), LANES)
+        groups[:, z * LANES : (z + 1) * LANES] = w_qkv[:, at]
+    half[...] = w_proj[:, : half.shape[1]]
+
+
+def first_chunk_body(info, groups, got_qkv, left, lent, vectors, got_vectors, first):
+    own_rows = left.shape[0]
+    width = 2 * left.shape[1]
     x, c, y = info[AT_X], info[AT_C], info[AT_Y]
     qkv = 3 * width // 4
     low = low_half((own_rows, LANES))
     for core in range(2):
         rows = slice(core * own_rows, (core + 1) * own_rows)
-        mine = c == core
-        for pair in range(w_qkv.shape[1] // (8 * HALF)):
-            groups = []
-            for z in range(2):
-                at = pl.ds(pl.multiple_of((2 * pair + z) * 4 * HALF + x * LANES, LANES), LANES)
-                groups.append(jnp.where(mine, w_qkv[:, at], got_qkv[:, at]).astype(F32))
-            first[rows, pair * LANES : (pair + 1) * LANES] = join(c, *groups, low).astype(BF16)
-        for p in range(w_fc.shape[1] // (4 * LANES)):
-            at = pl.ds(pl.multiple_of(p * 4 * LANES + (2 * c + x) * LANES, LANES), LANES)
-            second[rows, p * LANES : (p + 1) * LANES] = jnp.where(mine, w_fc[:, at], got_fc[:, at])
-    half = jnp.where(x == y, w_proj[:, : width // 2], lent[:, width // 2 :])
+        for pair in range(groups.shape[1] // (2 * LANES)):
+            both = []
+            for z in (2 * pair, 2 * pair + 1):
+                at = pl.ds(pl.multiple_of(z * 4 * HALF + x * LANES, LANES), LANES)
+                mine = groups[:, z * LANES : (z + 1) * LANES]
+                both.append(jnp.where(c == core, mine, got_qkv[:, at]).astype(F32))
+            first[rows, pair * LANES : (pair + 1) * LANES] = join(c, *both, low).astype(BF16)
+    half = jnp.where(x == y, left[...], lent[:, width // 2 :])
     first[:own_rows, qkv:] = half[:, : width // 4]
     first[own_rows : 2 * own_rows, qkv:] = half[:, width // 4 :]
-    piece = w_out.shape[0] // 2
-    second[2 * own_rows :, :] = w_out[pl.ds(pl.multiple_of(x * piece, piece), piece), :]
-    mine = vectors[...].astype(F32)
-    other = got_vectors[...].astype(F32)
-    lower = jnp.where(c == 0, mine[0:8], other[0:8])
-    upper = jnp.where(c == 0, other[0:8], mine[0:8])
-    blank = jnp.zeros(lower.shape, F32)
-    small = jnp.concatenate([lower, blank], axis=1) + turn(jnp.concatenate([upper, blank], axis=1))
-    heads = jnp.concatenate([mine[8:16], blank], axis=1)
-    heads = heads + turn(jnp.concatenate([mine[16:24], blank], axis=1))
-    both = shifts[...].astype(F32)
-    shift = jnp.broadcast_to(jnp.where(x == 0, both[0:1], both[1:2]), small.shape)
+    mine = vectors[0:8, :].astype(F32)
+    other = got_vectors[0:8, :].astype(F32)
+    shifts = vectors[8:16, :].astype(F32)
+    blank = jnp.zeros(mine.shape, F32)
+    lower = jnp.concatenate([jnp.where(c == 0, mine, other), blank], axis=1)
+    upper = jnp.concatenate([blank, jnp.where(c == 0, other, mine)], axis=1)
+    small = lower + upper
+    wide = jnp.concatenate([mine, blank], axis=1)
+    heads = jnp.where(low_half((1, LANES)), wide[6:7], turn(wide)[7:8])
+    shifts = jnp.concatenate([shifts, blank], axis=1)
+    shifts = jnp.where(x == 0, shifts, jnp.concatenate([shifts[2:], shifts[:2]], axis=0))
+    shift = jnp.where(low_half((1, LANES)), shifts[0:1], turn(shifts)[1:2])
     row = lax.broadcasted_iota(jnp.int32, small.shape, 0)
     small = jnp.where(row == 6, shift, jnp.where(row == 7, heads, small))
     first[2 * own_rows :, :] = jnp.zeros((SMALL_ROWS, width), BF16)
     first[2 * own_rows : 2 * own_rows + 8, :LANES] = small.astype(BF16)
+
+
+def second_chunks_body(info, w_fc, got_fc, came_forth, came_back, forth, back, sems):
+    own_rows = w_fc.shape[0]
+    chip_rows = 2 * own_rows
+    x, c = info[AT_X], info[AT_C]
+    copies = [
+        (came_forth, forth.at[pl.ds(chip_rows, chip_rows), :]),
+        (came_back, back.at[pl.ds(0, chip_rows), :]),
+    ]
+    for p in range(w_fc.shape[1] // (4 * LANES)):
+        source = pl.ds(pl.multiple_of(p * 4 * LANES + (2 * c + x) * LANES, LANES), LANES)
+        lanes = pl.ds(p * LANES, LANES)
+        for weight, core in ((w_fc, c), (got_fc, 1 - c)):
+            row = pl.multiple_of(core * own_rows, own_rows)
+            copies.append((weight.at[:, source], forth.at[pl.ds(row, own_rows), lanes]))
+    for copy in run_copies(copies, sems):
+        copy.wait()
+    back[chip_rows:, :] = forth[:chip_rows, :]
 
 
 def run_copies(copies, sems):
@@ -560,12 +586,28 @@
     return started
 
 
+def blocks_body(*refs):
+    blocks = refs[:RANKS]
+    units, masks = refs[RANKS:]
+    rows = units.shape[0] // RANKS
+    down = lax.broadcasted_iota(jnp.int32, (rows, rows), 0)
+    across = lax.broadcasted_iota(jnp.int32, (rows, rows), 1)
+    for b, block in enumerate(blocks):
+        center, inverse = statistics(block[:rows, :].astype(F32))
+        units[b * rows : (b + 1) * rows, :] = center * inverse
+        notes = block[rows : rows + SMALL_ROWS, : 2 * LANES].astype(F32)
+        seg_row, use_row = notes[0:1, :rows], notes[1:2, :rows]
+        seg_column = jnp.sum(jnp.where(down == across, seg_row, 0.0), axis=1, keepdims=True)
+        visible = (seg_column == seg_row) & (across <= down) & (use_row > 0)
+        masks[b] = jnp.where(visible, 1.0, 0.0)
+
+
 def attention_body(info, *refs):
-    blocks, chunks = refs[:RANKS], refs[RANKS : RANKS + ORIGINS]
+    units, masks, chunks = refs[0], refs[1], refs[2 : 2 + ORIGINS]
     normed, qkv, probs, context, send, keep_own, keep_away, qkv_weight, proj_weight, smalls = refs[
-        RANKS + ORIGINS : RANKS + ORIGINS + 10
+        2 + ORIGINS : 2 + ORIGINS + 10
     ]
-    masks, sems = refs[RANKS + ORIGINS + 10 :]
+    (sems,) = refs[2 + ORIGINS + 10 :]
     x = info[AT_X]
     width = normed.shape[1]
     rows = normed.shape[0] // RANKS
@@ -606,21 +648,11 @@
             )
     started = run_copies(copies, sems)
 
-    down = lax.broadcasted_iota(jnp.int32, (rows, rows), 0)
-    across = lax.broadcasted_iota(jnp.int32, (rows, rows), 1)
-    for b, block in enumerate(blocks):
-        notes = block[rows : rows + SMALL_ROWS, : 2 * LANES].astype(F32)
-        seg_row, use_row = notes[0:1, :rows], notes[1:2, :rows]
-        seg_column = jnp.sum(jnp.where(down == across, seg_row, 0.0), axis=1, keepdims=True)
-        visible = (seg_column == seg_row) & (across <= down) & (use_row > 0)
-        masks[b] = jnp.where(visible, 1.0, 0.0)
     for copy in started:
         copy.wait()
     gain = smalls[0:1, :].astype(F32)
     shift = smalls[1:2, :].astype(F32)
-    for b, block in enumerate(blocks):
-        center, inverse = statistics(block[:rows, :].astype(F32))
-        normed[b * rows : (b + 1) * rows, :] = (center * inverse * gain + shift).astype(BF16)
+    normed[...] = (units[...] * gain + shift).astype(BF16)
 
     low_row = low_half((8, LANES))
     biases = jnp.broadcast_to(smalls[7:8, :].astype(F32), (8, width))
@@ -683,35 +715,62 @@
     return keep_own[...] + near[0].astype(F32) + away[...].astype(F32)
 
 
-def second_norm_body(tokens, keep_own, near, away, smalls, middle, normed):
-    values = tokens[...].astype(F32) + smalls[2:3, :].astype(F32) + total(keep_own, near, away)
-    middle[...] = values
-    center, inverse = statistics(values)
+def message_body(keep_own, keep_away, near, message):
+    message[0] = (keep_own[...] + near[0].astype(F32)).astype(BF16)
+    message[1] = (keep_away[...] + near[1].astype(F32)).astype(BF16)
+
+
+def ends_body(forth, back, forth_end, back_end):
+    forth_end[...] = forth[: forth_end.shape[0], :]
+    back_end[...] = back[back.shape[0] - back_end.shape[0] :, :]
+
+
+def second_norm_body(block, block_other, keep_own, keep_away, near, got, smalls, middle, normed):
+    rows = keep_own.shape[0]
     gain, shift = smalls[3:4, :].astype(F32), smalls[4:5, :].astype(F32)
-    normed[...] = (center * inverse * gain + shift).astype(BF16)
-
-
-def feed_body(info, *refs):
-    inputs, d_outs = refs[:RANKS], refs[RANKS : 2 * RANKS]
-    chunks, smalls = refs[2 * RANKS : 2 * RANKS + ORIGINS], refs[2 * RANKS + ORIGINS]
-    given, d_out, hidden, d_pre, send, keep_own, keep_away, sums, out_weight = refs[
-        2 * RANKS + ORIGINS + 1 : 2 * RANKS + ORIGINS + 10
-    ]
-    fc_weight, sems = refs[2 * RANKS + ORIGINS + 10 :]
-    rows = inputs[0].shape[0]
+    for i, (tokens, keep) in enumerate(((block, keep_own), (block_other, keep_away))):
+        values = tokens[:rows, :].astype(F32) + smalls[2:3, :].astype(F32)
+        values = values + (keep[...] + near[i].astype(F32) + got[1 - i].astype(F32))
+        middle[i] = values
+        center, inverse = statistics(values)
+        normed[i] = (center * inverse * gain + shift).astype(BF16)
+
+
+def feed_body(info, normed, beside, *refs):
+    d_outs = refs[:RANKS]
+    (out_chunk, two_forth, two_back, three_forth, three_back, four_forth, four_back) = refs[RANKS : RANKS + 7]
+    five_forth, five_back, six_forth, six_back, smalls = refs[RANKS + 7 : RANKS + 12]
+    given, d_out, hidden, d_pre, send, keep_own, keep_away, sums, out_weight, fc_weight, sems = refs[RANKS + 12 :]
+    rows = normed.shape[1]
     width = given.shape[1]
-    chip_rows = chunks[0].shape[0] // 2
+    size = out_chunk.shape[0]
+    half = size // 2
     copies = []
-    for i, chunk in enumerate(chunks):
-        at = pl.ds(pl.multiple_of(info[i] * chip_rows, chip_rows), chip_rows)
-        if i != ORIGINS - 1:
-            copies.append((chunk.at[pl.ds(0, chip_rows), :], fc_weight.at[at, :]))
-        if i != ORIGINS - 2:
-            start = 0 if i == ORIGINS - 1 else chip_rows
-            copies.append((chunk.at[pl.ds(start, chip_rows), :], out_weight.at[at, :]))
+    for ref, start, count, weight, index, row in (
+        (two_forth, 0, size, fc_weight, 0, 0),
+        (three_forth, 0, size, fc_weight, 1, 0),
+        (three_back, size, size, fc_weight, 2, 0),
+        (four_forth, 0, size, fc_weight, 3, 0),
+        (four_back, size, size, fc_weight, 4, 0),
+        (five_forth, 0, size, fc_weight, 5, 0),
+        (five_back, half, size, fc_weight, 6, 0),
+        (six_forth, 0, half, fc_weight, 7, 0),
+        (six_back, 0, half, fc_weight, 7, half),
+        (out_chunk, 0, size, out_weight, 0, 0),
+        (two_forth, size, size, out_weight, 1, 0),
+        (two_back, 0, size, out_weight, 2, 0),
+        (three_forth, size, size, out_weight, 3, 0),
+        (three_back, 0, size, out_weight, 4, 0),
+        (four_forth, size, size, out_weight, 5, 0),
+        (four_back, 0, size, out_weight, 6, 0),
+        (five_forth, size, half, out_weight, 7, 0),
+        (five_back, 0, half, out_weight, 7, half),
+    ):
+        at = pl.multiple_of(info[index] * size + row, half)
+        copies.append((ref.at[pl.ds(start, count), :], weight.at[pl.ds(at, count), :]))
     started = run_copies(copies, sems)
     for b in range(RANKS):
-        given[b * rows : (b + 1) * rows, :] = inputs[b][...]
+        given[b * rows : (b + 1) * rows, :] = (beside if b % 2 else normed)[b // 2]
         d_out[b * rows : (b + 1) * rows, :] = d_outs[b][...]
     for copy in started:
         copy.wait()
@@ -750,37 +809,38 @@
 
 
 def mixed_body(info, middle, keep_own, near, away, smalls, mixed):
-    values = middle[...] + total(keep_own, near, away) + smalls[5:6, :].astype(F32)
-    mixed[...] = (used_rows(info, middle.shape[0]) * values).astype(BF16)
-
-
-def second_back_body(info, middle, cotangent, keep_own, near, away, smalls, d_middle, d_branch, sums):
-    d_values = total(keep_own, near, away)
-    d_top = used_rows(info, middle.shape[0]) * cotangent[...].astype(F32)
-    center, inverse = statistics(middle[...])
-    unit = center * inverse
-    result = d_top + norm_back(unit, inverse, d_values * smalls[3:4, :].astype(F32))
-    d_middle[...] = result
-    low = result.astype(BF16)
-    d_branch[...] = low
-    sums[...] = jnp.zeros(sums.shape, F32)
-    sums[2:3, :] = jnp.sum(low.astype(F32), axis=0, keepdims=True)
-    sums[3:4, :] = jnp.sum(d_values * unit, axis=0, keepdims=True)
-    sums[4:5, :] = jnp.sum(d_values, axis=0, keepdims=True)
-    sums[5:6, :] = jnp.sum(d_top, axis=0, keepdims=True)
-
-
-def attention_back_body(info, *refs):
-    d_branches, blocks = refs[:RANKS], refs[RANKS : 2 * RANKS]
-    qkv, probs, qkv_weight, proj_weight, sums_two, sums_fc = refs[2 * RANKS : 2 * RANKS + 6]
-    d_branch, d_qkv, send, keep_own, keep_away, sums = refs[2 * RANKS + 6 : 2 * RANKS + 12]
-    (d_context,) = refs[2 * RANKS + 12 :]
-    rows = d_branches[0].shape[0]
+    values = middle[0] + total(keep_own, near, away) + smalls[5:6, :].astype(F32)
+    mixed[...] = (used_rows(info, keep_own.shape[0]) * values).astype(BF16)
+
+
+def second_back_body(middle, d_top, d_other, keep_own, keep_away, near, got, smalls, d_middle, d_branch, sums):
+    gain = smalls[3:4, :].astype(F32)
+    for i, (d_out, keep) in enumerate(((d_top, keep_own), (d_other, keep_away))):
+        d_values = keep[...] + near[i].astype(F32) + got[1 - i].astype(F32)
+        center, inverse = statistics(middle[i])
+        unit = center * inverse
+        result = d_out[...].astype(F32) + norm_back(unit, inverse, d_values * gain)
+        low = result.astype(BF16)
+        d_branch[i] = low
+        if i == 0:
+            d_middle[...] = result
+            sums[...] = jnp.zeros(sums.shape, F32)
+            sums[2:3, :] = jnp.sum(low.astype(F32), axis=0, keepdims=True)
+            sums[3:4, :] = jnp.sum(d_values * unit, axis=0, keepdims=True)
+            sums[4:5, :] = jnp.sum(d_values, axis=0, keepdims=True)
+            sums[5:6, :] = jnp.sum(d_out[...].astype(F32), axis=0, keepdims=True)
+
+
+def attention_back_body(info, branches, beside, units, *refs):
+    qkv, probs, qkv_weight, proj_weight, sums_two, sums_fc = refs[:6]
+    d_branch, d_qkv, send, keep_own, keep_away, sums = refs[6:12]
+    (d_context,) = refs[12:]
+    rows = branches.shape[1]
     width = d_branch.shape[1]
     third = width // 4
     x = info[AT_X]
     for b in range(RANKS):
-        d_branch[b * rows : (b + 1) * rows, :] = d_branches[b][...]
+        d_branch[b * rows : (b + 1) * rows, :] = (beside if b % 2 else branches)[b // 2]
     d_context[...] = dot_cols(d_branch[...], proj_weight[...]).astype(BF16)
     scale = HALF ** (-0.5)
     low = low_half((1, LANES))
@@ -814,23 +874,12 @@
     lax.fori_loop(0, RANKS, attend, 0)
     sums[0:8, :] = sums_two[...] + sums_fc[...]
     sums[8:, :] = jnp.zeros((SMALL_ROWS - 8, width), F32)
-    stats = []
-    for block in blocks:
-        values = block[:rows, :].astype(F32)
-        mean = jnp.mean(values, axis=-1, keepdims=True)
-        center = values - mean
-        stats.append((mean, lax.rsqrt(jnp.mean(center * center, axis=-1, keepdims=True) + 1e-05)))
     for n in range(4):
         columns = slice(n * third, (n + 1) * third)
         product = dot_cols(d_qkv[...], qkv_weight[columns, :])
         store_parts(product, columns, rows, send, keep_own, keep_away)
         sums[1:2, columns] = jnp.sum(product, axis=0, keepdims=True)
-        along = jnp.zeros((1, third), F32)
-        for b, block in enumerate(blocks):
-            mean, inverse = stats[b]
-            unit = (block[:rows, columns].astype(F32) - mean) * inverse
-            along = along + jnp.sum(product[b * rows : (b + 1) * rows] * unit, axis=0, keepdims=True)
-        sums[0:1, columns] = along
+        sums[0:1, columns] = jnp.sum(product * units[:, columns], axis=0, keepdims=True)
     low_row = low_half((8, LANES))
     for pair in range(2):
         lanes = pair * LANES
@@ -990,7 +1039,7 @@
         ).astype(F32)
 
 
-def first_grads_body(info, own, near, other, cross, given, grad_qkv, grad_proj, *small_outs):
+def first_grads_body(info, own, near, other, cross, side, corner, grad_qkv, grad_proj, *small_outs):
     x, c, y = info[AT_X], info[AT_C], info[AT_Y]
     own_rows, width = grad_proj.shape
     qkv = 3 * width // 4
@@ -1011,12 +1060,12 @@
         block = slice(part * own_rows, (part + 1) * own_rows)
         left = jnp.where(x == y, own[block, qkv:], other[block, qkv:]).astype(F32)
         grad_proj[:, part * quarter : (part + 1) * quarter] = left
-        right = given[block, :].astype(F32)
+        right = jnp.where(x == y, side[block, :], corner[block, :]).astype(F32)
         grad_proj[:, 2 * quarter + part * quarter : 2 * quarter + (part + 1) * quarter] = right
-    mine, side, far, corner = (
+    mine, beside, far, across = (
         ref[2 * own_rows :, :LANES].astype(F32) for ref in (own, near, other, cross)
     )
-    summed = (mine + side) + (far + corner)
+    summed = (mine + beside) + (far + across)
     summed = jnp.where(c == 0, summed, turn(summed))
     heads = jnp.where(x == y, mine, far)
     for i in range(6):
@@ -1057,6 +1106,7 @@
     to_next = mover(lambda r, p, c: (r, after[p], c))
     to_back = mover(lambda r, p, c: (r, before[p], c))
     to_side = mover(lambda r, p, c: (r, p ^ 1, c))
+    to_corner = mover(lambda r, p, c: (r ^ 1, p ^ 1, c))
 
     def local(
         tokens,
@@ -1103,52 +1153,69 @@
             [origin(place + offset) for offset in offsets] + [x, c, p % 2, counts[0]]
         ).astype(jnp.int32)
 
-        got_qkv, got_fc, lent = to_core(w_qkv), to_core(w_fc), to_side(w_proj)
-        none = jnp.zeros((own_rows,), BF16)
+        got_qkv, lent = to_core(w_qkv), to_side(w_proj)
         vectors = jnp.stack(
-            [ln1_gain, ln1_bias, bias_proj, ln2_gain, ln2_bias, bias_out]
-            + [none] * 9
-            + [bias_query]
-            + [none] * 7
-            + [bias_value]
+            [ln1_gain, ln1_bias, bias_proj, ln2_gain, ln2_bias, bias_out, bias_query, bias_value]
+            + [bias_fc[i * own_rows : (i + 1) * own_rows] for i in range(4)]
+            + [jnp.zeros((own_rows,), BF16)] * 4
         )
         got_vectors = to_core(vectors)
+        groups, left = kernel_call(
+            own_part_body,
+            [SMEM_SPEC] + [VMEM_SPEC] * 2,
+            [((own_rows, 3 * width // 2), BF16), ((own_rows, width // 2), BF16)],
+        )(info, w_qkv, w_proj)
+        out_chunk = lax.dynamic_slice_in_dim(w_out, x * piece, piece, 0)
+        groups, out_chunk = tie(groups, out_chunk)
+        out_forth, out_back = to_next(out_chunk), to_back(out_chunk)
         block, d_top = kernel_call(
             tokens_body,
             [SMEM_SPEC] + [VMEM_SPEC] * 3,
             [((rows + SMALL_ROWS, width), BF16), ((rows, width), BF16)],
         )(info, tokens, segments.reshape(1, rows), cotangent)
-        first_chunk, second_chunk = kernel_call(
-            chunks_body, [SMEM_SPEC] + [VMEM_SPEC] * 10, [first_shape, second_shape], micros=2
-        )(
-            info, w_qkv, got_qkv, w_fc, got_fc, w_proj, lent, w_out, vectors, got_vectors,
-            bias_fc.reshape(2, piece),
-        )
-
-        firsts = [first_chunk]
+        (first_chunk,) = kernel_call(
+            first_chunk_body, [SMEM_SPEC] + [VMEM_SPEC] * 6, [first_shape], micros=2
+        )(info, groups, got_qkv, left, lent, vectors, got_vectors)
+
+        first_chunk, later_fc = tie(first_chunk, w_fc)
         forth, back = to_next(first_chunk), to_back(first_chunk)
+        got_fc = to_core(later_fc)
+        firsts = [first_chunk, forth, back]
+        forth, back, block = tie(forth, back, block)
         block_other = to_copy(block)
-        for step in range(1, half):
-            firsts += [forth, back]
-            if step < half - 1:
-                forth, back = to_next(forth), to_back(back)
-            if step == 1:
-                block_other, d_top, forth, back = tie(block_other, d_top, forth, back)
-                blocks = [block, to_core(block), block_other, to_core(block_other)]
-                d_other = to_copy(d_top)
-            if step == half - 2:
-                second_chunk, forth, back = tie(second_chunk, forth, back)
-                seconds = [second_chunk]
-                second_forth, second_back = to_next(second_chunk), to_back(second_chunk)
-        d_outs = [d_top, to_core(d_top), d_other, to_core(d_other)]
-        firsts += [to_next(forth[:own_rows]), to_back(back[own_rows:])]
+        blocks = [block, to_core(block), block_other, to_core(block_other)]
+        forth, back = to_next(forth), to_back(back)
+        firsts += [forth, back]
+        forth, back = to_next(forth), to_back(back)
+        firsts += [forth, back]
+        two_forth, two_back = kernel_call(
+            second_chunks_body,
+            [SMEM_SPEC] + [HBM_SPEC] * 4,
+            [second_shape, second_shape],
+            [pltpu.SemaphoreType.DMA((2 + 2 * n_pos,))],
+            micros=2,
+        )(info, w_fc, got_fc, out_forth, out_back)
+        blocks = tie(*blocks, forth[:own_rows], back[own_rows:], two_forth, two_back)
+        forth, back, two_forth, two_back = blocks[RANKS:]
+        blocks = blocks[:RANKS]
+        unit, masks = kernel_call(
+            blocks_body,
+            [VMEM_SPEC] * RANKS,
+            [((all_rows, width), F32), ((RANKS, rows, rows), F32)],
+            micros=2,
+        )(*blocks)
+        forth, back, two_forth, two_back, d_top = tie(
+            to_next(forth), to_back(back), two_forth, two_back, d_top
+        )
+        firsts += [forth, back]
+        three_forth, three_back = to_next(two_forth), to_back(two_back)
 
         parts = [((2, rows, width), BF16), ((rows, width), F32), ((rows, width), F32)]
-        tied = tie(*firsts, *blocks, *d_outs)
-        firsts, blocks, d_outs = tied[:ORIGINS], tied[ORIGINS : ORIGINS + RANKS], tied[ORIGINS + RANKS :]
+        two_blocks = ((2, rows, width), BF16)
+        d_other = to_copy(d_top)
         normed, qkv, probs, context, send, keep_own, keep_away, qkv_weight, proj_weight, smalls = kernel_call(
             attention_body,
-            [SMEM_SPEC] + [VMEM_SPEC] * RANKS + [ANY_SPEC] * ORIGINS,
+            [SMEM_SPEC] + [VMEM_SPEC] * 2 + [ANY_SPEC] * ORIGINS,
             [
                 ((all_rows, width), BF16),
                 ((all_rows, qkv_cols), BF16),
@@ -1159,30 +1226,37 @@
                 ((width // 4, width), BF16),
                 ((SMALL_ROWS, width), BF16),
             ],
-            [pltpu.VMEM((RANKS, rows, rows), F32), pltpu.SemaphoreType.DMA((5 * n_pos,))],
+            [pltpu.SemaphoreType.DMA((5 * n_pos,))],
             micros=8,
-        )(info, *blocks, *firsts)
-        send, second_forth, second_back = tie(send, second_forth, second_back)
-        seconds += [second_forth, second_back]
+        )(info, unit, masks, *firsts)
+        send, d_top, d_other, three_forth, three_back = tie(
+            send, d_top, d_other, three_forth, three_back
+        )
         near = to_core(send)
-        second_forth, second_back = to_next(second_forth), to_back(second_back)
-        away = to_copy(add(keep_away, near[1]))
-        away, second_forth, second_back = tie(away, second_forth, second_back)
-        seconds += [second_forth, second_back]
+        four_forth, four_back = to_next(three_forth), to_back(three_back)
+
+        def message(keep_own, keep_away, near):
+            return kernel_call(message_body, [VMEM_SPEC] * 3, [two_blocks], micros=0)(
+                keep_own, keep_away, near
+            )[0]
+
+        got = to_copy(message(keep_own, keep_away, near))
+        d_outs = [d_top, to_core(d_top), d_other, to_core(d_other)]
+        five_forth, five_back = kernel_call(
+            ends_body, [VMEM_SPEC] * 2, [((chip_rows + own_rows, width), BF16)] * 2, micros=6
+        )(four_forth, four_back)
+        five_forth, five_back = to_next(five_forth), to_back(five_back)
+        got, five_forth, five_back = tie(got, five_forth, five_back)
         middle, normed_two = kernel_call(
-            second_norm_body, [VMEM_SPEC] * 5, [((rows, width), F32), ((rows, width), BF16)]
-        )(tokens, keep_own, near, away, smalls)
-        second_forth, second_back = to_next(second_forth), to_back(second_back)
-        other = to_copy(normed_two)
+            second_norm_body, [VMEM_SPEC] * 7, [((2, rows, width), F32), two_blocks], micros=2
+        )(block, block_other, keep_own, keep_away, near, got, smalls)
         beside = to_core(normed_two)
-        other, beside, second_forth, second_back = tie(other, beside, second_forth, second_back)
-        seconds += [second_forth, second_back]
-        seconds += [to_next(second_forth[:chip_rows]), to_back(second_back[chip_rows:])]
-        inputs = [normed_two, beside, other, to_core(other)]
+        six_forth = to_next(five_forth[:own_rows])
+        six_back = to_back(five_back[chip_rows:])
 
         given, d_out, hidden, d_pre, send, keep_own, keep_away, sums_fc, out_weight = kernel_call(
             feed_body,
-            [SMEM_SPEC] + [VMEM_SPEC] * (2 * RANKS) + [ANY_SPEC] * ORIGINS + [VMEM_SPEC],
+            [SMEM_SPEC] + [VMEM_SPEC] * (2 + RANKS) + [ANY_SPEC] * 11 + [VMEM_SPEC],
             [
                 ((all_rows, width), BF16),
                 ((all_rows, width), BF16),
@@ -1192,52 +1266,52 @@
                 ((8, units), F32),
                 ((units, width), BF16),
             ],
-            [pltpu.VMEM((width, units), BF16), pltpu.SemaphoreType.DMA((2 * n_pos,))],
-            micros=10,
-        )(info, *inputs, *d_outs, *seconds, smalls)
+            [pltpu.VMEM((width, units), BF16), pltpu.SemaphoreType.DMA((18,))],
+            micros=8,
+        )(
+            info, normed_two, beside, *d_outs, out_chunk, two_forth, two_back, three_forth, three_back,
+            four_forth, four_back, five_forth, five_back, six_forth, six_back, smalls,
+        )
 
         near = to_core(send)
         near, given, d_out, hidden, d_pre = tie(near, given, d_out, hidden, d_pre)
-        away = to_copy(add(keep_away, near[1]))
+        got = to_copy(message(keep_own, keep_away, near))
         grad_w_out = dot_rows(hidden, d_out).astype(BF16)
         grad_w_fc = dot_rows(given, d_pre).astype(BF16)
-        away, grad_w_out, grad_w_fc = tie(away, grad_w_out, grad_w_fc)
         far_forth, far_back = kernel_call(
             second_far_body,
             [SMEM_SPEC] + [VMEM_SPEC] * 2,
             [((chip_rows, width), BF16), ((piece, width), BF16)],
         )(info, grad_w_fc, grad_w_out)
+        far_forth, far_back, hidden = tie(far_forth, far_back, hidden)
         far_forth, far_back = to_next(far_forth), to_back(far_back)
-
-        def second_hop(step, got_forth, got_back):
-            forth, back = kernel_call(
+        mix_send, mix_keep, mix_away = kernel_call(
+            feed_out_body, [VMEM_SPEC] * 2, parts, micros=2
+        )(hidden, out_weight)
+        mix_near = to_core(mix_send)
+
+        def second_sums(step, got_forth, got_back):
+            return kernel_call(
                 functools.partial(second_hop_body, step),
                 [SMEM_SPEC] + [VMEM_SPEC] * 4,
                 [second_shape, second_shape],
             )(info, got_forth, got_back, grad_w_fc, grad_w_out)
-            return to_next(forth), to_back(back)
-
-        d_middle, d_branch, sums_two = kernel_call(
+
+        second_forth, second_back = second_sums(half - 1, far_forth, far_back)
+        got, second_forth, second_back, mix_near = tie(got, second_forth, second_back, mix_near)
+        second_forth, second_back = to_next(second_forth), to_back(second_back)
+        d_middle, d_branches, sums_two = kernel_call(
             second_back_body,
-            [SMEM_SPEC] + [VMEM_SPEC] * 6,
-            [((rows, width), F32), ((rows, width), BF16), ((8, width), F32)],
-        )(info, middle, cotangent, keep_own, near, away, smalls)
-        other, beside = to_copy(d_branch), to_core(d_branch)
-        hidden, out_weight, d_branch = tie(hidden, out_weight, d_branch)
-        mix_send, mix_keep, mix_away = kernel_call(
-            feed_out_body, [VMEM_SPEC] * 2, parts, micros=2
-        )(hidden, out_weight)
-        mix_near = to_core(mix_send)
-        other, beside, far_forth, far_back, mix_near = tie(
-            other, beside, far_forth, far_back, mix_near
-        )
-        d_branches = [d_branch, beside, other, to_core(other)]
-        second_forth, second_back = second_hop(half - 1, far_forth, far_back)
+            [VMEM_SPEC] * 8,
+            [((rows, width), F32), two_blocks, ((8, width), F32)],
+            micros=2,
+        )(middle, d_top, d_other, keep_own, keep_away, near, got, smalls)
+        beside = to_core(d_branches)
         mix_away = to_copy(add(mix_away, mix_near[1]))
 
         d_branch, d_qkv, send, keep_own, keep_away, sums = kernel_call(
             attention_back_body,
-            [SMEM_SPEC] + [VMEM_SPEC] * (2 * RANKS + 6),
+            [SMEM_SPEC] + [VMEM_SPEC] * 9,
             [
                 ((all_rows, width), BF16),
                 ((all_rows, qkv_cols), BF16),
@@ -1246,11 +1320,7 @@
             ],
             [pltpu.VMEM((all_rows, width // 4), BF16)],
             micros=9,
-        )(info, *d_branches, *blocks, qkv, probs, qkv_weight, proj_weight, sums_two, sums_fc)
-        send, d_branch, d_qkv, second_forth, second_back, mix_away = tie(
-            send, d_branch, d_qkv, second_forth, second_back, mix_away
-        )
-        second_forth, second_back = second_hop(half - 2, second_forth, second_back)
+        )(info, d_branches, beside, unit, qkv, probs, qkv_weight, proj_weight, sums_two, sums_fc)
         grad_w_proj = dot_rows(context, d_branch).astype(BF16)
         grad_w_qkv = dot_rows(normed, d_qkv).astype(BF16)
         firsts = (grad_w_qkv, grad_w_proj, sums)
@@ -1259,37 +1329,53 @@
             [SMEM_SPEC] + [VMEM_SPEC] * 3,
             [((own_rows, width), BF16), ((own_rows + SMALL_ROWS, width), BF16)],
         )(info, *firsts)
-        near = to_core(send)
+        send, forth, back, second_forth, second_back, mix_away = tie(
+            send, forth, back, second_forth, second_back, mix_away
+        )
         forth, back = to_next(forth), to_back(back)
-        (mixed,) = kernel_call(mixed_body, [SMEM_SPEC] + [VMEM_SPEC] * 5, [((rows, width), BF16)])(
-            info, middle, mix_keep, mix_near, mix_away, smalls
-        )
-        away = to_copy(add(keep_away, near[1]))
-        for step in range(half - 1, 0, -1):
-            forth, back = kernel_call(
+        second_forth, second_back = second_sums(half - 2, second_forth, second_back)
+
+        def first_sums(step, forth, back):
+            return kernel_call(
                 functools.partial(first_hop_body, step),
                 [SMEM_SPEC] + [VMEM_SPEC] * 5,
                 [first_shape, first_shape],
             )(info, forth, back, *firsts)
-            forth, back = to_next(forth), to_back(back)
-            if step == half - 1:
-                second_forth, second_back, mixed = tie(second_forth, second_back, mixed)
-                for last in range(half - 3, 0, -1):
-                    second_forth, second_back = second_hop(last, second_forth, second_back)
-                forth, back, away = tie(forth, back, away)
-            elif step == half - 2:
-                forth, back, second_forth, second_back = tie(forth, back, second_forth, second_back)
-                (own_second,) = kernel_call(
-                    second_last_body, [SMEM_SPEC] + [VMEM_SPEC] * 4, [second_shape]
-                )(info, second_forth, second_back, grad_w_fc, grad_w_out)
-                near_second, other_second = to_core(own_second), to_copy(own_second)
+
+        second_forth, second_back = to_next(second_forth), to_back(second_back)
+        forth, back, send = tie(forth, back, send)
+        near = to_core(send)
+        away = to_copy(add(keep_away, near[1]))
+        forth, back = first_sums(3, forth, back)
+        forth, back = to_next(forth), to_back(back)
+        second_forth, second_back, away = tie(second_forth, second_back, away)
+        second_forth, second_back = second_sums(1, second_forth, second_back)
+        second_forth, second_back = to_next(second_forth), to_back(second_back)
+        (grad_tokens,) = kernel_call(first_back_body, [VMEM_SPEC] * 6, [((rows, width), F32)])(
+            tokens, d_middle, keep_own, near, away, smalls
+        )
+        forth, back, grad_tokens = tie(forth, back, grad_tokens)
+        forth, back = first_sums(2, forth, back)
+        forth, back = to_next(forth), to_back(back)
+        (mixed,) = kernel_call(mixed_body, [SMEM_SPEC] + [VMEM_SPEC] * 5, [((rows, width), BF16)])(
+            info, middle, mix_keep, mix_near, mix_away, smalls
+        )
+        forth, back, second_forth, second_back, mixed = tie(
+            forth, back, second_forth, second_back, mixed
+        )
+        (own_second,) = kernel_call(
+            second_last_body, [SMEM_SPEC] + [VMEM_SPEC] * 4, [second_shape]
+        )(info, second_forth, second_back, grad_w_fc, grad_w_out)
+        near_second, other_second = to_core(own_second), to_copy(own_second)
+        forth, back = first_sums(1, forth, back)
+        forth, back = to_next(forth), to_back(back)
+        forth, back, mixed = tie(forth, back, mixed)
         (own_first,) = kernel_call(
             first_last_body, [SMEM_SPEC] + [VMEM_SPEC] * 5, [first_shape]
         )(info, forth, back, *firsts)
         near_first, other_first = to_core(own_first), to_copy(own_first)
-        (grad_tokens,) = kernel_call(first_back_body, [VMEM_SPEC] * 6, [((rows, width), F32)])(
-            tokens, d_middle, keep_own, near, away, smalls
-        )
+        own_proj = own_first[:chip_rows, qkv_cols:]
+        given_side, given_far = to_side(own_proj), to_corner(own_proj)
 
         grad_w_fc, grad_w_out = kernel_call(
             hidden_grads_body,
@@ -1297,18 +1383,18 @@
             [((own_rows, 4 * units), F32), ((2 * piece, width), F32)],
         )(info, own_second, near_second, other_second, to_core(other_second))
 
-        given = jnp.where(
-            x == p % 2, other_first[:chip_rows, qkv_cols:], own_first[:chip_rows, qkv_cols:]
+        other_first, given_side, given_far, grad_w_fc, grad_w_out = tie(
+            other_first, given_side, given_far, grad_w_fc, grad_w_out
         )
         vector_shape = ((1, own_rows), F32)
         grad_w_qkv, grad_w_proj, *small = kernel_call(
             first_grads_body,
-            [SMEM_SPEC] + [VMEM_SPEC] * 5,
+            [SMEM_SPEC] + [VMEM_SPEC] * 6,
             [((own_rows, 3 * width), F32), ((own_rows, width), F32)]
             + [vector_shape] * 6
             + [((2, piece), F32)]
             + [vector_shape] * 2,
-        )(info, own_first, near_first, other_first, to_core(other_first), to_side(given))
+        )(info, own_first, near_first, other_first, to_core(other_first), given_side, given_far)
         small = [value.reshape(-1) for value in small]
         return (
             mixed,

time: 228 us -> 217 us (0.952)
  waiting for transfers between devices: 114 us -> 108 us
  local copies, waits for them, and re-layouts: 8.03 us -> 3.8 us
    ppermute x63 -> x62, waiting for transfers between devices: 114 us -> 108 us  [mover(): return lambda v: lax.ppermute(v, MESH_AXES, pairs)]
    unnamed x20 -> x16, local copies, waits for them, and re-layouts: 5.67 us -> 1.93 us
    pallas_call x13 -> x19, Pallas kernels: 34.2 us -> 35.6 us  [the longest x1 8.54 us: local(): kernel_call(attention_back_body, [SMEM_SPEC] + [VMEM_SPEC] * 9, [((all_ro...]
    ppermute x63 -> x62, starting transfers between devices: 53 us -> 52.4 us  [mover(): return lambda v: lax.ppermute(v, MESH_AXES, pairs)]
  transfers between devices with their start and end apart: 63 -> 62, of which waited for: 38 -> 28; matrix products, arithmetic and copies ran while one was open for 4% -> 4% of each run, Pallas kernels for 13% -> 14%
where the time goes in v2:
time: 217 us
  waiting for transfers between devices  108 us (50%)
  starting transfers between devices  52.4 us (24%)
  Pallas kernels  45.3 us (21%)
  matrix products  5.72 us (3%)
  local copies, waits for them, and re-layouts  3.8 us (2%)
    ppermute x62, waiting for transfers between devices, mover(): return lambda v: lax.ppermute(v, MESH_AXES, pairs)  108 us
    ppermute x62, starting transfers between devices, mover(): return lambda v: lax.ppermute(v, MESH_AXES, pairs)  52.4 us
    pallas_call x1, Pallas kernels, local(): kernel_call(attention_back_body, [SMEM_SPEC] + [VMEM_SPEC] * 9, [((all_ro...  8.54 us
    pallas_call x1, Pallas kernels, local(): kernel_call(feed_body, [SMEM_SPEC] + [VMEM_SPEC] * (2 + RANKS) + [ANY_SPE...  8.46 us
    pallas_call x1, Pallas kernels, local(): kernel_call(attention_body, [SMEM_SPEC] + [VMEM_SPEC] * 2 + [ANY_SPEC] *...  7.22 us
    dot_general x4, matrix products, dot_rows(): lax.dot_general(left, right, (((0,), (0,)), ((), ())), preferred_element_...  5.72 us
  transfers between devices with their start and end apart: 62, of which 28 were waited for; matrix products, arithmetic and copies ran while one was open for 4% of the time, Pallas kernels for 14%

profile of v2, /device:TPU:0, one launch (start us, length us, event | category | flops | bytes accessed | tf_op | source)
XLA Modules:
  0.0 217.3 jit_solution(15996114011980265477)
XLA Ops:
  1.2 2.6 %collective-permute-start.1 = (bf16[64,1024]{1,0:T(8,128)(2,1)}, bf16[64,1024]{1,0:T(8,128)(2,1)S(1)}, u32[]{:S(2)}, u32[]{:S(2)}) collective-permute-start(bf16[64,1024]{1,0:T(8,128)(2,1)} %w_proj.1), channel_id=1, source_target_pairs={{0,2},{1,3},{2,0},{3,1},{4,6},{5,7},{6,4},{7,5},{8,10},{9,11},{10,... | collective-permute-start | bytes 393224 | tf_op jit(solution)/shard_map/ppermute | solution.py:1102
  6.7 1.0 copy-done.4
  7.7 0.9 copy-done.6
  10.7 1.4 collective-permute-start.3
  13.4 6.6 %collective-permute-done.4.refs_4_ = bf16[144,1024]{1,0:T(8,128)(2,1)S(1)} collective-permute-done((bf16[144,1024]{1,0:T(8,128)(2,1)S(1)}, bf16[144,1024]{1,0:T(8,128)(2,1)S(1)}, u32[]{:S(2)}, u32[]{:S(2)}) %collective-permute-start.4) | collective-permute-done | bytes 294944 | tf_op jit(solution)/shard_map/ppermute | solution.py:1102
  19.9 1.5 collective-permute-start.5
  21.4 1.6 collective-permute-start.13
  23.0 1.6 collective-permute-start.8
  25.0 5.6 %collective-permute-done.13.came_forth = bf16[128,1024]{1,0:T(8,128)(2,1)S(1)} collective-permute-done((bf16[128,1024]{1,0:T(8,128)(2,1)S(1)}, bf16[128,1024]{1,0:T(8,128)(2,1)S(1)}, u32[]{:S(2)}, u32[]{:S(2)}) %collective-permute-start.13) | collective-permute-done | bytes 262176 | tf_op jit(solution)/shard_map/ppermute | solution.py:1102
  31.2 3.3 %collective-permute-done.8.refs_5_ = bf16[144,1024]{1,0:T(8,128)(2,1)S(1)} collective-permute-done((bf16[144,1024]{1,0:T(8,128)(2,1)S(1)}, bf16[144,1024]{1,0:T(8,128)(2,1)S(1)}, u32[]{:S(2)}, u32[]{:S(2)}) %collective-permute-start.8) | collective-permute-done | bytes 294944 | tf_op jit(solution)/shard_map/ppermute | solution.py:1102
  34.4 1.6 collective-permute-start.9
  37.4 3.8 %collective-permute-done.9.refs_7_ = bf16[144,1024]{1,0:T(8,128)(2,1)S(1)} collective-permute-done((bf16[144,1024]{1,0:T(8,128)(2,1)S(1)}, bf16[144,1024]{1,0:T(8,128)(2,1)S(1)}, u32[]{:S(2)}, u32[]{:S(2)}) %collective-permute-start.9) | collective-permute-done | bytes 294944 | tf_op jit(solution)/shard_map/ppermute | solution.py:1102
  41.2 2.4 %collective-permute-done.11.refs_8_ = bf16[144,1024]{1,0:T(8,128)(2,1)S(1)} collective-permute-done((bf16[144,1024]{1,0:T(8,128)(2,1)S(1)}, bf16[144,1024]{1,0:T(8,128)(2,1)S(1)}, u32[]{:S(2)}, u32[]{:S(2)}) %collective-permute-start.11) | collective-permute-done | bytes 294944 | tf_op jit(solution)/shard_map/ppermute | solution.py:1102
  44.1 1.6 collective-permute-start.15
  45.7 4.8 %collective-permute-done.15.refs_9_ = bf16[64,1024]{1,0:T(8,128)(2,1)S(1)} collective-permute-done((bf16[64,1024]{1,0:T(8,128)(2,1)S(1)}, bf16[64,1024]{1,0:T(8,128)(2,1)S(1)}, u32[]{:S(2)}, u32[]{:S(2)}) %collective-permute-start.15) | collective-permute-done | bytes 131104 | tf_op jit(solution)/shard_map/ppermute | solution.py:1102
  50.4 1.6 collective-permute-start.18
  53.0 0.9 shard_map.284
  53.9 7.2 %shard_map.285 = (bf16[640,1024]{1,0:T(8,128)(2,1)S(1)}, bf16[640,768]{1,0:T(8,128)(2,1)S(1)}, bf16[16,160,160]{2,1,0:T(8,128)(2,1)S(1)}, bf16[640,256]{1,0:T(8,...) custom-call(s32[13]{0:T(128)S(1)} %stack.90.info, ...), custom_call_target="tpu_custom_call" | custom-call | bytes 24000000 | tf_op jit(solution)/shard_map/pallas_call | solution.py:1216
  61.2 1.6 collective-permute-start.22
  63.5 1.5 collective-permute-start.21
  65.0 10.6 %collective-permute-done.22.forth.refs_9_ = bf16[256,1024]{1,0:T(8,128)(2,1)S(1)} collective-permute-done((bf16[256,1024]{1,0:T(8,128)(2,1)S(1)}, bf16[256,1024]{1,0:T(8,128)(2,1)S(1)}, u32[]{:S(2)}, u32[]{:S(2)}) %collective-permute-start.22) | collective-permute-done | bytes 524320 | tf_op jit(solution)/shard_map/ppermute | solution.py:1102
  75.6 1.3 collective-permute-done.23.back.refs_10_
  76.9 1.6 collective-permute-start.24
  79.0 8.3 %collective-permute-done.24.refs_11_ = bf16[192,1024]{1,0:T(8,128)(2,1)S(1)} collective-permute-done((bf16[192,1024]{1,0:T(8,128)(2,1)S(1)}, bf16[192,1024]{1,0:T(8,128)(2,1)S(1)}, u32[]{:S(2)}, u32[]{:S(2)}) %collective-permute-start.24) | collective-permute-done | bytes 393248 | tf_op jit(solution)/shard_map/ppermute | solution.py:1102
  87.3 1.3 collective-permute-done.25.refs_12_
  90.5 1.6 collective-permute-start.29
  92.4 3.5 %collective-permute-done.30.refs_14_ = bf16[64,1024]{1,0:T(8,128)(2,1)S(1)} collective-permute-done((bf16[64,1024]{1,0:T(8,128)(2,1)S(1)}, bf16[64,1024]{1,0:T(8,128)(2,1)S(1)}, u32[]{:S(2)}, u32[]{:S(2)}) %collective-permute-start.30) | collective-permute-done | bytes 131104 | tf_op jit(solution)/shard_map/ppermute | solution.py:1102
  96.2 8.5 %shard_map.289 = (bf16[640,1024]{1,0:T(8,128)(2,1)S(1)}, bf16[640,1024]{1,0:T(8,128)(2,1)S(1)}, bf16[640,1024]{1,0:T(8,128)(2,1)S(1)}, bf16[640,1024]{1,0:T(8,12...) custom-call(s32[13]{0:T(128)S(1)} %stack.90.info, ...), custom_call_target="tpu_custom_call" | custom-call | bytes 24000000 | tf_op jit(solution)/shard_map/pallas_call | solution.py:1257
  104.7 2.1 collective-permute-done.31.near
  106.9 1.6 collective-permute-start.32
  108.5 1.8 convolution_convert_fusion.1.grad_fc
  110.3 1.8 convolution_convert_fusion.grad_out
  112.8 1.5 shard_map.293
  114.4 1.6 collective-permute-start.33
  116.5 6.6 %collective-permute-done.33.got_forth = bf16[128,1024]{1,0:T(8,128)(2,1)S(1)} collective-permute-done((bf16[128,1024]{1,0:T(8,128)(2,1)S(1)}, bf16[128,1024]{1,0:T(8,128)(2,1)S(1)}, u32[]{:S(2)}, u32[]{:S(2)}) %collective-permute-start.33) | collective-permute-done | bytes 262176 | tf_op jit(solution)/shard_map/ppermute | solution.py:1102
  123.1 1.3 collective-permute-done.34.got_back
  125.1 1.2 shard_map.294
  127.1 1.5 collective-permute-start.37
  129.1 8.5 %shard_map.295 = (bf16[640,1024]{1,0:T(8,128)(2,1)S(1)}, bf16[640,768]{1,0:T(8,128)(2,1)S(1)}, bf16[2,160,1024]{2,1,0:T(8,128)(2,1)S(1)}, f32[160,1024]{1,0:T(8,...) custom-call(s32[13]{0:T(128)S(1)} %stack.90.info, bf16[2,160,1024]{2,1,0:T(8,128)(2,1)S(1)} %get-tuple-element.221.branches, ...), custom_call_target="tpu_custom_call" | custom-call | bytes 27000000 | tf_op jit(solution)/shard_map/pallas_call | solution.py:1312
  138.3 1.4 convolution_convert_fusion.2.grad_qkv
  141.1 1.2 collective-permute-done.38.got_back
  142.9 1.5 collective-permute-start.40
  144.4 3.5 %collective-permute-done.40.got_forth = bf16[64,1024]{1,0:T(8,128)(2,1)S(1)} collective-permute-done((bf16[64,1024]{1,0:T(8,128)(2,1)S(1)}, bf16[64,1024]{1,0:T(8,128)(2,1)S(1)}, u32[]{:S(2)}, u32[]{:S(2)}) %collective-permute-start.40) | collective-permute-done | bytes 131104 | tf_op jit(solution)/shard_map/ppermute | solution.py:1102
  148.6 1.6 collective-permute-start.45
  150.8 1.5 collective-permute-start.47
  153.0 1.6 collective-permute-start.42
  155.0 8.4 %collective-permute-done.45.got_forth = bf16[256,1024]{1,0:T(8,128)(2,1)S(1)} collective-permute-done((bf16[256,1024]{1,0:T(8,128)(2,1)S(1)}, bf16[256,1024]{1,0:T(8,128)(2,1)S(1)}, u32[]{:S(2)}, u32[]{:S(2)}) %collective-permute-start.45) | collective-permute-done | bytes 524320 | tf_op jit(solution)/shard_map/ppermute | solution.py:1102
  163.4 1.6 collective-permute-done.46.got_back
  165.8 1.2 collective-permute-start.50
  167.8 1.4 shard_map.299
  169.7 1.6 collective-permute-done.43.got_back
  172.0 1.2 collective-permute-start.48
  174.0 1.4 shard_map.302
  175.5 11.4 %collective-permute-done.48.got_forth = bf16[144,1024]{1,0:T(8,128)(2,1)S(1)} collective-permute-done((bf16[144,1024]{1,0:T(8,128)(2,1)S(1)}, bf16[144,1024]{1,0:T(8,128)(2,1)S(1)}, u32[]{:S(2)}, u32[]{:S(2)}) %collective-permute-start.48) | collective-permute-done | bytes 294944 | tf_op jit(solution)/shard_map/ppermute | solution.py:1102
  186.9 1.2 collective-permute-done.49.got_back
  188.9 1.5 collective-permute-start.59
  191.1 1.2 collective-permute-start.52
  193.2 9.0 %collective-permute-done.59.other = bf16[256,1024]{1,0:T(8,128)(2,1)S(1)} collective-permute-done((bf16[256,1024]{1,0:T(8,128)(2,1)S(1)}, bf16[256,1024]{1,0:T(8,128)(2,1)S(1)}, u32[]{:S(2)}, u32[]{:S(2)}) %collective-permute-start.59) | collective-permute-done | bytes 524320 | tf_op jit(solution)/shard_map/ppermute | solution.py:1102
  202.8 1.5 collective-permute-start.55
  205.0 1.5 collective-permute-start.56
  206.5 2.2 shard_map.306
  208.6 5.0 %collective-permute-done.57.corner = bf16[128,256]{1,0:T(8,128)(2,1)S(1)} collective-permute-done((bf16[128,256]{1,0:T(8,128)(2,1)S(1)}, bf16[128,256]{1,0:T(8,128)(2,1)S(1)}, u32[]{:S(2)}, u32[]{:S(2)}) %collective-permute-start.57) | collective-permute-done | bytes 65568 | tf_op jit(solution)/shard_map/ppermute | solution.py:1102
  213.7 1.6 collective-permute-done.61.cross
  215.3 1.8 shard_map.307
  (120 shorter events, 28.8 us)
Async XLA Ops:
  0.7 8.6 %collective-permute-start = (bf16[64,3072]{1,0:T(8,128)(2,1)}, bf16[64,3072]{1,0:T(8,128)(2,1)S(1)}, u32[]{:S(2)}, u32[]{:S(2)}) collective-permute-start(bf16[64,3072]{1,0:T(8,128)(2,1)} %w_qkv.1), channel_id=1, source_target_pairs={{0,1},{1,0},{2,3},{3,2},{4,5},{5,4},{6,7},{7,6},{8,9},{9,8},{10,11... | collective-permute-start | bytes 1179656 | tf_op jit(solution)/shard_map/ppermute | solution.py:1102
  1.2 8.0 %collective-permute-start.1 = (bf16[64,1024]{1,0:T(8,128)(2,1)}, bf16[64,1024]{1,0:T(8,128)(2,1)S(1)}, u32[]{:S(2)}, u32[]{:S(2)}) collective-permute-start(bf16[64,1024]{1,0:T(8,128)(2,1)} %w_proj.1), channel_id=1, source_target_pairs={{0,2},{1,3},{2,0},{3,1},{4,6},{5,7},{6,4},{7,5},{8,10},{9,11},{10,... | collective-permute-start | bytes 393224 | tf_op jit(solution)/shard_map/ppermute | solution.py:1102
  5.5 3.7 %collective-permute-start.2 = (bf16[16,64]{1,0:T(8,128)(2,1)S(1)}, bf16[16,64]{1,0:T(8,128)(2,1)S(1)}, u32[]{:S(2)}, u32[]{:S(2)}) collective-permute-start(bf16[16,64]{1,0:T(8,128)(2,1)S(1)} %stack.104.vectors), channel_id=1, source_target_pairs={{0,1},{1,0},{2,3},{3,2},{4,5},{5,4},{6,7},{7,6},{8,9},{9,8},{10,11... | collective-permute-start | bytes 6152 | tf_op jit(solution)/shard_map/ppermute | solution.py:1102
  5.8 19.2 %copy-start.3 = (bf16[64,4096]{1,0:T(8,128)(2,1)S(1)}, bf16[64,4096]{1,0:T(8,128)(2,1)}, u32[]{:S(2)}) copy-start(bf16[64,4096]{1,0:T(8,128)(2,1)} %w_fc.1) | copy-start | bytes 1572868
  10.0 9.9 %collective-permute-start.4 = (bf16[144,1024]{1,0:T(8,128)(2,1)S(1)}, bf16[144,1024]{1,0:T(8,128)(2,1)S(1)}, u32[]{:S(2)}, u32[]{:S(2)}) collective-permute-start(bf16[144,1024]{1,0:T(8,128)(2,1)S(1)} %shard_map.281.refs_2_), channel_id=1, source_target_pairs={{0,2},{1,3},{2,6},{3,7},{4,0},{5,1},{6,10},{7,11},{8,4},{9,5},{10,... | collective-permute-start | bytes 884744 | tf_op jit(solution)/shard_map/ppermute | solution.py:1102
  10.7 9.2 %collective-permute-start.3 = (bf16[144,1024]{1,0:T(8,128)(2,1)S(1)}, bf16[144,1024]{1,0:T(8,128)(2,1)S(1)}, u32[]{:S(2)}, u32[]{:S(2)}) collective-permute-start(bf16[144,1024]{1,0:T(8,128)(2,1)S(1)} %shard_map.281.refs_2_), channel_id=1, source_target_pairs={{0,4},{1,5},{2,0},{3,1},{4,8},{5,9},{6,2},{7,3},{8,12},{9,13},{10,... | collective-permute-start | bytes 884744 | tf_op jit(solution)/shard_map/ppermute | solution.py:1102
  12.1 12.9 %collective-permute-start.14 = (bf16[128,1024]{1,0:T(8,128)(2,1)S(1)}, bf16[128,1024]{1,0:T(8,128)(2,1)S(1)}, u32[]{:S(2)}, u32[]{:S(2)}) collective-permute-start(bf16[128,1024]{1,0:T(8,128)(2,1)S(1)} %constant_dynamic-slice_fusion.refs_4_), channel_id=1, source_target_pairs={{0,2},{1,3},{2,6},{3,7},{4,0},{5,1},{6,10},{7,11},{8,4},{9,5},{10,... | collective-permute-start | bytes 786440 | tf_op jit(solution)/shard_map/ppermute | solution.py:1102
  19.9 10.7 %collective-permute-start.5 = (bf16[176,1024]{1,0:T(8,128)(2,1)S(1)}, bf16[176,1024]{1,0:T(8,128)(2,1)S(1)}, u32[]{:S(2)}, u32[]{:S(2)}) collective-permute-start(bf16[176,1024]{1,0:T(8,128)(2,1)S(1)} %get-tuple-element.167.refs_0_.block), channel_id=1, source_target_pairs={{0,16},{1,17},{2,18},{3,19},{4,20},{5,21},{6,22},{7,23},{8,24},{9,... | collective-permute-start | bytes 1081352 | tf_op jit(solution)/shard_map/ppermute | solution.py:1102
  21.4 9.2 %collective-permute-start.13 = (bf16[128,1024]{1,0:T(8,128)(2,1)S(1)}, bf16[128,1024]{1,0:T(8,128)(2,1)S(1)}, u32[]{:S(2)}, u32[]{:S(2)}) collective-permute-start(bf16[128,1024]{1,0:T(8,128)(2,1)S(1)} %constant_dynamic-slice_fusion.refs_4_), channel_id=1, source_target_pairs={{0,4},{1,5},{2,0},{3,1},{4,8},{5,9},{6,2},{7,3},{8,12},{9,13},{10,... | collective-permute-start | bytes 786440 | tf_op jit(solution)/shard_map/ppermute | solution.py:1102
  23.0 11.4 %collective-permute-start.8 = (bf16[144,1024]{1,0:T(8,128)(2,1)S(1)}, bf16[144,1024]{1,0:T(8,128)(2,1)S(1)}, u32[]{:S(2)}, u32[]{:S(2)}) collective-permute-start(bf16[144,1024]{1,0:T(8,128)(2,1)S(1)} %collective-permute-done.3.refs_3_), channel_id=1, source_target_pairs={{0,4},{1,5},{2,0},{3,1},{4,8},{5,9},{6,2},{7,3},{8,12},{9,13},{10,... | collective-permute-start | bytes 884744 | tf_op jit(solution)/shard_map/ppermute | solution.py:1102
  24.6 11.4 %collective-permute-start.10 = (bf16[144,1024]{1,0:T(8,128)(2,1)S(1)}, bf16[144,1024]{1,0:T(8,128)(2,1)S(1)}, u32[]{:S(2)}, u32[]{:S(2)}) collective-permute-start(bf16[144,1024]{1,0:T(8,128)(2,1)S(1)} %collective-permute-done.4.refs_4_), channel_id=1, source_target_pairs={{0,2},{1,3},{2,6},{3,7},{4,0},{5,1},{6,10},{7,11},{8,4},{9,5},{10,... | collective-permute-start | bytes 884744 | tf_op jit(solution)/shard_map/ppermute | solution.py:1102
  25.0 11.4 %collective-permute-start.12 = (bf16[64,4096]{1,0:T(8,128)(2,1)S(1)}, bf16[64,4096]{1,0:T(8,128)(2,1)S(1)}, u32[]{:S(2)}, u32[]{:S(2)}) collective-permute-start(bf16[64,4096]{1,0:T(8,128)(2,1)S(1)} %copy-done.3), channel_id=1, source_target_pairs={{0,1},{1,0},{2,3},{3,2},{4,5},{5,4},{6,7},{7,6},{8,9},{9,8},{10,11... | collective-permute-start | bytes 1572872 | tf_op jit(solution)/shard_map/ppermute | solution.py:1102
  30.7 12.9 %collective-permute-start.6 = (bf16[176,1024]{1,0:T(8,128)(2,1)S(1)}, bf16[176,1024]{1,0:T(8,128)(2,1)S(1)}, u32[]{:S(2)}, u32[]{:S(2)}) collective-permute-start(bf16[176,1024]{1,0:T(8,128)(2,1)S(1)} %get-tuple-element.167.refs_0_.block), channel_id=1, source_target_pairs={{0,1},{1,0},{2,3},{3,2},{4,5},{5,4},{6,7},{7,6},{8,9},{9,8},{10,11... | collective-permute-start | bytes 1081352 | tf_op jit(solution)/shard_map/ppermute | solution.py:1102
  30.7 12.9 %collective-permute-start.7 = (bf16[176,1024]{1,0:T(8,128)(2,1)S(1)}, bf16[176,1024]{1,0:T(8,128)(2,1)S(1)}, u32[]{:S(2)}, u32[]{:S(2)}) collective-permute-start(bf16[176,1024]{1,0:T(8,128)(2,1)S(1)} %collective-permute-done.5.refs_2_.block_other), channel_id=1, source_target_pairs={{0,1},{1,0},{2,3},{3,2},{4,5},{5,4},{6,7},{7,6},{8,9},{9,8},{10,11... | collective-permute-start | bytes 1081352 | tf_op jit(solution)/shard_map/ppermute | solution.py:1102
  34.4 6.7 %collective-permute-start.9 = (bf16[144,1024]{1,0:T(8,128)(2,1)S(1)}, bf16[144,1024]{1,0:T(8,128)(2,1)S(1)}, u32[]{:S(2)}, u32[]{:S(2)}) collective-permute-start(bf16[144,1024]{1,0:T(8,128)(2,1)S(1)} %collective-permute-done.8.refs_5_), channel_id=1, source_target_pairs={{0,4},{1,5},{2,0},{3,1},{4,8},{5,9},{6,2},{7,3},{8,12},{9,13},{10,... | collective-permute-start | bytes 884744 | tf_op jit(solution)/shard_map/ppermute | solution.py:1102
  36.0 7.5 %collective-permute-start.11 = (bf16[144,1024]{1,0:T(8,128)(2,1)S(1)}, bf16[144,1024]{1,0:T(8,128)(2,1)S(1)}, u32[]{:S(2)}, u32[]{:S(2)}) collective-permute-start(bf16[144,1024]{1,0:T(8,128)(2,1)S(1)} %collective-permute-done.10.refs_6_), channel_id=1, source_target_pairs={{0,2},{1,3},{2,6},{3,7},{4,0},{5,1},{6,10},{7,11},{8,4},{9,5},{10,... | collective-permute-start | bytes 884744 | tf_op jit(solution)/shard_map/ppermute | solution.py:1102
  43.6 6.8 %collective-permute-start.16 = (bf16[80,1024]{1,0:T(8,128)(2,1)S(1)}, bf16[80,1024]{1,0:T(8,128)(2,1)S(1)}, u32[]{:S(2)}, u32[]{:S(2)}) collective-permute-start(bf16[80,1024]{1,0:T(8,128)(2,1)S(1)} %slice.45), channel_id=1, source_target_pairs={{0,2},{1,3},{2,6},{3,7},{4,0},{5,1},{6,10},{7,11},{8,4},{9,5},{10,... | collective-permute-start | bytes 491528 | tf_op jit(solution)/shard_map/ppermute | solution.py:1102
  44.1 6.3 %collective-permute-start.15 = (bf16[64,1024]{1,0:T(8,128)(2,1)S(1)}, bf16[64,1024]{1,0:T(8,128)(2,1)S(1)}, u32[]{:S(2)}, u32[]{:S(2)}) collective-permute-start(bf16[64,1024]{1,0:T(8,128)(2,1)S(1)} %slice.44), channel_id=1, source_target_pairs={{0,4},{1,5},{2,0},{3,1},{4,8},{5,9},{6,2},{7,3},{8,12},{9,13},{10,... | collective-permute-start | bytes 393224 | tf_op jit(solution)/shard_map/ppermute | solution.py:1102
  50.4 10.7 %collective-permute-start.18 = (bf16[256,1024]{1,0:T(8,128)(2,1)S(1)}, bf16[256,1024]{1,0:T(8,128)(2,1)S(1)}, u32[]{:S(2)}, u32[]{:S(2)}) collective-permute-start(bf16[256,1024]{1,0:T(8,128)(2,1)S(1)} %get-tuple-element.184.refs_5_), channel_id=1, source_target_pairs={{0,4},{1,5},{2,0},{3,1},{4,8},{5,9},{6,2},{7,3},{8,12},{9,13},{10,... | collective-permute-start | bytes 1572872 | tf_op jit(solution)/shard_map/ppermute | solution.py:1102
  52.0 9.2 %collective-permute-start.19 = (bf16[256,1024]{1,0:T(8,128)(2,1)S(1)}, bf16[256,1024]{1,0:T(8,128)(2,1)S(1)}, u32[]{:S(2)}, u32[]{:S(2)}) collective-permute-start(bf16[256,1024]{1,0:T(8,128)(2,1)S(1)} %get-tuple-element.185.refs_6_), channel_id=1, source_target_pairs={{0,2},{1,3},{2,6},{3,7},{4,0},{5,1},{6,10},{7,11},{8,4},{9,5},{10,... | collective-permute-start | bytes 1572872 | tf_op jit(solution)/shard_map/ppermute | solution.py:1102
  52.5 8.7 %collective-permute-start.17 = (bf16[160,1024]{1,0:T(8,128)(2,1)S(1)}, bf16[160,1024]{1,0:T(8,128)(2,1)S(1)}, u32[]{:S(2)}, u32[]{:S(2)}) collective-permute-start(bf16[160,1024]{1,0:T(8,128)(2,1)S(1)} %get-tuple-element.194.refs_0_.d_top), channel_id=1, source_target_pairs={{0,16},{1,17},{2,18},{3,19},{4,20},{5,21},{6,22},{7,23},{8,24},{9,... | collective-permute-start | bytes 983048 | tf_op jit(solution)/shard_map/ppermute | solution.py:1102
  61.2 2.1 collective-permute-start.20
  61.2 14.3 %collective-permute-start.22 = (bf16[256,1024]{1,0:T(8,128)(2,1)S(1)}, bf16[256,1024]{1,0:T(8,128)(2,1)S(1)}, u32[]{:S(2)}, u32[]{:S(2)}) collective-permute-start(bf16[256,1024]{1,0:T(8,128)(2,1)S(1)} %collective-permute-done.18.refs_7_), channel_id=1, source_target_pairs={{0,4},{1,5},{2,0},{3,1},{4,8},{5,9},{6,2},{7,3},{8,12},{9,13},{10,... | collective-permute-start | bytes 1572872 | tf_op jit(solution)/shard_map/ppermute | solution.py:1102
  62.9 14.0 %collective-permute-start.23 = (bf16[256,1024]{1,0:T(8,128)(2,1)S(1)}, bf16[256,1024]{1,0:T(8,128)(2,1)S(1)}, u32[]{:S(2)}, u32[]{:S(2)}) collective-permute-start(bf16[256,1024]{1,0:T(8,128)(2,1)S(1)} %collective-permute-done.19.refs_8_), channel_id=1, source_target_pairs={{0,2},{1,3},{2,6},{3,7},{4,0},{5,1},{6,10},{7,11},{8,4},{9,5},{10,... | collective-permute-start | bytes 1572872 | tf_op jit(solution)/shard_map/ppermute | solution.py:1102
  63.5 25.2 %collective-permute-start.21 = (bf16[2,160,1024]{2,1,0:T(8,128)(2,1)S(1)}, bf16[2,160,1024]{2,1,0:T(8,128)(2,1)S(1)}, u32[]{:S(2)}, u32[]{:S(2)}) collective-permute-start(bf16[2,160,1024]{2,1,0:T(8,128)(2,1)S(1)} %shard_map.286), channel_id=1, source_target_pairs={{0,16},{1,17},{2,18},{3,19},{4,20},{5,21},{6,22},{7,23},{8,24},{9,... | collective-permute-start | bytes 1966088 | tf_op jit(solution)/shard_map/ppermute | solution.py:1102
  76.9 10.4 %collective-permute-start.24 = (bf16[192,1024]{1,0:T(8,128)(2,1)S(1)}, bf16[192,1024]{1,0:T(8,128)(2,1)S(1)}, u32[]{:S(2)}, u32[]{:S(2)}) collective-permute-start(bf16[192,1024]{1,0:T(8,128)(2,1)S(1)} %get-tuple-element.189), channel_id=1, source_target_pairs={{0,4},{1,5},{2,0},{3,1},{4,8},{5,9},{6,2},{7,3},{8,12},{9,13},{10,... | collective-permute-start | bytes 1179656 | tf_op jit(solution)/shard_map/ppermute | solution.py:1102
  78.5 10.1 %collective-permute-start.25 = (bf16[192,1024]{1,0:T(8,128)(2,1)S(1)}, bf16[192,1024]{1,0:T(8,128)(2,1)S(1)}, u32[]{:S(2)}, u32[]{:S(2)}) collective-permute-start(bf16[192,1024]{1,0:T(8,128)(2,1)S(1)} %get-tuple-element.190), channel_id=1, source_target_pairs={{0,2},{1,3},{2,6},{3,7},{4,0},{5,1},{6,10},{7,11},{8,4},{9,5},{10,... | collective-permute-start | bytes 1179656 | tf_op jit(solution)/shard_map/ppermute | solution.py:1102
  89.3 6.8 %collective-permute-start.26 = (bf16[2,160,1024]{2,1,0:T(8,128)(2,1)S(1)}, bf16[2,160,1024]{2,1,0:T(8,128)(2,1)S(1)}, u32[]{:S(2)}, u32[]{:S(2)}) collective-permute-start(bf16[2,160,1024]{2,1,0:T(8,128)(2,1)S(1)} %get-tuple-element.196.normed), channel_id=1, source_target_pairs={{0,1},{1,0},{2,3},{3,2},{4,5},{5,4},{6,7},{7,6},{8,9},{9,8},{10,11... | collective-permute-start | bytes 1966088 | tf_op jit(solution)/shard_map/ppermute | solution.py:1102
  89.4 2.7 %collective-permute-start.27 = (bf16[160,1024]{1,0:T(8,128)(2,1)S(1)}, bf16[160,1024]{1,0:T(8,128)(2,1)S(1)}, u32[]{:S(2)}, u32[]{:S(2)}) collective-permute-start(bf16[160,1024]{1,0:T(8,128)(2,1)S(1)} %get-tuple-element.194.refs_0_.d_top), channel_id=1, source_target_pairs={{0,1},{1,0},{2,3},{3,2},{4,5},{5,4},{6,7},{7,6},{8,9},{9,8},{10,11... | collective-permute-start | bytes 983048 | tf_op jit(solution)/shard_map/ppermute | solution.py:1102
  89.9 2.5 %collective-permute-start.28 = (bf16[160,1024]{1,0:T(8,128)(2,1)S(1)}, bf16[160,1024]{1,0:T(8,128)(2,1)S(1)}, u32[]{:S(2)}, u32[]{:S(2)}) collective-permute-start(bf16[160,1024]{1,0:T(8,128)(2,1)S(1)} %collective-permute-done.17.refs_2_.d_other), channel_id=1, source_target_pairs={{0,1},{1,0},{2,3},{3,2},{4,5},{5,4},{6,7},{7,6},{8,9},{9,8},{10,11... | collective-permute-start | bytes 983048 | tf_op jit(solution)/shard_map/ppermute | solution.py:1102
  90.0 5.9 %collective-permute-start.30 = (bf16[64,1024]{1,0:T(8,128)(2,1)S(1)}, bf16[64,1024]{1,0:T(8,128)(2,1)S(1)}, u32[]{:S(2)}, u32[]{:S(2)}) collective-permute-start(bf16[64,1024]{1,0:T(8,128)(2,1)S(1)} %slice.40), channel_id=1, source_target_pairs={{0,2},{1,3},{2,6},{3,7},{4,0},{5,1},{6,10},{7,11},{8,4},{9,5},{10,... | collective-permute-start | bytes 393224 | tf_op jit(solution)/shard_map/ppermute | solution.py:1102
  90.5 5.6 %collective-permute-start.29 = (bf16[64,1024]{1,0:T(8,128)(2,1)S(1)}, bf16[64,1024]{1,0:T(8,128)(2,1)S(1)}, u32[]{:S(2)}, u32[]{:S(2)}) collective-permute-start(bf16[64,1024]{1,0:T(8,128)(2,1)S(1)} %slice.39), channel_id=1, source_target_pairs={{0,4},{1,5},{2,0},{3,1},{4,8},{5,9},{6,2},{7,3},{8,12},{9,13},{10,... | collective-permute-start | bytes 393224 | tf_op jit(solution)/shard_map/ppermute | solution.py:1102
  104.6 2.2 collective-permute-start.31
  106.9 18.1 %collective-permute-start.32 = (bf16[2,160,1024]{2,1,0:T(8,128)(2,1)S(1)}, bf16[2,160,1024]{2,1,0:T(8,128)(2,1)S(1)}, u32[]{:S(2)}, u32[]{:S(2)}) collective-permute-start(bf16[2,160,1024]{2,1,0:T(8,128)(2,1)S(1)} %shard_map.290), channel_id=1, source_target_pairs={{0,16},{1,17},{2,18},{3,19},{4,20},{5,21},{6,22},{7,23},{8,24},{9,... | collective-permute-start | bytes 1966088 | tf_op jit(solution)/shard_map/ppermute | solution.py:1102
  114.3 10.8 %collective-permute-start.35 = (bf16[2,160,1024]{2,1,0:T(8,128)(2,1)S(1)}, bf16[2,160,1024]{2,1,0:T(8,128)(2,1)S(1)}, u32[]{:S(2)}, u32[]{:S(2)}) collective-permute-start(bf16[2,160,1024]{2,1,0:T(8,128)(2,1)S(1)} %get-tuple-element.219), channel_id=1, source_target_pairs={{0,1},{1,0},{2,3},{3,2},{4,5},{5,4},{6,7},{7,6},{8,9},{9,8},{10,11... | collective-permute-start | bytes 1966088 | tf_op jit(solution)/shard_map/ppermute | solution.py:1102
  114.4 8.7 %collective-permute-start.33 = (bf16[128,1024]{1,0:T(8,128)(2,1)S(1)}, bf16[128,1024]{1,0:T(8,128)(2,1)S(1)}, u32[]{:S(2)}, u32[]{:S(2)}) collective-permute-start(bf16[128,1024]{1,0:T(8,128)(2,1)S(1)} %get-tuple-element.213), channel_id=1, source_target_pairs={{0,4},{1,5},{2,0},{3,1},{4,8},{5,9},{6,2},{7,3},{8,12},{9,13},{10,... | collective-permute-start | bytes 786440 | tf_op jit(solution)/shard_map/ppermute | solution.py:1102
  116.0 8.4 %collective-permute-start.34 = (bf16[128,1024]{1,0:T(8,128)(2,1)S(1)}, bf16[128,1024]{1,0:T(8,128)(2,1)S(1)}, u32[]{:S(2)}, u32[]{:S(2)}) collective-permute-start(bf16[128,1024]{1,0:T(8,128)(2,1)S(1)} %get-tuple-element.214), channel_id=1, source_target_pairs={{0,2},{1,3},{2,6},{3,7},{4,0},{5,1},{6,10},{7,11},{8,4},{9,5},{10,... | collective-permute-start | bytes 786440 | tf_op jit(solution)/shard_map/ppermute | solution.py:1102
  126.3 2.8 %collective-permute-start.36 = (bf16[2,160,1024]{2,1,0:T(8,128)(2,1)S(1)}, bf16[2,160,1024]{2,1,0:T(8,128)(2,1)S(1)}, u32[]{:S(2)}, u32[]{:S(2)}) collective-permute-start(bf16[2,160,1024]{2,1,0:T(8,128)(2,1)S(1)} %get-tuple-element.221.branches), channel_id=1, source_target_pairs={{0,1},{1,0},{2,3},{3,2},{4,5},{5,4},{6,7},{7,6},{8,9},{9,8},{10,11... | collective-permute-start | bytes 1966088 | tf_op jit(solution)/shard_map/ppermute | solution.py:1102
  126.5 13.8 %collective-permute-start.39 = (bf16[160,1024]{1,0:T(8,128)(2,1)S(1)}, bf16[160,1024]{1,0:T(8,128)(2,1)S(1)}, u32[]{:S(2)}, u32[]{:S(2)}) collective-permute-start(bf16[160,1024]{1,0:T(8,128)(2,1)S(1)} %fusion.1), channel_id=1, source_target_pairs={{0,16},{1,17},{2,18},{3,19},{4,20},{5,21},{6,22},{7,23},{8,24},{9,... | collective-permute-start | bytes 983048 | tf_op jit(solution)/shard_map/ppermute | solution.py:1102
  127.1 14.0 %collective-permute-start.37 = (bf16[256,1024]{1,0:T(8,128)(2,1)S(1)}, bf16[256,1024]{1,0:T(8,128)(2,1)S(1)}, u32[]{:S(2)}, u32[]{:S(2)}) collective-permute-start(bf16[256,1024]{1,0:T(8,128)(2,1)S(1)} %get-tuple-element.236), channel_id=1, source_target_pairs={{0,4},{1,5},{2,0},{3,1},{4,8},{5,9},{6,2},{7,3},{8,12},{9,13},{10,... | collective-permute-start | bytes 1572872 | tf_op jit(solution)/shard_map/ppermute | solution.py:1102
  128.6 13.8 %collective-permute-start.38 = (bf16[256,1024]{1,0:T(8,128)(2,1)S(1)}, bf16[256,1024]{1,0:T(8,128)(2,1)S(1)}, u32[]{:S(2)}, u32[]{:S(2)}) collective-permute-start(bf16[256,1024]{1,0:T(8,128)(2,1)S(1)} %get-tuple-element.237), channel_id=1, source_target_pairs={{0,2},{1,3},{2,6},{3,7},{4,0},{5,1},{6,10},{7,11},{8,4},{9,5},{10,... | collective-permute-start | bytes 1572872 | tf_op jit(solution)/shard_map/ppermute | solution.py:1102
  142.4 5.5 %collective-permute-start.41 = (bf16[80,1024]{1,0:T(8,128)(2,1)S(1)}, bf16[80,1024]{1,0:T(8,128)(2,1)S(1)}, u32[]{:S(2)}, u32[]{:S(2)}) collective-permute-start(bf16[80,1024]{1,0:T(8,128)(2,1)S(1)} %get-tuple-element.241), channel_id=1, source_target_pairs={{0,2},{1,3},{2,6},{3,7},{4,0},{5,1},{6,10},{7,11},{8,4},{9,5},{10,... | collective-permute-start | bytes 491528 | tf_op jit(solution)/shard_map/ppermute | solution.py:1102
  142.9 5.0 %collective-permute-start.40 = (bf16[64,1024]{1,0:T(8,128)(2,1)S(1)}, bf16[64,1024]{1,0:T(8,128)(2,1)S(1)}, u32[]{:S(2)}, u32[]{:S(2)}) collective-permute-start(bf16[64,1024]{1,0:T(8,128)(2,1)S(1)} %get-tuple-element.240), channel_id=1, source_target_pairs={{0,4},{1,5},{2,0},{3,1},{4,8},{5,9},{6,2},{7,3},{8,12},{9,13},{10,... | collective-permute-start | bytes 393224 | tf_op jit(solution)/shard_map/ppermute | solution.py:1102
  147.8 2.9 %collective-permute-start.44 = (bf16[2,160,1024]{2,1,0:T(8,128)(2,1)S(1)}, bf16[2,160,1024]{2,1,0:T(8,128)(2,1)S(1)}, u32[]{:S(2)}, u32[]{:S(2)}) collective-permute-start(bf16[2,160,1024]{2,1,0:T(8,128)(2,1)S(1)} %get-tuple-element.249), channel_id=1, source_target_pairs={{0,1},{1,0},{2,3},{3,2},{4,5},{5,4},{6,7},{7,6},{8,9},{9,8},{10,11... | collective-permute-start | bytes 1966088 | tf_op jit(solution)/shard_map/ppermute | solution.py:1102
  148.6 14.8 %collective-permute-start.45 = (bf16[256,1024]{1,0:T(8,128)(2,1)S(1)}, bf16[256,1024]{1,0:T(8,128)(2,1)S(1)}, u32[]{:S(2)}, u32[]{:S(2)}) collective-permute-start(bf16[256,1024]{1,0:T(8,128)(2,1)S(1)} %get-tuple-element.252), channel_id=1, source_target_pairs={{0,4},{1,5},{2,0},{3,1},{4,8},{5,9},{6,2},{7,3},{8,12},{9,13},{10,... | collective-permute-start | bytes 1572872 | tf_op jit(solution)/shard_map/ppermute | solution.py:1102
  150.2 14.8 %collective-permute-start.46 = (bf16[256,1024]{1,0:T(8,128)(2,1)S(1)}, bf16[256,1024]{1,0:T(8,128)(2,1)S(1)}, u32[]{:S(2)}, u32[]{:S(2)}) collective-permute-start(bf16[256,1024]{1,0:T(8,128)(2,1)S(1)} %get-tuple-element.253), channel_id=1, source_target_pairs={{0,2},{1,3},{2,6},{3,7},{4,0},{5,1},{6,10},{7,11},{8,4},{9,5},{10,... | collective-permute-start | bytes 1572872 | tf_op jit(solution)/shard_map/ppermute | solution.py:1102
  150.8 14.2 %collective-permute-start.47 = (bf16[160,1024]{1,0:T(8,128)(2,1)S(1)}, bf16[160,1024]{1,0:T(8,128)(2,1)S(1)}, u32[]{:S(2)}, u32[]{:S(2)}) collective-permute-start(bf16[160,1024]{1,0:T(8,128)(2,1)S(1)} %fusion), channel_id=1, source_target_pairs={{0,16},{1,17},{2,18},{3,19},{4,20},{5,21},{6,22},{7,23},{8,24},{9,... | collective-permute-start | bytes 983048 | tf_op jit(solution)/shard_map/ppermute | solution.py:1102
  153.0 16.8 %collective-permute-start.42 = (bf16[144,1024]{1,0:T(8,128)(2,1)S(1)}, bf16[144,1024]{1,0:T(8,128)(2,1)S(1)}, u32[]{:S(2)}, u32[]{:S(2)}) collective-permute-start(bf16[144,1024]{1,0:T(8,128)(2,1)S(1)} %get-tuple-element.245), channel_id=1, source_target_pairs={{0,4},{1,5},{2,0},{3,1},{4,8},{5,9},{6,2},{7,3},{8,12},{9,13},{10,... | collective-permute-start | bytes 884744 | tf_op jit(solution)/shard_map/ppermute | solution.py:1102
  154.5 16.8 %collective-permute-start.43 = (bf16[144,1024]{1,0:T(8,128)(2,1)S(1)}, bf16[144,1024]{1,0:T(8,128)(2,1)S(1)}, u32[]{:S(2)}, u32[]{:S(2)}) collective-permute-start(bf16[144,1024]{1,0:T(8,128)(2,1)S(1)} %get-tuple-element.246), channel_id=1, source_target_pairs={{0,2},{1,3},{2,6},{3,7},{4,0},{5,1},{6,10},{7,11},{8,4},{9,5},{10,... | collective-permute-start | bytes 884744 | tf_op jit(solution)/shard_map/ppermute | solution.py:1102
  165.8 22.4 %collective-permute-start.50 = (bf16[256,1024]{1,0:T(8,128)(2,1)S(1)}, bf16[256,1024]{1,0:T(8,128)(2,1)S(1)}, u32[]{:S(2)}, u32[]{:S(2)}) collective-permute-start(bf16[256,1024]{1,0:T(8,128)(2,1)S(1)} %get-tuple-element.262), channel_id=1, source_target_pairs={{0,4},{1,5},{2,0},{3,1},{4,8},{5,9},{6,2},{7,3},{8,12},{9,13},{10,... | collective-permute-start | bytes 1572872 | tf_op jit(solution)/shard_map/ppermute | solution.py:1102
  167.0 21.1 %collective-permute-start.51 = (bf16[256,1024]{1,0:T(8,128)(2,1)S(1)}, bf16[256,1024]{1,0:T(8,128)(2,1)S(1)}, u32[]{:S(2)}, u32[]{:S(2)}) collective-permute-start(bf16[256,1024]{1,0:T(8,128)(2,1)S(1)} %get-tuple-element.263), channel_id=1, source_target_pairs={{0,2},{1,3},{2,6},{3,7},{4,0},{5,1},{6,10},{7,11},{8,4},{9,5},{10,... | collective-permute-start | bytes 1572872 | tf_op jit(solution)/shard_map/ppermute | solution.py:1102
  172.0 14.9 %collective-permute-start.48 = (bf16[144,1024]{1,0:T(8,128)(2,1)S(1)}, bf16[144,1024]{1,0:T(8,128)(2,1)S(1)}, u32[]{:S(2)}, u32[]{:S(2)}) collective-permute-start(bf16[144,1024]{1,0:T(8,128)(2,1)S(1)} %get-tuple-element.258), channel_id=1, source_target_pairs={{0,4},{1,5},{2,0},{3,1},{4,8},{5,9},{6,2},{7,3},{8,12},{9,13},{10,... | collective-permute-start | bytes 884744 | tf_op jit(solution)/shard_map/ppermute | solution.py:1102
  173.2 14.9 %collective-permute-start.49 = (bf16[144,1024]{1,0:T(8,128)(2,1)S(1)}, bf16[144,1024]{1,0:T(8,128)(2,1)S(1)}, u32[]{:S(2)}, u32[]{:S(2)}) collective-permute-start(bf16[144,1024]{1,0:T(8,128)(2,1)S(1)} %get-tuple-element.259), channel_id=1, source_target_pairs={{0,2},{1,3},{2,6},{3,7},{4,0},{5,1},{6,10},{7,11},{8,4},{9,5},{10,... | collective-permute-start | bytes 884744 | tf_op jit(solution)/shard_map/ppermute | solution.py:1102
  188.9 13.3 %collective-permute-start.59 = (bf16[256,1024]{1,0:T(8,128)(2,1)S(1)}, bf16[256,1024]{1,0:T(8,128)(2,1)S(1)}, u32[]{:S(2)}, u32[]{:S(2)}) collective-permute-start(bf16[256,1024]{1,0:T(8,128)(2,1)S(1)} %shard_map.305.own), channel_id=1, source_target_pairs={{0,16},{1,17},{2,18},{3,19},{4,20},{5,21},{6,22},{7,23},{8,24},{9,... | collective-permute-start | bytes 1572872 | tf_op jit(solution)/shard_map/ppermute | solution.py:1102
  191.1 11.1 %collective-permute-start.52 = (bf16[144,1024]{1,0:T(8,128)(2,1)S(1)}, bf16[144,1024]{1,0:T(8,128)(2,1)S(1)}, u32[]{:S(2)}, u32[]{:S(2)}) collective-permute-start(bf16[144,1024]{1,0:T(8,128)(2,1)S(1)} %get-tuple-element.268), channel_id=1, source_target_pairs={{0,4},{1,5},{2,0},{3,1},{4,8},{5,9},{6,2},{7,3},{8,12},{9,13},{10,... | collective-permute-start | bytes 884744 | tf_op jit(solution)/shard_map/ppermute | solution.py:1102
  192.3 9.9 %collective-permute-start.53 = (bf16[144,1024]{1,0:T(8,128)(2,1)S(1)}, bf16[144,1024]{1,0:T(8,128)(2,1)S(1)}, u32[]{:S(2)}, u32[]{:S(2)}) collective-permute-start(bf16[144,1024]{1,0:T(8,128)(2,1)S(1)} %get-tuple-element.269), channel_id=1, source_target_pairs={{0,2},{1,3},{2,6},{3,7},{4,0},{5,1},{6,10},{7,11},{8,4},{9,5},{10,... | collective-permute-start | bytes 884744 | tf_op jit(solution)/shard_map/ppermute | solution.py:1102
  193.2 13.3 %collective-permute-start.58 = (bf16[256,1024]{1,0:T(8,128)(2,1)S(1)}, bf16[256,1024]{1,0:T(8,128)(2,1)S(1)}, u32[]{:S(2)}, u32[]{:S(2)}) collective-permute-start(bf16[256,1024]{1,0:T(8,128)(2,1)S(1)} %shard_map.305.own), channel_id=1, source_target_pairs={{0,1},{1,0},{2,3},{3,2},{4,5},{5,4},{6,7},{7,6},{8,9},{9,8},{10,11... | collective-permute-start | bytes 1572872 | tf_op jit(solution)/shard_map/ppermute | solution.py:1102
  202.2 4.3 %collective-permute-start.60 = (bf16[256,1024]{1,0:T(8,128)(2,1)S(1)}, bf16[256,1024]{1,0:T(8,128)(2,1)S(1)}, u32[]{:S(2)}, u32[]{:S(2)}) collective-permute-start(bf16[256,1024]{1,0:T(8,128)(2,1)S(1)} %collective-permute-done.59.other), channel_id=1, source_target_pairs={{0,1},{1,0},{2,3},{3,2},{4,5},{5,4},{6,7},{7,6},{8,9},{9,8},{10,11... | collective-permute-start | bytes 1572872 | tf_op jit(solution)/shard_map/ppermute | solution.py:1102
  202.8 10.8 %collective-permute-start.55 = (bf16[144,1024]{1,0:T(8,128)(2,1)S(1)}, bf16[144,1024]{1,0:T(8,128)(2,1)S(1)}, u32[]{:S(2)}, u32[]{:S(2)}) collective-permute-start(bf16[144,1024]{1,0:T(8,128)(2,1)S(1)} %shard_map.304.own), channel_id=1, source_target_pairs={{0,16},{1,17},{2,18},{3,19},{4,20},{5,21},{6,22},{7,23},{8,24},{9,... | collective-permute-start | bytes 884744 | tf_op jit(solution)/shard_map/ppermute | solution.py:1102
  204.4 12.7 %copy-start.1 = (bf16[256,1024]{1,0:T(8,128)(2,1)S(1)}, bf16[256,1024]{1,0:T(8,128)(2,1)}, u32[]{:S(2)}) copy-start(bf16[256,1024]{1,0:T(8,128)(2,1)} %param.31) | copy-start | bytes 1572868
  204.4 9.3 %collective-permute-start.57 = (bf16[128,256]{1,0:T(8,128)(2,1)S(1)}, bf16[128,256]{1,0:T(8,128)(2,1)S(1)}, u32[]{:S(2)}, u32[]{:S(2)}) collective-permute-start(bf16[128,256]{1,0:T(8,128)(2,1)S(1)} %slice.47), channel_id=1, source_target_pairs={{0,18},{1,19},{2,16},{3,17},{4,22},{5,23},{6,20},{7,21},{8,26},{9,... | collective-permute-start | bytes 196616 | tf_op jit(solution)/shard_map/ppermute | solution.py:1102
  205.0 8.7 %collective-permute-start.56 = (bf16[128,256]{1,0:T(8,128)(2,1)S(1)}, bf16[128,256]{1,0:T(8,128)(2,1)S(1)}, u32[]{:S(2)}, u32[]{:S(2)}) collective-permute-start(bf16[128,256]{1,0:T(8,128)(2,1)S(1)} %slice.47), channel_id=1, source_target_pairs={{0,2},{1,3},{2,0},{3,1},{4,6},{5,7},{6,4},{7,5},{8,10},{9,11},{10,... | collective-permute-start | bytes 196616 | tf_op jit(solution)/shard_map/ppermute | solution.py:1102
  206.5 7.2 %collective-permute-start.54 = (bf16[144,1024]{1,0:T(8,128)(2,1)S(1)}, bf16[144,1024]{1,0:T(8,128)(2,1)S(1)}, u32[]{:S(2)}, u32[]{:S(2)}) collective-permute-start(bf16[144,1024]{1,0:T(8,128)(2,1)S(1)} %shard_map.304.own), channel_id=1, source_target_pairs={{0,1},{1,0},{2,3},{3,2},{4,5},{5,4},{6,7},{7,6},{8,9},{9,8},{10,11... | collective-permute-start | bytes 884744 | tf_op jit(solution)/shard_map/ppermute | solution.py:1102
  213.7 1.6 collective-permute-start.61
  (6 other events, 35.3 us)

commit v3 on v2

--- a/solution.py
+++ b/solution.py
@@ -558,23 +558,20 @@
     first[2 * own_rows : 2 * own_rows + 8, :LANES] = small.astype(BF16)
 
 
-def second_chunks_body(info, w_fc, got_fc, came_forth, came_back, forth, back, sems):
+def second_chunk_body(info, w_fc, got_fc, w_out, chunk, sems):
     own_rows = w_fc.shape[0]
-    chip_rows = 2 * own_rows
+    piece = w_out.shape[0] // 2
     x, c = info[AT_X], info[AT_C]
-    copies = [
-        (came_forth, forth.at[pl.ds(chip_rows, chip_rows), :]),
-        (came_back, back.at[pl.ds(0, chip_rows), :]),
-    ]
+    source = pl.ds(pl.multiple_of(x * piece, piece), piece)
+    copies = [(w_out.at[source, :], chunk.at[pl.ds(2 * own_rows, piece), :])]
     for p in range(w_fc.shape[1] // (4 * LANES)):
         source = pl.ds(pl.multiple_of(p * 4 * LANES + (2 * c + x) * LANES, LANES), LANES)
         lanes = pl.ds(p * LANES, LANES)
         for weight, core in ((w_fc, c), (got_fc, 1 - c)):
             row = pl.multiple_of(core * own_rows, own_rows)
-            copies.append((weight.at[:, source], forth.at[pl.ds(row, own_rows), lanes]))
+            copies.append((weight.at[:, source], chunk.at[pl.ds(row, own_rows), lanes]))
     for copy in run_copies(copies, sems):
         copy.wait()
-    back[chip_rows:, :] = forth[:chip_rows, :]
 
 
 def run_copies(copies, sems):
@@ -604,10 +601,8 @@
 
 def attention_body(info, *refs):
     units, masks, chunks = refs[0], refs[1], refs[2 : 2 + ORIGINS]
-    normed, qkv, probs, context, send, keep_own, keep_away, qkv_weight, proj_weight, smalls = refs[
-        2 + ORIGINS : 2 + ORIGINS + 10
-    ]
-    (sems,) = refs[2 + ORIGINS + 10 :]
+    normed, qkv, probs, context, send_own, send_away, keep_own, keep_away = refs[2 + ORIGINS : 10 + ORIGINS]
+    qkv_weight, proj_weight, smalls, sems = refs[10 + ORIGINS :]
     x = info[AT_X]
     width = normed.shape[1]
     rows = normed.shape[0] // RANKS
@@ -698,39 +693,41 @@
             context[at, lanes : lanes + LANES] = jnp.where(low, outs[0], outs[1]).astype(BF16)
         return carry
 
-    lax.fori_loop(0, RANKS, attend, 0)
+    lax.fori_loop(0, RANKS, attend, 0, unroll=True)
     for n in range(4):
         columns = slice(n * third, (n + 1) * third)
-        store_parts(dot(context[...], proj_weight[:, columns]), columns, rows, send, keep_own, keep_away)
-
-
-def store_parts(product, columns, rows, send, keep_own, keep_away):
+        store_parts(dot(context[...], proj_weight[:, columns]), columns, rows, send_own, send_away, keep_own, keep_away)
+
+
+def store_parts(product, columns, rows, send_own, send_away, keep_own, keep_away):
     keep_own[:, columns] = product[:rows]
-    send[0, :, columns] = product[rows : 2 * rows].astype(BF16)
+    send_own[:, columns] = product[rows : 2 * rows].astype(BF16)
     keep_away[:, columns] = product[2 * rows : 3 * rows]
-    send[1, :, columns] = product[3 * rows :].astype(BF16)
-
-
-def total(keep_own, near, away):
-    return keep_own[...] + near[0].astype(F32) + away[...].astype(F32)
-
-
-def message_body(keep_own, keep_away, near, message):
-    message[0] = (keep_own[...] + near[0].astype(F32)).astype(BF16)
-    message[1] = (keep_away[...] + near[1].astype(F32)).astype(BF16)
-
-
-def ends_body(forth, back, forth_end, back_end):
-    forth_end[...] = forth[: forth_end.shape[0], :]
-    back_end[...] = back[back.shape[0] - back_end.shape[0] :, :]
-
-
-def second_norm_body(block, block_other, keep_own, keep_away, near, got, smalls, middle, normed):
+    send_away[:, columns] = product[3 * rows :].astype(BF16)
+
+
+def total(keep, near, far):
+    return keep[...] + near[...].astype(F32) + far.astype(F32)
+
+
+def add_body(left, right, result):
+    result[...] = add(left[...], right[...])
+
+
+def message_body(keep_own, keep_away, near_own, near_away, message):
+    message[0] = (keep_own[...] + near_own[...].astype(F32)).astype(BF16)
+    message[1] = (keep_away[...] + near_away[...].astype(F32)).astype(BF16)
+
+
+def second_norm_body(
+    block, block_other, keep_own, keep_away, near_own, near_away, got, smalls, middle, normed
+):
     rows = keep_own.shape[0]
     gain, shift = smalls[3:4, :].astype(F32), smalls[4:5, :].astype(F32)
-    for i, (tokens, keep) in enumerate(((block, keep_own), (block_other, keep_away))):
+    both = ((block, keep_own, near_own), (block_other, keep_away, near_away))
+    for i, (tokens, keep, near) in enumerate(both):
         values = tokens[:rows, :].astype(F32) + smalls[2:3, :].astype(F32)
-        values = values + (keep[...] + near[i].astype(F32) + got[1 - i].astype(F32))
+        values = values + total(keep, near, got[1 - i])
         middle[i] = values
         center, inverse = statistics(values)
         normed[i] = (center * inverse * gain + shift).astype(BF16)
@@ -738,36 +735,22 @@
 
 def feed_body(info, normed, beside, *refs):
     d_outs = refs[:RANKS]
-    (out_chunk, two_forth, two_back, three_forth, three_back, four_forth, four_back) = refs[RANKS : RANKS + 7]
-    five_forth, five_back, six_forth, six_back, smalls = refs[RANKS + 7 : RANKS + 12]
-    given, d_out, hidden, d_pre, send, keep_own, keep_away, sums, out_weight, fc_weight, sems = refs[RANKS + 12 :]
+    chunks, smalls = refs[RANKS : RANKS + ORIGINS], refs[RANKS + ORIGINS]
+    given, d_out, hidden, d_pre, send_own, send_away, keep_own, keep_away = refs[
+        RANKS + ORIGINS + 1 : RANKS + ORIGINS + 9
+    ]
+    sums, out_weight, fc_weight, sems = refs[RANKS + ORIGINS + 9 :]
     rows = normed.shape[1]
     width = given.shape[1]
-    size = out_chunk.shape[0]
-    half = size // 2
+    chip_rows = chunks[0].shape[0] // 2
     copies = []
-    for ref, start, count, weight, index, row in (
-        (two_forth, 0, size, fc_weight, 0, 0),
-        (three_forth, 0, size, fc_weight, 1, 0),
-        (three_back, size, size, fc_weight, 2, 0),
-        (four_forth, 0, size, fc_weight, 3, 0),
-        (four_back, size, size, fc_weight, 4, 0),
-        (five_forth, 0, size, fc_weight, 5, 0),
-        (five_back, half, size, fc_weight, 6, 0),
-        (six_forth, 0, half, fc_weight, 7, 0),
-        (six_back, 0, half, fc_weight, 7, half),
-        (out_chunk, 0, size, out_weight, 0, 0),
-        (two_forth, size, size, out_weight, 1, 0),
-        (two_back, 0, size, out_weight, 2, 0),
-        (three_forth, size, size, out_weight, 3, 0),
-        (three_back, 0, size, out_weight, 4, 0),
-        (four_forth, size, size, out_weight, 5, 0),
-        (four_back, 0, size, out_weight, 6, 0),
-        (five_forth, size, half, out_weight, 7, 0),
-        (five_back, 0, half, out_weight, 7, half),
-    ):
-        at = pl.multiple_of(info[index] * size + row, half)
-        copies.append((ref.at[pl.ds(start, count), :], weight.at[pl.ds(at, count), :]))
+    for i, chunk in enumerate(chunks):
+        at = pl.ds(pl.multiple_of(info[i] * chip_rows, chip_rows), chip_rows)
+        if i != ORIGINS - 1:
+            copies.append((chunk.at[pl.ds(0, chip_rows), :], fc_weight.at[at, :]))
+        if i != ORIGINS - 2:
+            start = 0 if i == ORIGINS - 1 else chip_rows
+            copies.append((chunk.at[pl.ds(start, chip_rows), :], out_weight.at[at, :]))
     started = run_copies(copies, sems)
     for b in range(RANKS):
         given[b * rows : (b + 1) * rows, :] = (beside if b % 2 else normed)[b // 2]
@@ -793,35 +776,38 @@
         sums[6:7, columns] = jnp.sum(low.astype(F32), axis=0, keepdims=True)
         return carry
 
-    lax.fori_loop(0, width // tile, units, 0)
+    lax.fori_loop(0, width // tile, units, 0, unroll=True)
     for n in range(width // tile):
         columns = slice(n * tile, (n + 1) * tile)
         product = dot_cols(d_pre[...], fc_weight[columns, :])
-        store_parts(product, columns, rows, send, keep_own, keep_away)
-
-
-def feed_out_body(hidden, out_weight, send, keep_own, keep_away):
+        store_parts(product, columns, rows, send_own, send_away, keep_own, keep_away)
+
+
+def feed_out_body(hidden, out_weight, send_own, send_away, keep_own, keep_away):
     rows = keep_own.shape[0]
     tile = 2 * LANES
     for n in range(out_weight.shape[1] // tile):
         columns = slice(n * tile, (n + 1) * tile)
-        store_parts(dot(hidden[...], out_weight[:, columns]), columns, rows, send, keep_own, keep_away)
+        store_parts(dot(hidden[...], out_weight[:, columns]), columns, rows, send_own, send_away, keep_own, keep_away)
 
 
 def mixed_body(info, middle, keep_own, near, away, smalls, mixed):
-    values = middle[0] + total(keep_own, near, away) + smalls[5:6, :].astype(F32)
+    values = middle[0] + total(keep_own, near, away[...]) + smalls[5:6, :].astype(F32)
     mixed[...] = (used_rows(info, keep_own.shape[0]) * values).astype(BF16)
 
 
-def second_back_body(middle, d_top, d_other, keep_own, keep_away, near, got, smalls, d_middle, d_branch, sums):
+def second_back_body(
+    middle, d_top, d_other, keep_own, keep_away, near_own, near_away, got, smalls, d_middle, branch_own, branch_away, sums
+):
     gain = smalls[3:4, :].astype(F32)
-    for i, (d_out, keep) in enumerate(((d_top, keep_own), (d_other, keep_away))):
-        d_values = keep[...] + near[i].astype(F32) + got[1 - i].astype(F32)
+    both = ((d_top, keep_own, near_own), (d_other, keep_away, near_away))
+    for i, (d_out, keep, near) in enumerate(both):
+        d_values = total(keep, near, got[1 - i])
         center, inverse = statistics(middle[i])
         unit = center * inverse
         result = d_out[...].astype(F32) + norm_back(unit, inverse, d_values * gain)
         low = result.astype(BF16)
-        d_branch[i] = low
+        (branch_own if i == 0 else branch_away)[...] = low
         if i == 0:
             d_middle[...] = result
             sums[...] = jnp.zeros(sums.shape, F32)
@@ -831,16 +817,16 @@
             sums[5:6, :] = jnp.sum(d_out[...].astype(F32), axis=0, keepdims=True)
 
 
-def attention_back_body(info, branches, beside, units, *refs):
+def attention_back_body(info, *refs):
+    branches, units, refs = refs[:RANKS], refs[RANKS], refs[RANKS + 1 :]
     qkv, probs, qkv_weight, proj_weight, sums_two, sums_fc = refs[:6]
-    d_branch, d_qkv, send, keep_own, keep_away, sums = refs[6:12]
-    (d_context,) = refs[12:]
-    rows = branches.shape[1]
+    d_branch, d_qkv, send_own, send_away, keep_own, keep_away, sums, d_context = refs[6:]
+    rows = branches[0].shape[0]
     width = d_branch.shape[1]
     third = width // 4
     x = info[AT_X]
     for b in range(RANKS):
-        d_branch[b * rows : (b + 1) * rows, :] = (beside if b % 2 else branches)[b // 2]
+        d_branch[b * rows : (b + 1) * rows, :] = branches[b][...]
     d_context[...] = dot_cols(d_branch[...], proj_weight[...]).astype(BF16)
     scale = HALF ** (-0.5)
     low = low_half((1, LANES))
@@ -871,13 +857,13 @@
                 d_qkv[at, n * third + lanes : n * third + lanes + LANES] = merged
         return carry
 
-    lax.fori_loop(0, RANKS, attend, 0)
+    lax.fori_loop(0, RANKS, attend, 0, unroll=True)
     sums[0:8, :] = sums_two[...] + sums_fc[...]
     sums[8:, :] = jnp.zeros((SMALL_ROWS - 8, width), F32)
     for n in range(4):
         columns = slice(n * third, (n + 1) * third)
         product = dot_cols(d_qkv[...], qkv_weight[columns, :])
-        store_parts(product, columns, rows, send, keep_own, keep_away)
+        store_parts(product, columns, rows, send_own, send_away, keep_own, keep_away)
         sums[1:2, columns] = jnp.sum(product, axis=0, keepdims=True)
         sums[0:1, columns] = jnp.sum(product * units[:, columns], axis=0, keepdims=True)
     low_row = low_half((8, LANES))
@@ -899,7 +885,7 @@
 
 def first_back_body(tokens, d_middle, keep_own, near, away, smalls, result):
     center, inverse = statistics(tokens[...].astype(F32))
-    d_unit = total(keep_own, near, away) * smalls[0:1, :].astype(F32)
+    d_unit = total(keep_own, near, away[...]) * smalls[0:1, :].astype(F32)
     result[...] = d_middle[...] + norm_back(center * inverse, inverse, d_unit)
 
 
@@ -1165,9 +1151,6 @@
             [SMEM_SPEC] + [VMEM_SPEC] * 2,
             [((own_rows, 3 * width // 2), BF16), ((own_rows, width // 2), BF16)],
         )(info, w_qkv, w_proj)
-        out_chunk = lax.dynamic_slice_in_dim(w_out, x * piece, piece, 0)
-        groups, out_chunk = tie(groups, out_chunk)
-        out_forth, out_back = to_next(out_chunk), to_back(out_chunk)
         block, d_top = kernel_call(
             tokens_body,
             [SMEM_SPEC] + [VMEM_SPEC] * 3,
@@ -1185,35 +1168,36 @@
         block_other = to_copy(block)
         blocks = [block, to_core(block), block_other, to_core(block_other)]
         forth, back = to_next(forth), to_back(back)
+        (second_chunk,) = kernel_call(
+            second_chunk_body,
+            [SMEM_SPEC] + [HBM_SPEC] * 3,
+            [second_shape],
+            [pltpu.SemaphoreType.DMA((1 + 2 * n_pos,))],
+            micros=2,
+        )(info, w_fc, got_fc, w_out)
+        forth, back, second_chunk = tie(forth, back, second_chunk)
+        seconds = [second_chunk]
         firsts += [forth, back]
         forth, back = to_next(forth), to_back(back)
+        second_forth, second_back = to_next(second_chunk), to_back(second_chunk)
         firsts += [forth, back]
-        two_forth, two_back = kernel_call(
-            second_chunks_body,
-            [SMEM_SPEC] + [HBM_SPEC] * 4,
-            [second_shape, second_shape],
-            [pltpu.SemaphoreType.DMA((2 + 2 * n_pos,))],
-            micros=2,
-        )(info, w_fc, got_fc, out_forth, out_back)
-        blocks = tie(*blocks, forth[:own_rows], back[own_rows:], two_forth, two_back)
-        forth, back, two_forth, two_back = blocks[RANKS:]
-        blocks = blocks[:RANKS]
         unit, masks = kernel_call(
             blocks_body,
             [VMEM_SPEC] * RANKS,
             [((all_rows, width), F32), ((RANKS, rows, rows), F32)],
             micros=2,
         )(*blocks)
-        forth, back, two_forth, two_back, d_top = tie(
-            to_next(forth), to_back(back), two_forth, two_back, d_top
-        )
-        firsts += [forth, back]
-        three_forth, three_back = to_next(two_forth), to_back(two_back)
-
-        parts = [((2, rows, width), BF16), ((rows, width), F32), ((rows, width), F32)]
+        unit, masks, forth, back = tie(unit, masks, forth, back)
+        d_top, *firsts = tie(d_top, *firsts, to_next(forth[:own_rows]), to_back(back[own_rows:]))
+        seconds += [second_forth, second_back]
+        second_forth, second_back = to_next(second_forth), to_back(second_back)
+
+        parts = [((rows, width), BF16)] * 2 + [((rows, width), F32)] * 2
         two_blocks = ((2, rows, width), BF16)
         d_other = to_copy(d_top)
-        normed, qkv, probs, context, send, keep_own, keep_away, qkv_weight, proj_weight, smalls = kernel_call(
+        (
+            normed, qkv, probs, context, send_own, send_away, keep_own, keep_away, qkv_weight, proj_weight, smalls
+        ) = kernel_call(
             attention_body,
             [SMEM_SPEC] + [VMEM_SPEC] * 2 + [ANY_SPEC] * ORIGINS,
             [
@@ -1229,34 +1213,33 @@
             [pltpu.SemaphoreType.DMA((5 * n_pos,))],
             micros=8,
         )(info, unit, masks, *firsts)
-        send, d_top, d_other, three_forth, three_back = tie(
-            send, d_top, d_other, three_forth, three_back
-        )
-        near = to_core(send)
-        four_forth, four_back = to_next(three_forth), to_back(three_back)
-
-        def message(keep_own, keep_away, near):
-            return kernel_call(message_body, [VMEM_SPEC] * 3, [two_blocks], micros=0)(
-                keep_own, keep_away, near
-            )[0]
-
-        got = to_copy(message(keep_own, keep_away, near))
+        send_own, send_away, d_top, d_other = tie(send_own, send_away, d_top, d_other)
+        near_own, near_away = to_core(send_own), to_core(send_away)
+        near_own, near_away, second_forth, second_back = tie(
+            near_own, near_away, second_forth, second_back
+        )
+
+        def message(*parts):
+            return kernel_call(message_body, [VMEM_SPEC] * 4, [two_blocks], micros=0)(*parts)[0]
+
+        got = to_copy(message(keep_own, keep_away, near_own, near_away))
+        seconds += [second_forth, second_back]
+        second_forth, second_back = to_next(second_forth), to_back(second_back)
         d_outs = [d_top, to_core(d_top), d_other, to_core(d_other)]
-        five_forth, five_back = kernel_call(
-            ends_body, [VMEM_SPEC] * 2, [((chip_rows + own_rows, width), BF16)] * 2, micros=6
-        )(four_forth, four_back)
-        five_forth, five_back = to_next(five_forth), to_back(five_back)
-        got, five_forth, five_back = tie(got, five_forth, five_back)
+        seconds += [second_forth, second_back]
+        second_forth, second_back = second_forth[:chip_rows], second_back[chip_rows:]
+        got, second_forth, second_back = tie(got, second_forth, second_back)
+        seconds += [to_next(second_forth), to_back(second_back)]
         middle, normed_two = kernel_call(
-            second_norm_body, [VMEM_SPEC] * 7, [((2, rows, width), F32), two_blocks], micros=2
-        )(block, block_other, keep_own, keep_away, near, got, smalls)
+            second_norm_body, [VMEM_SPEC] * 8, [((2, rows, width), F32), two_blocks], micros=2
+        )(block, block_other, keep_own, keep_away, near_own, near_away, got, smalls)
         beside = to_core(normed_two)
-        six_forth = to_next(five_forth[:own_rows])
-        six_back = to_back(five_back[chip_rows:])
-
-        given, d_out, hidden, d_pre, send, keep_own, keep_away, sums_fc, out_weight = kernel_call(
+
+        (
+            given, d_out, hidden, d_pre, send_own, send_away, keep_own, keep_away, sums_fc, out_weight
+        ) = kernel_call(
             feed_body,
-            [SMEM_SPEC] + [VMEM_SPEC] * (2 + RANKS) + [ANY_SPEC] * 11 + [VMEM_SPEC],
+            [SMEM_SPEC] + [VMEM_SPEC] * (2 + RANKS) + [ANY_SPEC] * ORIGINS + [VMEM_SPEC],
             [
                 ((all_rows, width), BF16),
                 ((all_rows, width), BF16),
@@ -1266,16 +1249,20 @@
                 ((8, units), F32),
                 ((units, width), BF16),
             ],
-            [pltpu.VMEM((width, units), BF16), pltpu.SemaphoreType.DMA((18,))],
+            [pltpu.VMEM((width, units), BF16), pltpu.SemaphoreType.DMA((2 * n_pos,))],
             micros=8,
         )(
-            info, normed_two, beside, *d_outs, out_chunk, two_forth, two_back, three_forth, three_back,
-            four_forth, four_back, five_forth, five_back, six_forth, six_back, smalls,
-        )
-
-        near = to_core(send)
-        near, given, d_out, hidden, d_pre = tie(near, given, d_out, hidden, d_pre)
-        got = to_copy(message(keep_own, keep_away, near))
+            info, normed_two, beside, *d_outs, *seconds, smalls
+        )
+
+        near_own, near_away = to_core(send_own), to_core(send_away)
+        mix_own, mix_away, mix_keep, mix_keep_away = kernel_call(
+            feed_out_body, [VMEM_SPEC] * 2, parts, micros=2
+        )(hidden, out_weight)
+        near_own, near_away, given, d_out, hidden, d_pre, mix_own, mix_away = tie(
+            near_own, near_away, given, d_out, hidden, d_pre, mix_own, mix_away
+        )
+        got = to_copy(message(keep_own, keep_away, near_own, near_away))
         grad_w_out = dot_rows(hidden, d_out).astype(BF16)
         grad_w_fc = dot_rows(given, d_pre).astype(BF16)
         far_forth, far_back = kernel_call(
@@ -1283,12 +1270,9 @@
             [SMEM_SPEC] + [VMEM_SPEC] * 2,
             [((chip_rows, width), BF16), ((piece, width), BF16)],
         )(info, grad_w_fc, grad_w_out)
-        far_forth, far_back, hidden = tie(far_forth, far_back, hidden)
+        far_forth, far_back, mix_own, mix_away = tie(far_forth, far_back, mix_own, mix_away)
         far_forth, far_back = to_next(far_forth), to_back(far_back)
-        mix_send, mix_keep, mix_away = kernel_call(
-            feed_out_body, [VMEM_SPEC] * 2, parts, micros=2
-        )(hidden, out_weight)
-        mix_near = to_core(mix_send)
+        mix_own, mix_away = to_core(mix_own), to_core(mix_away)
 
         def second_sums(step, got_forth, got_back):
             return kernel_call(
@@ -1298,20 +1282,22 @@
             )(info, got_forth, got_back, grad_w_fc, grad_w_out)
 
         second_forth, second_back = second_sums(half - 1, far_forth, far_back)
-        got, second_forth, second_back, mix_near = tie(got, second_forth, second_back, mix_near)
+        got, second_forth, second_back, mix_own, mix_away = tie(
+            got, second_forth, second_back, mix_own, mix_away
+        )
         second_forth, second_back = to_next(second_forth), to_back(second_back)
-        d_middle, d_branches, sums_two = kernel_call(
+        d_middle, branch_own, branch_away, sums_two = kernel_call(
             second_back_body,
-            [VMEM_SPEC] * 8,
-            [((rows, width), F32), two_blocks, ((8, width), F32)],
-            micros=2,
-        )(middle, d_top, d_other, keep_own, keep_away, near, got, smalls)
-        beside = to_core(d_branches)
-        mix_away = to_copy(add(mix_away, mix_near[1]))
-
-        d_branch, d_qkv, send, keep_own, keep_away, sums = kernel_call(
+            [VMEM_SPEC] * 9,
+            [((rows, width), F32), ((rows, width), BF16), ((rows, width), BF16), ((8, width), F32)],
+            micros=1,
+        )(middle, d_top, d_other, keep_own, keep_away, near_own, near_away, got, smalls)
+        branches = [branch_own, to_core(branch_own), branch_away, to_core(branch_away)]
+        mix_away = to_copy(add(mix_keep_away, mix_away))
+
+        d_branch, d_qkv, send_own, send_away, keep_own, keep_away, sums = kernel_call(
             attention_back_body,
-            [SMEM_SPEC] + [VMEM_SPEC] * 9,
+            [SMEM_SPEC] + [VMEM_SPEC] * 11,
             [
                 ((all_rows, width), BF16),
                 ((all_rows, qkv_cols), BF16),
@@ -1319,8 +1305,8 @@
                 ((SMALL_ROWS, width), F32),
             ],
             [pltpu.VMEM((all_rows, width // 4), BF16)],
-            micros=9,
-        )(info, d_branches, beside, unit, qkv, probs, qkv_weight, proj_weight, sums_two, sums_fc)
+            micros=1,
+        )(info, *branches, unit, qkv, probs, qkv_weight, proj_weight, sums_two, sums_fc)
         grad_w_proj = dot_rows(context, d_branch).astype(BF16)
         grad_w_qkv = dot_rows(normed, d_qkv).astype(BF16)
         firsts = (grad_w_qkv, grad_w_proj, sums)
@@ -1329,8 +1315,8 @@
             [SMEM_SPEC] + [VMEM_SPEC] * 3,
             [((own_rows, width), BF16), ((own_rows + SMALL_ROWS, width), BF16)],
         )(info, *firsts)
-        send, forth, back, second_forth, second_back, mix_away = tie(
-            send, forth, back, second_forth, second_back, mix_away
+        forth, back, second_forth, second_back, mix_away = tie(
+            forth, back, second_forth, second_back, mix_away
         )
         forth, back = to_next(forth), to_back(back)
         second_forth, second_back = second_sums(half - 2, second_forth, second_back)
@@ -1343,22 +1329,26 @@
             )(info, forth, back, *firsts)
 
         second_forth, second_back = to_next(second_forth), to_back(second_back)
-        forth, back, send = tie(forth, back, send)
-        near = to_core(send)
-        away = to_copy(add(keep_away, near[1]))
+        forth, back, send_own, send_away = tie(forth, back, send_own, send_away)
+        near_away, near_own = to_core(send_away), to_core(send_own)
+        near_away, near_own = tie(near_away, near_own)
+        (away,) = kernel_call(
+            add_body, [VMEM_SPEC] * 2, [((rows, width), BF16)], micros=1
+        )(keep_away, near_away)
         forth, back = first_sums(3, forth, back)
         forth, back = to_next(forth), to_back(back)
+        away = to_copy(away)
         second_forth, second_back, away = tie(second_forth, second_back, away)
         second_forth, second_back = second_sums(1, second_forth, second_back)
         second_forth, second_back = to_next(second_forth), to_back(second_back)
         (grad_tokens,) = kernel_call(first_back_body, [VMEM_SPEC] * 6, [((rows, width), F32)])(
-            tokens, d_middle, keep_own, near, away, smalls
+            tokens, d_middle, keep_own, near_own, away, smalls
         )
         forth, back, grad_tokens = tie(forth, back, grad_tokens)
         forth, back = first_sums(2, forth, back)
         forth, back = to_next(forth), to_back(back)
         (mixed,) = kernel_call(mixed_body, [SMEM_SPEC] + [VMEM_SPEC] * 5, [((rows, width), BF16)])(
-            info, middle, mix_keep, mix_near, mix_away, smalls
+            info, middle, mix_keep, mix_own, mix_away, smalls
         )
         forth, back, second_forth, second_back, mixed = tie(
             forth, back, second_forth, second_back, mixed
@@ -1369,7 +1359,7 @@
         near_second, other_second = to_core(own_second), to_copy(own_second)
         forth, back = first_sums(1, forth, back)
         forth, back = to_next(forth), to_back(back)
-        forth, back, mixed = tie(forth, back, mixed)
+        forth, back, near_second, other_second = tie(forth, back, near_second, other_second)
         (own_first,) = kernel_call(
             first_last_body, [SMEM_SPEC] + [VMEM_SPEC] * 5, [first_shape]
         )(info, forth, back, *firsts)

time: 217 us -> 214 us (0.986)
  Pallas kernels: 45.3 us -> 42.7 us
    ppermute x62 -> x65, starting transfers between devices: 52.4 us -> 50.7 us  [mover(): return lambda v: lax.ppermute(v, MESH_AXES, pairs)]
    ppermute x62 -> x65, waiting for transfers between devices: 108 us -> 109 us  [mover(): return lambda v: lax.ppermute(v, MESH_AXES, pairs)]
  transfers between devices with their start and end apart: 62 -> 65, of which waited for: 28 -> 33; matrix products, arithmetic and copies ran while one was open for 4% -> 4% of each run, Pallas kernels for 14% -> 14%
where the time goes in v3:
time: 214 us
  waiting for transfers between devices  109 us (51%)
  starting transfers between devices  50.7 us (24%)
  Pallas kernels  42.7 us (20%)
  matrix products  5.72 us (3%)
  local copies, waits for them, and re-layouts  3.78 us (2%)
    ppermute x65, waiting for transfers between devices, mover(): return lambda v: lax.ppermute(v, MESH_AXES, pairs)  109 us
    ppermute x65, starting transfers between devices, mover(): return lambda v: lax.ppermute(v, MESH_AXES, pairs)  50.7 us
    pallas_call x1, Pallas kernels, local(): kernel_call(attention_back_body, [SMEM_SPEC] + [VMEM_SPEC] * 11, [((all_r...  8.16 us
    pallas_call x1, Pallas kernels, local(): kernel_call(feed_body, [SMEM_SPEC] + [VMEM_SPEC] * (2 + RANKS) + [ANY_SPE...  6.97 us
    pallas_call x1, Pallas kernels, local(): kernel_call(attention_body, [SMEM_SPEC] + [VMEM_SPEC] * 2 + [ANY_SPEC] *...  6.59 us
    dot_general x4, matrix products, dot_rows(): lax.dot_general(left, right, (((0,), (0,)), ((), ())), preferred_element_...  5.72 us
  transfers between devices with their start and end apart: 65, of which 33 were waited for; matrix products, arithmetic and copies ran while one was open for 4% of the time, Pallas kernels for 14%

profile of v3, /device:TPU:0, one launch (start us, length us, event | category | flops | bytes accessed | tf_op | source)
XLA Modules:
  0.0 214.2 jit_solution(13313009991521687491)
XLA Ops:
  1.2 2.6 %collective-permute-start.1 = (bf16[64,1024]{1,0:T(8,128)(2,1)}, bf16[64,1024]{1,0:T(8,128)(2,1)S(1)}, u32[]{:S(2)}, u32[]{:S(2)}) collective-permute-start(bf16[64,1024]{1,0:T(8,128)(2,1)} %w_proj.1), channel_id=1, source_target_pairs={{0,2},{1,3},{2,0},{3,1},{4,6},{5,7},{6,4},{7,5},{8,10},{9,11},{10,... | collective-permute-start | bytes 393224 | tf_op jit(solution)/shard_map/ppermute | solution.py:1088
  6.6 1.0 copy-done.3
  10.7 1.3 collective-permute-start.3
  12.6 6.5 %collective-permute-done.4.refs_4_ = bf16[144,1024]{1,0:T(8,128)(2,1)S(1)} collective-permute-done((bf16[144,1024]{1,0:T(8,128)(2,1)S(1)}, bf16[144,1024]{1,0:T(8,128)(2,1)S(1)}, u32[]{:S(2)}, u32[]{:S(2)}) %collective-permute-start.4) | collective-permute-done | bytes 294944 | tf_op jit(solution)/shard_map/ppermute | solution.py:1088
  19.2 1.7 collective-permute-start.6
  20.9 1.5 collective-permute-start.8
  22.9 6.1 %collective-permute-done.6.refs_2_.block_other = bf16[176,1024]{1,0:T(8,128)(2,1)S(1)} collective-permute-done((bf16[176,1024]{1,0:T(8,128)(2,1)S(1)}, bf16[176,1024]{1,0:T(8,128)(2,1)S(1)}, u32[]{:S(2)}, u32[]{:S(2)}) %collective-permute-start.6) | collective-permute-done | bytes 360480 | tf_op jit(solution)/shard_map/ppermute | solution.py:1088
  30.1 1.6 collective-permute-start.11
  32.1 1.1 collective-permute-start.20
  33.2 1.0 collective-permute-start.18
  35.1 4.9 %collective-permute-done.11.refs_7_ = bf16[144,1024]{1,0:T(8,128)(2,1)S(1)} collective-permute-done((bf16[144,1024]{1,0:T(8,128)(2,1)S(1)}, bf16[144,1024]{1,0:T(8,128)(2,1)S(1)}, u32[]{:S(2)}, u32[]{:S(2)}) %collective-permute-start.11) | collective-permute-done | bytes 294944 | tf_op jit(solution)/shard_map/ppermute | solution.py:1088
  39.9 1.6 collective-permute-done.12.refs_8_
  42.1 1.6 collective-permute-start.13
  43.7 9.7 %collective-permute-done.13.refs_9_ = bf16[64,1024]{1,0:T(8,128)(2,1)S(1)} collective-permute-done((bf16[64,1024]{1,0:T(8,128)(2,1)S(1)}, bf16[64,1024]{1,0:T(8,128)(2,1)S(1)}, u32[]{:S(2)}, u32[]{:S(2)}) %collective-permute-start.13) | collective-permute-done | bytes 131104 | tf_op jit(solution)/shard_map/ppermute | solution.py:1088
  53.4 2.0 collective-permute-done.14.refs_10_
  55.4 1.5 collective-permute-start.15
  57.3 1.6 collective-permute-start.19
  58.9 6.6 %shard_map.285 = (bf16[640,1024]{1,0:T(8,128)(2,1)S(1)}, bf16[640,768]{1,0:T(8,128)(2,1)S(1)}, bf16[16,160,160]{2,1,0:T(8,128)(2,1)S(1)}, bf16[640,256]{1,0:T(8,...) custom-call(s32[13]{0:T(128)S(1)} %stack.90.info, ...), custom_call_target="tpu_custom_call" | custom-call | bytes 24000000 | tf_op jit(solution)/shard_map/pallas_call | solution.py:1200
  66.1 3.7 %collective-permute-done.21.refs_8_ = bf16[256,1024]{1,0:T(8,128)(2,1)S(1)} collective-permute-done((bf16[256,1024]{1,0:T(8,128)(2,1)S(1)}, bf16[256,1024]{1,0:T(8,128)(2,1)S(1)}, u32[]{:S(2)}, u32[]{:S(2)}) %collective-permute-start.21) | collective-permute-done | bytes 524320 | tf_op jit(solution)/shard_map/ppermute | solution.py:1088
  70.5 1.6 collective-permute-start.23
  72.6 9.5 %collective-permute-done.23.refs_9_ = bf16[256,1024]{1,0:T(8,128)(2,1)S(1)} collective-permute-done((bf16[256,1024]{1,0:T(8,128)(2,1)S(1)}, bf16[256,1024]{1,0:T(8,128)(2,1)S(1)}, u32[]{:S(2)}, u32[]{:S(2)}) %collective-permute-start.23) | collective-permute-done | bytes 524320 | tf_op jit(solution)/shard_map/ppermute | solution.py:1088
  82.1 1.3 collective-permute-done.24.refs_10_
  83.4 1.4 collective-permute-done.22.got
  86.2 1.6 collective-permute-start.28
  88.6 6.2 %collective-permute-done.28.refs_11_ = bf16[128,1024]{1,0:T(8,128)(2,1)S(1)} collective-permute-done((bf16[128,1024]{1,0:T(8,128)(2,1)S(1)}, bf16[128,1024]{1,0:T(8,128)(2,1)S(1)}, u32[]{:S(2)}, u32[]{:S(2)}) %collective-permute-start.28) | collective-permute-done | bytes 262176 | tf_op jit(solution)/shard_map/ppermute | solution.py:1088
  94.8 1.3 collective-permute-done.29.refs_12_
  96.1 7.0 %shard_map.288 = (bf16[640,1024]{1,0:T(8,128)(2,1)S(1)}, bf16[640,1024]{1,0:T(8,128)(2,1)S(1)}, bf16[640,1024]{1,0:T(8,128)(2,1)S(1)}, bf16[640,1024]{1,0:T(8,12...) custom-call(s32[13]{0:T(128)S(1)} %stack.90.info, ...), custom_call_target="tpu_custom_call" | custom-call | bytes 24000000 | tf_op jit(solution)/shard_map/pallas_call | solution.py:1240
  103.7 1.5 shard_map.289
  105.8 1.8 convolution_convert_fusion.1.grad_fc
  107.7 1.8 convolution_convert_fusion.grad_out
  110.7 1.7 collective-permute-start.33
  112.7 6.3 %collective-permute-done.33.got_forth = bf16[128,1024]{1,0:T(8,128)(2,1)S(1)} collective-permute-done((bf16[128,1024]{1,0:T(8,128)(2,1)S(1)}, bf16[128,1024]{1,0:T(8,128)(2,1)S(1)}, u32[]{:S(2)}, u32[]{:S(2)}) %collective-permute-start.33) | collective-permute-done | bytes 262176 | tf_op jit(solution)/shard_map/ppermute | solution.py:1088
  119.0 1.4 collective-permute-done.34.got_back
  121.2 1.1 collective-permute-done.32.got
  122.3 1.2 shard_map.293
  124.6 1.7 collective-permute-start.39
  126.7 8.2 %shard_map.294 = (bf16[640,1024]{1,0:T(8,128)(2,1)S(1)}, bf16[640,768]{1,0:T(8,128)(2,1)S(1)}, bf16[160,1024]{1,0:T(8,128)(2,1)S(1)}, bf16[160,1024]{1,0:T(8,128...) custom-call(s32[13]{0:T(128)S(1)} %stack.90.info, ...), custom_call_target="tpu_custom_call" | custom-call | bytes 3000000 | tf_op jit(solution)/shard_map/pallas_call | solution.py:1298
  135.4 1.4 convolution_convert_fusion.2.grad_qkv
  137.4 0.9 collective-permute-done.39.got_forth
  138.4 1.3 collective-permute-done.40.got_back
  140.1 1.6 collective-permute-start.42
  141.7 3.4 %collective-permute-done.42.got_forth = bf16[64,1024]{1,0:T(8,128)(2,1)S(1)} collective-permute-done((bf16[64,1024]{1,0:T(8,128)(2,1)S(1)}, bf16[64,1024]{1,0:T(8,128)(2,1)S(1)}, u32[]{:S(2)}, u32[]{:S(2)}) %collective-permute-start.42) | collective-permute-done | bytes 131104 | tf_op jit(solution)/shard_map/ppermute | solution.py:1088
  146.4 1.6 collective-permute-start.48
  148.6 1.5 collective-permute-start.50
  150.7 1.6 collective-permute-start.44
  152.8 8.5 %collective-permute-done.48.got_forth = bf16[256,1024]{1,0:T(8,128)(2,1)S(1)} collective-permute-done((bf16[256,1024]{1,0:T(8,128)(2,1)S(1)}, bf16[256,1024]{1,0:T(8,128)(2,1)S(1)}, u32[]{:S(2)}, u32[]{:S(2)}) %collective-permute-start.48) | collective-permute-done | bytes 524320 | tf_op jit(solution)/shard_map/ppermute | solution.py:1088
  161.2 1.6 collective-permute-done.49.got_back
  163.7 1.5 collective-permute-start.53
  165.7 1.4 shard_map.299
  167.6 1.6 collective-permute-done.45.got_back
  169.9 1.5 collective-permute-start.51
  171.9 1.4 shard_map.302
  173.4 10.8 %collective-permute-done.51.got_forth = bf16[144,1024]{1,0:T(8,128)(2,1)S(1)} collective-permute-done((bf16[144,1024]{1,0:T(8,128)(2,1)S(1)}, bf16[144,1024]{1,0:T(8,128)(2,1)S(1)}, u32[]{:S(2)}, u32[]{:S(2)}) %collective-permute-start.51) | collective-permute-done | bytes 294944 | tf_op jit(solution)/shard_map/ppermute | solution.py:1088
  184.2 1.3 collective-permute-done.52.got_back
  186.2 1.5 collective-permute-start.58
  188.4 1.5 collective-permute-start.55
  190.5 7.4 %collective-permute-done.55.got_forth = bf16[144,1024]{1,0:T(8,128)(2,1)S(1)} collective-permute-done((bf16[144,1024]{1,0:T(8,128)(2,1)S(1)}, bf16[144,1024]{1,0:T(8,128)(2,1)S(1)}, u32[]{:S(2)}, u32[]{:S(2)}) %collective-permute-start.55) | collective-permute-done | bytes 294944 | tf_op jit(solution)/shard_map/ppermute | solution.py:1088
  197.9 1.2 collective-permute-done.56.got_back
  199.8 1.4 collective-permute-start.60
  201.9 1.5 collective-permute-start.61
  203.4 2.2 %shard_map.306 = (f32[64,4096]{1,0:T(8,128)}, f32[256,1024]{1,0:T(8,128)}) custom-call(s32[13]{0:T(128)S(1)} %stack.90.info, bf16[256,1024]{1,0:T(8,128)(2,1)S(1)} %shard_map.304.own, bf16[256,1024]{1,0:T(8,128)(2,1)S(1)} %collective-permute-done.57.near, bf16[256,1024]{1,0:T(8,128)(2,1)S(1)} %collective-permute-done.58.other, ...), custom_call_target="tpu_custom_call" | custom-call | bytes 3000000 | tf_op jit(solution)/shard_map/pallas_call | solution.py:1370
  205.5 5.1 %collective-permute-done.62.corner = bf16[128,256]{1,0:T(8,128)(2,1)S(1)} collective-permute-done((bf16[128,256]{1,0:T(8,128)(2,1)S(1)}, bf16[128,256]{1,0:T(8,128)(2,1)S(1)}, u32[]{:S(2)}, u32[]{:S(2)}) %collective-permute-start.62) | collective-permute-done | bytes 65568 | tf_op jit(solution)/shard_map/ppermute | solution.py:1088
  210.6 1.6 collective-permute-done.64.cross
  212.2 1.8 shard_map.307
  (122 shorter events, 29.9 us)
Async XLA Ops:
  0.7 8.5 %collective-permute-start = (bf16[64,3072]{1,0:T(8,128)(2,1)}, bf16[64,3072]{1,0:T(8,128)(2,1)S(1)}, u32[]{:S(2)}, u32[]{:S(2)}) collective-permute-start(bf16[64,3072]{1,0:T(8,128)(2,1)} %w_qkv.1), channel_id=1, source_target_pairs={{0,1},{1,0},{2,3},{3,2},{4,5},{5,4},{6,7},{7,6},{8,9},{9,8},{10,11... | collective-permute-start | bytes 1179656 | tf_op jit(solution)/shard_map/ppermute | solution.py:1088
  1.2 7.9 %collective-permute-start.1 = (bf16[64,1024]{1,0:T(8,128)(2,1)}, bf16[64,1024]{1,0:T(8,128)(2,1)S(1)}, u32[]{:S(2)}, u32[]{:S(2)}) collective-permute-start(bf16[64,1024]{1,0:T(8,128)(2,1)} %w_proj.1), channel_id=1, source_target_pairs={{0,2},{1,3},{2,0},{3,1},{4,6},{5,7},{6,4},{7,5},{8,10},{9,11},{10,... | collective-permute-start | bytes 393224 | tf_op jit(solution)/shard_map/ppermute | solution.py:1088
  5.5 3.6 %collective-permute-start.2 = (bf16[16,64]{1,0:T(8,128)(2,1)S(1)}, bf16[16,64]{1,0:T(8,128)(2,1)S(1)}, u32[]{:S(2)}, u32[]{:S(2)}) collective-permute-start(bf16[16,64]{1,0:T(8,128)(2,1)S(1)} %stack.104.vectors), channel_id=1, source_target_pairs={{0,1},{1,0},{2,3},{3,2},{4,5},{5,4},{6,7},{7,6},{8,9},{9,8},{10,11... | collective-permute-start | bytes 6152 | tf_op jit(solution)/shard_map/ppermute | solution.py:1088
  9.9 9.3 %collective-permute-start.4 = (bf16[144,1024]{1,0:T(8,128)(2,1)S(1)}, bf16[144,1024]{1,0:T(8,128)(2,1)S(1)}, u32[]{:S(2)}, u32[]{:S(2)}) collective-permute-start(bf16[144,1024]{1,0:T(8,128)(2,1)S(1)} %shard_map.281.refs_2_), channel_id=1, source_target_pairs={{0,2},{1,3},{2,6},{3,7},{4,0},{5,1},{6,10},{7,11},{8,4},{9,5},{10,... | collective-permute-start | bytes 884744 | tf_op jit(solution)/shard_map/ppermute | solution.py:1088
  10.7 8.6 %collective-permute-start.3 = (bf16[144,1024]{1,0:T(8,128)(2,1)S(1)}, bf16[144,1024]{1,0:T(8,128)(2,1)S(1)}, u32[]{:S(2)}, u32[]{:S(2)}) collective-permute-start(bf16[144,1024]{1,0:T(8,128)(2,1)S(1)} %shard_map.281.refs_2_), channel_id=1, source_target_pairs={{0,4},{1,5},{2,0},{3,1},{4,8},{5,9},{6,2},{7,3},{8,12},{9,13},{10,... | collective-permute-start | bytes 884744 | tf_op jit(solution)/shard_map/ppermute | solution.py:1088
  12.0 17.0 %collective-permute-start.10 = (bf16[64,4096]{1,0:T(8,128)(2,1)S(1)}, bf16[64,4096]{1,0:T(8,128)(2,1)S(1)}, u32[]{:S(2)}, u32[]{:S(2)}) collective-permute-start(bf16[64,4096]{1,0:T(8,128)(2,1)S(1)} %copy-done.1), channel_id=1, source_target_pairs={{0,1},{1,0},{2,3},{3,2},{4,5},{5,4},{6,7},{7,6},{8,9},{9,8},{10,11... | collective-permute-start | bytes 1572872 | tf_op jit(solution)/shard_map/ppermute | solution.py:1088
  19.2 9.8 %collective-permute-start.6 = (bf16[176,1024]{1,0:T(8,128)(2,1)S(1)}, bf16[176,1024]{1,0:T(8,128)(2,1)S(1)}, u32[]{:S(2)}, u32[]{:S(2)}) collective-permute-start(bf16[176,1024]{1,0:T(8,128)(2,1)S(1)} %get-tuple-element.173.refs_0_.block), channel_id=1, source_target_pairs={{0,16},{1,17},{2,18},{3,19},{4,20},{5,21},{6,22},{7,23},{8,24},{9,... | collective-permute-start | bytes 1081352 | tf_op jit(solution)/shard_map/ppermute | solution.py:1088
  20.9 9.0 %collective-permute-start.8 = (bf16[144,1024]{1,0:T(8,128)(2,1)S(1)}, bf16[144,1024]{1,0:T(8,128)(2,1)S(1)}, u32[]{:S(2)}, u32[]{:S(2)}) collective-permute-start(bf16[144,1024]{1,0:T(8,128)(2,1)S(1)} %collective-permute-done.3.refs_3_), channel_id=1, source_target_pairs={{0,4},{1,5},{2,0},{3,1},{4,8},{5,9},{6,2},{7,3},{8,12},{9,13},{10,... | collective-permute-start | bytes 884744 | tf_op jit(solution)/shard_map/ppermute | solution.py:1088
  22.4 7.7 %collective-permute-start.9 = (bf16[144,1024]{1,0:T(8,128)(2,1)S(1)}, bf16[144,1024]{1,0:T(8,128)(2,1)S(1)}, u32[]{:S(2)}, u32[]{:S(2)}) collective-permute-start(bf16[144,1024]{1,0:T(8,128)(2,1)S(1)} %collective-permute-done.4.refs_4_), channel_id=1, source_target_pairs={{0,2},{1,3},{2,6},{3,7},{4,0},{5,1},{6,10},{7,11},{8,4},{9,5},{10,... | collective-permute-start | bytes 884744 | tf_op jit(solution)/shard_map/ppermute | solution.py:1088
  22.9 10.3 %collective-permute-start.5 = (bf16[176,1024]{1,0:T(8,128)(2,1)S(1)}, bf16[176,1024]{1,0:T(8,128)(2,1)S(1)}, u32[]{:S(2)}, u32[]{:S(2)}) collective-permute-start(bf16[176,1024]{1,0:T(8,128)(2,1)S(1)} %get-tuple-element.173.refs_0_.block), channel_id=1, source_target_pairs={{0,1},{1,0},{2,3},{3,2},{4,5},{5,4},{6,7},{7,6},{8,9},{9,8},{10,11... | collective-permute-start | bytes 1081352 | tf_op jit(solution)/shard_map/ppermute | solution.py:1088
  29.0 5.2 %collective-permute-start.7 = (bf16[176,1024]{1,0:T(8,128)(2,1)S(1)}, bf16[176,1024]{1,0:T(8,128)(2,1)S(1)}, u32[]{:S(2)}, u32[]{:S(2)}) collective-permute-start(bf16[176,1024]{1,0:T(8,128)(2,1)S(1)} %collective-permute-done.6.refs_2_.block_other), channel_id=1, source_target_pairs={{0,1},{1,0},{2,3},{3,2},{4,5},{5,4},{6,7},{7,6},{8,9},{9,8},{10,11... | collective-permute-start | bytes 1081352 | tf_op jit(solution)/shard_map/ppermute | solution.py:1088
  30.1 9.8 %collective-permute-start.11 = (bf16[144,1024]{1,0:T(8,128)(2,1)S(1)}, bf16[144,1024]{1,0:T(8,128)(2,1)S(1)}, u32[]{:S(2)}, u32[]{:S(2)}) collective-permute-start(bf16[144,1024]{1,0:T(8,128)(2,1)S(1)} %collective-permute-done.8.refs_5_), channel_id=1, source_target_pairs={{0,4},{1,5},{2,0},{3,1},{4,8},{5,9},{6,2},{7,3},{8,12},{9,13},{10,... | collective-permute-start | bytes 884744 | tf_op jit(solution)/shard_map/ppermute | solution.py:1088
  31.7 9.9 %collective-permute-start.12 = (bf16[144,1024]{1,0:T(8,128)(2,1)S(1)}, bf16[144,1024]{1,0:T(8,128)(2,1)S(1)}, u32[]{:S(2)}, u32[]{:S(2)}) collective-permute-start(bf16[144,1024]{1,0:T(8,128)(2,1)S(1)} %collective-permute-done.9.refs_6_), channel_id=1, source_target_pairs={{0,2},{1,3},{2,6},{3,7},{4,0},{5,1},{6,10},{7,11},{8,4},{9,5},{10,... | collective-permute-start | bytes 884744 | tf_op jit(solution)/shard_map/ppermute | solution.py:1088
  32.1 24.8 %collective-permute-start.20 = (bf16[256,1024]{1,0:T(8,128)(2,1)S(1)}, bf16[256,1024]{1,0:T(8,128)(2,1)S(1)}, u32[]{:S(2)}, u32[]{:S(2)}) collective-permute-start(bf16[256,1024]{1,0:T(8,128)(2,1)S(1)} %shard_map.284.refs_4_), channel_id=1, source_target_pairs={{0,2},{1,3},{2,6},{3,7},{4,0},{5,1},{6,10},{7,11},{8,4},{9,5},{10,... | collective-permute-start | bytes 1572872 | tf_op jit(solution)/shard_map/ppermute | solution.py:1088
  33.2 24.1 %collective-permute-start.18 = (bf16[256,1024]{1,0:T(8,128)(2,1)S(1)}, bf16[256,1024]{1,0:T(8,128)(2,1)S(1)}, u32[]{:S(2)}, u32[]{:S(2)}) collective-permute-start(bf16[256,1024]{1,0:T(8,128)(2,1)S(1)} %shard_map.284.refs_4_), channel_id=1, source_target_pairs={{0,4},{1,5},{2,0},{3,1},{4,8},{5,9},{6,2},{7,3},{8,12},{9,13},{10,... | collective-permute-start | bytes 1572872 | tf_op jit(solution)/shard_map/ppermute | solution.py:1088
  41.6 13.8 %collective-permute-start.14 = (bf16[80,1024]{1,0:T(8,128)(2,1)S(1)}, bf16[80,1024]{1,0:T(8,128)(2,1)S(1)}, u32[]{:S(2)}, u32[]{:S(2)}) collective-permute-start(bf16[80,1024]{1,0:T(8,128)(2,1)S(1)} %slice.32), channel_id=1, source_target_pairs={{0,2},{1,3},{2,6},{3,7},{4,0},{5,1},{6,10},{7,11},{8,4},{9,5},{10,... | collective-permute-start | bytes 491528 | tf_op jit(solution)/shard_map/ppermute | solution.py:1088
  42.1 11.3 %collective-permute-start.13 = (bf16[64,1024]{1,0:T(8,128)(2,1)S(1)}, bf16[64,1024]{1,0:T(8,128)(2,1)S(1)}, u32[]{:S(2)}, u32[]{:S(2)}) collective-permute-start(bf16[64,1024]{1,0:T(8,128)(2,1)S(1)} %slice.31), channel_id=1, source_target_pairs={{0,4},{1,5},{2,0},{3,1},{4,8},{5,9},{6,2},{7,3},{8,12},{9,13},{10,... | collective-permute-start | bytes 393224 | tf_op jit(solution)/shard_map/ppermute | solution.py:1088
  55.4 10.1 %collective-permute-start.15 = (bf16[160,1024]{1,0:T(8,128)(2,1)S(1)}, bf16[160,1024]{1,0:T(8,128)(2,1)S(1)}, u32[]{:S(2)}, u32[]{:S(2)}) collective-permute-start(bf16[160,1024]{1,0:T(8,128)(2,1)S(1)} %get-tuple-element.211.refs_0_.d_top), channel_id=1, source_target_pairs={{0,16},{1,17},{2,18},{3,19},{4,20},{5,21},{6,22},{7,23},{8,24},{9,... | collective-permute-start | bytes 983048 | tf_op jit(solution)/shard_map/ppermute | solution.py:1088
  56.9 12.9 %collective-permute-start.21 = (bf16[256,1024]{1,0:T(8,128)(2,1)S(1)}, bf16[256,1024]{1,0:T(8,128)(2,1)S(1)}, u32[]{:S(2)}, u32[]{:S(2)}) collective-permute-start(bf16[256,1024]{1,0:T(8,128)(2,1)S(1)} %collective-permute-done.20.refs_6_), channel_id=1, source_target_pairs={{0,2},{1,3},{2,6},{3,7},{4,0},{5,1},{6,10},{7,11},{8,4},{9,5},{10,... | collective-permute-start | bytes 1572872 | tf_op jit(solution)/shard_map/ppermute | solution.py:1088
  57.3 12.7 %collective-permute-start.19 = (bf16[256,1024]{1,0:T(8,128)(2,1)S(1)}, bf16[256,1024]{1,0:T(8,128)(2,1)S(1)}, u32[]{:S(2)}, u32[]{:S(2)}) collective-permute-start(bf16[256,1024]{1,0:T(8,128)(2,1)S(1)} %collective-permute-done.18.refs_5_), channel_id=1, source_target_pairs={{0,4},{1,5},{2,0},{3,1},{4,8},{5,9},{6,2},{7,3},{8,12},{9,13},{10,... | collective-permute-start | bytes 1572872 | tf_op jit(solution)/shard_map/ppermute | solution.py:1088
  65.5 4.5 %collective-permute-start.16 = (bf16[160,1024]{1,0:T(8,128)(2,1)S(1)}, bf16[160,1024]{1,0:T(8,128)(2,1)S(1)}, u32[]{:S(2)}, u32[]{:S(2)}) collective-permute-start(bf16[160,1024]{1,0:T(8,128)(2,1)S(1)} %get-tuple-element.201), channel_id=1, source_target_pairs={{0,1},{1,0},{2,3},{3,2},{4,5},{5,4},{6,7},{7,6},{8,9},{9,8},{10,11... | collective-permute-start | bytes 983048 | tf_op jit(solution)/shard_map/ppermute | solution.py:1088
  65.6 4.4 %collective-permute-start.17 = (bf16[160,1024]{1,0:T(8,128)(2,1)S(1)}, bf16[160,1024]{1,0:T(8,128)(2,1)S(1)}, u32[]{:S(2)}, u32[]{:S(2)}) collective-permute-start(bf16[160,1024]{1,0:T(8,128)(2,1)S(1)} %get-tuple-element.202), channel_id=1, source_target_pairs={{0,1},{1,0},{2,3},{3,2},{4,5},{5,4},{6,7},{7,6},{8,9},{9,8},{10,11... | collective-permute-start | bytes 983048 | tf_op jit(solution)/shard_map/ppermute | solution.py:1088
  70.1 14.7 %collective-permute-start.22 = (bf16[2,160,1024]{2,1,0:T(8,128)(2,1)S(1)}, bf16[2,160,1024]{2,1,0:T(8,128)(2,1)S(1)}, u32[]{:S(2)}, u32[]{:S(2)}) collective-permute-start(bf16[2,160,1024]{2,1,0:T(8,128)(2,1)S(1)} %shard_map.286), channel_id=1, source_target_pairs={{0,16},{1,17},{2,18},{3,19},{4,20},{5,21},{6,22},{7,23},{8,24},{9,... | collective-permute-start | bytes 1966088 | tf_op jit(solution)/shard_map/ppermute | solution.py:1088
  70.5 11.5 %collective-permute-start.23 = (bf16[256,1024]{1,0:T(8,128)(2,1)S(1)}, bf16[256,1024]{1,0:T(8,128)(2,1)S(1)}, u32[]{:S(2)}, u32[]{:S(2)}) collective-permute-start(bf16[256,1024]{1,0:T(8,128)(2,1)S(1)} %collective-permute-done.19.refs_7_), channel_id=1, source_target_pairs={{0,4},{1,5},{2,0},{3,1},{4,8},{5,9},{6,2},{7,3},{8,12},{9,13},{10,... | collective-permute-start | bytes 1572872 | tf_op jit(solution)/shard_map/ppermute | solution.py:1088
  72.1 11.3 %collective-permute-start.24 = (bf16[256,1024]{1,0:T(8,128)(2,1)S(1)}, bf16[256,1024]{1,0:T(8,128)(2,1)S(1)}, u32[]{:S(2)}, u32[]{:S(2)}) collective-permute-start(bf16[256,1024]{1,0:T(8,128)(2,1)S(1)} %collective-permute-done.21.refs_8_), channel_id=1, source_target_pairs={{0,2},{1,3},{2,6},{3,7},{4,0},{5,1},{6,10},{7,11},{8,4},{9,5},{10,... | collective-permute-start | bytes 1572872 | tf_op jit(solution)/shard_map/ppermute | solution.py:1088
  85.5 10.6 %collective-permute-start.25 = (bf16[2,160,1024]{2,1,0:T(8,128)(2,1)S(1)}, bf16[2,160,1024]{2,1,0:T(8,128)(2,1)S(1)}, u32[]{:S(2)}, u32[]{:S(2)}) collective-permute-start(bf16[2,160,1024]{2,1,0:T(8,128)(2,1)S(1)} %get-tuple-element.213.normed), channel_id=1, source_target_pairs={{0,1},{1,0},{2,3},{3,2},{4,5},{5,4},{6,7},{7,6},{8,9},{9,8},{10,11... | collective-permute-start | bytes 1966088 | tf_op jit(solution)/shard_map/ppermute | solution.py:1088
  85.6 2.6 %collective-permute-start.26 = (bf16[160,1024]{1,0:T(8,128)(2,1)S(1)}, bf16[160,1024]{1,0:T(8,128)(2,1)S(1)}, u32[]{:S(2)}, u32[]{:S(2)}) collective-permute-start(bf16[160,1024]{1,0:T(8,128)(2,1)S(1)} %get-tuple-element.211.refs_0_.d_top), channel_id=1, source_target_pairs={{0,1},{1,0},{2,3},{3,2},{4,5},{5,4},{6,7},{7,6},{8,9},{9,8},{10,11... | collective-permute-start | bytes 983048 | tf_op jit(solution)/shard_map/ppermute | solution.py:1088
  86.1 2.5 %collective-permute-start.27 = (bf16[160,1024]{1,0:T(8,128)(2,1)S(1)}, bf16[160,1024]{1,0:T(8,128)(2,1)S(1)}, u32[]{:S(2)}, u32[]{:S(2)}) collective-permute-start(bf16[160,1024]{1,0:T(8,128)(2,1)S(1)} %collective-permute-done.15.refs_2_.d_other), channel_id=1, source_target_pairs={{0,1},{1,0},{2,3},{3,2},{4,5},{5,4},{6,7},{7,6},{8,9},{9,8},{10,11... | collective-permute-start | bytes 983048 | tf_op jit(solution)/shard_map/ppermute | solution.py:1088
  86.2 8.7 %collective-permute-start.28 = (bf16[128,1024]{1,0:T(8,128)(2,1)S(1)}, bf16[128,1024]{1,0:T(8,128)(2,1)S(1)}, u32[]{:S(2)}, u32[]{:S(2)}) collective-permute-start(bf16[128,1024]{1,0:T(8,128)(2,1)S(1)} %slice.36), channel_id=1, source_target_pairs={{0,4},{1,5},{2,0},{3,1},{4,8},{5,9},{6,2},{7,3},{8,12},{9,13},{10,... | collective-permute-start | bytes 786440 | tf_op jit(solution)/shard_map/ppermute | solution.py:1088
  87.8 8.4 %collective-permute-start.29 = (bf16[128,1024]{1,0:T(8,128)(2,1)S(1)}, bf16[128,1024]{1,0:T(8,128)(2,1)S(1)}, u32[]{:S(2)}, u32[]{:S(2)}) collective-permute-start(bf16[128,1024]{1,0:T(8,128)(2,1)S(1)} %slice.37), channel_id=1, source_target_pairs={{0,2},{1,3},{2,6},{3,7},{4,0},{5,1},{6,10},{7,11},{8,4},{9,5},{10,... | collective-permute-start | bytes 786440 | tf_op jit(solution)/shard_map/ppermute | solution.py:1088
  103.1 2.1 collective-permute-start.30
  103.2 2.1 collective-permute-start.31
  105.4 16.8 %collective-permute-start.32 = (bf16[2,160,1024]{2,1,0:T(8,128)(2,1)S(1)}, bf16[2,160,1024]{2,1,0:T(8,128)(2,1)S(1)}, u32[]{:S(2)}, u32[]{:S(2)}) collective-permute-start(bf16[2,160,1024]{2,1,0:T(8,128)(2,1)S(1)} %shard_map.290), channel_id=1, source_target_pairs={{0,16},{1,17},{2,18},{3,19},{4,20},{5,21},{6,22},{7,23},{8,24},{9,... | collective-permute-start | bytes 1966088 | tf_op jit(solution)/shard_map/ppermute | solution.py:1088
  110.1 11.0 %collective-permute-start.35 = (bf16[160,1024]{1,0:T(8,128)(2,1)S(1)}, bf16[160,1024]{1,0:T(8,128)(2,1)S(1)}, u32[]{:S(2)}, u32[]{:S(2)}) collective-permute-start(bf16[160,1024]{1,0:T(8,128)(2,1)S(1)} %get-tuple-element.241), channel_id=1, source_target_pairs={{0,1},{1,0},{2,3},{3,2},{4,5},{5,4},{6,7},{7,6},{8,9},{9,8},{10,11... | collective-permute-start | bytes 983048 | tf_op jit(solution)/shard_map/ppermute | solution.py:1088
  110.2 10.9 %collective-permute-start.36 = (bf16[160,1024]{1,0:T(8,128)(2,1)S(1)}, bf16[160,1024]{1,0:T(8,128)(2,1)S(1)}, u32[]{:S(2)}, u32[]{:S(2)}) collective-permute-start(bf16[160,1024]{1,0:T(8,128)(2,1)S(1)} %get-tuple-element.242), channel_id=1, source_target_pairs={{0,1},{1,0},{2,3},{3,2},{4,5},{5,4},{6,7},{7,6},{8,9},{9,8},{10,11... | collective-permute-start | bytes 983048 | tf_op jit(solution)/shard_map/ppermute | solution.py:1088
  110.7 8.3 %collective-permute-start.33 = (bf16[128,1024]{1,0:T(8,128)(2,1)S(1)}, bf16[128,1024]{1,0:T(8,128)(2,1)S(1)}, u32[]{:S(2)}, u32[]{:S(2)}) collective-permute-start(bf16[128,1024]{1,0:T(8,128)(2,1)S(1)} %get-tuple-element.237), channel_id=1, source_target_pairs={{0,4},{1,5},{2,0},{3,1},{4,8},{5,9},{6,2},{7,3},{8,12},{9,13},{10,... | collective-permute-start | bytes 786440 | tf_op jit(solution)/shard_map/ppermute | solution.py:1088
  112.4 8.0 %collective-permute-start.34 = (bf16[128,1024]{1,0:T(8,128)(2,1)S(1)}, bf16[128,1024]{1,0:T(8,128)(2,1)S(1)}, u32[]{:S(2)}, u32[]{:S(2)}) collective-permute-start(bf16[128,1024]{1,0:T(8,128)(2,1)S(1)} %get-tuple-element.238), channel_id=1, source_target_pairs={{0,2},{1,3},{2,6},{3,7},{4,0},{5,1},{6,10},{7,11},{8,4},{9,5},{10,... | collective-permute-start | bytes 786440 | tf_op jit(solution)/shard_map/ppermute | solution.py:1088
  123.5 3.2 %collective-permute-start.37 = (bf16[160,1024]{1,0:T(8,128)(2,1)S(1)}, bf16[160,1024]{1,0:T(8,128)(2,1)S(1)}, u32[]{:S(2)}, u32[]{:S(2)}) collective-permute-start(bf16[160,1024]{1,0:T(8,128)(2,1)S(1)} %get-tuple-element.244.refs_0_), channel_id=1, source_target_pairs={{0,1},{1,0},{2,3},{3,2},{4,5},{5,4},{6,7},{7,6},{8,9},{9,8},{10,11... | collective-permute-start | bytes 983048 | tf_op jit(solution)/shard_map/ppermute | solution.py:1088
  123.5 3.1 %collective-permute-start.38 = (bf16[160,1024]{1,0:T(8,128)(2,1)S(1)}, bf16[160,1024]{1,0:T(8,128)(2,1)S(1)}, u32[]{:S(2)}, u32[]{:S(2)}) collective-permute-start(bf16[160,1024]{1,0:T(8,128)(2,1)S(1)} %get-tuple-element.245.refs_2_), channel_id=1, source_target_pairs={{0,1},{1,0},{2,3},{3,2},{4,5},{5,4},{6,7},{7,6},{8,9},{9,8},{10,11... | collective-permute-start | bytes 983048 | tf_op jit(solution)/shard_map/ppermute | solution.py:1088
  124.1 13.3 %collective-permute-start.41 = (bf16[160,1024]{1,0:T(8,128)(2,1)S(1)}, bf16[160,1024]{1,0:T(8,128)(2,1)S(1)}, u32[]{:S(2)}, u32[]{:S(2)}) collective-permute-start(bf16[160,1024]{1,0:T(8,128)(2,1)S(1)} %add_convert_fusion), channel_id=1, source_target_pairs={{0,16},{1,17},{2,18},{3,19},{4,20},{5,21},{6,22},{7,23},{8,24},{9,... | collective-permute-start | bytes 983048 | tf_op jit(solution)/shard_map/ppermute | solution.py:1088
  124.6 13.8 %collective-permute-start.39 = (bf16[256,1024]{1,0:T(8,128)(2,1)S(1)}, bf16[256,1024]{1,0:T(8,128)(2,1)S(1)}, u32[]{:S(2)}, u32[]{:S(2)}) collective-permute-start(bf16[256,1024]{1,0:T(8,128)(2,1)S(1)} %get-tuple-element.258), channel_id=1, source_target_pairs={{0,4},{1,5},{2,0},{3,1},{4,8},{5,9},{6,2},{7,3},{8,12},{9,13},{10,... | collective-permute-start | bytes 1572872 | tf_op jit(solution)/shard_map/ppermute | solution.py:1088
  126.3 13.4 %collective-permute-start.40 = (bf16[256,1024]{1,0:T(8,128)(2,1)S(1)}, bf16[256,1024]{1,0:T(8,128)(2,1)S(1)}, u32[]{:S(2)}, u32[]{:S(2)}) collective-permute-start(bf16[256,1024]{1,0:T(8,128)(2,1)S(1)} %get-tuple-element.259), channel_id=1, source_target_pairs={{0,2},{1,3},{2,6},{3,7},{4,0},{5,1},{6,10},{7,11},{8,4},{9,5},{10,... | collective-permute-start | bytes 1572872 | tf_op jit(solution)/shard_map/ppermute | solution.py:1088
  139.7 5.4 %collective-permute-start.43 = (bf16[80,1024]{1,0:T(8,128)(2,1)S(1)}, bf16[80,1024]{1,0:T(8,128)(2,1)S(1)}, u32[]{:S(2)}, u32[]{:S(2)}) collective-permute-start(bf16[80,1024]{1,0:T(8,128)(2,1)S(1)} %get-tuple-element.263), channel_id=1, source_target_pairs={{0,2},{1,3},{2,6},{3,7},{4,0},{5,1},{6,10},{7,11},{8,4},{9,5},{10,... | collective-permute-start | bytes 491528 | tf_op jit(solution)/shard_map/ppermute | solution.py:1088
  140.1 5.0 %collective-permute-start.42 = (bf16[64,1024]{1,0:T(8,128)(2,1)S(1)}, bf16[64,1024]{1,0:T(8,128)(2,1)S(1)}, u32[]{:S(2)}, u32[]{:S(2)}) collective-permute-start(bf16[64,1024]{1,0:T(8,128)(2,1)S(1)} %get-tuple-element.262), channel_id=1, source_target_pairs={{0,4},{1,5},{2,0},{3,1},{4,8},{5,9},{6,2},{7,3},{8,12},{9,13},{10,... | collective-permute-start | bytes 393224 | tf_op jit(solution)/shard_map/ppermute | solution.py:1088
  145.1 3.4 %collective-permute-start.46 = (bf16[160,1024]{1,0:T(8,128)(2,1)S(1)}, bf16[160,1024]{1,0:T(8,128)(2,1)S(1)}, u32[]{:S(2)}, u32[]{:S(2)}) collective-permute-start(bf16[160,1024]{1,0:T(8,128)(2,1)S(1)} %get-tuple-element.272), channel_id=1, source_target_pairs={{0,1},{1,0},{2,3},{3,2},{4,5},{5,4},{6,7},{7,6},{8,9},{9,8},{10,11... | collective-permute-start | bytes 983048 | tf_op jit(solution)/shard_map/ppermute | solution.py:1088
  145.1 3.4 %collective-permute-start.47 = (bf16[160,1024]{1,0:T(8,128)(2,1)S(1)}, bf16[160,1024]{1,0:T(8,128)(2,1)S(1)}, u32[]{:S(2)}, u32[]{:S(2)}) collective-permute-start(bf16[160,1024]{1,0:T(8,128)(2,1)S(1)} %get-tuple-element.273), channel_id=1, source_target_pairs={{0,1},{1,0},{2,3},{3,2},{4,5},{5,4},{6,7},{7,6},{8,9},{9,8},{10,11... | collective-permute-start | bytes 983048 | tf_op jit(solution)/shard_map/ppermute | solution.py:1088
  146.4 14.8 %collective-permute-start.48 = (bf16[256,1024]{1,0:T(8,128)(2,1)S(1)}, bf16[256,1024]{1,0:T(8,128)(2,1)S(1)}, u32[]{:S(2)}, u32[]{:S(2)}) collective-permute-start(bf16[256,1024]{1,0:T(8,128)(2,1)S(1)} %get-tuple-element.277), channel_id=1, source_target_pairs={{0,4},{1,5},{2,0},{3,1},{4,8},{5,9},{6,2},{7,3},{8,12},{9,13},{10,... | collective-permute-start | bytes 1572872 | tf_op jit(solution)/shard_map/ppermute | solution.py:1088
  148.0 14.8 %collective-permute-start.49 = (bf16[256,1024]{1,0:T(8,128)(2,1)S(1)}, bf16[256,1024]{1,0:T(8,128)(2,1)S(1)}, u32[]{:S(2)}, u32[]{:S(2)}) collective-permute-start(bf16[256,1024]{1,0:T(8,128)(2,1)S(1)} %get-tuple-element.278), channel_id=1, source_target_pairs={{0,2},{1,3},{2,6},{3,7},{4,0},{5,1},{6,10},{7,11},{8,4},{9,5},{10,... | collective-permute-start | bytes 1572872 | tf_op jit(solution)/shard_map/ppermute | solution.py:1088
  148.6 14.3 %collective-permute-start.50 = (bf16[160,1024]{1,0:T(8,128)(2,1)S(1)}, bf16[160,1024]{1,0:T(8,128)(2,1)S(1)}, u32[]{:S(2)}, u32[]{:S(2)}) collective-permute-start(bf16[160,1024]{1,0:T(8,128)(2,1)S(1)} %shard_map.298), channel_id=1, source_target_pairs={{0,16},{1,17},{2,18},{3,19},{4,20},{5,21},{6,22},{7,23},{8,24},{9,... | collective-permute-start | bytes 983048 | tf_op jit(solution)/shard_map/ppermute | solution.py:1088
  150.7 16.9 %collective-permute-start.44 = (bf16[144,1024]{1,0:T(8,128)(2,1)S(1)}, bf16[144,1024]{1,0:T(8,128)(2,1)S(1)}, u32[]{:S(2)}, u32[]{:S(2)}) collective-permute-start(bf16[144,1024]{1,0:T(8,128)(2,1)S(1)} %get-tuple-element.268), channel_id=1, source_target_pairs={{0,4},{1,5},{2,0},{3,1},{4,8},{5,9},{6,2},{7,3},{8,12},{9,13},{10,... | collective-permute-start | bytes 884744 | tf_op jit(solution)/shard_map/ppermute | solution.py:1088
  152.3 16.9 %collective-permute-start.45 = (bf16[144,1024]{1,0:T(8,128)(2,1)S(1)}, bf16[144,1024]{1,0:T(8,128)(2,1)S(1)}, u32[]{:S(2)}, u32[]{:S(2)}) collective-permute-start(bf16[144,1024]{1,0:T(8,128)(2,1)S(1)} %get-tuple-element.269), channel_id=1, source_target_pairs={{0,2},{1,3},{2,6},{3,7},{4,0},{5,1},{6,10},{7,11},{8,4},{9,5},{10,... | collective-permute-start | bytes 884744 | tf_op jit(solution)/shard_map/ppermute | solution.py:1088
  163.7 21.8 %collective-permute-start.53 = (bf16[256,1024]{1,0:T(8,128)(2,1)S(1)}, bf16[256,1024]{1,0:T(8,128)(2,1)S(1)}, u32[]{:S(2)}, u32[]{:S(2)}) collective-permute-start(bf16[256,1024]{1,0:T(8,128)(2,1)S(1)} %get-tuple-element.288), channel_id=1, source_target_pairs={{0,4},{1,5},{2,0},{3,1},{4,8},{5,9},{6,2},{7,3},{8,12},{9,13},{10,... | collective-permute-start | bytes 1572872 | tf_op jit(solution)/shard_map/ppermute | solution.py:1088
  165.2 20.3 %collective-permute-start.54 = (bf16[256,1024]{1,0:T(8,128)(2,1)S(1)}, bf16[256,1024]{1,0:T(8,128)(2,1)S(1)}, u32[]{:S(2)}, u32[]{:S(2)}) collective-permute-start(bf16[256,1024]{1,0:T(8,128)(2,1)S(1)} %get-tuple-element.289), channel_id=1, source_target_pairs={{0,2},{1,3},{2,6},{3,7},{4,0},{5,1},{6,10},{7,11},{8,4},{9,5},{10,... | collective-permute-start | bytes 1572872 | tf_op jit(solution)/shard_map/ppermute | solution.py:1088
  169.9 14.3 %collective-permute-start.51 = (bf16[144,1024]{1,0:T(8,128)(2,1)S(1)}, bf16[144,1024]{1,0:T(8,128)(2,1)S(1)}, u32[]{:S(2)}, u32[]{:S(2)}) collective-permute-start(bf16[144,1024]{1,0:T(8,128)(2,1)S(1)} %get-tuple-element.284), channel_id=1, source_target_pairs={{0,4},{1,5},{2,0},{3,1},{4,8},{5,9},{6,2},{7,3},{8,12},{9,13},{10,... | collective-permute-start | bytes 884744 | tf_op jit(solution)/shard_map/ppermute | solution.py:1088
  171.4 14.1 %collective-permute-start.52 = (bf16[144,1024]{1,0:T(8,128)(2,1)S(1)}, bf16[144,1024]{1,0:T(8,128)(2,1)S(1)}, u32[]{:S(2)}, u32[]{:S(2)}) collective-permute-start(bf16[144,1024]{1,0:T(8,128)(2,1)S(1)} %get-tuple-element.285), channel_id=1, source_target_pairs={{0,2},{1,3},{2,6},{3,7},{4,0},{5,1},{6,10},{7,11},{8,4},{9,5},{10,... | collective-permute-start | bytes 884744 | tf_op jit(solution)/shard_map/ppermute | solution.py:1088
  186.2 12.9 %collective-permute-start.58 = (bf16[256,1024]{1,0:T(8,128)(2,1)S(1)}, bf16[256,1024]{1,0:T(8,128)(2,1)S(1)}, u32[]{:S(2)}, u32[]{:S(2)}) collective-permute-start(bf16[256,1024]{1,0:T(8,128)(2,1)S(1)} %shard_map.304.own), channel_id=1, source_target_pairs={{0,16},{1,17},{2,18},{3,19},{4,20},{5,21},{6,22},{7,23},{8,24},{9,... | collective-permute-start | bytes 1572872 | tf_op jit(solution)/shard_map/ppermute | solution.py:1088
  187.7 11.4 %collective-permute-start.57 = (bf16[256,1024]{1,0:T(8,128)(2,1)S(1)}, bf16[256,1024]{1,0:T(8,128)(2,1)S(1)}, u32[]{:S(2)}, u32[]{:S(2)}) collective-permute-start(bf16[256,1024]{1,0:T(8,128)(2,1)S(1)} %shard_map.304.own), channel_id=1, source_target_pairs={{0,1},{1,0},{2,3},{3,2},{4,5},{5,4},{6,7},{7,6},{8,9},{9,8},{10,11... | collective-permute-start | bytes 1572872 | tf_op jit(solution)/shard_map/ppermute | solution.py:1088
  188.4 9.5 %collective-permute-start.55 = (bf16[144,1024]{1,0:T(8,128)(2,1)S(1)}, bf16[144,1024]{1,0:T(8,128)(2,1)S(1)}, u32[]{:S(2)}, u32[]{:S(2)}) collective-permute-start(bf16[144,1024]{1,0:T(8,128)(2,1)S(1)} %get-tuple-element.297), channel_id=1, source_target_pairs={{0,4},{1,5},{2,0},{3,1},{4,8},{5,9},{6,2},{7,3},{8,12},{9,13},{10,... | collective-permute-start | bytes 884744 | tf_op jit(solution)/shard_map/ppermute | solution.py:1088
  189.9 9.1 %collective-permute-start.56 = (bf16[144,1024]{1,0:T(8,128)(2,1)S(1)}, bf16[144,1024]{1,0:T(8,128)(2,1)S(1)}, u32[]{:S(2)}, u32[]{:S(2)}) collective-permute-start(bf16[144,1024]{1,0:T(8,128)(2,1)S(1)} %get-tuple-element.298), channel_id=1, source_target_pairs={{0,2},{1,3},{2,6},{3,7},{4,0},{5,1},{6,10},{7,11},{8,4},{9,5},{10,... | collective-permute-start | bytes 884744 | tf_op jit(solution)/shard_map/ppermute | solution.py:1088
  199.1 4.3 %collective-permute-start.63 = (bf16[256,1024]{1,0:T(8,128)(2,1)S(1)}, bf16[256,1024]{1,0:T(8,128)(2,1)S(1)}, u32[]{:S(2)}, u32[]{:S(2)}) collective-permute-start(bf16[256,1024]{1,0:T(8,128)(2,1)S(1)} %collective-permute-done.58.other), channel_id=1, source_target_pairs={{0,1},{1,0},{2,3},{3,2},{4,5},{5,4},{6,7},{7,6},{8,9},{9,8},{10,11... | collective-permute-start | bytes 1572872 | tf_op jit(solution)/shard_map/ppermute | solution.py:1088
  199.8 10.9 %collective-permute-start.60 = (bf16[144,1024]{1,0:T(8,128)(2,1)S(1)}, bf16[144,1024]{1,0:T(8,128)(2,1)S(1)}, u32[]{:S(2)}, u32[]{:S(2)}) collective-permute-start(bf16[144,1024]{1,0:T(8,128)(2,1)S(1)} %shard_map.305.own), channel_id=1, source_target_pairs={{0,16},{1,17},{2,18},{3,19},{4,20},{5,21},{6,22},{7,23},{8,24},{9,... | collective-permute-start | bytes 884744 | tf_op jit(solution)/shard_map/ppermute | solution.py:1088
  201.1 9.5 %collective-permute-start.62 = (bf16[128,256]{1,0:T(8,128)(2,1)S(1)}, bf16[128,256]{1,0:T(8,128)(2,1)S(1)}, u32[]{:S(2)}, u32[]{:S(2)}) collective-permute-start(bf16[128,256]{1,0:T(8,128)(2,1)S(1)} %slice.38), channel_id=1, source_target_pairs={{0,18},{1,19},{2,16},{3,17},{4,22},{5,23},{6,20},{7,21},{8,26},{9,... | collective-permute-start | bytes 196616 | tf_op jit(solution)/shard_map/ppermute | solution.py:1088
  201.9 8.7 %collective-permute-start.61 = (bf16[128,256]{1,0:T(8,128)(2,1)S(1)}, bf16[128,256]{1,0:T(8,128)(2,1)S(1)}, u32[]{:S(2)}, u32[]{:S(2)}) collective-permute-start(bf16[128,256]{1,0:T(8,128)(2,1)S(1)} %slice.38), channel_id=1, source_target_pairs={{0,2},{1,3},{2,0},{3,1},{4,6},{5,7},{6,4},{7,5},{8,10},{9,11},{10,... | collective-permute-start | bytes 196616 | tf_op jit(solution)/shard_map/ppermute | solution.py:1088
  203.4 7.2 %collective-permute-start.59 = (bf16[144,1024]{1,0:T(8,128)(2,1)S(1)}, bf16[144,1024]{1,0:T(8,128)(2,1)S(1)}, u32[]{:S(2)}, u32[]{:S(2)}) collective-permute-start(bf16[144,1024]{1,0:T(8,128)(2,1)S(1)} %shard_map.305.own), channel_id=1, source_target_pairs={{0,1},{1,0},{2,3},{3,2},{4,5},{5,4},{6,7},{7,6},{8,9},{9,8},{10,11... | collective-permute-start | bytes 884744 | tf_op jit(solution)/shard_map/ppermute | solution.py:1088
  (8 other events, 56.5 us)

commit v4 on v3

--- a/solution.py
+++ b/solution.py
@@ -993,36 +993,36 @@
             at += value.shape[1]
 
 
-def four_parts(info, own, near, other, cross):
-    x, c = info[AT_X], info[AT_C]
-
-    def reader(copy, core):
-        def read(rows, lanes):
-            same = jnp.where(c == core, own[rows, lanes], near[rows, lanes])
-            far = jnp.where(c == core, other[rows, lanes], cross[rows, lanes])
-            return jnp.where(x == copy, same, far).astype(F32)
-
-        return read
-
-    return reader
+def at_each_place(info, body):
+    for x in range(2):
+        for c in range(2):
+            pl.when((info[AT_X] == x) & (info[AT_C] == c))(functools.partial(body, x, c))
+
+
+def part_of(x, c, copy, core, own, near, other, cross):
+    if copy == x:
+        return own if core == c else near
+    return other if core == c else cross
 
 
 def hidden_grads_body(info, own, near, other, cross, grad_fc, grad_out):
-    x, c = info[AT_X], info[AT_C]
     own_rows = grad_fc.shape[0]
     width = own.shape[1]
     piece = grad_out.shape[0] // 2
-    reader = four_parts(info, own, near, other, cross)
-    rows = pl.ds(pl.multiple_of(c * own_rows, own_rows), own_rows)
-    for copy in range(2):
-        for core in range(2):
-            read = reader(copy, core)
-            for p in range(width // LANES):
-                at = p * 4 * LANES + core * 2 * LANES + copy * LANES
-                grad_fc[:, at : at + LANES] = read(rows, slice(p * LANES, (p + 1) * LANES))
-        grad_out[copy * piece : (copy + 1) * piece, :] = jnp.where(
-            x == copy, own[2 * own_rows :, :], other[2 * own_rows :, :]
-        ).astype(F32)
+
+    def gather(x, c):
+        rows = slice(c * own_rows, (c + 1) * own_rows)
+        for copy in range(2):
+            for core in range(2):
+                part = part_of(x, c, copy, core, own, near, other, cross)
+                for p in range(width // LANES):
+                    at = p * 4 * LANES + core * 2 * LANES + copy * LANES
+                    lanes = slice(p * LANES, (p + 1) * LANES)
+                    grad_fc[:, at : at + LANES] = part[rows, lanes].astype(F32)
+            half = own if x == copy else other
+            grad_out[copy * piece : (copy + 1) * piece, :] = half[2 * own_rows :, :].astype(F32)
+
+    at_each_place(info, gather)
 
 
 def first_grads_body(info, own, near, other, cross, side, corner, grad_qkv, grad_proj, *small_outs):
@@ -1031,17 +1031,21 @@
     qkv = 3 * width // 4
     quarter = width // 4
     low = low_half((own_rows, LANES))
-    reader = four_parts(info, own, near, other, cross)
-    rows = pl.ds(pl.multiple_of(c * own_rows, own_rows), own_rows)
-    for copy in range(2):
-        first, second = reader(copy, 0), reader(copy, 1)
-        for pair in range(qkv // LANES):
-            lanes = slice(pair * LANES, (pair + 1) * LANES)
-            one, two = first(rows, lanes), second(rows, lanes)
-            at = pair * 8 * HALF + copy * LANES
-            grad_qkv[:, at : at + LANES] = jnp.where(low, one, turn(two))
-            at += 4 * HALF
-            grad_qkv[:, at : at + LANES] = jnp.where(low, turn(one), two)
+
+    def gather(x, c):
+        rows = slice(c * own_rows, (c + 1) * own_rows)
+        for copy in range(2):
+            first = part_of(x, c, copy, 0, own, near, other, cross)
+            second = part_of(x, c, copy, 1, own, near, other, cross)
+            for pair in range(qkv // LANES):
+                lanes = slice(pair * LANES, (pair + 1) * LANES)
+                one, two = first[rows, lanes].astype(F32), second[rows, lanes].astype(F32)
+                at = pair * 8 * HALF + copy * LANES
+                grad_qkv[:, at : at + LANES] = jnp.where(low, one, turn(two))
+                at += 4 * HALF
+                grad_qkv[:, at : at + LANES] = jnp.where(low, turn(one), two)
+
+    at_each_place(info, gather)
     for part in range(2):
         block = slice(part * own_rows, (part + 1) * own_rows)
         left = jnp.where(x == y, own[block, qkv:], other[block, qkv:]).astype(F32)
@@ -1279,6 +1283,7 @@
                 functools.partial(second_hop_body, step),
                 [SMEM_SPEC] + [VMEM_SPEC] * 4,
                 [second_shape, second_shape],
+                micros=3,
             )(info, got_forth, got_back, grad_w_fc, grad_w_out)
 
         second_forth, second_back = second_sums(half - 1, far_forth, far_back)
@@ -1326,6 +1331,7 @@
                 functools.partial(first_hop_body, step),
                 [SMEM_SPEC] + [VMEM_SPEC] * 5,
                 [first_shape, first_shape],
+                micros=4,
             )(info, forth, back, *firsts)
 
         second_forth, second_back = to_next(second_forth), to_back(second_back)

time: 214 us -> 214 us (level)
  no operation moved by 1% of the time
where the time goes in v4:
time: 214 us
  waiting for transfers between devices  109 us (51%)
  starting transfers between devices  50.7 us (24%)
  Pallas kernels  42.6 us (20%)
  matrix products  5.72 us (3%)
  local copies, waits for them, and re-layouts  3.78 us (2%)
    ppermute x65, waiting for transfers between devices, mover(): return lambda v: lax.ppermute(v, MESH_AXES, pairs)  109 us
    ppermute x65, starting transfers between devices, mover(): return lambda v: lax.ppermute(v, MESH_AXES, pairs)  50.7 us
    pallas_call x1, Pallas kernels, local(): kernel_call(attention_back_body, [SMEM_SPEC] + [VMEM_SPEC] * 11, [((all_r...  8.16 us
    pallas_call x1, Pallas kernels, local(): kernel_call(feed_body, [SMEM_SPEC] + [VMEM_SPEC] * (2 + RANKS) + [ANY_SPE...  6.97 us
    pallas_call x1, Pallas kernels, local(): kernel_call(attention_body, [SMEM_SPEC] + [VMEM_SPEC] * 2 + [ANY_SPEC] *...  6.59 us
    dot_general x4, matrix products, dot_rows(): lax.dot_general(left, right, (((0,), (0,)), ((), ())), preferred_element_...  5.72 us
  transfers between devices with their start and end apart: 65, of which 33 were waited for; matrix products, arithmetic and copies ran while one was open for 4% of the time, Pallas kernels for 14%

profile of v4, /device:TPU:0, one launch (start us, length us, event | category | flops | bytes accessed | tf_op | source)
XLA Modules:
  0.0 214.1 jit_solution(4959087752090526024)
XLA Ops:
  1.2 2.6 %collective-permute-start.1 = (bf16[64,1024]{1,0:T(8,128)(2,1)}, bf16[64,1024]{1,0:T(8,128)(2,1)S(1)}, u32[]{:S(2)}, u32[]{:S(2)}) collective-permute-start(bf16[64,1024]{1,0:T(8,128)(2,1)} %w_proj.1), channel_id=1, source_target_pairs={{0,2},{1,3},{2,0},{3,1},{4,6},{5,7},{6,4},{7,5},{8,10},{9,11},{10,... | collective-permute-start | bytes 393224 | tf_op jit(solution)/shard_map/ppermute | solution.py:1092
  6.6 1.0 copy-done.3
  10.7 1.3 collective-permute-start.3
  12.6 6.5 %collective-permute-done.4.refs_4_ = bf16[144,1024]{1,0:T(8,128)(2,1)S(1)} collective-permute-done((bf16[144,1024]{1,0:T(8,128)(2,1)S(1)}, bf16[144,1024]{1,0:T(8,128)(2,1)S(1)}, u32[]{:S(2)}, u32[]{:S(2)}) %collective-permute-start.4) | collective-permute-done | bytes 294944 | tf_op jit(solution)/shard_map/ppermute | solution.py:1092
  19.2 1.7 collective-permute-start.6
  20.9 1.5 collective-permute-start.8
  22.9 6.1 %collective-permute-done.6.refs_2_.block_other = bf16[176,1024]{1,0:T(8,128)(2,1)S(1)} collective-permute-done((bf16[176,1024]{1,0:T(8,128)(2,1)S(1)}, bf16[176,1024]{1,0:T(8,128)(2,1)S(1)}, u32[]{:S(2)}, u32[]{:S(2)}) %collective-permute-start.6) | collective-permute-done | bytes 360480 | tf_op jit(solution)/shard_map/ppermute | solution.py:1092
  30.1 1.6 collective-permute-start.11
  32.1 1.1 collective-permute-start.20
  33.2 1.0 collective-permute-start.18
  35.1 4.9 %collective-permute-done.11.refs_7_ = bf16[144,1024]{1,0:T(8,128)(2,1)S(1)} collective-permute-done((bf16[144,1024]{1,0:T(8,128)(2,1)S(1)}, bf16[144,1024]{1,0:T(8,128)(2,1)S(1)}, u32[]{:S(2)}, u32[]{:S(2)}) %collective-permute-start.11) | collective-permute-done | bytes 294944 | tf_op jit(solution)/shard_map/ppermute | solution.py:1092
  39.9 1.6 collective-permute-done.12.refs_8_
  42.1 1.6 collective-permute-start.13
  43.7 9.7 %collective-permute-done.13.refs_9_ = bf16[64,1024]{1,0:T(8,128)(2,1)S(1)} collective-permute-done((bf16[64,1024]{1,0:T(8,128)(2,1)S(1)}, bf16[64,1024]{1,0:T(8,128)(2,1)S(1)}, u32[]{:S(2)}, u32[]{:S(2)}) %collective-permute-start.13) | collective-permute-done | bytes 131104 | tf_op jit(solution)/shard_map/ppermute | solution.py:1092
  53.4 2.0 collective-permute-done.14.refs_10_
  55.4 1.5 collective-permute-start.15
  57.3 1.6 collective-permute-start.19
  58.9 6.6 %shard_map.285 = (bf16[640,1024]{1,0:T(8,128)(2,1)S(1)}, bf16[640,768]{1,0:T(8,128)(2,1)S(1)}, bf16[16,160,160]{2,1,0:T(8,128)(2,1)S(1)}, bf16[640,256]{1,0:T(8,...) custom-call(s32[13]{0:T(128)S(1)} %stack.90.info, ...), custom_call_target="tpu_custom_call" | custom-call | bytes 24000000 | tf_op jit(solution)/shard_map/pallas_call | solution.py:1204
  66.1 3.7 %collective-permute-done.21.refs_8_ = bf16[256,1024]{1,0:T(8,128)(2,1)S(1)} collective-permute-done((bf16[256,1024]{1,0:T(8,128)(2,1)S(1)}, bf16[256,1024]{1,0:T(8,128)(2,1)S(1)}, u32[]{:S(2)}, u32[]{:S(2)}) %collective-permute-start.21) | collective-permute-done | bytes 524320 | tf_op jit(solution)/shard_map/ppermute | solution.py:1092
  70.5 1.6 collective-permute-start.23
  72.6 9.5 %collective-permute-done.23.refs_9_ = bf16[256,1024]{1,0:T(8,128)(2,1)S(1)} collective-permute-done((bf16[256,1024]{1,0:T(8,128)(2,1)S(1)}, bf16[256,1024]{1,0:T(8,128)(2,1)S(1)}, u32[]{:S(2)}, u32[]{:S(2)}) %collective-permute-start.23) | collective-permute-done | bytes 524320 | tf_op jit(solution)/shard_map/ppermute | solution.py:1092
  82.1 1.3 collective-permute-done.24.refs_10_
  83.4 1.4 collective-permute-done.22.got
  86.2 1.6 collective-permute-start.28
  88.6 6.2 %collective-permute-done.28.refs_11_ = bf16[128,1024]{1,0:T(8,128)(2,1)S(1)} collective-permute-done((bf16[128,1024]{1,0:T(8,128)(2,1)S(1)}, bf16[128,1024]{1,0:T(8,128)(2,1)S(1)}, u32[]{:S(2)}, u32[]{:S(2)}) %collective-permute-start.28) | collective-permute-done | bytes 262176 | tf_op jit(solution)/shard_map/ppermute | solution.py:1092
  94.8 1.3 collective-permute-done.29.refs_12_
  96.1 7.0 %shard_map.288 = (bf16[640,1024]{1,0:T(8,128)(2,1)S(1)}, bf16[640,1024]{1,0:T(8,128)(2,1)S(1)}, bf16[640,1024]{1,0:T(8,128)(2,1)S(1)}, bf16[640,1024]{1,0:T(8,12...) custom-call(s32[13]{0:T(128)S(1)} %stack.90.info, ...), custom_call_target="tpu_custom_call" | custom-call | bytes 24000000 | tf_op jit(solution)/shard_map/pallas_call | solution.py:1244
  103.7 1.5 shard_map.289
  105.8 1.8 convolution_convert_fusion.1.grad_fc
  107.7 1.8 convolution_convert_fusion.grad_out
  110.7 1.7 collective-permute-start.33
  112.7 6.3 %collective-permute-done.33.got_forth = bf16[128,1024]{1,0:T(8,128)(2,1)S(1)} collective-permute-done((bf16[128,1024]{1,0:T(8,128)(2,1)S(1)}, bf16[128,1024]{1,0:T(8,128)(2,1)S(1)}, u32[]{:S(2)}, u32[]{:S(2)}) %collective-permute-start.33) | collective-permute-done | bytes 262176 | tf_op jit(solution)/shard_map/ppermute | solution.py:1092
  119.0 1.4 collective-permute-done.34.got_back
  121.2 1.1 collective-permute-done.32.got
  122.3 1.2 shard_map.293
  124.6 1.7 collective-permute-start.39
  126.7 8.2 %shard_map.294 = (bf16[640,1024]{1,0:T(8,128)(2,1)S(1)}, bf16[640,768]{1,0:T(8,128)(2,1)S(1)}, bf16[160,1024]{1,0:T(8,128)(2,1)S(1)}, bf16[160,1024]{1,0:T(8,128...) custom-call(s32[13]{0:T(128)S(1)} %stack.90.info, ...), custom_call_target="tpu_custom_call" | custom-call | bytes 3000000 | tf_op jit(solution)/shard_map/pallas_call | solution.py:1303
  135.4 1.4 convolution_convert_fusion.2.grad_qkv
  137.4 0.9 collective-permute-done.39.got_forth
  138.4 1.3 collective-permute-done.40.got_back
  140.1 1.6 collective-permute-start.42
  141.7 3.4 %collective-permute-done.42.got_forth = bf16[64,1024]{1,0:T(8,128)(2,1)S(1)} collective-permute-done((bf16[64,1024]{1,0:T(8,128)(2,1)S(1)}, bf16[64,1024]{1,0:T(8,128)(2,1)S(1)}, u32[]{:S(2)}, u32[]{:S(2)}) %collective-permute-start.42) | collective-permute-done | bytes 131104 | tf_op jit(solution)/shard_map/ppermute | solution.py:1092
  146.4 1.6 collective-permute-start.48
  148.6 1.5 collective-permute-start.50
  150.7 1.6 collective-permute-start.44
  152.8 8.5 %collective-permute-done.48.got_forth = bf16[256,1024]{1,0:T(8,128)(2,1)S(1)} collective-permute-done((bf16[256,1024]{1,0:T(8,128)(2,1)S(1)}, bf16[256,1024]{1,0:T(8,128)(2,1)S(1)}, u32[]{:S(2)}, u32[]{:S(2)}) %collective-permute-start.48) | collective-permute-done | bytes 524320 | tf_op jit(solution)/shard_map/ppermute | solution.py:1092
  161.2 1.6 collective-permute-done.49.got_back
  163.7 1.5 collective-permute-start.53
  165.7 1.4 shard_map.299
  167.6 1.6 collective-permute-done.45.got_back
  169.9 1.5 collective-permute-start.51
  171.9 1.4 shard_map.302
  173.4 10.8 %collective-permute-done.51.got_forth = bf16[144,1024]{1,0:T(8,128)(2,1)S(1)} collective-permute-done((bf16[144,1024]{1,0:T(8,128)(2,1)S(1)}, bf16[144,1024]{1,0:T(8,128)(2,1)S(1)}, u32[]{:S(2)}, u32[]{:S(2)}) %collective-permute-start.51) | collective-permute-done | bytes 294944 | tf_op jit(solution)/shard_map/ppermute | solution.py:1092
  184.2 1.3 collective-permute-done.52.got_back
  186.2 1.5 collective-permute-start.58
  188.4 1.5 collective-permute-start.55
  190.5 7.4 %collective-permute-done.55.got_forth = bf16[144,1024]{1,0:T(8,128)(2,1)S(1)} collective-permute-done((bf16[144,1024]{1,0:T(8,128)(2,1)S(1)}, bf16[144,1024]{1,0:T(8,128)(2,1)S(1)}, u32[]{:S(2)}, u32[]{:S(2)}) %collective-permute-start.55) | collective-permute-done | bytes 294944 | tf_op jit(solution)/shard_map/ppermute | solution.py:1092
  197.9 1.2 collective-permute-done.56.got_back
  199.8 1.4 collective-permute-start.60
  201.9 1.5 collective-permute-start.61
  203.4 2.1 shard_map.306
  205.5 5.1 %collective-permute-done.62.corner = bf16[128,256]{1,0:T(8,128)(2,1)S(1)} collective-permute-done((bf16[128,256]{1,0:T(8,128)(2,1)S(1)}, bf16[128,256]{1,0:T(8,128)(2,1)S(1)}, u32[]{:S(2)}, u32[]{:S(2)}) %collective-permute-start.62) | collective-permute-done | bytes 65568 | tf_op jit(solution)/shard_map/ppermute | solution.py:1092
  210.6 1.6 collective-permute-done.64.cross
  212.2 1.7 shard_map.307
  (122 shorter events, 29.9 us)
Async XLA Ops:
  0.7 8.5 %collective-permute-start = (bf16[64,3072]{1,0:T(8,128)(2,1)}, bf16[64,3072]{1,0:T(8,128)(2,1)S(1)}, u32[]{:S(2)}, u32[]{:S(2)}) collective-permute-start(bf16[64,3072]{1,0:T(8,128)(2,1)} %w_qkv.1), channel_id=1, source_target_pairs={{0,1},{1,0},{2,3},{3,2},{4,5},{5,4},{6,7},{7,6},{8,9},{9,8},{10,11... | collective-permute-start | bytes 1179656 | tf_op jit(solution)/shard_map/ppermute | solution.py:1092
  1.2 7.9 %collective-permute-start.1 = (bf16[64,1024]{1,0:T(8,128)(2,1)}, bf16[64,1024]{1,0:T(8,128)(2,1)S(1)}, u32[]{:S(2)}, u32[]{:S(2)}) collective-permute-start(bf16[64,1024]{1,0:T(8,128)(2,1)} %w_proj.1), channel_id=1, source_target_pairs={{0,2},{1,3},{2,0},{3,1},{4,6},{5,7},{6,4},{7,5},{8,10},{9,11},{10,... | collective-permute-start | bytes 393224 | tf_op jit(solution)/shard_map/ppermute | solution.py:1092
  5.5 3.6 %collective-permute-start.2 = (bf16[16,64]{1,0:T(8,128)(2,1)S(1)}, bf16[16,64]{1,0:T(8,128)(2,1)S(1)}, u32[]{:S(2)}, u32[]{:S(2)}) collective-permute-start(bf16[16,64]{1,0:T(8,128)(2,1)S(1)} %stack.104.vectors), channel_id=1, source_target_pairs={{0,1},{1,0},{2,3},{3,2},{4,5},{5,4},{6,7},{7,6},{8,9},{9,8},{10,11... | collective-permute-start | bytes 6152 | tf_op jit(solution)/shard_map/ppermute | solution.py:1092
  9.9 9.3 %collective-permute-start.4 = (bf16[144,1024]{1,0:T(8,128)(2,1)S(1)}, bf16[144,1024]{1,0:T(8,128)(2,1)S(1)}, u32[]{:S(2)}, u32[]{:S(2)}) collective-permute-start(bf16[144,1024]{1,0:T(8,128)(2,1)S(1)} %shard_map.281.refs_2_), channel_id=1, source_target_pairs={{0,2},{1,3},{2,6},{3,7},{4,0},{5,1},{6,10},{7,11},{8,4},{9,5},{10,... | collective-permute-start | bytes 884744 | tf_op jit(solution)/shard_map/ppermute | solution.py:1092
  10.7 8.6 %collective-permute-start.3 = (bf16[144,1024]{1,0:T(8,128)(2,1)S(1)}, bf16[144,1024]{1,0:T(8,128)(2,1)S(1)}, u32[]{:S(2)}, u32[]{:S(2)}) collective-permute-start(bf16[144,1024]{1,0:T(8,128)(2,1)S(1)} %shard_map.281.refs_2_), channel_id=1, source_target_pairs={{0,4},{1,5},{2,0},{3,1},{4,8},{5,9},{6,2},{7,3},{8,12},{9,13},{10,... | collective-permute-start | bytes 884744 | tf_op jit(solution)/shard_map/ppermute | solution.py:1092
  12.0 17.0 %collective-permute-start.10 = (bf16[64,4096]{1,0:T(8,128)(2,1)S(1)}, bf16[64,4096]{1,0:T(8,128)(2,1)S(1)}, u32[]{:S(2)}, u32[]{:S(2)}) collective-permute-start(bf16[64,4096]{1,0:T(8,128)(2,1)S(1)} %copy-done.1), channel_id=1, source_target_pairs={{0,1},{1,0},{2,3},{3,2},{4,5},{5,4},{6,7},{7,6},{8,9},{9,8},{10,11... | collective-permute-start | bytes 1572872 | tf_op jit(solution)/shard_map/ppermute | solution.py:1092
  19.2 9.8 %collective-permute-start.6 = (bf16[176,1024]{1,0:T(8,128)(2,1)S(1)}, bf16[176,1024]{1,0:T(8,128)(2,1)S(1)}, u32[]{:S(2)}, u32[]{:S(2)}) collective-permute-start(bf16[176,1024]{1,0:T(8,128)(2,1)S(1)} %get-tuple-element.173.refs_0_.block), channel_id=1, source_target_pairs={{0,16},{1,17},{2,18},{3,19},{4,20},{5,21},{6,22},{7,23},{8,24},{9,... | collective-permute-start | bytes 1081352 | tf_op jit(solution)/shard_map/ppermute | solution.py:1092
  20.9 9.0 %collective-permute-start.8 = (bf16[144,1024]{1,0:T(8,128)(2,1)S(1)}, bf16[144,1024]{1,0:T(8,128)(2,1)S(1)}, u32[]{:S(2)}, u32[]{:S(2)}) collective-permute-start(bf16[144,1024]{1,0:T(8,128)(2,1)S(1)} %collective-permute-done.3.refs_3_), channel_id=1, source_target_pairs={{0,4},{1,5},{2,0},{3,1},{4,8},{5,9},{6,2},{7,3},{8,12},{9,13},{10,... | collective-permute-start | bytes 884744 | tf_op jit(solution)/shard_map/ppermute | solution.py:1092
  22.4 7.7 %collective-permute-start.9 = (bf16[144,1024]{1,0:T(8,128)(2,1)S(1)}, bf16[144,1024]{1,0:T(8,128)(2,1)S(1)}, u32[]{:S(2)}, u32[]{:S(2)}) collective-permute-start(bf16[144,1024]{1,0:T(8,128)(2,1)S(1)} %collective-permute-done.4.refs_4_), channel_id=1, source_target_pairs={{0,2},{1,3},{2,6},{3,7},{4,0},{5,1},{6,10},{7,11},{8,4},{9,5},{10,... | collective-permute-start | bytes 884744 | tf_op jit(solution)/shard_map/ppermute | solution.py:1092
  22.9 10.3 %collective-permute-start.5 = (bf16[176,1024]{1,0:T(8,128)(2,1)S(1)}, bf16[176,1024]{1,0:T(8,128)(2,1)S(1)}, u32[]{:S(2)}, u32[]{:S(2)}) collective-permute-start(bf16[176,1024]{1,0:T(8,128)(2,1)S(1)} %get-tuple-element.173.refs_0_.block), channel_id=1, source_target_pairs={{0,1},{1,0},{2,3},{3,2},{4,5},{5,4},{6,7},{7,6},{8,9},{9,8},{10,11... | collective-permute-start | bytes 1081352 | tf_op jit(solution)/shard_map/ppermute | solution.py:1092
  29.0 5.2 %collective-permute-start.7 = (bf16[176,1024]{1,0:T(8,128)(2,1)S(1)}, bf16[176,1024]{1,0:T(8,128)(2,1)S(1)}, u32[]{:S(2)}, u32[]{:S(2)}) collective-permute-start(bf16[176,1024]{1,0:T(8,128)(2,1)S(1)} %collective-permute-done.6.refs_2_.block_other), channel_id=1, source_target_pairs={{0,1},{1,0},{2,3},{3,2},{4,5},{5,4},{6,7},{7,6},{8,9},{9,8},{10,11... | collective-permute-start | bytes 1081352 | tf_op jit(solution)/shard_map/ppermute | solution.py:1092
  30.1 9.8 %collective-permute-start.11 = (bf16[144,1024]{1,0:T(8,128)(2,1)S(1)}, bf16[144,1024]{1,0:T(8,128)(2,1)S(1)}, u32[]{:S(2)}, u32[]{:S(2)}) collective-permute-start(bf16[144,1024]{1,0:T(8,128)(2,1)S(1)} %collective-permute-done.8.refs_5_), channel_id=1, source_target_pairs={{0,4},{1,5},{2,0},{3,1},{4,8},{5,9},{6,2},{7,3},{8,12},{9,13},{10,... | collective-permute-start | bytes 884744 | tf_op jit(solution)/shard_map/ppermute | solution.py:1092
  31.7 9.9 %collective-permute-start.12 = (bf16[144,1024]{1,0:T(8,128)(2,1)S(1)}, bf16[144,1024]{1,0:T(8,128)(2,1)S(1)}, u32[]{:S(2)}, u32[]{:S(2)}) collective-permute-start(bf16[144,1024]{1,0:T(8,128)(2,1)S(1)} %collective-permute-done.9.refs_6_), channel_id=1, source_target_pairs={{0,2},{1,3},{2,6},{3,7},{4,0},{5,1},{6,10},{7,11},{8,4},{9,5},{10,... | collective-permute-start | bytes 884744 | tf_op jit(solution)/shard_map/ppermute | solution.py:1092
  32.1 24.8 %collective-permute-start.20 = (bf16[256,1024]{1,0:T(8,128)(2,1)S(1)}, bf16[256,1024]{1,0:T(8,128)(2,1)S(1)}, u32[]{:S(2)}, u32[]{:S(2)}) collective-permute-start(bf16[256,1024]{1,0:T(8,128)(2,1)S(1)} %shard_map.284.refs_4_), channel_id=1, source_target_pairs={{0,2},{1,3},{2,6},{3,7},{4,0},{5,1},{6,10},{7,11},{8,4},{9,5},{10,... | collective-permute-start | bytes 1572872 | tf_op jit(solution)/shard_map/ppermute | solution.py:1092
  33.2 24.1 %collective-permute-start.18 = (bf16[256,1024]{1,0:T(8,128)(2,1)S(1)}, bf16[256,1024]{1,0:T(8,128)(2,1)S(1)}, u32[]{:S(2)}, u32[]{:S(2)}) collective-permute-start(bf16[256,1024]{1,0:T(8,128)(2,1)S(1)} %shard_map.284.refs_4_), channel_id=1, source_target_pairs={{0,4},{1,5},{2,0},{3,1},{4,8},{5,9},{6,2},{7,3},{8,12},{9,13},{10,... | collective-permute-start | bytes 1572872 | tf_op jit(solution)/shard_map/ppermute | solution.py:1092
  41.6 13.8 %collective-permute-start.14 = (bf16[80,1024]{1,0:T(8,128)(2,1)S(1)}, bf16[80,1024]{1,0:T(8,128)(2,1)S(1)}, u32[]{:S(2)}, u32[]{:S(2)}) collective-permute-start(bf16[80,1024]{1,0:T(8,128)(2,1)S(1)} %slice.32), channel_id=1, source_target_pairs={{0,2},{1,3},{2,6},{3,7},{4,0},{5,1},{6,10},{7,11},{8,4},{9,5},{10,... | collective-permute-start | bytes 491528 | tf_op jit(solution)/shard_map/ppermute | solution.py:1092
  42.1 11.3 %collective-permute-start.13 = (bf16[64,1024]{1,0:T(8,128)(2,1)S(1)}, bf16[64,1024]{1,0:T(8,128)(2,1)S(1)}, u32[]{:S(2)}, u32[]{:S(2)}) collective-permute-start(bf16[64,1024]{1,0:T(8,128)(2,1)S(1)} %slice.31), channel_id=1, source_target_pairs={{0,4},{1,5},{2,0},{3,1},{4,8},{5,9},{6,2},{7,3},{8,12},{9,13},{10,... | collective-permute-start | bytes 393224 | tf_op jit(solution)/shard_map/ppermute | solution.py:1092
  55.4 10.1 %collective-permute-start.15 = (bf16[160,1024]{1,0:T(8,128)(2,1)S(1)}, bf16[160,1024]{1,0:T(8,128)(2,1)S(1)}, u32[]{:S(2)}, u32[]{:S(2)}) collective-permute-start(bf16[160,1024]{1,0:T(8,128)(2,1)S(1)} %get-tuple-element.211.refs_0_.d_top), channel_id=1, source_target_pairs={{0,16},{1,17},{2,18},{3,19},{4,20},{5,21},{6,22},{7,23},{8,24},{9,... | collective-permute-start | bytes 983048 | tf_op jit(solution)/shard_map/ppermute | solution.py:1092
  56.9 12.9 %collective-permute-start.21 = (bf16[256,1024]{1,0:T(8,128)(2,1)S(1)}, bf16[256,1024]{1,0:T(8,128)(2,1)S(1)}, u32[]{:S(2)}, u32[]{:S(2)}) collective-permute-start(bf16[256,1024]{1,0:T(8,128)(2,1)S(1)} %collective-permute-done.20.refs_6_), channel_id=1, source_target_pairs={{0,2},{1,3},{2,6},{3,7},{4,0},{5,1},{6,10},{7,11},{8,4},{9,5},{10,... | collective-permute-start | bytes 1572872 | tf_op jit(solution)/shard_map/ppermute | solution.py:1092
  57.3 12.7 %collective-permute-start.19 = (bf16[256,1024]{1,0:T(8,128)(2,1)S(1)}, bf16[256,1024]{1,0:T(8,128)(2,1)S(1)}, u32[]{:S(2)}, u32[]{:S(2)}) collective-permute-start(bf16[256,1024]{1,0:T(8,128)(2,1)S(1)} %collective-permute-done.18.refs_5_), channel_id=1, source_target_pairs={{0,4},{1,5},{2,0},{3,1},{4,8},{5,9},{6,2},{7,3},{8,12},{9,13},{10,... | collective-permute-start | bytes 1572872 | tf_op jit(solution)/shard_map/ppermute | solution.py:1092
  65.5 4.5 %collective-permute-start.16 = (bf16[160,1024]{1,0:T(8,128)(2,1)S(1)}, bf16[160,1024]{1,0:T(8,128)(2,1)S(1)}, u32[]{:S(2)}, u32[]{:S(2)}) collective-permute-start(bf16[160,1024]{1,0:T(8,128)(2,1)S(1)} %get-tuple-element.201), channel_id=1, source_target_pairs={{0,1},{1,0},{2,3},{3,2},{4,5},{5,4},{6,7},{7,6},{8,9},{9,8},{10,11... | collective-permute-start | bytes 983048 | tf_op jit(solution)/shard_map/ppermute | solution.py:1092
  65.6 4.4 %collective-permute-start.17 = (bf16[160,1024]{1,0:T(8,128)(2,1)S(1)}, bf16[160,1024]{1,0:T(8,128)(2,1)S(1)}, u32[]{:S(2)}, u32[]{:S(2)}) collective-permute-start(bf16[160,1024]{1,0:T(8,128)(2,1)S(1)} %get-tuple-element.202), channel_id=1, source_target_pairs={{0,1},{1,0},{2,3},{3,2},{4,5},{5,4},{6,7},{7,6},{8,9},{9,8},{10,11... | collective-permute-start | bytes 983048 | tf_op jit(solution)/shard_map/ppermute | solution.py:1092
  70.1 14.7 %collective-permute-start.22 = (bf16[2,160,1024]{2,1,0:T(8,128)(2,1)S(1)}, bf16[2,160,1024]{2,1,0:T(8,128)(2,1)S(1)}, u32[]{:S(2)}, u32[]{:S(2)}) collective-permute-start(bf16[2,160,1024]{2,1,0:T(8,128)(2,1)S(1)} %shard_map.286), channel_id=1, source_target_pairs={{0,16},{1,17},{2,18},{3,19},{4,20},{5,21},{6,22},{7,23},{8,24},{9,... | collective-permute-start | bytes 1966088 | tf_op jit(solution)/shard_map/ppermute | solution.py:1092
  70.5 11.5 %collective-permute-start.23 = (bf16[256,1024]{1,0:T(8,128)(2,1)S(1)}, bf16[256,1024]{1,0:T(8,128)(2,1)S(1)}, u32[]{:S(2)}, u32[]{:S(2)}) collective-permute-start(bf16[256,1024]{1,0:T(8,128)(2,1)S(1)} %collective-permute-done.19.refs_7_), channel_id=1, source_target_pairs={{0,4},{1,5},{2,0},{3,1},{4,8},{5,9},{6,2},{7,3},{8,12},{9,13},{10,... | collective-permute-start | bytes 1572872 | tf_op jit(solution)/shard_map/ppermute | solution.py:1092
  72.1 11.3 %collective-permute-start.24 = (bf16[256,1024]{1,0:T(8,128)(2,1)S(1)}, bf16[256,1024]{1,0:T(8,128)(2,1)S(1)}, u32[]{:S(2)}, u32[]{:S(2)}) collective-permute-start(bf16[256,1024]{1,0:T(8,128)(2,1)S(1)} %collective-permute-done.21.refs_8_), channel_id=1, source_target_pairs={{0,2},{1,3},{2,6},{3,7},{4,0},{5,1},{6,10},{7,11},{8,4},{9,5},{10,... | collective-permute-start | bytes 1572872 | tf_op jit(solution)/shard_map/ppermute | solution.py:1092
  85.5 10.6 %collective-permute-start.25 = (bf16[2,160,1024]{2,1,0:T(8,128)(2,1)S(1)}, bf16[2,160,1024]{2,1,0:T(8,128)(2,1)S(1)}, u32[]{:S(2)}, u32[]{:S(2)}) collective-permute-start(bf16[2,160,1024]{2,1,0:T(8,128)(2,1)S(1)} %get-tuple-element.213.normed), channel_id=1, source_target_pairs={{0,1},{1,0},{2,3},{3,2},{4,5},{5,4},{6,7},{7,6},{8,9},{9,8},{10,11... | collective-permute-start | bytes 1966088 | tf_op jit(solution)/shard_map/ppermute | solution.py:1092
  85.6 2.6 %collective-permute-start.26 = (bf16[160,1024]{1,0:T(8,128)(2,1)S(1)}, bf16[160,1024]{1,0:T(8,128)(2,1)S(1)}, u32[]{:S(2)}, u32[]{:S(2)}) collective-permute-start(bf16[160,1024]{1,0:T(8,128)(2,1)S(1)} %get-tuple-element.211.refs_0_.d_top), channel_id=1, source_target_pairs={{0,1},{1,0},{2,3},{3,2},{4,5},{5,4},{6,7},{7,6},{8,9},{9,8},{10,11... | collective-permute-start | bytes 983048 | tf_op jit(solution)/shard_map/ppermute | solution.py:1092
  86.1 2.5 %collective-permute-start.27 = (bf16[160,1024]{1,0:T(8,128)(2,1)S(1)}, bf16[160,1024]{1,0:T(8,128)(2,1)S(1)}, u32[]{:S(2)}, u32[]{:S(2)}) collective-permute-start(bf16[160,1024]{1,0:T(8,128)(2,1)S(1)} %collective-permute-done.15.refs_2_.d_other), channel_id=1, source_target_pairs={{0,1},{1,0},{2,3},{3,2},{4,5},{5,4},{6,7},{7,6},{8,9},{9,8},{10,11... | collective-permute-start | bytes 983048 | tf_op jit(solution)/shard_map/ppermute | solution.py:1092
  86.2 8.7 %collective-permute-start.28 = (bf16[128,1024]{1,0:T(8,128)(2,1)S(1)}, bf16[128,1024]{1,0:T(8,128)(2,1)S(1)}, u32[]{:S(2)}, u32[]{:S(2)}) collective-permute-start(bf16[128,1024]{1,0:T(8,128)(2,1)S(1)} %slice.36), channel_id=1, source_target_pairs={{0,4},{1,5},{2,0},{3,1},{4,8},{5,9},{6,2},{7,3},{8,12},{9,13},{10,... | collective-permute-start | bytes 786440 | tf_op jit(solution)/shard_map/ppermute | solution.py:1092
  87.8 8.4 %collective-permute-start.29 = (bf16[128,1024]{1,0:T(8,128)(2,1)S(1)}, bf16[128,1024]{1,0:T(8,128)(2,1)S(1)}, u32[]{:S(2)}, u32[]{:S(2)}) collective-permute-start(bf16[128,1024]{1,0:T(8,128)(2,1)S(1)} %slice.37), channel_id=1, source_target_pairs={{0,2},{1,3},{2,6},{3,7},{4,0},{5,1},{6,10},{7,11},{8,4},{9,5},{10,... | collective-permute-start | bytes 786440 | tf_op jit(solution)/shard_map/ppermute | solution.py:1092
  103.1 2.1 collective-permute-start.30
  103.2 2.1 collective-permute-start.31
  105.4 16.8 %collective-permute-start.32 = (bf16[2,160,1024]{2,1,0:T(8,128)(2,1)S(1)}, bf16[2,160,1024]{2,1,0:T(8,128)(2,1)S(1)}, u32[]{:S(2)}, u32[]{:S(2)}) collective-permute-start(bf16[2,160,1024]{2,1,0:T(8,128)(2,1)S(1)} %shard_map.290), channel_id=1, source_target_pairs={{0,16},{1,17},{2,18},{3,19},{4,20},{5,21},{6,22},{7,23},{8,24},{9,... | collective-permute-start | bytes 1966088 | tf_op jit(solution)/shard_map/ppermute | solution.py:1092
  110.1 11.0 %collective-permute-start.35 = (bf16[160,1024]{1,0:T(8,128)(2,1)S(1)}, bf16[160,1024]{1,0:T(8,128)(2,1)S(1)}, u32[]{:S(2)}, u32[]{:S(2)}) collective-permute-start(bf16[160,1024]{1,0:T(8,128)(2,1)S(1)} %get-tuple-element.241), channel_id=1, source_target_pairs={{0,1},{1,0},{2,3},{3,2},{4,5},{5,4},{6,7},{7,6},{8,9},{9,8},{10,11... | collective-permute-start | bytes 983048 | tf_op jit(solution)/shard_map/ppermute | solution.py:1092
  110.2 10.9 %collective-permute-start.36 = (bf16[160,1024]{1,0:T(8,128)(2,1)S(1)}, bf16[160,1024]{1,0:T(8,128)(2,1)S(1)}, u32[]{:S(2)}, u32[]{:S(2)}) collective-permute-start(bf16[160,1024]{1,0:T(8,128)(2,1)S(1)} %get-tuple-element.242), channel_id=1, source_target_pairs={{0,1},{1,0},{2,3},{3,2},{4,5},{5,4},{6,7},{7,6},{8,9},{9,8},{10,11... | collective-permute-start | bytes 983048 | tf_op jit(solution)/shard_map/ppermute | solution.py:1092
  110.7 8.3 %collective-permute-start.33 = (bf16[128,1024]{1,0:T(8,128)(2,1)S(1)}, bf16[128,1024]{1,0:T(8,128)(2,1)S(1)}, u32[]{:S(2)}, u32[]{:S(2)}) collective-permute-start(bf16[128,1024]{1,0:T(8,128)(2,1)S(1)} %get-tuple-element.237), channel_id=1, source_target_pairs={{0,4},{1,5},{2,0},{3,1},{4,8},{5,9},{6,2},{7,3},{8,12},{9,13},{10,... | collective-permute-start | bytes 786440 | tf_op jit(solution)/shard_map/ppermute | solution.py:1092
  112.4 8.0 %collective-permute-start.34 = (bf16[128,1024]{1,0:T(8,128)(2,1)S(1)}, bf16[128,1024]{1,0:T(8,128)(2,1)S(1)}, u32[]{:S(2)}, u32[]{:S(2)}) collective-permute-start(bf16[128,1024]{1,0:T(8,128)(2,1)S(1)} %get-tuple-element.238), channel_id=1, source_target_pairs={{0,2},{1,3},{2,6},{3,7},{4,0},{5,1},{6,10},{7,11},{8,4},{9,5},{10,... | collective-permute-start | bytes 786440 | tf_op jit(solution)/shard_map/ppermute | solution.py:1092
  123.5 3.2 %collective-permute-start.37 = (bf16[160,1024]{1,0:T(8,128)(2,1)S(1)}, bf16[160,1024]{1,0:T(8,128)(2,1)S(1)}, u32[]{:S(2)}, u32[]{:S(2)}) collective-permute-start(bf16[160,1024]{1,0:T(8,128)(2,1)S(1)} %get-tuple-element.244.refs_0_), channel_id=1, source_target_pairs={{0,1},{1,0},{2,3},{3,2},{4,5},{5,4},{6,7},{7,6},{8,9},{9,8},{10,11... | collective-permute-start | bytes 983048 | tf_op jit(solution)/shard_map/ppermute | solution.py:1092
  123.5 3.1 %collective-permute-start.38 = (bf16[160,1024]{1,0:T(8,128)(2,1)S(1)}, bf16[160,1024]{1,0:T(8,128)(2,1)S(1)}, u32[]{:S(2)}, u32[]{:S(2)}) collective-permute-start(bf16[160,1024]{1,0:T(8,128)(2,1)S(1)} %get-tuple-element.245.refs_2_), channel_id=1, source_target_pairs={{0,1},{1,0},{2,3},{3,2},{4,5},{5,4},{6,7},{7,6},{8,9},{9,8},{10,11... | collective-permute-start | bytes 983048 | tf_op jit(solution)/shard_map/ppermute | solution.py:1092
  124.1 13.3 %collective-permute-start.41 = (bf16[160,1024]{1,0:T(8,128)(2,1)S(1)}, bf16[160,1024]{1,0:T(8,128)(2,1)S(1)}, u32[]{:S(2)}, u32[]{:S(2)}) collective-permute-start(bf16[160,1024]{1,0:T(8,128)(2,1)S(1)} %add_convert_fusion), channel_id=1, source_target_pairs={{0,16},{1,17},{2,18},{3,19},{4,20},{5,21},{6,22},{7,23},{8,24},{9,... | collective-permute-start | bytes 983048 | tf_op jit(solution)/shard_map/ppermute | solution.py:1092
  124.6 13.8 %collective-permute-start.39 = (bf16[256,1024]{1,0:T(8,128)(2,1)S(1)}, bf16[256,1024]{1,0:T(8,128)(2,1)S(1)}, u32[]{:S(2)}, u32[]{:S(2)}) collective-permute-start(bf16[256,1024]{1,0:T(8,128)(2,1)S(1)} %get-tuple-element.258), channel_id=1, source_target_pairs={{0,4},{1,5},{2,0},{3,1},{4,8},{5,9},{6,2},{7,3},{8,12},{9,13},{10,... | collective-permute-start | bytes 1572872 | tf_op jit(solution)/shard_map/ppermute | solution.py:1092
  126.3 13.4 %collective-permute-start.40 = (bf16[256,1024]{1,0:T(8,128)(2,1)S(1)}, bf16[256,1024]{1,0:T(8,128)(2,1)S(1)}, u32[]{:S(2)}, u32[]{:S(2)}) collective-permute-start(bf16[256,1024]{1,0:T(8,128)(2,1)S(1)} %get-tuple-element.259), channel_id=1, source_target_pairs={{0,2},{1,3},{2,6},{3,7},{4,0},{5,1},{6,10},{7,11},{8,4},{9,5},{10,... | collective-permute-start | bytes 1572872 | tf_op jit(solution)/shard_map/ppermute | solution.py:1092
  139.7 5.4 %collective-permute-start.43 = (bf16[80,1024]{1,0:T(8,128)(2,1)S(1)}, bf16[80,1024]{1,0:T(8,128)(2,1)S(1)}, u32[]{:S(2)}, u32[]{:S(2)}) collective-permute-start(bf16[80,1024]{1,0:T(8,128)(2,1)S(1)} %get-tuple-element.263), channel_id=1, source_target_pairs={{0,2},{1,3},{2,6},{3,7},{4,0},{5,1},{6,10},{7,11},{8,4},{9,5},{10,... | collective-permute-start | bytes 491528 | tf_op jit(solution)/shard_map/ppermute | solution.py:1092
  140.1 5.0 %collective-permute-start.42 = (bf16[64,1024]{1,0:T(8,128)(2,1)S(1)}, bf16[64,1024]{1,0:T(8,128)(2,1)S(1)}, u32[]{:S(2)}, u32[]{:S(2)}) collective-permute-start(bf16[64,1024]{1,0:T(8,128)(2,1)S(1)} %get-tuple-element.262), channel_id=1, source_target_pairs={{0,4},{1,5},{2,0},{3,1},{4,8},{5,9},{6,2},{7,3},{8,12},{9,13},{10,... | collective-permute-start | bytes 393224 | tf_op jit(solution)/shard_map/ppermute | solution.py:1092
  145.1 3.4 %collective-permute-start.46 = (bf16[160,1024]{1,0:T(8,128)(2,1)S(1)}, bf16[160,1024]{1,0:T(8,128)(2,1)S(1)}, u32[]{:S(2)}, u32[]{:S(2)}) collective-permute-start(bf16[160,1024]{1,0:T(8,128)(2,1)S(1)} %get-tuple-element.272), channel_id=1, source_target_pairs={{0,1},{1,0},{2,3},{3,2},{4,5},{5,4},{6,7},{7,6},{8,9},{9,8},{10,11... | collective-permute-start | bytes 983048 | tf_op jit(solution)/shard_map/ppermute | solution.py:1092
  145.1 3.4 %collective-permute-start.47 = (bf16[160,1024]{1,0:T(8,128)(2,1)S(1)}, bf16[160,1024]{1,0:T(8,128)(2,1)S(1)}, u32[]{:S(2)}, u32[]{:S(2)}) collective-permute-start(bf16[160,1024]{1,0:T(8,128)(2,1)S(1)} %get-tuple-element.273), channel_id=1, source_target_pairs={{0,1},{1,0},{2,3},{3,2},{4,5},{5,4},{6,7},{7,6},{8,9},{9,8},{10,11... | collective-permute-start | bytes 983048 | tf_op jit(solution)/shard_map/ppermute | solution.py:1092
  146.4 14.8 %collective-permute-start.48 = (bf16[256,1024]{1,0:T(8,128)(2,1)S(1)}, bf16[256,1024]{1,0:T(8,128)(2,1)S(1)}, u32[]{:S(2)}, u32[]{:S(2)}) collective-permute-start(bf16[256,1024]{1,0:T(8,128)(2,1)S(1)} %get-tuple-element.277), channel_id=1, source_target_pairs={{0,4},{1,5},{2,0},{3,1},{4,8},{5,9},{6,2},{7,3},{8,12},{9,13},{10,... | collective-permute-start | bytes 1572872 | tf_op jit(solution)/shard_map/ppermute | solution.py:1092
  148.0 14.8 %collective-permute-start.49 = (bf16[256,1024]{1,0:T(8,128)(2,1)S(1)}, bf16[256,1024]{1,0:T(8,128)(2,1)S(1)}, u32[]{:S(2)}, u32[]{:S(2)}) collective-permute-start(bf16[256,1024]{1,0:T(8,128)(2,1)S(1)} %get-tuple-element.278), channel_id=1, source_target_pairs={{0,2},{1,3},{2,6},{3,7},{4,0},{5,1},{6,10},{7,11},{8,4},{9,5},{10,... | collective-permute-start | bytes 1572872 | tf_op jit(solution)/shard_map/ppermute | solution.py:1092
  148.6 14.3 %collective-permute-start.50 = (bf16[160,1024]{1,0:T(8,128)(2,1)S(1)}, bf16[160,1024]{1,0:T(8,128)(2,1)S(1)}, u32[]{:S(2)}, u32[]{:S(2)}) collective-permute-start(bf16[160,1024]{1,0:T(8,128)(2,1)S(1)} %shard_map.298), channel_id=1, source_target_pairs={{0,16},{1,17},{2,18},{3,19},{4,20},{5,21},{6,22},{7,23},{8,24},{9,... | collective-permute-start | bytes 983048 | tf_op jit(solution)/shard_map/ppermute | solution.py:1092
  150.7 16.9 %collective-permute-start.44 = (bf16[144,1024]{1,0:T(8,128)(2,1)S(1)}, bf16[144,1024]{1,0:T(8,128)(2,1)S(1)}, u32[]{:S(2)}, u32[]{:S(2)}) collective-permute-start(bf16[144,1024]{1,0:T(8,128)(2,1)S(1)} %get-tuple-element.268), channel_id=1, source_target_pairs={{0,4},{1,5},{2,0},{3,1},{4,8},{5,9},{6,2},{7,3},{8,12},{9,13},{10,... | collective-permute-start | bytes 884744 | tf_op jit(solution)/shard_map/ppermute | solution.py:1092
  152.3 16.9 %collective-permute-start.45 = (bf16[144,1024]{1,0:T(8,128)(2,1)S(1)}, bf16[144,1024]{1,0:T(8,128)(2,1)S(1)}, u32[]{:S(2)}, u32[]{:S(2)}) collective-permute-start(bf16[144,1024]{1,0:T(8,128)(2,1)S(1)} %get-tuple-element.269), channel_id=1, source_target_pairs={{0,2},{1,3},{2,6},{3,7},{4,0},{5,1},{6,10},{7,11},{8,4},{9,5},{10,... | collective-permute-start | bytes 884744 | tf_op jit(solution)/shard_map/ppermute | solution.py:1092
  163.7 21.8 %collective-permute-start.53 = (bf16[256,1024]{1,0:T(8,128)(2,1)S(1)}, bf16[256,1024]{1,0:T(8,128)(2,1)S(1)}, u32[]{:S(2)}, u32[]{:S(2)}) collective-permute-start(bf16[256,1024]{1,0:T(8,128)(2,1)S(1)} %get-tuple-element.288), channel_id=1, source_target_pairs={{0,4},{1,5},{2,0},{3,1},{4,8},{5,9},{6,2},{7,3},{8,12},{9,13},{10,... | collective-permute-start | bytes 1572872 | tf_op jit(solution)/shard_map/ppermute | solution.py:1092
  165.2 20.3 %collective-permute-start.54 = (bf16[256,1024]{1,0:T(8,128)(2,1)S(1)}, bf16[256,1024]{1,0:T(8,128)(2,1)S(1)}, u32[]{:S(2)}, u32[]{:S(2)}) collective-permute-start(bf16[256,1024]{1,0:T(8,128)(2,1)S(1)} %get-tuple-element.289), channel_id=1, source_target_pairs={{0,2},{1,3},{2,6},{3,7},{4,0},{5,1},{6,10},{7,11},{8,4},{9,5},{10,... | collective-permute-start | bytes 1572872 | tf_op jit(solution)/shard_map/ppermute | solution.py:1092
  169.9 14.3 %collective-permute-start.51 = (bf16[144,1024]{1,0:T(8,128)(2,1)S(1)}, bf16[144,1024]{1,0:T(8,128)(2,1)S(1)}, u32[]{:S(2)}, u32[]{:S(2)}) collective-permute-start(bf16[144,1024]{1,0:T(8,128)(2,1)S(1)} %get-tuple-element.284), channel_id=1, source_target_pairs={{0,4},{1,5},{2,0},{3,1},{4,8},{5,9},{6,2},{7,3},{8,12},{9,13},{10,... | collective-permute-start | bytes 884744 | tf_op jit(solution)/shard_map/ppermute | solution.py:1092
  171.4 14.1 %collective-permute-start.52 = (bf16[144,1024]{1,0:T(8,128)(2,1)S(1)}, bf16[144,1024]{1,0:T(8,128)(2,1)S(1)}, u32[]{:S(2)}, u32[]{:S(2)}) collective-permute-start(bf16[144,1024]{1,0:T(8,128)(2,1)S(1)} %get-tuple-element.285), channel_id=1, source_target_pairs={{0,2},{1,3},{2,6},{3,7},{4,0},{5,1},{6,10},{7,11},{8,4},{9,5},{10,... | collective-permute-start | bytes 884744 | tf_op jit(solution)/shard_map/ppermute | solution.py:1092
  186.2 12.9 %collective-permute-start.58 = (bf16[256,1024]{1,0:T(8,128)(2,1)S(1)}, bf16[256,1024]{1,0:T(8,128)(2,1)S(1)}, u32[]{:S(2)}, u32[]{:S(2)}) collective-permute-start(bf16[256,1024]{1,0:T(8,128)(2,1)S(1)} %shard_map.304.own), channel_id=1, source_target_pairs={{0,16},{1,17},{2,18},{3,19},{4,20},{5,21},{6,22},{7,23},{8,24},{9,... | collective-permute-start | bytes 1572872 | tf_op jit(solution)/shard_map/ppermute | solution.py:1092
  187.7 11.4 %collective-permute-start.57 = (bf16[256,1024]{1,0:T(8,128)(2,1)S(1)}, bf16[256,1024]{1,0:T(8,128)(2,1)S(1)}, u32[]{:S(2)}, u32[]{:S(2)}) collective-permute-start(bf16[256,1024]{1,0:T(8,128)(2,1)S(1)} %shard_map.304.own), channel_id=1, source_target_pairs={{0,1},{1,0},{2,3},{3,2},{4,5},{5,4},{6,7},{7,6},{8,9},{9,8},{10,11... | collective-permute-start | bytes 1572872 | tf_op jit(solution)/shard_map/ppermute | solution.py:1092
  188.4 9.5 %collective-permute-start.55 = (bf16[144,1024]{1,0:T(8,128)(2,1)S(1)}, bf16[144,1024]{1,0:T(8,128)(2,1)S(1)}, u32[]{:S(2)}, u32[]{:S(2)}) collective-permute-start(bf16[144,1024]{1,0:T(8,128)(2,1)S(1)} %get-tuple-element.297), channel_id=1, source_target_pairs={{0,4},{1,5},{2,0},{3,1},{4,8},{5,9},{6,2},{7,3},{8,12},{9,13},{10,... | collective-permute-start | bytes 884744 | tf_op jit(solution)/shard_map/ppermute | solution.py:1092
  189.9 9.1 %collective-permute-start.56 = (bf16[144,1024]{1,0:T(8,128)(2,1)S(1)}, bf16[144,1024]{1,0:T(8,128)(2,1)S(1)}, u32[]{:S(2)}, u32[]{:S(2)}) collective-permute-start(bf16[144,1024]{1,0:T(8,128)(2,1)S(1)} %get-tuple-element.298), channel_id=1, source_target_pairs={{0,2},{1,3},{2,6},{3,7},{4,0},{5,1},{6,10},{7,11},{8,4},{9,5},{10,... | collective-permute-start | bytes 884744 | tf_op jit(solution)/shard_map/ppermute | solution.py:1092
  199.1 4.3 %collective-permute-start.63 = (bf16[256,1024]{1,0:T(8,128)(2,1)S(1)}, bf16[256,1024]{1,0:T(8,128)(2,1)S(1)}, u32[]{:S(2)}, u32[]{:S(2)}) collective-permute-start(bf16[256,1024]{1,0:T(8,128)(2,1)S(1)} %collective-permute-done.58.other), channel_id=1, source_target_pairs={{0,1},{1,0},{2,3},{3,2},{4,5},{5,4},{6,7},{7,6},{8,9},{9,8},{10,11... | collective-permute-start | bytes 1572872 | tf_op jit(solution)/shard_map/ppermute | solution.py:1092
  199.8 10.9 %collective-permute-start.60 = (bf16[144,1024]{1,0:T(8,128)(2,1)S(1)}, bf16[144,1024]{1,0:T(8,128)(2,1)S(1)}, u32[]{:S(2)}, u32[]{:S(2)}) collective-permute-start(bf16[144,1024]{1,0:T(8,128)(2,1)S(1)} %shard_map.305.own), channel_id=1, source_target_pairs={{0,16},{1,17},{2,18},{3,19},{4,20},{5,21},{6,22},{7,23},{8,24},{9,... | collective-permute-start | bytes 884744 | tf_op jit(solution)/shard_map/ppermute | solution.py:1092
  201.1 9.5 %collective-permute-start.62 = (bf16[128,256]{1,0:T(8,128)(2,1)S(1)}, bf16[128,256]{1,0:T(8,128)(2,1)S(1)}, u32[]{:S(2)}, u32[]{:S(2)}) collective-permute-start(bf16[128,256]{1,0:T(8,128)(2,1)S(1)} %slice.38), channel_id=1, source_target_pairs={{0,18},{1,19},{2,16},{3,17},{4,22},{5,23},{6,20},{7,21},{8,26},{9,... | collective-permute-start | bytes 196616 | tf_op jit(solution)/shard_map/ppermute | solution.py:1092
  201.9 8.7 %collective-permute-start.61 = (bf16[128,256]{1,0:T(8,128)(2,1)S(1)}, bf16[128,256]{1,0:T(8,128)(2,1)S(1)}, u32[]{:S(2)}, u32[]{:S(2)}) collective-permute-start(bf16[128,256]{1,0:T(8,128)(2,1)S(1)} %slice.38), channel_id=1, source_target_pairs={{0,2},{1,3},{2,0},{3,1},{4,6},{5,7},{6,4},{7,5},{8,10},{9,11},{10,... | collective-permute-start | bytes 196616 | tf_op jit(solution)/shard_map/ppermute | solution.py:1092
  203.4 7.2 %collective-permute-start.59 = (bf16[144,1024]{1,0:T(8,128)(2,1)S(1)}, bf16[144,1024]{1,0:T(8,128)(2,1)S(1)}, u32[]{:S(2)}, u32[]{:S(2)}) collective-permute-start(bf16[144,1024]{1,0:T(8,128)(2,1)S(1)} %shard_map.305.own), channel_id=1, source_target_pairs={{0,1},{1,0},{2,3},{3,2},{4,5},{5,4},{6,7},{7,6},{8,9},{9,8},{10,11... | collective-permute-start | bytes 884744 | tf_op jit(solution)/shard_map/ppermute | solution.py:1092
  (8 other events, 56.5 us)
